TPU v7x, 32 devices: a whole 2x2x4 slice. The times are simulated.
32 devices in a mesh: sens: 4 (over x, core), src: 8 (over z, y).
Axes of the slice: x: 2, y: 2, z: 4, core: 2. Of those that a mesh axis runs over, the one named last changes fastest.
Arguments:
- operator: bfloat16 [128, 2, 512, 1024], P(None, None, 'sens', 'src'), may hold values from -0.375 to 0.375
- right_side: float32 [128, 2, 32, 1024], P('sens', None, None, 'src'), may hold values from -6 to 6
- noise_weights: float32 [128, 512], P('src', 'sens'), may hold values from 0.25 to 4
- damping: float32 [128], P('sens'), may hold values from 1 to 16
Outputs:
- solution: float32 [128, 2, 32, 1024], P('sens', None, None, 'src')
- residual: float32 [128, 2, 32, 1024], P('sens', None, None, 'src')
All inputs are finite; a program needn't handle non-finite values.
Results may differ from a plain program's by a relative error of at most 0.025.
Values may be sent and summed in bfloat16 or wider, within the bound.
No kernel may reach another device: no remote copies, remote signals or barrier semaphores. Data moves between devices by JAX's collectives and lax.ppermute only.
A program may use at most 128 MiB of HBM per device.

v0:
```python
import functools

import jax
import jax.numpy as jnp
from jax import lax
from jax.experimental import pallas as pl
from jax.experimental.pallas import tpu as pltpu
from jax.sharding import PartitionSpec as P

CHUNKS = 2
KERNEL_BYTES = 16 * 2 ** 20
PRODUCT_BYTES = 56 * 2 ** 20
F32 = jnp.float32
BF16 = jnp.bfloat16
ANYWHERE = pl.BlockSpec(memory_space=pl.ANY)
NT = (((1,), (1,)), ((), ()))
NN = (((1,), (0,)), ((), ()))


def largest_divisor(extent, most):
    return next(size for size in range(min(extent, most), 0, -1) if extent % size == 0)


def turned(block, sign):
    half = block.shape[0] // 2
    upper, lower = block[:half], block[half:]
    return jnp.concatenate([-lower, upper] if sign < 0 else [lower, -upper], axis=0)


def forward_rows(vector, near, far):
    left = jnp.concatenate([vector, turned(vector, -1)], axis=1)
    right = jnp.concatenate(
        [jnp.concatenate([part[0], part[1]], axis=1) for part in (near, far)], axis=0
    )
    return lax.dot_general(left, right, NT, preferred_element_type=F32)


def adjoint_rows(field, near, far):
    sensors = near[0].shape[0]
    total = None
    for part, piece in ((near, field[:, :sensors]), (far, field[:, sensors:])):
        left = jnp.concatenate([piece, turned(piece, 1)], axis=1)
        right = jnp.concatenate(part, axis=0)
        term = lax.dot_general(left, right, NN, preferred_element_type=F32)
        total = term if total is None else total + term
    return total


def cost(flops, moved):
    return pl.CostEstimate(flops=flops // 1000, bytes_accessed=moved // 1000, transcendentals=0)


class Plan:
    def __init__(self, operator, right_side, n_sens, n_src, chunks):
        self.freqs, _, self.sensors, self.sources = operator.shape
        self.block = right_side.shape[0]
        self.rows = right_side.shape[1] * right_side.shape[2]
        self.pairs = n_sens // 2
        self.groups = n_src // 2
        self.chunks = chunks
        self.part = self.block // chunks
        self.step = largest_divisor(self.part, 8)
        self.steps = self.part // self.step
        self.flops = 16 * self.part * self.rows * self.sensors * self.sources * 2
        self.piece = self.part * self.rows // self.groups


class Parts:
    def __init__(self, plan, chunk, m, blk_of, refs):
        (whole, far), (near_buf, far_buf, sems) = refs
        self.buffers, self.copies = (near_buf, far_buf), {}
        for phase in range(2):
            for t in range(plan.steps):
                slot = phase * plan.steps + t
                side = m[0] ^ blk_of(phase, m)
                rows = pl.ds(t * plan.step, plan.step)
                near_rows = pl.ds(chunk * plan.part + t * plan.step, plan.step)
                self.copies[phase, t] = [
                    pltpu.make_async_copy(ref, buffer.at[slot], sems.at[slot, place])
                    for place, (ref, buffer) in enumerate((
                        (whole.at[side, m[1], near_rows], near_buf),
                        (far.at[side, rows], far_buf),
                    ))
                ]
        for copies in self.copies.values():
            for copy in copies:
                copy.start()

    def get(self, plan, phase, t):
        for copy in self.copies[phase, t]:
            copy.wait()
        slot = phase * plan.steps + t
        return [
            tuple(tuple(buffer[slot, f, c] for c in range(2)) for buffer in self.buffers)
            for f in range(plan.step)
        ]

    @staticmethod
    def scratch(plan):
        buffer = pltpu.VMEM((2 * plan.steps, plan.step, 2, plan.sensors, plan.sources), BF16)
        return [buffer, buffer, pltpu.SemaphoreType.DMA((2 * plan.steps, 2))]


def cut_call(plan, chunk, meta, whole, wait=()):
    def kernel(m, whole_ref, *refs):
        out_ref, buffer, sems = refs[len(wait):]
        slots = [(side, t) for side in range(plan.pairs) for t in range(plan.steps)]
        ins, outs = [], []
        for slot, (side, t) in enumerate(slots):
            rows = pl.ds(chunk * plan.part + t * plan.step, plan.step)
            ins.append(pltpu.make_async_copy(
                whole_ref.at[side, 1 - m[1], rows], buffer.at[slot], sems.at[0, slot]
            ))
            outs.append(pltpu.make_async_copy(
                buffer.at[slot], out_ref.at[side, pl.ds(t * plan.step, plan.step)], sems.at[1, slot]
            ))
        for copy in ins:
            copy.start()
        for slot in range(len(slots)):
            ins[slot].wait()
            outs[slot].start()
        for copy in outs:
            copy.wait()

    shape = (plan.pairs, plan.part, 2, plan.sensors, plan.sources)
    return pl.pallas_call(
        kernel,
        in_specs=[pl.BlockSpec(memory_space=pltpu.SMEM), ANYWHERE] + [ANYWHERE] * len(wait),
        out_specs=ANYWHERE,
        out_shape=jax.ShapeDtypeStruct(shape, BF16),
        scratch_shapes=[
            pltpu.VMEM((plan.pairs * plan.steps, plan.step) + shape[2:], BF16),
            pltpu.SemaphoreType.DMA((2, plan.pairs * plan.steps)),
        ],
        cost_estimate=cost(0, 8 * plan.part * plan.sensors * plan.sources),
        compiler_params=pltpu.CompilerParams(vmem_limit_bytes=PRODUCT_BYTES),
        name="cut",
    )(meta, whole, *wait)


def cast_call(plan, chunk, start, wait=()):
    shape = (plan.part, plan.rows, plan.sources)

    def kernel(start_ref, *refs):
        out_ref, buffer, sem = refs[len(wait):]
        rows = pl.ds(chunk * plan.part, plan.part)
        copy = pltpu.make_async_copy(start_ref.at[rows], buffer, sem)
        copy.start()
        copy.wait()
        out_ref[...] = buffer[...].astype(BF16)

    return pl.pallas_call(
        kernel,
        in_specs=[ANYWHERE] + [ANYWHERE] * len(wait),
        out_specs=pl.BlockSpec(memory_space=pltpu.VMEM),
        out_shape=jax.ShapeDtypeStruct(shape, BF16),
        scratch_shapes=[pltpu.VMEM(shape, F32), pltpu.SemaphoreType.DMA(())],
        cost_estimate=cost(0, 6 * plan.part * plan.rows * plan.sources),
        compiler_params=pltpu.CompilerParams(vmem_limit_bytes=KERNEL_BYTES),
        name="cast",
    )(start, *wait)


def forward_call(plan, chunk, meta, whole, far, first, vectors, wait=()):
    blk_of = lambda p, m: 1 - (m[2] ^ p)

    def kernel(m, whole, far, one_ref, two_ref, *refs):
        outs, scratch = refs[len(wait):len(wait) + 2], refs[len(wait) + 2:]
        parts = Parts(plan, chunk, m, blk_of, ((whole, far), scratch))
        for phase in range(2):
            blk = blk_of(phase, m)
            for t in range(plan.steps):
                for i, (near_part, far_part) in enumerate(parts.get(plan, phase, t)):
                    f = t * plan.step + i
                    if first:
                        vector = jnp.where(blk == 0, one_ref[f].astype(BF16), two_ref[f])
                    else:
                        vector = one_ref[blk, f].astype(F32) + two_ref[1 - blk, f].astype(F32)
                    outs[phase][f] = forward_rows(vector.astype(BF16), near_part, far_part).astype(BF16)

    size = (plan.part, plan.rows, plan.sources)
    if first:
        vec_specs = [
            pl.BlockSpec(size, lambda i: (chunk, 0, 0)),
            pl.BlockSpec(size, lambda i: (0, 0, 0)),
        ]
    else:
        vec_specs = [pl.BlockSpec((2,) + size, lambda i: (0, 0, 0, 0))] * 2
    shape = (plan.part, plan.rows, 2 * plan.sensors)
    return pl.pallas_call(
        kernel,
        grid=(1,),
        in_specs=[pl.BlockSpec(memory_space=pltpu.SMEM)] + [ANYWHERE] * 2 + vec_specs
        + [ANYWHERE] * len(wait),
        out_specs=[pl.BlockSpec(shape, lambda i: (0, 0, 0))] * 2,
        out_shape=[jax.ShapeDtypeStruct(shape, BF16)] * 2,
        scratch_shapes=Parts.scratch(plan),
        cost_estimate=cost(plan.flops, 16 * plan.part * plan.sensors * plan.sources),
        compiler_params=pltpu.CompilerParams(vmem_limit_bytes=PRODUCT_BYTES),
        name="forward",
    )(meta, whole, far, *vectors, *wait)


def adjoint_call(plan, chunk, meta, whole, far, halves, last, wait=()):
    blk_of = lambda p, m: 1 - p
    n_out = 2 if last else 1

    def kernel(m, whole, far, own_ref, got_ref, *refs):
        outs, scratch = refs[len(wait):len(wait) + n_out], refs[len(wait) + n_out:]
        parts = Parts(plan, chunk, m, blk_of, ((whole, far), scratch))
        for phase in range(2):
            blk = blk_of(phase, m)
            for t in range(plan.steps):
                for i, (near_part, far_part) in enumerate(parts.get(plan, phase, t)):
                    f = t * plan.step + i
                    field = jnp.where(blk == m[2], own_ref[f], got_ref[f])
                    back = adjoint_rows(field, near_part, far_part)
                    if last:
                        outs[phase][f] = back.astype(outs[phase].dtype)
                    else:
                        outs[0][blk, f] = back.astype(BF16)

    size = (plan.part, plan.rows, 2 * plan.sensors)
    shape = (plan.part, plan.rows, plan.sources)
    if last:
        out_specs = [pl.BlockSpec(shape, lambda i: (0, 0, 0))] * 2
        out_shape = [jax.ShapeDtypeStruct(shape, BF16), jax.ShapeDtypeStruct(shape, F32)]
    else:
        out_specs = pl.BlockSpec((2,) + shape, lambda i: (0, 0, 0, 0))
        out_shape = jax.ShapeDtypeStruct((2,) + shape, BF16)
    return pl.pallas_call(
        kernel,
        grid=(1,),
        in_specs=[pl.BlockSpec(memory_space=pltpu.SMEM)] + [ANYWHERE] * 2
        + [pl.BlockSpec(size, lambda i: (0, 0, 0))] * 2 + [ANYWHERE] * len(wait),
        out_specs=out_specs,
        out_shape=out_shape,
        scratch_shapes=Parts.scratch(plan),
        cost_estimate=cost(plan.flops, 16 * plan.part * plan.sensors * plan.sources),
        compiler_params=pltpu.CompilerParams(vmem_limit_bytes=PRODUCT_BYTES),
        name="adjoint",
    )(meta, whole, far, *halves, *wait)


def split_call(plan, meta, keep, got, wait=()):
    piece, groups = plan.piece, plan.groups
    width = keep.shape[-1]

    def kernel(m, keep_ref, got_ref, *refs):
        mine_ref, *sends = refs[len(wait):]
        for d in range(groups):
            place = pl.ds(pl.multiple_of((m[3] ^ d) * piece, piece), piece)
            total = keep_ref[place].astype(F32) + got_ref[place].astype(F32)
            if d == 0:
                mine_ref[...] = total
            else:
                sends[d - 1][...] = total.astype(BF16)

    whole = pl.BlockSpec(memory_space=pltpu.VMEM)
    return pl.pallas_call(
        kernel,
        in_specs=[pl.BlockSpec(memory_space=pltpu.SMEM), whole, whole] + [ANYWHERE] * len(wait),
        out_specs=[whole] * groups,
        out_shape=[jax.ShapeDtypeStruct((piece, width), F32)]
        + [jax.ShapeDtypeStruct((piece, width), BF16)] * (groups - 1),
        cost_estimate=cost(groups * piece * width, groups * piece * width * 8),
        compiler_params=pltpu.CompilerParams(vmem_limit_bytes=KERNEL_BYTES),
        name="split",
    )(meta, keep.reshape(-1, width), got.reshape(-1, width), *wait)


def place_call(plan, meta, pieces, wait=()):
    piece, groups = plan.piece, plan.groups
    width = pieces[0].shape[-1]

    def kernel(m, *refs):
        for d in range(groups):
            place = pl.ds(pl.multiple_of((m[3] ^ d) * piece, piece), piece)
            refs[-1][place] = refs[d][...]

    whole = pl.BlockSpec(memory_space=pltpu.VMEM)
    out = pl.pallas_call(
        kernel,
        in_specs=[pl.BlockSpec(memory_space=pltpu.SMEM)] + [whole] * groups
        + [ANYWHERE] * len(wait),
        out_specs=whole,
        out_shape=jax.ShapeDtypeStruct((groups * piece, width), BF16),
        cost_estimate=cost(0, groups * piece * width * 4),
        compiler_params=pltpu.CompilerParams(vmem_limit_bytes=KERNEL_BYTES),
        name="place",
    )(meta, *pieces, *wait)
    return out.reshape(plan.part, plan.rows, width)


def ordered(array, *earlier):
    def kernel(*refs):
        del refs

    return pl.pallas_call(
        kernel,
        in_specs=[ANYWHERE] * (1 + len(earlier)),
        out_specs=ANYWHERE,
        out_shape=jax.ShapeDtypeStruct(array.shape, array.dtype),
        input_output_aliases={0: 0},
        cost_estimate=cost(0, 0),
        compiler_params=pltpu.CompilerParams(vmem_limit_bytes=KERNEL_BYTES),
        name="ordered",
    )(array, *earlier)


def lanes(array):
    total = jnp.sum(array.reshape(-1, 8, array.shape[-1]), axis=0)
    return sum(total[:, i:i + 128] for i in range(0, array.shape[-1], 128))


def sensor_call(plan, chunk, meta, weights, pieces, norms, alpha=None, damping=None, old=None):
    piece, rows, groups = plan.piece, plan.rows, plan.groups
    width = pieces[0].shape[-1]
    count = max(1, piece // rows)
    high = piece // count
    second = old is not None

    def kernel(m, *refs):
        if second:
            alpha_ref, damp_ref, old_ref, *refs = refs
        weights_ref, norms_ref, *refs = refs
        ins, (out_ref, *more) = refs[:groups], refs[groups:]
        stats_ref = more[-1]
        square = cross = jnp.zeros((8, 128), F32)
        for c in range(count):
            at = pl.ds(c * high, high)
            freq = chunk * plan.part + (m[3] * piece + c * high) // rows
            field = ins[0][at]
            for ref in ins[1:]:
                field = field + ref[at].astype(F32)
            if second:
                factor = 1.0 - alpha_ref[0] * damp_ref[freq]
                field = factor * old_ref[at] - alpha_ref[0] * field
            scaled = weights_ref[pl.ds(freq, 1)] * field
            out_ref[at] = scaled.astype(BF16)
            square = square + lanes(scaled * field)
            if second:
                cross = cross + lanes(scaled * old_ref[at])
            else:
                more[0][at] = field
        stats_ref[0:8] = norms_ref[0:8]
        stats_ref[8:16] = norms_ref[8:16] + square
        stats_ref[16:24] = norms_ref[16:24] + cross

    whole = pl.BlockSpec(memory_space=pltpu.VMEM)
    scalars = pl.BlockSpec(memory_space=pltpu.SMEM)
    first_out = [] if second else [jax.ShapeDtypeStruct((piece, width), F32)]
    extra = (alpha, damping, old) if second else ()
    out_shape = [jax.ShapeDtypeStruct((piece, width), BF16)] + first_out
    out_shape = out_shape + [jax.ShapeDtypeStruct((24, 128), F32)]
    return pl.pallas_call(
        kernel,
        in_specs=[scalars] + ([scalars] * 2 + [whole] if second else []) + [whole] * (2 + groups),
        out_specs=[whole] * len(out_shape),
        out_shape=out_shape,
        cost_estimate=cost(8 * piece * width, 16 * piece * width),
        compiler_params=pltpu.CompilerParams(vmem_limit_bytes=KERNEL_BYTES),
        name="sensor",
    )(meta, *extra, weights, norms, *pieces)


def norms_call(plan, chunk, damping, start):
    block = (plan.part, plan.rows, plan.sources)

    def kernel(damp_ref, start_ref, stats_ref):
        plain = damped = jnp.zeros((8, 128), F32)
        for f in range(plan.part):
            term = lanes(start_ref[f] * start_ref[f])
            plain = plain + term
            damped = damped + damp_ref[chunk * plan.part + f] * term
        stats_ref[0:8] = plain
        stats_ref[8:16] = damped
        stats_ref[16:24] = jnp.zeros((8, 128), F32)

    return pl.pallas_call(
        kernel,
        grid=(1,),
        in_specs=[
            pl.BlockSpec(memory_space=pltpu.SMEM),
            pl.BlockSpec(block, lambda i: (chunk, 0, 0)),
        ],
        out_specs=pl.BlockSpec((24, 128), lambda i: (0, 0)),
        out_shape=jax.ShapeDtypeStruct((24, 128), F32),
        cost_estimate=cost(2 * start.size, 4 * start.size),
        compiler_params=pltpu.CompilerParams(vmem_limit_bytes=KERNEL_BYTES),
        name="norms",
    )(damping, start)


def residual_call(plan, chunk, alpha, damping, start, mine, got):
    part, rows, sources = plan.part, plan.rows, plan.sources

    def kernel(alpha_ref, damp_ref, start_ref, mine_ref, got_ref, image_ref, out_ref, stats_ref):
        plain = damped = mixed = jnp.zeros((8, 128), F32)
        for f in range(part):
            damp = damp_ref[chunk * part + f]
            begin = start_ref[f]
            image = mine_ref[f].astype(F32) + got_ref[f].astype(F32) + damp * begin
            residual = begin - alpha_ref[0] * image
            image_ref[f] = image
            out_ref[f] = residual
            term = lanes(residual * residual)
            plain = plain + term
            damped = damped + damp * term
            mixed = mixed + damp * lanes(residual * begin)
        stats_ref[0:8] = plain
        stats_ref[8:16] = damped
        stats_ref[16:24] = mixed

    block = (part, rows, sources)
    scalars = pl.BlockSpec(memory_space=pltpu.SMEM)
    out = jax.ShapeDtypeStruct(block, F32)
    return pl.pallas_call(
        kernel,
        grid=(1,),
        in_specs=[
            scalars,
            scalars,
            pl.BlockSpec(block, lambda i: (chunk, 0, 0)),
            pl.BlockSpec((None,) + block, lambda i: (0, 0, 0, 0)),
            pl.BlockSpec((None,) + block, lambda i: (1, 0, 0, 0)),
        ],
        out_specs=[
            pl.BlockSpec(block, lambda i: (0, 0, 0)),
            pl.BlockSpec(block, lambda i: (0, 0, 0)),
            pl.BlockSpec((24, 128), lambda i: (0, 0)),
        ],
        out_shape=[out, out, jax.ShapeDtypeStruct((24, 128), F32)],
        cost_estimate=cost(8 * part * rows * sources, 16 * part * rows * sources),
        compiler_params=pltpu.CompilerParams(vmem_limit_bytes=KERNEL_BYTES),
        name="residual",
    )(alpha, damping, start, mine, got)


def body(n_sens, n_src, operator, right_side, noise_weights, damping):
    plan = Plan(operator, right_side, n_sens, n_src, CHUNKS)
    sens, src = lax.axis_index("sens"), lax.axis_index("src")
    pair, core, half, group = sens // 2, sens % 2, src % 2, src // 2
    meta = jnp.stack([pair, core, half, group]).astype(jnp.int32)
    part, rows, block = plan.part, plan.rows, plan.block
    levels = range(n_src.bit_length() - 1)
    chunks = range(plan.chunks)

    def to_core(array):
        return lax.ppermute(array, "sens", [(i, i ^ 1) for i in range(n_sens)])

    def to_pair(array):
        return lax.ppermute(array, "sens", [(i, i ^ 2) for i in range(n_sens)])

    def to_src(array, step):
        return lax.ppermute(array, "src", [(j, j ^ step) for j in range(n_src)])

    def in_turn(arrays, move):
        moved = []
        for k, array in enumerate(arrays):
            if k > 0:
                array = arrays[k] = ordered(array, moved[-1])
            moved.append(move(array))
        return moved

    def total(sums):
        steps = [sums]
        steps.append(steps[-1] + to_core(steps[-1]))
        steps.append(steps[-1] + to_pair(steps[-1]))
        for level in levels:
            steps.append(steps[-1] + to_src(steps[-1], 1 << level))
        return jnp.sum(steps[-1].reshape(-1, 8 * 128), axis=1), steps

    def double(table, level):
        other = to_src(table, 1 << level)
        low = (src >> level) % 2 == 0
        return jnp.concatenate([jnp.where(low, table, other), jnp.where(low, other, table)], axis=0)

    whole = operator.reshape(plan.pairs, 2, block, 2, plan.sensors, plan.sources)
    start = right_side.reshape(block, rows, plan.sources)

    casts = [cast_call(plan, k, start) for k in chunks]
    cuts = [cut_call(plan, k, meta, whole, (casts[0],)) for k in chunks]
    got_b = in_turn(list(casts), to_pair)
    far, pairs = [to_core(cut) for cut in cuts], []
    for k in chunks:
        wait = tuple(casts[1:]) + tuple(cuts[1:]) if k == 0 else ()
        pairs.append(forward_call(plan, k, meta, whole, far[k], True, (start, got_b[k]), wait))
    weights = double(ordered(noise_weights, pairs[-1][0]), 0)

    for level in levels[1:]:
        weights = double(weights, level)
    weights = weights.reshape(plan.pairs, 2, block, plan.sensors)
    weights_near = lax.dynamic_index_in_dim(weights, core, 1, keepdims=False)
    weights_far = to_core(lax.dynamic_index_in_dim(weights, 1 - core, 1, keepdims=False))
    weights = jnp.concatenate([weights_near, weights_far], axis=-1)
    weights = lax.dynamic_index_in_dim(weights, pair ^ half, 0, keepdims=False)
    damping_row = jnp.where(half == 0, damping, to_pair(damping))
    steps = [2 * d for d in range(1, plan.groups)]

    def reduce_field(keep, got, wait=()):
        mine, *sends = split_call(plan, meta, keep, got, wait)
        return [mine] + [to_src(piece, step) for piece, step in zip(sends, steps)]

    def to_half(array):
        return to_src(array, 1)

    def both_products(scaled, scalar_steps, last, then):
        outs, wait = [], ()
        for k in chunks:
            pieces = [scaled[k]] + [to_src(scaled[k], step) for step in steps]
            own = place_call(plan, meta, pieces, wait)
            halves = (own, to_half(own))
            wait = () if k == 0 else (outs[k - 1][1][0], scalar_steps[-1])
            out = adjoint_call(plan, k, meta, whole, far[k], halves, last, wait)
            outs.append((out, then(k, out)))
            wait = (out[0] if last else out, scalar_steps[3])
        return outs

    sends = [send for send, _ in pairs]
    got = in_turn(sends, to_half)
    pieces = [reduce_field(pairs[k][1], got[k], tuple(sends[k + 1:k + 2])) for k in chunks]
    scaled, field, stats = zip(*[
        sensor_call(plan, k, meta, weights, pieces[k], norms_call(plan, k, damping, start))
        for k in chunks
    ])
    sums, steps_0 = total(sum(stats))
    norm_0, curve_0 = sums[0], sums[1]
    alpha_0 = (norm_0 / curve_0)[None]

    def go_on(k, back):
        got = to_pair(back)
        send, keep = forward_call(plan, k, meta, whole, far[k], False, (back, got))
        return send, keep, got

    outs = both_products(scaled, steps_0, False, go_on)
    back = [out for out, _ in outs]
    sends, keeps, got_back = zip(*[rest for _, rest in outs])
    got = in_turn(list(sends), to_half)
    image_0, residual, norms = zip(*[
        residual_call(plan, k, alpha_0, damping, start, back[k], got_back[k]) for k in chunks
    ])
    pieces = [reduce_field(keeps[k], got[k]) for k in chunks]
    scaled, stats = zip(*[
        sensor_call(plan, k, meta, weights, pieces[k], norms[k], alpha_0, damping_row, field[k])
        for k in chunks
    ])
    sums, steps_1 = total(sum(stats))
    norm_1 = sums[0]
    beta = norm_1 / norm_0
    curve_1 = sums[1] + 2.0 * beta * sums[2] + beta * beta * curve_0
    alpha_1 = norm_1 / curve_1

    outs = both_products(scaled, steps_1, True, lambda k, out: (to_pair(out[0]),))
    final = [out[1] + rest[0].astype(F32) for out, rest in outs]
    residual, image_0 = jnp.concatenate(residual), jnp.concatenate(image_0)
    image_1 = jnp.concatenate(final) + damping[:, None, None] * residual + beta * image_0
    solution = alpha_0 * start + alpha_1 * (residual + beta * start)
    residual = residual - alpha_1 * image_1
    return solution.reshape(right_side.shape), residual.reshape(right_side.shape)


def solution(mesh):
    in_specs = (
        P(None, None, "sens", "src"),
        P("sens", None, None, "src"),
        P("src", "sens"),
        P("sens"),
    )
    out_specs = (P("sens", None, None, "src"), P("sens", None, None, "src"))
    shard = functools.partial(body, mesh.shape["sens"], mesh.shape["src"])
    return jax.shard_map(shard, mesh=mesh, in_specs=in_specs, out_specs=out_specs, check_vma=False)
```

profile of v0, /device:TPU:0, one launch (start us, length us, event | category | flops | bytes accessed | tf_op | source)
XLA Modules:
  0.0 248.0 jit_solution(16185584469446889935)
XLA Ops:
  3.9 3.1 %cut.3 = bf16[2,16,2,128,128]{4,3,2,1,0:T(8,128)(2,1)} custom-call(s32[4]{0:T(128)} %pad_add_fusion.m, bf16[2,2,32,2,128,128]{5,4,3,2,1,0:T(8,128)(2,1)} %bitcast.64, bf16[16,64,128]{2,1,0:T(8,128)(2,1)} %copy-done.11), custom_call_target="tpu_custom_call" | custom-call | bytes 2097 | tf_op jit(solution)/shard_map/cut/pallas_call | solution.py:126
  7.6 3.1 %cut.2.refs_1_ = bf16[2,16,2,128,128]{4,3,2,1,0:T(8,128)(2,1)} custom-call(s32[4]{0:T(128)} %pad_add_fusion.m, bf16[2,2,32,2,128,128]{5,4,3,2,1,0:T(8,128)(2,1)} %bitcast.65, bf16[16,64,128]{2,1,0:T(8,128)(2,1)} %copy-done.11), custom_call_target="tpu_custom_call" | custom-call | bytes 2097 | tf_op jit(solution)/shard_map/cut/pallas_call | solution.py:126
  10.9 2.8 %collective-permute-start.1 = (bf16[16,64,128]{2,1,0:T(8,128)(2,1)S(1)}, bf16[16,64,128]{2,1,0:T(8,128)(2,1)S(1)}, u32[]{:S(2)}, u32[]{:S(2)}) collective-permute-start(bf16[16,64,128]{2,1,0:T(8,128)(2,1)S(1)} %copy-done.12), channel_id=1, source_target_pairs={{0,16},{8,24},{16,0},{24,8},{1,17},{9,25},{17,1},{25,9},{2,18},{10... | collective-permute-start | bytes 786440 | tf_op jit(solution)/shard_map/ppermute | solution.py:453
  14.5 5.8 %collective-permute-done.1.refs_1_.two_ref = bf16[16,64,128]{2,1,0:T(8,128)(2,1)S(1)} collective-permute-done((bf16[16,64,128]{2,1,0:T(8,128)(2,1)S(1)}, bf16[16,64,128]{2,1,0:T(8,128)(2,1)S(1)}, u32[]{:S(2)}, u32[]{:S(2)}) %collective-permute-start.1) | collective-permute-done | bytes 262176 | tf_op jit(solution)/shard_map/ppermute | solution.py:453
  22.4 5.0 %forward.5 = (bf16[16,64,256]{2,1,0:T(8,128)(2,1)}, bf16[16,64,256]{2,1,0:T(8,128)(2,1)}) custom-call(s32[4]{0:T(128)} %pad_add_fusion.m, bf16[2,2,32,2,128,128]{5,4,3,2,1,0:T(8,128)(2,1)} %bitcast.66, bf16[2,16,2,128,128]{4,3,2,1,0:T(8,128)(2,1)} %copy-done.47, f32[32,64,128]{2,1,0:T(8,128)} %bitcast.37, bf16[16,64,128]{2,1,0:T(8,128)(2,1)} %copy-done.23, ...), custom_call_target="tpu_custom_call" | custom-call | flops 536870 | bytes 4194 | tf_op jit(solution)/shard_map/forward/pallas_call | solution.py:190
  28.4 1.7 collective-permute-start.2
  30.1 6.1 %collective-permute-done.2.two_ref = bf16[16,64,128]{2,1,0:T(8,128)(2,1)S(1)} collective-permute-done((bf16[16,64,128]{2,1,0:T(8,128)(2,1)S(1)}, bf16[16,64,128]{2,1,0:T(8,128)(2,1)S(1)}, u32[]{:S(2)}, u32[]{:S(2)}) %collective-permute-start.2) | collective-permute-done | bytes 262176 | tf_op jit(solution)/shard_map/ppermute | solution.py:453
  36.9 5.0 %forward.4 = (bf16[16,64,256]{2,1,0:T(8,128)(2,1)}, bf16[16,64,256]{2,1,0:T(8,128)(2,1)}) custom-call(s32[4]{0:T(128)} %pad_add_fusion.m, bf16[2,2,32,2,128,128]{5,4,3,2,1,0:T(8,128)(2,1)} %bitcast.67, bf16[2,16,2,128,128]{4,3,2,1,0:T(8,128)(2,1)} %copy-done.46, f32[32,64,128]{2,1,0:T(8,128)} %bitcast.38, bf16[16,64,128]{2,1,0:T(8,128)(2,1)} %copy-done.52), custom_call_target="tpu_custom_call" | custom-call | flops 536870 | bytes 4194 | tf_op jit(solution)/shard_map/forward/pallas_call | solution.py:190
  44.5 2.2 collective-permute-done.3
  50.4 2.6 %collective-permute-start.5 = (f32[64,128]{1,0:T(8,128)S(1)}, f32[64,128]{1,0:T(8,128)S(1)}, u32[]{:S(2)}, u32[]{:S(2)}) collective-permute-start(f32[64,128]{1,0:T(8,128)S(1)} %pad_maximum_fusion.2), channel_id=1, source_target_pairs={{0,4},{1,5},{2,6},{3,7},{4,0},{5,1},{6,2},{7,3},{8,12},{9,13},{10,... | collective-permute-start | bytes 98312 | tf_op jit(solution)/shard_map/ppermute | solution.py:456
  53.0 2.3 collective-permute-done.5
  55.4 3.5 %collective-permute-done.8.refs_1_ = bf16[16,64,256]{2,1,0:T(8,128)(2,1)S(1)} collective-permute-done((bf16[16,64,256]{2,1,0:T(8,128)(2,1)S(1)}, bf16[16,64,256]{2,1,0:T(8,128)(2,1)S(1)}, u32[]{:S(2)}, u32[]{:S(2)}) %collective-permute-start.8) | collective-permute-done | bytes 524320 | tf_op jit(solution)/shard_map/ppermute | solution.py:456
  63.2 2.6 %collective-permute-start.10 = (bf16[256,256]{1,0:T(8,128)(2,1)}, bf16[256,256]{1,0:T(8,128)(2,1)S(1)}, u32[]{:S(2)}, u32[]{:S(2)}) collective-permute-start(bf16[256,256]{1,0:T(8,128)(2,1)} %get-tuple-element.51), channel_id=1, source_target_pairs={{0,4},{1,5},{2,6},{3,7},{4,0},{5,1},{6,2},{7,3},{8,12},{9,13},{10,... | collective-permute-start | bytes 393224 | tf_op jit(solution)/shard_map/ppermute | solution.py:456
  67.3 6.4 %collective-permute-done.10.refs_4_ = bf16[256,256]{1,0:T(8,128)(2,1)S(1)} collective-permute-done((bf16[256,256]{1,0:T(8,128)(2,1)}, bf16[256,256]{1,0:T(8,128)(2,1)S(1)}, u32[]{:S(2)}, u32[]{:S(2)}) %collective-permute-start.10) | collective-permute-done | bytes 131104 | tf_op jit(solution)/shard_map/ppermute | solution.py:456
  75.5 1.8 collective-permute-start.22
  77.3 1.8 collective-permute-start.23
  83.1 6.6 %collective-permute-done.23.refs_2_ = bf16[256,256]{1,0:T(8,128)(2,1)S(1)} collective-permute-done((bf16[256,256]{1,0:T(8,128)(2,1)S(1)}, bf16[256,256]{1,0:T(8,128)(2,1)S(1)}, u32[]{:S(2)}, u32[]{:S(2)}) %collective-permute-start.23) | collective-permute-done | bytes 131104 | tf_op jit(solution)/shard_map/ppermute | solution.py:456
  91.9 3.6 %collective-permute-done.12 = bf16[16,64,256]{2,1,0:T(8,128)(2,1)S(1)} collective-permute-done((bf16[16,64,256]{2,1,0:T(8,128)(2,1)S(1)}, bf16[16,64,256]{2,1,0:T(8,128)(2,1)S(1)}, u32[]{:S(2)}, u32[]{:S(2)}) %collective-permute-start.12) | collective-permute-done | bytes 524320 | tf_op jit(solution)/shard_map/ppermute | solution.py:456
  96.2 2.7 %collective-permute-start.14 = (bf16[256,256]{1,0:T(8,128)(2,1)S(1)}, bf16[256,256]{1,0:T(8,128)(2,1)S(1)}, u32[]{:S(2)}, u32[]{:S(2)}) collective-permute-start(bf16[256,256]{1,0:T(8,128)(2,1)S(1)} %get-tuple-element.57), channel_id=1, source_target_pairs={{0,4},{1,5},{2,6},{3,7},{4,0},{5,1},{6,2},{7,3},{8,12},{9,13},{10,... | collective-permute-start | bytes 393224 | tf_op jit(solution)/shard_map/ppermute | solution.py:456
  98.8 1.7 collective-permute-start.15
  100.5 4.4 %collective-permute-done.25.got_ref = bf16[16,64,256]{2,1,0:T(8,128)(2,1)S(1)} collective-permute-done((bf16[16,64,256]{2,1,0:T(8,128)(2,1)S(1)}, bf16[16,64,256]{2,1,0:T(8,128)(2,1)S(1)}, u32[]{:S(2)}, u32[]{:S(2)}) %collective-permute-start.25) | collective-permute-done | bytes 524320 | tf_op jit(solution)/shard_map/ppermute | solution.py:456
  105.8 4.5 %adjoint.4.mine_ref.one_ref.refs_4_ = bf16[2,16,64,128]{3,2,1,0:T(8,128)(2,1)} custom-call(s32[4]{0:T(128)} %pad_add_fusion.m, bf16[2,2,32,2,128,128]{5,4,3,2,1,0:T(8,128)(2,1)} %bitcast.68, bf16[2,16,2,128,128]{4,3,2,1,0:T(8,128)(2,1)} %copy-done.47, bf16[16,64,256]{2,1,0:T(8,128)(2,1)} %bitcast.52, bf16[16,64,256]{2,1,0:T(8,128)(2,1)} %copy-done.50), custom_call_target="tpu_custom_call" | custom-call | flops 536870 | bytes 4194 | tf_op jit(solution)/shard_map/adjoint/pallas_call | solution.py:231
  114.3 1.8 collective-permute-start.32
  119.4 3.8 %collective-permute-done.17 = f32[24,128]{1,0:T(8,128)S(1)} collective-permute-done((f32[24,128]{1,0:T(8,128)S(1)}, f32[24,128]{1,0:T(8,128)S(1)}, u32[]{:S(2)}, u32[]{:S(2)}) %collective-permute-start.17) | collective-permute-done | bytes 12320 | tf_op jit(solution)/shard_map/ppermute | solution.py:453
  124.7 2.2 collective-permute-done.18
  130.2 2.5 %collective-permute-done.19 = f32[24,128]{1,0:T(8,128)S(1)} collective-permute-done((f32[24,128]{1,0:T(8,128)S(1)}, f32[24,128]{1,0:T(8,128)S(1)}, u32[]{:S(2)}, u32[]{:S(2)}) %collective-permute-start.19) | collective-permute-done | bytes 12320 | tf_op jit(solution)/shard_map/ppermute | solution.py:456
  132.8 2.8 %collective-permute-start.20 = (f32[24,128]{1,0:T(8,128)S(1)}, f32[24,128]{1,0:T(8,128)S(1)}, u32[]{:S(2)}, u32[]{:S(2)}) collective-permute-start(f32[24,128]{1,0:T(8,128)S(1)} %add.106), channel_id=1, source_target_pairs={{0,4},{1,5},{2,6},{3,7},{4,0},{5,1},{6,2},{7,3},{8,12},{9,13},{10,... | collective-permute-start | bytes 36872 | tf_op jit(solution)/shard_map/ppermute | solution.py:456
  136.4 5.1 %forward.6 = (bf16[16,64,256]{2,1,0:T(8,128)(2,1)}, bf16[16,64,256]{2,1,0:T(8,128)(2,1)}) custom-call(s32[4]{0:T(128)} %pad_add_fusion.m, bf16[2,2,32,2,128,128]{5,4,3,2,1,0:T(8,128)(2,1)} %bitcast.69, bf16[2,16,2,128,128]{4,3,2,1,0:T(8,128)(2,1)} %copy-done.47, bf16[2,16,64,128]{3,2,1,0:T(8,128)(2,1)} %adjoint.4.mine_ref.one_ref.refs_4_, ...), custom_call_target="tpu_custom_call" | custom-call | flops 536870 | bytes 4194 | tf_op jit(solution)/shard_map/forward/pallas_call | solution.py:190
  143.6 4.6 %adjoint.5.mine_ref.one_ref = bf16[2,16,64,128]{3,2,1,0:T(8,128)(2,1)} custom-call(s32[4]{0:T(128)} %pad_add_fusion.m, bf16[2,2,32,2,128,128]{5,4,3,2,1,0:T(8,128)(2,1)} %bitcast.70, bf16[2,16,2,128,128]{4,3,2,1,0:T(8,128)(2,1)} %copy-done.46, bf16[16,64,256]{2,1,0:T(8,128)(2,1)} %bitcast.54, bf16[16,64,256]{2,1,0:T(8,128)(2,1)} %copy-done.51, ...), custom_call_target="tpu_custom_call" | custom-call | flops 536870 | bytes 4194 | tf_op jit(solution)/shard_map/adjoint/pallas_call | solution.py:231
  150.3 2.0 collective-permute-done.27.refs_1_
  155.8 2.9 %collective-permute-start.30 = (bf16[256,256]{1,0:T(8,128)(2,1)}, bf16[256,256]{1,0:T(8,128)(2,1)}, u32[]{:S(2)}, u32[]{:S(2)}) collective-permute-start(bf16[256,256]{1,0:T(8,128)(2,1)} %get-tuple-element.68), channel_id=1, source_target_pairs={{0,6},{1,7},{2,4},{3,5},{4,2},{5,3},{6,0},{7,1},{8,14},{9,15},{10,... | collective-permute-start | bytes 393224 | tf_op jit(solution)/shard_map/ppermute | solution.py:456
  159.5 5.1 %forward.7 = (bf16[16,64,256]{2,1,0:T(8,128)(2,1)}, bf16[16,64,256]{2,1,0:T(8,128)(2,1)}) custom-call(s32[4]{0:T(128)} %pad_add_fusion.m, bf16[2,2,32,2,128,128]{5,4,3,2,1,0:T(8,128)(2,1)} %bitcast.71, bf16[2,16,2,128,128]{4,3,2,1,0:T(8,128)(2,1)} %copy-done.46, bf16[2,16,64,128]{3,2,1,0:T(8,128)(2,1)} %adjoint.5.mine_ref.one_ref, ...), custom_call_target="tpu_custom_call" | custom-call | flops 536870 | bytes 4194 | tf_op jit(solution)/shard_map/forward/pallas_call | solution.py:190
  173.0 2.9 %collective-permute-start.47 = (bf16[256,256]{1,0:T(8,128)(2,1)S(1)}, bf16[256,256]{1,0:T(8,128)(2,1)S(1)}, u32[]{:S(2)}, u32[]{:S(2)}) collective-permute-start(bf16[256,256]{1,0:T(8,128)(2,1)S(1)} %get-tuple-element.82.refs_0_), channel_id=1, source_target_pairs={{0,6},{1,7},{2,4},{3,5},{4,2},{5,3},{6,0},{7,1},{8,14},{9,15},{10,... | collective-permute-start | bytes 393224 | tf_op jit(solution)/shard_map/ppermute | solution.py:456
  175.9 1.8 collective-permute-done.45.refs_1_
  177.7 3.2 %collective-permute-done.46.refs_2_ = bf16[256,256]{1,0:T(8,128)(2,1)S(1)} collective-permute-done((bf16[256,256]{1,0:T(8,128)(2,1)S(1)}, bf16[256,256]{1,0:T(8,128)(2,1)S(1)}, u32[]{:S(2)}, u32[]{:S(2)}) %collective-permute-start.46) | collective-permute-done | bytes 131104 | tf_op jit(solution)/shard_map/ppermute | solution.py:456
  181.5 2.7 %collective-permute-start.48 = (bf16[16,64,256]{2,1,0:T(8,128)(2,1)S(1)}, bf16[16,64,256]{2,1,0:T(8,128)(2,1)S(1)}, u32[]{:S(2)}, u32[]{:S(2)}) collective-permute-start(bf16[16,64,256]{2,1,0:T(8,128)(2,1)S(1)} %bitcast.48), channel_id=1, source_target_pairs={{0,1},{1,0},{2,3},{3,2},{4,5},{5,4},{6,7},{7,6},{8,9},{9,8},{10,11... | collective-permute-start | bytes 1572872 | tf_op jit(solution)/shard_map/ppermute | solution.py:456
  186.4 2.0 collective-permute-start.37
  192.8 7.8 %collective-permute-done.38.refs_7_ = bf16[256,256]{1,0:T(8,128)(2,1)S(1)} collective-permute-done((bf16[256,256]{1,0:T(8,128)(2,1)S(1)}, bf16[256,256]{1,0:T(8,128)(2,1)S(1)}, u32[]{:S(2)}, u32[]{:S(2)}) %collective-permute-start.38) | collective-permute-done | bytes 131104 | tf_op jit(solution)/shard_map/ppermute | solution.py:456
  201.3 2.0 collective-permute-start.50
  207.0 3.7 %collective-permute-done.41 = f32[24,128]{1,0:T(8,128)S(1)} collective-permute-done((f32[24,128]{1,0:T(8,128)S(1)}, f32[24,128]{1,0:T(8,128)S(1)}, u32[]{:S(2)}, u32[]{:S(2)}) %collective-permute-start.41) | collective-permute-done | bytes 12320 | tf_op jit(solution)/shard_map/ppermute | solution.py:453
  211.1 3.3 %collective-permute-done.42 = f32[24,128]{1,0:T(8,128)S(1)} collective-permute-done((f32[24,128]{1,0:T(8,128)S(1)}, f32[24,128]{1,0:T(8,128)S(1)}, u32[]{:S(2)}, u32[]{:S(2)}) %collective-permute-start.42) | collective-permute-done | bytes 12320 | tf_op jit(solution)/shard_map/ppermute | solution.py:456
  215.1 4.5 %adjoint.6 = (bf16[16,64,128]{2,1,0:T(8,128)(2,1)}, f32[16,64,128]{2,1,0:T(8,128)}) custom-call(s32[4]{0:T(128)} %pad_add_fusion.m, bf16[2,2,32,2,128,128]{5,4,3,2,1,0:T(8,128)(2,1)} %bitcast.72, bf16[2,16,2,128,128]{4,3,2,1,0:T(8,128)(2,1)} %copy-done.47, bf16[16,64,256]{2,1,0:T(8,128)(2,1)} %bitcast.49, bf16[16,64,256]{2,1,0:T(8,128)(2,1)} %copy-done.49), custom_call_target="tpu_custom_call" | custom-call | flops 536870 | bytes 4194 | tf_op jit(solution)/shard_map/adjoint/pallas_call | solution.py:231
  222.8 2.6 %collective-permute-done.43 = f32[24,128]{1,0:T(8,128)S(1)} collective-permute-done((f32[24,128]{1,0:T(8,128)S(1)}, f32[24,128]{1,0:T(8,128)S(1)}, u32[]{:S(2)}, u32[]{:S(2)}) %collective-permute-start.43) | collective-permute-done | bytes 12320 | tf_op jit(solution)/shard_map/ppermute | solution.py:456
  225.5 2.0 collective-permute-start.44
  227.5 2.6 %collective-permute-done.44 = f32[24,128]{1,0:T(8,128)S(1)} collective-permute-done((f32[24,128]{1,0:T(8,128)S(1)}, f32[24,128]{1,0:T(8,128)S(1)}, u32[]{:S(2)}, u32[]{:S(2)}) %collective-permute-start.44) | collective-permute-done | bytes 12320 | tf_op jit(solution)/shard_map/ppermute | solution.py:456
  231.0 2.7 %collective-permute-done.53.got_ref = bf16[16,64,256]{2,1,0:T(8,128)(2,1)} collective-permute-done((bf16[16,64,256]{2,1,0:T(8,128)(2,1)S(1)}, bf16[16,64,256]{2,1,0:T(8,128)(2,1)}, u32[]{:S(2)}, u32[]{:S(2)}) %collective-permute-start.53) | collective-permute-done | bytes 524320 | tf_op jit(solution)/shard_map/ppermute | solution.py:456
  233.7 4.5 %adjoint.7 = (bf16[16,64,128]{2,1,0:T(8,128)(2,1)}, f32[16,64,128]{2,1,0:T(8,128)}) custom-call(s32[4]{0:T(128)} %pad_add_fusion.m, bf16[2,2,32,2,128,128]{5,4,3,2,1,0:T(8,128)(2,1)} %bitcast.73, bf16[2,16,2,128,128]{4,3,2,1,0:T(8,128)(2,1)} %copy-done.46, bf16[16,64,256]{2,1,0:T(8,128)(2,1)} %bitcast.46, ...), custom_call_target="tpu_custom_call" | custom-call | flops 536870 | bytes 4194 | tf_op jit(solution)/shard_map/adjoint/pallas_call | solution.py:231
  246.1 1.9 fusion.2
  (234 shorter events, 79.0 us)
Async XLA Ops:
  7.1 13.3 %collective-permute-start.7 = (bf16[2,16,2,128,128]{4,3,2,1,0:T(8,128)(2,1)}, bf16[2,16,2,128,128]{4,3,2,1,0:T(8,128)(2,1)S(1)}, u32[]{:S(2)}, u32[]{:S(2)}) collective-permute-start(bf16[2,16,2,128,128]{4,3,2,1,0:T(8,128)(2,1)} %cut.3), channel_id=1, source_target_pairs={{0,8},{8,0},{16,24},{24,16},{1,9},{9,1},{17,25},{25,17},{2,10},{10... | collective-permute-start | bytes 6291464 | tf_op jit(solution)/shard_map/ppermute | solution.py:450
  10.7 19.4 %collective-permute-start = (bf16[2,16,2,128,128]{4,3,2,1,0:T(8,128)(2,1)}, bf16[2,16,2,128,128]{4,3,2,1,0:T(8,128)(2,1)S(1)}, u32[]{:S(2)}, u32[]{:S(2)}) collective-permute-start(bf16[2,16,2,128,128]{4,3,2,1,0:T(8,128)(2,1)} %cut.2.refs_1_), channel_id=1, source_target_pairs={{0,8},{8,0},{16,24},{24,16},{1,9},{9,1},{17,25},{25,17},{2,10},{10... | collective-permute-start | bytes 6291464 | tf_op jit(solution)/shard_map/ppermute | solution.py:450
  10.9 9.4 %collective-permute-start.1 = (bf16[16,64,128]{2,1,0:T(8,128)(2,1)S(1)}, bf16[16,64,128]{2,1,0:T(8,128)(2,1)S(1)}, u32[]{:S(2)}, u32[]{:S(2)}) collective-permute-start(bf16[16,64,128]{2,1,0:T(8,128)(2,1)S(1)} %copy-done.12), channel_id=1, source_target_pairs={{0,16},{8,24},{16,0},{24,8},{1,17},{9,25},{17,1},{25,9},{2,18},{10... | collective-permute-start | bytes 786440 | tf_op jit(solution)/shard_map/ppermute | solution.py:453
  28.4 7.8 %collective-permute-start.2 = (bf16[16,64,128]{2,1,0:T(8,128)(2,1)S(1)}, bf16[16,64,128]{2,1,0:T(8,128)(2,1)S(1)}, u32[]{:S(2)}, u32[]{:S(2)}) collective-permute-start(bf16[16,64,128]{2,1,0:T(8,128)(2,1)S(1)} %ordered.4), channel_id=1, source_target_pairs={{0,16},{8,24},{16,0},{24,8},{1,17},{9,25},{17,1},{25,9},{2,18},{10... | collective-permute-start | bytes 786440 | tf_op jit(solution)/shard_map/ppermute | solution.py:453
  46.7 3.7 %collective-permute-start.4 = (f32[32,128]{1,0:T(8,128)S(1)}, f32[32,128]{1,0:T(8,128)S(1)}, u32[]{:S(2)}, u32[]{:S(2)}) collective-permute-start(f32[32,128]{1,0:T(8,128)S(1)} %pad_maximum_fusion.3), channel_id=1, source_target_pairs={{0,2},{1,3},{2,0},{3,1},{4,6},{5,7},{6,4},{7,5},{8,10},{9,11},{10,... | collective-permute-start | bytes 49160 | tf_op jit(solution)/shard_map/ppermute | solution.py:456
  48.2 10.8 %collective-permute-start.8 = (bf16[16,64,256]{2,1,0:T(8,128)(2,1)S(1)}, bf16[16,64,256]{2,1,0:T(8,128)(2,1)S(1)}, u32[]{:S(2)}, u32[]{:S(2)}) collective-permute-start(bf16[16,64,256]{2,1,0:T(8,128)(2,1)S(1)} %copy-done.53), channel_id=1, source_target_pairs={{0,1},{1,0},{2,3},{3,2},{4,5},{5,4},{6,7},{7,6},{8,9},{9,8},{10,11... | collective-permute-start | bytes 1572872 | tf_op jit(solution)/shard_map/ppermute | solution.py:456
  50.4 4.9 %collective-permute-start.5 = (f32[64,128]{1,0:T(8,128)S(1)}, f32[64,128]{1,0:T(8,128)S(1)}, u32[]{:S(2)}, u32[]{:S(2)}) collective-permute-start(f32[64,128]{1,0:T(8,128)S(1)} %pad_maximum_fusion.2), channel_id=1, source_target_pairs={{0,4},{1,5},{2,6},{3,7},{4,0},{5,1},{6,2},{7,3},{8,12},{9,13},{10,... | collective-permute-start | bytes 98312 | tf_op jit(solution)/shard_map/ppermute | solution.py:456
  55.4 12.0 %collective-permute-start.6 = (f32[2,32,128]{2,1,0:T(8,128)S(1)}, f32[2,32,128]{2,1,0:T(8,128)S(1)}, u32[]{:S(2)}, u32[]{:S(2)}) collective-permute-start(f32[2,32,128]{2,1,0:T(8,128)S(1)} %get-tuple-element.96), channel_id=1, source_target_pairs={{0,8},{8,0},{16,24},{24,16},{1,9},{9,1},{17,25},{25,17},{2,10},{10... | collective-permute-start | bytes 98312 | tf_op jit(solution)/shard_map/ppermute | solution.py:450
  63.2 10.5 %collective-permute-start.10 = (bf16[256,256]{1,0:T(8,128)(2,1)}, bf16[256,256]{1,0:T(8,128)(2,1)S(1)}, u32[]{:S(2)}, u32[]{:S(2)}) collective-permute-start(bf16[256,256]{1,0:T(8,128)(2,1)} %get-tuple-element.51), channel_id=1, source_target_pairs={{0,4},{1,5},{2,6},{3,7},{4,0},{5,1},{6,2},{7,3},{8,12},{9,13},{10,... | collective-permute-start | bytes 393224 | tf_op jit(solution)/shard_map/ppermute | solution.py:456
  65.8 8.0 %collective-permute-start.11 = (bf16[256,256]{1,0:T(8,128)(2,1)}, bf16[256,256]{1,0:T(8,128)(2,1)S(1)}, u32[]{:S(2)}, u32[]{:S(2)}) collective-permute-start(bf16[256,256]{1,0:T(8,128)(2,1)} %get-tuple-element.52), channel_id=1, source_target_pairs={{0,6},{1,7},{2,4},{3,5},{4,2},{5,3},{6,0},{7,1},{8,14},{9,15},{10,... | collective-permute-start | bytes 393224 | tf_op jit(solution)/shard_map/ppermute | solution.py:456
  66.4 7.7 %collective-permute-start.9 = (bf16[256,256]{1,0:T(8,128)(2,1)}, bf16[256,256]{1,0:T(8,128)(2,1)S(1)}, u32[]{:S(2)}, u32[]{:S(2)}) collective-permute-start(bf16[256,256]{1,0:T(8,128)(2,1)} %get-tuple-element.50), channel_id=1, source_target_pairs={{0,2},{1,3},{2,0},{3,1},{4,6},{5,7},{6,4},{7,5},{8,10},{9,11},{10,... | collective-permute-start | bytes 393224 | tf_op jit(solution)/shard_map/ppermute | solution.py:456
  75.5 7.6 %collective-permute-start.22 = (bf16[256,256]{1,0:T(8,128)(2,1)S(1)}, bf16[256,256]{1,0:T(8,128)(2,1)S(1)}, u32[]{:S(2)}, u32[]{:S(2)}) collective-permute-start(bf16[256,256]{1,0:T(8,128)(2,1)S(1)} %get-tuple-element.61.refs_0_), channel_id=1, source_target_pairs={{0,2},{1,3},{2,0},{3,1},{4,6},{5,7},{6,4},{7,5},{8,10},{9,11},{10,... | collective-permute-start | bytes 393224 | tf_op jit(solution)/shard_map/ppermute | solution.py:456
  77.3 12.4 %collective-permute-start.23 = (bf16[256,256]{1,0:T(8,128)(2,1)S(1)}, bf16[256,256]{1,0:T(8,128)(2,1)S(1)}, u32[]{:S(2)}, u32[]{:S(2)}) collective-permute-start(bf16[256,256]{1,0:T(8,128)(2,1)S(1)} %get-tuple-element.61.refs_0_), channel_id=1, source_target_pairs={{0,4},{1,5},{2,6},{3,7},{4,0},{5,1},{6,2},{7,3},{8,12},{9,13},{10,... | collective-permute-start | bytes 393224 | tf_op jit(solution)/shard_map/ppermute | solution.py:456
  79.1 10.6 %collective-permute-start.24 = (bf16[256,256]{1,0:T(8,128)(2,1)S(1)}, bf16[256,256]{1,0:T(8,128)(2,1)S(1)}, u32[]{:S(2)}, u32[]{:S(2)}) collective-permute-start(bf16[256,256]{1,0:T(8,128)(2,1)S(1)} %get-tuple-element.61.refs_0_), channel_id=1, source_target_pairs={{0,6},{1,7},{2,4},{3,5},{4,2},{5,3},{6,0},{7,1},{8,14},{9,15},{10,... | collective-permute-start | bytes 393224 | tf_op jit(solution)/shard_map/ppermute | solution.py:456
  80.6 14.9 %collective-permute-start.12 = (bf16[16,64,256]{2,1,0:T(8,128)(2,1)S(1)}, bf16[16,64,256]{2,1,0:T(8,128)(2,1)S(1)}, u32[]{:S(2)}, u32[]{:S(2)}) collective-permute-start(bf16[16,64,256]{2,1,0:T(8,128)(2,1)S(1)} %copy-done.9), channel_id=1, source_target_pairs={{0,1},{1,0},{2,3},{3,2},{4,5},{5,4},{6,7},{7,6},{8,9},{9,8},{10,11... | collective-permute-start | bytes 1572872 | tf_op jit(solution)/shard_map/ppermute | solution.py:456
  90.3 14.7 %collective-permute-start.25 = (bf16[16,64,256]{2,1,0:T(8,128)(2,1)S(1)}, bf16[16,64,256]{2,1,0:T(8,128)(2,1)S(1)}, u32[]{:S(2)}, u32[]{:S(2)}) collective-permute-start(bf16[16,64,256]{2,1,0:T(8,128)(2,1)S(1)} %bitcast.51), channel_id=1, source_target_pairs={{0,1},{1,0},{2,3},{3,2},{4,5},{5,4},{6,7},{7,6},{8,9},{9,8},{10,11... | collective-permute-start | bytes 1572872 | tf_op jit(solution)/shard_map/ppermute | solution.py:456
  96.1 16.4 %collective-permute-start.13 = (bf16[256,256]{1,0:T(8,128)(2,1)S(1)}, bf16[256,256]{1,0:T(8,128)(2,1)S(1)}, u32[]{:S(2)}, u32[]{:S(2)}) collective-permute-start(bf16[256,256]{1,0:T(8,128)(2,1)S(1)} %get-tuple-element.56), channel_id=1, source_target_pairs={{0,2},{1,3},{2,0},{3,1},{4,6},{5,7},{6,4},{7,5},{8,10},{9,11},{10,... | collective-permute-start | bytes 393224 | tf_op jit(solution)/shard_map/ppermute | solution.py:456
  96.2 16.3 %collective-permute-start.14 = (bf16[256,256]{1,0:T(8,128)(2,1)S(1)}, bf16[256,256]{1,0:T(8,128)(2,1)S(1)}, u32[]{:S(2)}, u32[]{:S(2)}) collective-permute-start(bf16[256,256]{1,0:T(8,128)(2,1)S(1)} %get-tuple-element.57), channel_id=1, source_target_pairs={{0,4},{1,5},{2,6},{3,7},{4,0},{5,1},{6,2},{7,3},{8,12},{9,13},{10,... | collective-permute-start | bytes 393224 | tf_op jit(solution)/shard_map/ppermute | solution.py:456
  98.8 13.7 %collective-permute-start.15 = (bf16[256,256]{1,0:T(8,128)(2,1)S(1)}, bf16[256,256]{1,0:T(8,128)(2,1)S(1)}, u32[]{:S(2)}, u32[]{:S(2)}) collective-permute-start(bf16[256,256]{1,0:T(8,128)(2,1)S(1)} %get-tuple-element.58), channel_id=1, source_target_pairs={{0,6},{1,7},{2,4},{3,5},{4,2},{5,3},{6,0},{7,1},{8,14},{9,15},{10,... | collective-permute-start | bytes 393224 | tf_op jit(solution)/shard_map/ppermute | solution.py:456
  110.3 25.3 %collective-permute-start.26 = (bf16[2,16,64,128]{3,2,1,0:T(8,128)(2,1)}, bf16[2,16,64,128]{3,2,1,0:T(8,128)(2,1)S(1)}, u32[]{:S(2)}, u32[]{:S(2)}) collective-permute-start(bf16[2,16,64,128]{3,2,1,0:T(8,128)(2,1)} %adjoint.4.mine_ref.one_ref.refs_4_), channel_id=1, source_target_pairs={{0,16},{8,24},{16,0},{24,8},{1,17},{9,25},{17,1},{25,9},{2,18},{10... | collective-permute-start | bytes 1572872 | tf_op jit(solution)/shard_map/ppermute | solution.py:453
  113.2 13.7 %collective-permute-start.31 = (bf16[256,256]{1,0:T(8,128)(2,1)S(1)}, bf16[256,256]{1,0:T(8,128)(2,1)S(1)}, u32[]{:S(2)}, u32[]{:S(2)}) collective-permute-start(bf16[256,256]{1,0:T(8,128)(2,1)S(1)} %get-tuple-element.71.refs_0_), channel_id=1, source_target_pairs={{0,2},{1,3},{2,0},{3,1},{4,6},{5,7},{6,4},{7,5},{8,10},{9,11},{10,... | collective-permute-start | bytes 393224 | tf_op jit(solution)/shard_map/ppermute | solution.py:456
  114.3 12.5 %collective-permute-start.32 = (bf16[256,256]{1,0:T(8,128)(2,1)S(1)}, bf16[256,256]{1,0:T(8,128)(2,1)S(1)}, u32[]{:S(2)}, u32[]{:S(2)}) collective-permute-start(bf16[256,256]{1,0:T(8,128)(2,1)S(1)} %get-tuple-element.71.refs_0_), channel_id=1, source_target_pairs={{0,4},{1,5},{2,6},{3,7},{4,0},{5,1},{6,2},{7,3},{8,12},{9,13},{10,... | collective-permute-start | bytes 393224 | tf_op jit(solution)/shard_map/ppermute | solution.py:456
  116.2 10.7 %collective-permute-start.33 = (bf16[256,256]{1,0:T(8,128)(2,1)S(1)}, bf16[256,256]{1,0:T(8,128)(2,1)S(1)}, u32[]{:S(2)}, u32[]{:S(2)}) collective-permute-start(bf16[256,256]{1,0:T(8,128)(2,1)S(1)} %get-tuple-element.71.refs_0_), channel_id=1, source_target_pairs={{0,6},{1,7},{2,4},{3,5},{4,2},{5,3},{6,0},{7,1},{8,14},{9,15},{10,... | collective-permute-start | bytes 393224 | tf_op jit(solution)/shard_map/ppermute | solution.py:456
  118.8 4.3 %collective-permute-start.17 = (f32[24,128]{1,0:T(8,128)S(1)}, f32[24,128]{1,0:T(8,128)S(1)}, u32[]{:S(2)}, u32[]{:S(2)}) collective-permute-start(f32[24,128]{1,0:T(8,128)S(1)} %add.103), channel_id=1, source_target_pairs={{0,16},{8,24},{16,0},{24,8},{1,17},{9,25},{17,1},{25,9},{2,18},{10... | collective-permute-start | bytes 36872 | tf_op jit(solution)/shard_map/ppermute | solution.py:453
  127.5 15.3 %collective-permute-start.34 = (bf16[16,64,256]{2,1,0:T(8,128)(2,1)S(1)}, bf16[16,64,256]{2,1,0:T(8,128)(2,1)S(1)}, u32[]{:S(2)}, u32[]{:S(2)}) collective-permute-start(bf16[16,64,256]{2,1,0:T(8,128)(2,1)S(1)} %bitcast.53), channel_id=1, source_target_pairs={{0,1},{1,0},{2,3},{3,2},{4,5},{5,4},{6,7},{7,6},{8,9},{9,8},{10,11... | collective-permute-start | bytes 1572872 | tf_op jit(solution)/shard_map/ppermute | solution.py:456
  132.8 9.3 %collective-permute-start.20 = (f32[24,128]{1,0:T(8,128)S(1)}, f32[24,128]{1,0:T(8,128)S(1)}, u32[]{:S(2)}, u32[]{:S(2)}) collective-permute-start(f32[24,128]{1,0:T(8,128)S(1)} %add.106), channel_id=1, source_target_pairs={{0,4},{1,5},{2,6},{3,7},{4,0},{5,1},{6,2},{7,3},{8,12},{9,13},{10,... | collective-permute-start | bytes 36872 | tf_op jit(solution)/shard_map/ppermute | solution.py:456
  141.5 10.7 %collective-permute-start.27 = (bf16[16,64,256]{2,1,0:T(8,128)(2,1)}, bf16[16,64,256]{2,1,0:T(8,128)(2,1)S(1)}, u32[]{:S(2)}, u32[]{:S(2)}) collective-permute-start(bf16[16,64,256]{2,1,0:T(8,128)(2,1)} %get-tuple-element.64.refs_0_), channel_id=1, source_target_pairs={{0,1},{1,0},{2,3},{3,2},{4,5},{5,4},{6,7},{7,6},{8,9},{9,8},{10,11... | collective-permute-start | bytes 1572872 | tf_op jit(solution)/shard_map/ppermute | solution.py:456
  148.2 10.5 %collective-permute-start.35 = (bf16[2,16,64,128]{3,2,1,0:T(8,128)(2,1)}, bf16[2,16,64,128]{3,2,1,0:T(8,128)(2,1)S(1)}, u32[]{:S(2)}, u32[]{:S(2)}) collective-permute-start(bf16[2,16,64,128]{3,2,1,0:T(8,128)(2,1)} %adjoint.5.mine_ref.one_ref), channel_id=1, source_target_pairs={{0,16},{8,24},{16,0},{24,8},{1,17},{9,25},{17,1},{25,9},{2,18},{10... | collective-permute-start | bytes 1572872 | tf_op jit(solution)/shard_map/ppermute | solution.py:453
  149.8 16.4 %collective-permute-start.21 = (f32[32]{0:T(128)S(1)}, f32[32]{0:T(128)S(1)}, u32[]{:S(2)}, u32[]{:S(2)}) collective-permute-start(f32[32]{0:T(128)S(1)} %copy-done.45), channel_id=1, source_target_pairs={{0,16},{8,24},{16,0},{24,8},{1,17},{9,25},{17,1},{25,9},{2,18},{10... | collective-permute-start | bytes 392 | tf_op jit(solution)/shard_map/ppermute | solution.py:453
  154.3 14.8 %collective-permute-start.28 = (bf16[256,256]{1,0:T(8,128)(2,1)}, bf16[256,256]{1,0:T(8,128)(2,1)}, u32[]{:S(2)}, u32[]{:S(2)}) collective-permute-start(bf16[256,256]{1,0:T(8,128)(2,1)} %get-tuple-element.66), channel_id=1, source_target_pairs={{0,2},{1,3},{2,0},{3,1},{4,6},{5,7},{6,4},{7,5},{8,10},{9,11},{10,... | collective-permute-start | bytes 393224 | tf_op jit(solution)/shard_map/ppermute | solution.py:456
  154.6 14.5 %collective-permute-start.29 = (bf16[256,256]{1,0:T(8,128)(2,1)}, bf16[256,256]{1,0:T(8,128)(2,1)}, u32[]{:S(2)}, u32[]{:S(2)}) collective-permute-start(bf16[256,256]{1,0:T(8,128)(2,1)} %get-tuple-element.67), channel_id=1, source_target_pairs={{0,4},{1,5},{2,6},{3,7},{4,0},{5,1},{6,2},{7,3},{8,12},{9,13},{10,... | collective-permute-start | bytes 393224 | tf_op jit(solution)/shard_map/ppermute | solution.py:456
  155.8 13.3 %collective-permute-start.30 = (bf16[256,256]{1,0:T(8,128)(2,1)}, bf16[256,256]{1,0:T(8,128)(2,1)}, u32[]{:S(2)}, u32[]{:S(2)}) collective-permute-start(bf16[256,256]{1,0:T(8,128)(2,1)} %get-tuple-element.68), channel_id=1, source_target_pairs={{0,6},{1,7},{2,4},{3,5},{4,2},{5,3},{6,0},{7,1},{8,14},{9,15},{10,... | collective-permute-start | bytes 393224 | tf_op jit(solution)/shard_map/ppermute | solution.py:456
  164.6 19.5 %collective-permute-start.36 = (bf16[16,64,256]{2,1,0:T(8,128)(2,1)}, bf16[16,64,256]{2,1,0:T(8,128)(2,1)}, u32[]{:S(2)}, u32[]{:S(2)}) collective-permute-start(bf16[16,64,256]{2,1,0:T(8,128)(2,1)} %ordered.7), channel_id=1, source_target_pairs={{0,1},{1,0},{2,3},{3,2},{4,5},{5,4},{6,7},{7,6},{8,9},{9,8},{10,11... | collective-permute-start | bytes 1572872 | tf_op jit(solution)/shard_map/ppermute | solution.py:456
  171.4 6.3 %collective-permute-start.45 = (bf16[256,256]{1,0:T(8,128)(2,1)S(1)}, bf16[256,256]{1,0:T(8,128)(2,1)S(1)}, u32[]{:S(2)}, u32[]{:S(2)}) collective-permute-start(bf16[256,256]{1,0:T(8,128)(2,1)S(1)} %get-tuple-element.82.refs_0_), channel_id=1, source_target_pairs={{0,2},{1,3},{2,0},{3,1},{4,6},{5,7},{6,4},{7,5},{8,10},{9,11},{10,... | collective-permute-start | bytes 393224 | tf_op jit(solution)/shard_map/ppermute | solution.py:456
  171.8 9.1 %collective-permute-start.46 = (bf16[256,256]{1,0:T(8,128)(2,1)S(1)}, bf16[256,256]{1,0:T(8,128)(2,1)S(1)}, u32[]{:S(2)}, u32[]{:S(2)}) collective-permute-start(bf16[256,256]{1,0:T(8,128)(2,1)S(1)} %get-tuple-element.82.refs_0_), channel_id=1, source_target_pairs={{0,4},{1,5},{2,6},{3,7},{4,0},{5,1},{6,2},{7,3},{8,12},{9,13},{10,... | collective-permute-start | bytes 393224 | tf_op jit(solution)/shard_map/ppermute | solution.py:456
  173.0 7.9 %collective-permute-start.47 = (bf16[256,256]{1,0:T(8,128)(2,1)S(1)}, bf16[256,256]{1,0:T(8,128)(2,1)S(1)}, u32[]{:S(2)}, u32[]{:S(2)}) collective-permute-start(bf16[256,256]{1,0:T(8,128)(2,1)S(1)} %get-tuple-element.82.refs_0_), channel_id=1, source_target_pairs={{0,6},{1,7},{2,4},{3,5},{4,2},{5,3},{6,0},{7,1},{8,14},{9,15},{10,... | collective-permute-start | bytes 393224 | tf_op jit(solution)/shard_map/ppermute | solution.py:456
  181.5 32.9 %collective-permute-start.48 = (bf16[16,64,256]{2,1,0:T(8,128)(2,1)S(1)}, bf16[16,64,256]{2,1,0:T(8,128)(2,1)S(1)}, u32[]{:S(2)}, u32[]{:S(2)}) collective-permute-start(bf16[16,64,256]{2,1,0:T(8,128)(2,1)S(1)} %bitcast.48), channel_id=1, source_target_pairs={{0,1},{1,0},{2,3},{3,2},{4,5},{5,4},{6,7},{7,6},{8,9},{9,8},{10,11... | collective-permute-start | bytes 1572872 | tf_op jit(solution)/shard_map/ppermute | solution.py:456
  186.4 6.4 %collective-permute-start.37 = (bf16[256,256]{1,0:T(8,128)(2,1)S(1)}, bf16[256,256]{1,0:T(8,128)(2,1)S(1)}, u32[]{:S(2)}, u32[]{:S(2)}) collective-permute-start(bf16[256,256]{1,0:T(8,128)(2,1)S(1)} %get-tuple-element.76), channel_id=1, source_target_pairs={{0,2},{1,3},{2,0},{3,1},{4,6},{5,7},{6,4},{7,5},{8,10},{9,11},{10,... | collective-permute-start | bytes 393224 | tf_op jit(solution)/shard_map/ppermute | solution.py:456
  188.4 12.2 %collective-permute-start.38 = (bf16[256,256]{1,0:T(8,128)(2,1)S(1)}, bf16[256,256]{1,0:T(8,128)(2,1)S(1)}, u32[]{:S(2)}, u32[]{:S(2)}) collective-permute-start(bf16[256,256]{1,0:T(8,128)(2,1)S(1)} %get-tuple-element.77), channel_id=1, source_target_pairs={{0,4},{1,5},{2,6},{3,7},{4,0},{5,1},{6,2},{7,3},{8,12},{9,13},{10,... | collective-permute-start | bytes 393224 | tf_op jit(solution)/shard_map/ppermute | solution.py:456
  189.5 11.1 %collective-permute-start.39 = (bf16[256,256]{1,0:T(8,128)(2,1)S(1)}, bf16[256,256]{1,0:T(8,128)(2,1)S(1)}, u32[]{:S(2)}, u32[]{:S(2)}) collective-permute-start(bf16[256,256]{1,0:T(8,128)(2,1)S(1)} %get-tuple-element.78), channel_id=1, source_target_pairs={{0,6},{1,7},{2,4},{3,5},{4,2},{5,3},{6,0},{7,1},{8,14},{9,15},{10,... | collective-permute-start | bytes 393224 | tf_op jit(solution)/shard_map/ppermute | solution.py:456
  201.3 18.4 %collective-permute-start.50 = (bf16[256,256]{1,0:T(8,128)(2,1)S(1)}, bf16[256,256]{1,0:T(8,128)(2,1)S(1)}, u32[]{:S(2)}, u32[]{:S(2)}) collective-permute-start(bf16[256,256]{1,0:T(8,128)(2,1)S(1)} %get-tuple-element.85.refs_0_), channel_id=1, source_target_pairs={{0,2},{1,3},{2,0},{3,1},{4,6},{5,7},{6,4},{7,5},{8,10},{9,11},{10,... | collective-permute-start | bytes 393224 | tf_op jit(solution)/shard_map/ppermute | solution.py:456
  203.3 16.4 %collective-permute-start.51 = (bf16[256,256]{1,0:T(8,128)(2,1)S(1)}, bf16[256,256]{1,0:T(8,128)(2,1)S(1)}, u32[]{:S(2)}, u32[]{:S(2)}) collective-permute-start(bf16[256,256]{1,0:T(8,128)(2,1)S(1)} %get-tuple-element.85.refs_0_), channel_id=1, source_target_pairs={{0,4},{1,5},{2,6},{3,7},{4,0},{5,1},{6,2},{7,3},{8,12},{9,13},{10,... | collective-permute-start | bytes 393224 | tf_op jit(solution)/shard_map/ppermute | solution.py:456
  204.4 15.3 %collective-permute-start.52 = (bf16[256,256]{1,0:T(8,128)(2,1)S(1)}, bf16[256,256]{1,0:T(8,128)(2,1)S(1)}, u32[]{:S(2)}, u32[]{:S(2)}) collective-permute-start(bf16[256,256]{1,0:T(8,128)(2,1)S(1)} %get-tuple-element.85.refs_0_), channel_id=1, source_target_pairs={{0,6},{1,7},{2,4},{3,5},{4,2},{5,3},{6,0},{7,1},{8,14},{9,15},{10,... | collective-permute-start | bytes 393224 | tf_op jit(solution)/shard_map/ppermute | solution.py:456
  206.9 3.7 %collective-permute-start.41 = (f32[24,128]{1,0:T(8,128)S(1)}, f32[24,128]{1,0:T(8,128)S(1)}, u32[]{:S(2)}, u32[]{:S(2)}) collective-permute-start(f32[24,128]{1,0:T(8,128)S(1)} %add.109), channel_id=1, source_target_pairs={{0,16},{8,24},{16,0},{24,8},{1,17},{9,25},{17,1},{25,9},{2,18},{10... | collective-permute-start | bytes 36872 | tf_op jit(solution)/shard_map/ppermute | solution.py:453
  221.3 12.5 %collective-permute-start.53 = (bf16[16,64,256]{2,1,0:T(8,128)(2,1)S(1)}, bf16[16,64,256]{2,1,0:T(8,128)(2,1)}, u32[]{:S(2)}, u32[]{:S(2)}) collective-permute-start(bf16[16,64,256]{2,1,0:T(8,128)(2,1)S(1)} %bitcast.45), channel_id=1, source_target_pairs={{0,1},{1,0},{2,3},{3,2},{4,5},{5,4},{6,7},{7,6},{8,9},{9,8},{10,11... | collective-permute-start | bytes 1572872 | tf_op jit(solution)/shard_map/ppermute | solution.py:456
  221.8 9.2 %collective-permute-start.49 = (bf16[16,64,128]{2,1,0:T(8,128)(2,1)S(1)}, bf16[16,64,128]{2,1,0:T(8,128)(2,1)S(1)}, u32[]{:S(2)}, u32[]{:S(2)}) collective-permute-start(bf16[16,64,128]{2,1,0:T(8,128)(2,1)S(1)} %copy-done.38), channel_id=1, source_target_pairs={{0,16},{8,24},{16,0},{24,8},{1,17},{9,25},{17,1},{25,9},{2,18},{10... | collective-permute-start | bytes 786440 | tf_op jit(solution)/shard_map/ppermute | solution.py:453
  225.5 4.6 %collective-permute-start.44 = (f32[24,128]{1,0:T(8,128)S(1)}, f32[24,128]{1,0:T(8,128)S(1)}, u32[]{:S(2)}, u32[]{:S(2)}) collective-permute-start(f32[24,128]{1,0:T(8,128)S(1)} %add.112), channel_id=1, source_target_pairs={{0,4},{1,5},{2,6},{3,7},{4,0},{5,1},{6,2},{7,3},{8,12},{9,13},{10,... | collective-permute-start | bytes 36872 | tf_op jit(solution)/shard_map/ppermute | solution.py:456
  238.3 6.6 %collective-permute-start.54 = (bf16[16,64,128]{2,1,0:T(8,128)(2,1)}, bf16[16,64,128]{2,1,0:T(8,128)(2,1)S(1)}, u32[]{:S(2)}, u32[]{:S(2)}) collective-permute-start(bf16[16,64,128]{2,1,0:T(8,128)(2,1)} %get-tuple-element.87), channel_id=1, source_target_pairs={{0,16},{8,24},{16,0},{24,8},{1,17},{9,25},{17,1},{25,9},{2,18},{10... | collective-permute-start | bytes 786440 | tf_op jit(solution)/shard_map/ppermute | solution.py:453
  (61 other events, 505.9 us)
where the time goes:
time: 249 us; the launch traced here: 248 us
  waiting for transfers between devices  84.6 us (34%)
  starting transfers between devices  71.3 us (29%)
  Pallas kernels  57.4 us (23%)
  local copies, waits for them, and re-layouts  21.7 us (9%)
  between operations  6.51 us (3%)
  other arithmetic  6.5 us (3%)
    ppermute x41, waiting for transfers between devices, to_src(): return lax.ppermute(array, 'src', [(j, j ^ step) for j in range(n_src)])  62.2 us
    ppermute x41, starting transfers between devices, to_src(): return lax.ppermute(array, 'src', [(j, j ^ step) for j in range(n_src)])  61.3 us
    unnamed x109, local copies, waits for them, and re-layouts  20.3 us
    pallas_call x4, Pallas kernels, forward_call(): pl.pallas_call(kernel, grid=(1,), in_specs=[pl.BlockSpec(memory_space=plt...  20.2 us
    ppermute x9, waiting for transfers between devices, to_pair(): return lax.ppermute(array, 'sens', [(i, i ^ 2) for i in range(n_sens)])  20 us
    pallas_call x4, Pallas kernels, adjoint_call(): pl.pallas_call(kernel, grid=(1,), in_specs=[pl.BlockSpec(memory_space=plt...  18.2 us
    ppermute x9, starting transfers between devices, to_pair(): return lax.ppermute(array, 'sens', [(i, i ^ 2) for i in range(n_sens)])  9.08 us
    pallas_call x2, Pallas kernels, cut_call(): pl.pallas_call(kernel, in_specs=[pl.BlockSpec(memory_space=pltpu.SMEM), A...  6.2 us
  transfers between devices with their start and end apart: 55, of which 28 were waited for; matrix products, arithmetic and copies ran while one was open for 2% of the time, Pallas kernels for 18%

commit v1 on v0

--- a/solution.py
+++ b/solution.py
@@ -82,14 +82,20 @@
                         (far.at[side, rows], far_buf),
                     ))
                 ]
-        for copies in self.copies.values():
-            for copy in copies:
-                copy.start()
+        self.order = list(self.copies)
+        for slot in self.order[:2]:
+            self.start(slot)
+
+    def start(self, slot):
+        for copy in self.copies[slot]:
+            copy.start()
 
     def get(self, plan, phase, t):
         for copy in self.copies[phase, t]:
             copy.wait()
         slot = phase * plan.steps + t
+        for later in self.order[slot + 2:slot + 3]:
+            self.start(later)
         return [
             tuple(tuple(buffer[slot, f, c] for c in range(2)) for buffer in self.buffers)
             for f in range(plan.step)
@@ -313,7 +319,9 @@
     return sum(total[:, i:i + 128] for i in range(0, array.shape[-1], 128))
 
 
-def sensor_call(plan, chunk, meta, weights, pieces, norms, alpha=None, damping=None, old=None):
+def sensor_call(
+    plan, chunk, meta, weights, pieces, norms, alpha=None, damping=None, old=None, wait=()
+):
     piece, rows, groups = plan.piece, plan.rows, plan.groups
     width = pieces[0].shape[-1]
     count = max(1, piece // rows)
@@ -324,7 +332,7 @@
         if second:
             alpha_ref, damp_ref, old_ref, *refs = refs
         weights_ref, norms_ref, *refs = refs
-        ins, (out_ref, *more) = refs[:groups], refs[groups:]
+        ins, (out_ref, *more) = refs[:groups], refs[groups + len(wait):]
         stats_ref = more[-1]
         square = cross = jnp.zeros((8, 128), F32)
         for c in range(count):
@@ -355,13 +363,14 @@
     out_shape = out_shape + [jax.ShapeDtypeStruct((24, 128), F32)]
     return pl.pallas_call(
         kernel,
-        in_specs=[scalars] + ([scalars] * 2 + [whole] if second else []) + [whole] * (2 + groups),
+        in_specs=[scalars] + ([scalars] * 2 + [whole] if second else []) + [whole] * (2 + groups)
+        + [ANYWHERE] * len(wait),
         out_specs=[whole] * len(out_shape),
         out_shape=out_shape,
         cost_estimate=cost(8 * piece * width, 16 * piece * width),
         compiler_params=pltpu.CompilerParams(vmem_limit_bytes=KERNEL_BYTES),
         name="sensor",
-    )(meta, *extra, weights, norms, *pieces)
+    )(meta, *extra, weights, norms, *pieces, *wait)
 
 
 def norms_call(plan, chunk, damping, start):
@@ -463,13 +472,15 @@
             moved.append(move(array))
         return moved
 
-    def total(sums):
-        steps = [sums]
-        steps.append(steps[-1] + to_core(steps[-1]))
-        steps.append(steps[-1] + to_pair(steps[-1]))
-        for level in levels:
-            steps.append(steps[-1] + to_src(steps[-1], 1 << level))
-        return jnp.sum(steps[-1].reshape(-1, 8 * 128), axis=1), steps
+    def total_near(sums):
+        sums = sums + to_core(sums)
+        sums = sums + to_pair(sums)
+        return sums + to_src(sums, 1)
+
+    def total_far(sums):
+        for level in levels[1:]:
+            sums = sums + to_src(sums, 1 << level)
+        return sums, jnp.sum(sums.reshape(-1, 8 * 128), axis=1)
 
     def double(table, level):
         other = to_src(table, 1 << level)
@@ -482,13 +493,15 @@
     casts = [cast_call(plan, k, start) for k in chunks]
     cuts = [cut_call(plan, k, meta, whole, (casts[0],)) for k in chunks]
     got_b = in_turn(list(casts), to_pair)
+    weights = noise_weights
+    for level in levels[:2]:
+        weights = double(weights, level)
     far, pairs = [to_core(cut) for cut in cuts], []
     for k in chunks:
-        wait = tuple(casts[1:]) + tuple(cuts[1:]) if k == 0 else ()
+        wait = tuple(casts[1:]) + tuple(cuts[1:]) + (weights,) if k == 0 else ()
         pairs.append(forward_call(plan, k, meta, whole, far[k], True, (start, got_b[k]), wait))
-    weights = double(ordered(noise_weights, pairs[-1][0]), 0)
-
-    for level in levels[1:]:
+
+    for level in levels[2:]:
         weights = double(weights, level)
     weights = weights.reshape(plan.pairs, 2, block, plan.sensors)
     weights_near = lax.dynamic_index_in_dim(weights, core, 1, keepdims=False)
@@ -505,35 +518,41 @@
     def to_half(array):
         return to_src(array, 1)
 
-    def both_products(scaled, scalar_steps, last, then):
-        outs, wait = [], ()
+    def both_products(scaled, near_sums, last, then):
+        outs, wait, sums = [], (), None
         for k in chunks:
             pieces = [scaled[k]] + [to_src(scaled[k], step) for step in steps]
             own = place_call(plan, meta, pieces, wait)
             halves = (own, to_half(own))
-            wait = () if k == 0 else (outs[k - 1][1][0], scalar_steps[-1])
-            out = adjoint_call(plan, k, meta, whole, far[k], halves, last, wait)
+            if k == 1:
+                after = outs[0][1][0]
+                far_sums, sums = total_far(near_sums if last else ordered(near_sums, after))
+                wait = (after, far_sums)
+            out = adjoint_call(plan, k, meta, whole, far[k], halves, last, wait if k > 0 else ())
             outs.append((out, then(k, out)))
-            wait = (out[0] if last else out, scalar_steps[3])
-        return outs
+            wait = (out[0] if last else out, near_sums)
+        return outs, total_far(near_sums)[1] if sums is None else sums
 
     sends = [send for send, _ in pairs]
     got = in_turn(sends, to_half)
     pieces = [reduce_field(pairs[k][1], got[k], tuple(sends[k + 1:k + 2])) for k in chunks]
     scaled, field, stats = zip(*[
-        sensor_call(plan, k, meta, weights, pieces[k], norms_call(plan, k, damping, start))
+        sensor_call(
+            plan, k, meta, weights, pieces[k], norms_call(plan, k, damping, start),
+            wait=tuple(got[k + 1:k + 2]),
+        )
         for k in chunks
     ])
-    sums, steps_0 = total(sum(stats))
-    norm_0, curve_0 = sums[0], sums[1]
-    alpha_0 = (norm_0 / curve_0)[None]
+    near_0 = total_near(sum(stats))
 
     def go_on(k, back):
         got = to_pair(back)
         send, keep = forward_call(plan, k, meta, whole, far[k], False, (back, got))
         return send, keep, got
 
-    outs = both_products(scaled, steps_0, False, go_on)
+    outs, sums = both_products(scaled, near_0, False, go_on)
+    norm_0, curve_0 = sums[0], sums[1]
+    alpha_0 = (norm_0 / curve_0)[None]
     back = [out for out, _ in outs]
     sends, keeps, got_back = zip(*[rest for _, rest in outs])
     got = in_turn(list(sends), to_half)
@@ -545,13 +564,13 @@
         sensor_call(plan, k, meta, weights, pieces[k], norms[k], alpha_0, damping_row, field[k])
         for k in chunks
     ])
-    sums, steps_1 = total(sum(stats))
+    near_1 = total_near(sum(stats))
+    outs, sums = both_products(scaled, near_1, True, lambda k, out: (to_pair(out[0]),))
     norm_1 = sums[0]
     beta = norm_1 / norm_0
     curve_1 = sums[1] + 2.0 * beta * sums[2] + beta * beta * curve_0
     alpha_1 = norm_1 / curve_1
 
-    outs = both_products(scaled, steps_1, True, lambda k, out: (to_pair(out[0]),))
     final = [out[1] + rest[0].astype(F32) for out, rest in outs]
     residual, image_0 = jnp.concatenate(residual), jnp.concatenate(image_0)
     image_1 = jnp.concatenate(final) + damping[:, None, None] * residual + beta * image_0

time: 249 us -> 239 us (0.960)
  waiting for transfers between devices: 84.6 us -> 72.2 us
  local copies, waits for them, and re-layouts: 21.7 us -> 17.2 us
  Pallas kernels: 57.4 us -> 60.9 us
  starting transfers between devices: 71.3 us -> 73.9 us
    ppermute x41, waiting for transfers between devices: 62.2 us -> 55.3 us  [to_src(): return lax.ppermute(array, 'src', [(j, j ^ step) for j in range(n_src)])]
    ppermute x9, waiting for transfers between devices: 20 us -> 14.5 us  [to_pair(): return lax.ppermute(array, 'sens', [(i, i ^ 2) for i in range(n_sens)])]
    unnamed x109 -> x92, local copies, waits for them, and re-layouts: 20.3 us -> 15.7 us
    pallas_call x4, Pallas kernels: 18.2 us -> 21 us  [adjoint_call(): pl.pallas_call(kernel, grid=(1,), in_specs=[pl.BlockSpec(memory_space=plt...]
  transfers between devices with their start and end apart: 55 -> 55, of which waited for: 28 -> 24; matrix products, arithmetic and copies ran while one was open for 2% -> 2% of each run, Pallas kernels for 18% -> 21%
where the time goes in v1:
time: 239 us; the launch traced here: 238 us
  starting transfers between devices  73.9 us (31%)
  waiting for transfers between devices  72.2 us (30%)
  Pallas kernels  60.9 us (25%)
  local copies, waits for them, and re-layouts  17.2 us (7%)
  other arithmetic  7.11 us (3%)
  between operations  6.75 us (3%)
    ppermute x41, starting transfers between devices, to_src(): return lax.ppermute(array, 'src', [(j, j ^ step) for j in range(n_src)])  62.2 us
    ppermute x41, waiting for transfers between devices, to_src(): return lax.ppermute(array, 'src', [(j, j ^ step) for j in range(n_src)])  55.3 us
    pallas_call x4, Pallas kernels, forward_call(): pl.pallas_call(kernel, grid=(1,), in_specs=[pl.BlockSpec(memory_space=plt...  21.6 us
    pallas_call x4, Pallas kernels, adjoint_call(): pl.pallas_call(kernel, grid=(1,), in_specs=[pl.BlockSpec(memory_space=plt...  21 us
    unnamed x92, local copies, waits for them, and re-layouts  15.7 us
    ppermute x9, waiting for transfers between devices, to_pair(): return lax.ppermute(array, 'sens', [(i, i ^ 2) for i in range(n_sens)])  14.5 us
    ppermute x9, starting transfers between devices, to_pair(): return lax.ppermute(array, 'sens', [(i, i ^ 2) for i in range(n_sens)])  10.8 us
    pallas_call x2, Pallas kernels, cut_call(): pl.pallas_call(kernel, in_specs=[pl.BlockSpec(memory_space=pltpu.SMEM), A...  6.27 us
  transfers between devices with their start and end apart: 55, of which 24 were waited for; matrix products, arithmetic and copies ran while one was open for 2% of the time, Pallas kernels for 21%

profile of v1, /device:TPU:0, one launch (start us, length us, event | category | flops | bytes accessed | tf_op | source)
XLA Modules:
  0.0 238.1 jit_solution(9771639813417631854)
XLA Ops:
  3.3 3.2 %cut.2 = bf16[2,16,2,128,128]{4,3,2,1,0:T(8,128)(2,1)} custom-call(s32[4]{0:T(128)} %pad_add_fusion.m, bf16[2,2,32,2,128,128]{5,4,3,2,1,0:T(8,128)(2,1)} %bitcast.64, bf16[16,64,128]{2,1,0:T(8,128)(2,1)} %copy-done.6), custom_call_target="tpu_custom_call" | custom-call | bytes 2097 | tf_op jit(solution)/shard_map/cut/pallas_call | solution.py:132
  7.0 3.1 %cut.3.refs_1_ = bf16[2,16,2,128,128]{4,3,2,1,0:T(8,128)(2,1)} custom-call(s32[4]{0:T(128)} %pad_add_fusion.m, bf16[2,2,32,2,128,128]{5,4,3,2,1,0:T(8,128)(2,1)} %bitcast.65, bf16[16,64,128]{2,1,0:T(8,128)(2,1)} %copy-done.6), custom_call_target="tpu_custom_call" | custom-call | bytes 2097 | tf_op jit(solution)/shard_map/cut/pallas_call | solution.py:132
  10.4 2.8 %collective-permute-start = (f32[16,128]{1,0:T(8,128)S(1)}, f32[16,128]{1,0:T(8,128)S(1)}, u32[]{:S(2)}, u32[]{:S(2)}) collective-permute-start(f32[16,128]{1,0:T(8,128)S(1)} %copy-done.45), channel_id=1, source_target_pairs={{0,1},{1,0},{2,3},{3,2},{4,5},{5,4},{6,7},{7,6},{8,9},{9,8},{10,11... | collective-permute-start | bytes 24584 | tf_op jit(solution)/shard_map/ppermute | solution.py:465
  14.9 2.1 collective-permute-start.1
  19.8 4.0 %collective-permute-done.5.two_ref.refs_1_ = bf16[16,64,128]{2,1,0:T(8,128)(2,1)S(1)} collective-permute-done((bf16[16,64,128]{2,1,0:T(8,128)(2,1)S(1)}, bf16[16,64,128]{2,1,0:T(8,128)(2,1)S(1)}, u32[]{:S(2)}, u32[]{:S(2)}) %collective-permute-start.5) | collective-permute-done | bytes 262176 | tf_op jit(solution)/shard_map/ppermute | solution.py:462
  24.6 5.4 %forward.4 = (bf16[16,64,256]{2,1,0:T(8,128)(2,1)}, bf16[16,64,256]{2,1,0:T(8,128)(2,1)}) custom-call(s32[4]{0:T(128)} %pad_add_fusion.m, bf16[2,2,32,2,128,128]{5,4,3,2,1,0:T(8,128)(2,1)} %bitcast.66, bf16[2,16,2,128,128]{4,3,2,1,0:T(8,128)(2,1)} %collective-permute-done.4.far, f32[32,64,128]{2,1,0:T(8,128)} %bitcast.37, bf16[16,64,128]{2,1,0:T(8,128)(2,1)} %copy-done.18, ...), custom_call_target="tpu_custom_call" | custom-call | flops 536870 | bytes 4194 | tf_op jit(solution)/shard_map/forward/pallas_call | solution.py:196
  34.0 2.6 %collective-permute-start.2 = (f32[64,128]{1,0:T(8,128)S(1)}, f32[64,128]{1,0:T(8,128)S(1)}, u32[]{:S(2)}, u32[]{:S(2)}) collective-permute-start(f32[64,128]{1,0:T(8,128)S(1)} %copy-done.44), channel_id=1, source_target_pairs={{0,4},{1,5},{2,6},{3,7},{4,0},{5,1},{6,2},{7,3},{8,12},{9,13},{10,... | collective-permute-start | bytes 98312 | tf_op jit(solution)/shard_map/ppermute | solution.py:465
  36.6 2.3 collective-permute-done.8.two_ref
  39.6 5.4 %forward.5 = (bf16[16,64,256]{2,1,0:T(8,128)(2,1)}, bf16[16,64,256]{2,1,0:T(8,128)(2,1)}) custom-call(s32[4]{0:T(128)} %pad_add_fusion.m, bf16[2,2,32,2,128,128]{5,4,3,2,1,0:T(8,128)(2,1)} %bitcast.67, bf16[2,16,2,128,128]{4,3,2,1,0:T(8,128)(2,1)} %collective-permute-done.7.far, f32[32,64,128]{2,1,0:T(8,128)} %bitcast.38, bf16[16,64,128]{2,1,0:T(8,128)(2,1)} %copy-done.43), custom_call_target="tpu_custom_call" | custom-call | flops 536870 | bytes 4194 | tf_op jit(solution)/shard_map/forward/pallas_call | solution.py:196
  47.2 2.6 %collective-permute-start.10 = (bf16[256,256]{1,0:T(8,128)(2,1)S(1)}, bf16[256,256]{1,0:T(8,128)(2,1)S(1)}, u32[]{:S(2)}, u32[]{:S(2)}) collective-permute-start(bf16[256,256]{1,0:T(8,128)(2,1)S(1)} %get-tuple-element.51), channel_id=1, source_target_pairs={{0,4},{1,5},{2,6},{3,7},{4,0},{5,1},{6,2},{7,3},{8,12},{9,13},{10,... | collective-permute-start | bytes 393224 | tf_op jit(solution)/shard_map/ppermute | solution.py:465
  51.8 3.4 %collective-permute-done.9.refs_3_ = bf16[256,256]{1,0:T(8,128)(2,1)S(1)} collective-permute-done((bf16[256,256]{1,0:T(8,128)(2,1)S(1)}, bf16[256,256]{1,0:T(8,128)(2,1)S(1)}, u32[]{:S(2)}, u32[]{:S(2)}) %collective-permute-start.9) | collective-permute-done | bytes 131104 | tf_op jit(solution)/shard_map/ppermute | solution.py:465
  55.2 4.9 %collective-permute-done.11.refs_5_ = bf16[256,256]{1,0:T(8,128)(2,1)S(1)} collective-permute-done((bf16[256,256]{1,0:T(8,128)(2,1)S(1)}, bf16[256,256]{1,0:T(8,128)(2,1)S(1)}, u32[]{:S(2)}, u32[]{:S(2)}) %collective-permute-start.11) | collective-permute-done | bytes 131104 | tf_op jit(solution)/shard_map/ppermute | solution.py:465
  61.5 2.9 %collective-permute-start.21 = (bf16[256,256]{1,0:T(8,128)(2,1)S(1)}, bf16[256,256]{1,0:T(8,128)(2,1)S(1)}, u32[]{:S(2)}, u32[]{:S(2)}) collective-permute-start(bf16[256,256]{1,0:T(8,128)(2,1)S(1)} %get-tuple-element.60.refs_0_), channel_id=1, source_target_pairs={{0,6},{1,7},{2,4},{3,5},{4,2},{5,3},{6,0},{7,1},{8,14},{9,15},{10,... | collective-permute-start | bytes 393224 | tf_op jit(solution)/shard_map/ppermute | solution.py:465
  66.5 1.9 collective-permute-done.21.refs_3_
  68.3 8.1 %collective-permute-done.20.refs_2_ = bf16[256,256]{1,0:T(8,128)(2,1)S(1)} collective-permute-done((bf16[256,256]{1,0:T(8,128)(2,1)S(1)}, bf16[256,256]{1,0:T(8,128)(2,1)S(1)}, u32[]{:S(2)}, u32[]{:S(2)}) %collective-permute-start.20) | collective-permute-done | bytes 131104 | tf_op jit(solution)/shard_map/ppermute | solution.py:465
  77.1 1.9 collective-permute-start.22
  79.7 3.2 %collective-permute-start.14 = (bf16[256,256]{1,0:T(8,128)(2,1)S(1)}, bf16[256,256]{1,0:T(8,128)(2,1)S(1)}, u32[]{:S(2)}, u32[]{:S(2)}) collective-permute-start(bf16[256,256]{1,0:T(8,128)(2,1)S(1)} %get-tuple-element.57), channel_id=1, source_target_pairs={{0,4},{1,5},{2,6},{3,7},{4,0},{5,1},{6,2},{7,3},{8,12},{9,13},{10,... | collective-permute-start | bytes 393224 | tf_op jit(solution)/shard_map/ppermute | solution.py:465
  84.1 7.0 %collective-permute-done.22.got_ref = bf16[16,64,256]{2,1,0:T(8,128)(2,1)S(1)} collective-permute-done((bf16[16,64,256]{2,1,0:T(8,128)(2,1)S(1)}, bf16[16,64,256]{2,1,0:T(8,128)(2,1)S(1)}, u32[]{:S(2)}, u32[]{:S(2)}) %collective-permute-start.22) | collective-permute-done | bytes 524320 | tf_op jit(solution)/shard_map/ppermute | solution.py:465
  91.9 5.2 %adjoint.4.one_ref.mine_ref.refs_4_ = bf16[2,16,64,128]{3,2,1,0:T(8,128)(2,1)} custom-call(s32[4]{0:T(128)} %pad_add_fusion.m, bf16[2,2,32,2,128,128]{5,4,3,2,1,0:T(8,128)(2,1)} %bitcast.68, bf16[2,16,2,128,128]{4,3,2,1,0:T(8,128)(2,1)} %collective-permute-done.4.far, bf16[16,64,256]{2,1,0:T(8,128)(2,1)} %bitcast.52, bf16[16,64,256]{2,1,0:T(8,128)(2,1)} %copy-done.41), custom_call_target="tpu_custom_call" | custom-call | flops 536870 | bytes 4194 | tf_op jit(solution)/shard_map/adjoint/pallas_call | solution.py:237
  99.9 2.6 %collective-permute-start.33 = (bf16[256,256]{1,0:T(8,128)(2,1)S(1)}, bf16[256,256]{1,0:T(8,128)(2,1)S(1)}, u32[]{:S(2)}, u32[]{:S(2)}) collective-permute-start(bf16[256,256]{1,0:T(8,128)(2,1)S(1)} %get-tuple-element.71.refs_0_), channel_id=1, source_target_pairs={{0,6},{1,7},{2,4},{3,5},{4,2},{5,3},{6,0},{7,1},{8,14},{9,15},{10,... | collective-permute-start | bytes 393224 | tf_op jit(solution)/shard_map/ppermute | solution.py:465
  102.5 1.8 collective-permute-start.31
  106.1 4.6 %collective-permute-done.17 = f32[24,128]{1,0:T(8,128)S(1)} collective-permute-done((f32[24,128]{1,0:T(8,128)S(1)}, f32[24,128]{1,0:T(8,128)S(1)}, u32[]{:S(2)}, u32[]{:S(2)}) %collective-permute-start.17) | collective-permute-done | bytes 12320 | tf_op jit(solution)/shard_map/ppermute | solution.py:462
  112.4 2.0 collective-permute-done.18
  115.0 1.7 collective-permute-start.34
  117.5 5.4 %forward.6 = (bf16[16,64,256]{2,1,0:T(8,128)(2,1)}, bf16[16,64,256]{2,1,0:T(8,128)(2,1)}) custom-call(s32[4]{0:T(128)} %pad_add_fusion.m, bf16[2,2,32,2,128,128]{5,4,3,2,1,0:T(8,128)(2,1)} %bitcast.69, bf16[2,16,2,128,128]{4,3,2,1,0:T(8,128)(2,1)} %collective-permute-done.4.far, bf16[2,16,64,128]{3,2,1,0:T(8,128)(2,1)} %adjoint.4.one_ref.mine_ref.refs_4_, ...), custom_call_target="tpu_custom_call" | custom-call | flops 536870 | bytes 4194 | tf_op jit(solution)/shard_map/forward/pallas_call | solution.py:196
  123.1 3.7 %collective-permute-done.24 = f32[24,128]{1,0:T(8,128)S(1)} collective-permute-done((f32[24,128]{1,0:T(8,128)S(1)}, f32[24,128]{1,0:T(8,128)S(1)}, u32[]{:S(2)}, u32[]{:S(2)}) %collective-permute-start.24) | collective-permute-done | bytes 12320 | tf_op jit(solution)/shard_map/ppermute | solution.py:465
  127.9 3.5 %collective-permute-done.25 = f32[24,128]{1,0:T(8,128)S(1)} collective-permute-done((f32[24,128]{1,0:T(8,128)S(1)}, f32[24,128]{1,0:T(8,128)S(1)}, u32[]{:S(2)}, u32[]{:S(2)}) %collective-permute-start.25) | collective-permute-done | bytes 12320 | tf_op jit(solution)/shard_map/ppermute | solution.py:465
  133.0 5.2 %adjoint.5.mine_ref.one_ref = bf16[2,16,64,128]{3,2,1,0:T(8,128)(2,1)} custom-call(s32[4]{0:T(128)} %pad_add_fusion.m, bf16[2,2,32,2,128,128]{5,4,3,2,1,0:T(8,128)(2,1)} %bitcast.70, bf16[2,16,2,128,128]{4,3,2,1,0:T(8,128)(2,1)} %collective-permute-done.7.far, bf16[16,64,256]{2,1,0:T(8,128)(2,1)} %bitcast.55, bf16[16,64,256]{2,1,0:T(8,128)(2,1)} %copy-done.42, ...), custom_call_target="tpu_custom_call" | custom-call | flops 536870 | bytes 4194 | tf_op jit(solution)/shard_map/adjoint/pallas_call | solution.py:237
  142.4 2.9 %collective-permute-start.29 = (bf16[256,256]{1,0:T(8,128)(2,1)}, bf16[256,256]{1,0:T(8,128)(2,1)}, u32[]{:S(2)}, u32[]{:S(2)}) collective-permute-start(bf16[256,256]{1,0:T(8,128)(2,1)} %get-tuple-element.67), channel_id=1, source_target_pairs={{0,4},{1,5},{2,6},{3,7},{4,0},{5,1},{6,2},{7,3},{8,12},{9,13},{10,... | collective-permute-start | bytes 393224 | tf_op jit(solution)/shard_map/ppermute | solution.py:465
  148.5 5.4 %forward.7 = (bf16[16,64,256]{2,1,0:T(8,128)(2,1)}, bf16[16,64,256]{2,1,0:T(8,128)(2,1)}) custom-call(s32[4]{0:T(128)} %pad_add_fusion.m, bf16[2,2,32,2,128,128]{5,4,3,2,1,0:T(8,128)(2,1)} %bitcast.71, bf16[2,16,2,128,128]{4,3,2,1,0:T(8,128)(2,1)} %collective-permute-done.7.far, bf16[2,16,64,128]{3,2,1,0:T(8,128)(2,1)} %adjoint.5.mine_ref.one_ref, ...), custom_call_target="tpu_custom_call" | custom-call | flops 536870 | bytes 4194 | tf_op jit(solution)/shard_map/forward/pallas_call | solution.py:196
  160.7 2.3 collective-permute-start.47
  162.9 2.2 collective-permute-start.45
  165.1 2.5 %collective-permute-done.47.refs_3_ = bf16[256,256]{1,0:T(8,128)(2,1)S(1)} collective-permute-done((bf16[256,256]{1,0:T(8,128)(2,1)S(1)}, bf16[256,256]{1,0:T(8,128)(2,1)S(1)}, u32[]{:S(2)}, u32[]{:S(2)}) %collective-permute-start.47) | collective-permute-done | bytes 131104 | tf_op jit(solution)/shard_map/ppermute | solution.py:465
  167.6 2.7 %collective-permute-done.46.refs_2_ = bf16[256,256]{1,0:T(8,128)(2,1)S(1)} collective-permute-done((bf16[256,256]{1,0:T(8,128)(2,1)S(1)}, bf16[256,256]{1,0:T(8,128)(2,1)S(1)}, u32[]{:S(2)}, u32[]{:S(2)}) %collective-permute-start.46) | collective-permute-done | bytes 131104 | tf_op jit(solution)/shard_map/ppermute | solution.py:465
  170.9 3.3 %collective-permute-start.48 = (bf16[16,64,256]{2,1,0:T(8,128)(2,1)S(1)}, bf16[16,64,256]{2,1,0:T(8,128)(2,1)S(1)}, u32[]{:S(2)}, u32[]{:S(2)}) collective-permute-start(bf16[16,64,256]{2,1,0:T(8,128)(2,1)S(1)} %bitcast.48), channel_id=1, source_target_pairs={{0,1},{1,0},{2,3},{3,2},{4,5},{5,4},{6,7},{7,6},{8,9},{9,8},{10,11... | collective-permute-start | bytes 1572872 | tf_op jit(solution)/shard_map/ppermute | solution.py:465
  177.0 2.8 %collective-permute-start.38 = (bf16[256,256]{1,0:T(8,128)(2,1)S(1)}, bf16[256,256]{1,0:T(8,128)(2,1)S(1)}, u32[]{:S(2)}, u32[]{:S(2)}) collective-permute-start(bf16[256,256]{1,0:T(8,128)(2,1)S(1)} %get-tuple-element.77), channel_id=1, source_target_pairs={{0,4},{1,5},{2,6},{3,7},{4,0},{5,1},{6,2},{7,3},{8,12},{9,13},{10,... | collective-permute-start | bytes 393224 | tf_op jit(solution)/shard_map/ppermute | solution.py:465
  184.0 5.3 %collective-permute-done.38.refs_7_ = bf16[256,256]{1,0:T(8,128)(2,1)S(1)} collective-permute-done((bf16[256,256]{1,0:T(8,128)(2,1)S(1)}, bf16[256,256]{1,0:T(8,128)(2,1)S(1)}, u32[]{:S(2)}, u32[]{:S(2)}) %collective-permute-start.38) | collective-permute-done | bytes 131104 | tf_op jit(solution)/shard_map/ppermute | solution.py:465
  189.9 2.4 collective-permute-start.52
  192.3 1.9 collective-permute-start.51
  196.7 2.6 %collective-permute-done.41 = f32[24,128]{1,0:T(8,128)S(1)} collective-permute-done((f32[24,128]{1,0:T(8,128)S(1)}, f32[24,128]{1,0:T(8,128)S(1)}, u32[]{:S(2)}, u32[]{:S(2)}) %collective-permute-start.41) | collective-permute-done | bytes 12320 | tf_op jit(solution)/shard_map/ppermute | solution.py:462
  200.0 2.9 %collective-permute-done.42 = f32[24,128]{1,0:T(8,128)S(1)} collective-permute-done((f32[24,128]{1,0:T(8,128)S(1)}, f32[24,128]{1,0:T(8,128)S(1)}, u32[]{:S(2)}, u32[]{:S(2)}) %collective-permute-start.42) | collective-permute-done | bytes 12320 | tf_op jit(solution)/shard_map/ppermute | solution.py:465
  203.8 5.3 %adjoint.6 = (bf16[16,64,128]{2,1,0:T(8,128)(2,1)}, f32[16,64,128]{2,1,0:T(8,128)}) custom-call(s32[4]{0:T(128)} %pad_add_fusion.m, bf16[2,2,32,2,128,128]{5,4,3,2,1,0:T(8,128)(2,1)} %bitcast.72, bf16[2,16,2,128,128]{4,3,2,1,0:T(8,128)(2,1)} %collective-permute-done.4.far, bf16[16,64,256]{2,1,0:T(8,128)(2,1)} %bitcast.49, bf16[16,64,256]{2,1,0:T(8,128)(2,1)} %copy-done.40), custom_call_target="tpu_custom_call" | custom-call | flops 536870 | bytes 4194 | tf_op jit(solution)/shard_map/adjoint/pallas_call | solution.py:237
  213.0 1.7 collective-permute-start.43
  214.8 2.0 collective-permute-done.43
  216.7 2.9 %collective-permute-start.44 = (f32[24,128]{1,0:T(8,128)S(1)}, f32[24,128]{1,0:T(8,128)S(1)}, u32[]{:S(2)}, u32[]{:S(2)}) collective-permute-start(f32[24,128]{1,0:T(8,128)S(1)} %add.112), channel_id=1, source_target_pairs={{0,4},{1,5},{2,6},{3,7},{4,0},{5,1},{6,2},{7,3},{8,12},{9,13},{10,... | collective-permute-start | bytes 36872 | tf_op jit(solution)/shard_map/ppermute | solution.py:465
  219.6 1.7 collective-permute-done.44
  222.9 5.2 %adjoint.7 = (bf16[16,64,128]{2,1,0:T(8,128)(2,1)}, f32[16,64,128]{2,1,0:T(8,128)}) custom-call(s32[4]{0:T(128)} %pad_add_fusion.m, bf16[2,2,32,2,128,128]{5,4,3,2,1,0:T(8,128)(2,1)} %bitcast.73, bf16[2,16,2,128,128]{4,3,2,1,0:T(8,128)(2,1)} %collective-permute-done.7.far, bf16[16,64,256]{2,1,0:T(8,128)(2,1)} %bitcast.46, ...), custom_call_target="tpu_custom_call" | custom-call | flops 536870 | bytes 4194 | tf_op jit(solution)/shard_map/adjoint/pallas_call | solution.py:237
  236.2 1.9 fusion.2
  (217 shorter events, 69.0 us)
Async XLA Ops:
  6.5 17.4 %collective-permute-start.4 = (bf16[2,16,2,128,128]{4,3,2,1,0:T(8,128)(2,1)}, bf16[2,16,2,128,128]{4,3,2,1,0:T(8,128)(2,1)}, u32[]{:S(2)}, u32[]{:S(2)}) collective-permute-start(bf16[2,16,2,128,128]{4,3,2,1,0:T(8,128)(2,1)} %cut.2), channel_id=1, source_target_pairs={{0,8},{8,0},{16,24},{24,16},{1,9},{9,1},{17,25},{25,17},{2,10},{10... | collective-permute-start | bytes 6291464 | tf_op jit(solution)/shard_map/ppermute | solution.py:459
  10.1 26.5 %collective-permute-start.7 = (bf16[2,16,2,128,128]{4,3,2,1,0:T(8,128)(2,1)}, bf16[2,16,2,128,128]{4,3,2,1,0:T(8,128)(2,1)}, u32[]{:S(2)}, u32[]{:S(2)}) collective-permute-start(bf16[2,16,2,128,128]{4,3,2,1,0:T(8,128)(2,1)} %cut.3.refs_1_), channel_id=1, source_target_pairs={{0,8},{8,0},{16,24},{24,16},{1,9},{9,1},{17,25},{25,17},{2,10},{10... | collective-permute-start | bytes 6291464 | tf_op jit(solution)/shard_map/ppermute | solution.py:459
  10.4 4.5 %collective-permute-start = (f32[16,128]{1,0:T(8,128)S(1)}, f32[16,128]{1,0:T(8,128)S(1)}, u32[]{:S(2)}, u32[]{:S(2)}) collective-permute-start(f32[16,128]{1,0:T(8,128)S(1)} %copy-done.45), channel_id=1, source_target_pairs={{0,1},{1,0},{2,3},{3,2},{4,5},{5,4},{6,7},{7,6},{8,9},{9,8},{10,11... | collective-permute-start | bytes 24584 | tf_op jit(solution)/shard_map/ppermute | solution.py:465
  14.9 4.4 %collective-permute-start.1 = (f32[32,128]{1,0:T(8,128)S(1)}, f32[32,128]{1,0:T(8,128)S(1)}, u32[]{:S(2)}, u32[]{:S(2)}) collective-permute-start(f32[32,128]{1,0:T(8,128)S(1)} %pad_maximum_fusion.3), channel_id=1, source_target_pairs={{0,2},{1,3},{2,0},{3,1},{4,6},{5,7},{6,4},{7,5},{8,10},{9,11},{10,... | collective-permute-start | bytes 49160 | tf_op jit(solution)/shard_map/ppermute | solution.py:465
  16.9 6.9 %collective-permute-start.5 = (bf16[16,64,128]{2,1,0:T(8,128)(2,1)S(1)}, bf16[16,64,128]{2,1,0:T(8,128)(2,1)S(1)}, u32[]{:S(2)}, u32[]{:S(2)}) collective-permute-start(bf16[16,64,128]{2,1,0:T(8,128)(2,1)S(1)} %copy-done.7), channel_id=1, source_target_pairs={{0,16},{8,24},{16,0},{24,8},{1,17},{9,25},{17,1},{25,9},{2,18},{10... | collective-permute-start | bytes 786440 | tf_op jit(solution)/shard_map/ppermute | solution.py:462
  30.0 15.1 %collective-permute-start.6 = (bf16[16,64,256]{2,1,0:T(8,128)(2,1)}, bf16[16,64,256]{2,1,0:T(8,128)(2,1)S(1)}, u32[]{:S(2)}, u32[]{:S(2)}) collective-permute-start(bf16[16,64,256]{2,1,0:T(8,128)(2,1)} %get-tuple-element.47), channel_id=1, source_target_pairs={{0,1},{1,0},{2,3},{3,2},{4,5},{5,4},{6,7},{7,6},{8,9},{9,8},{10,11... | collective-permute-start | bytes 1572872 | tf_op jit(solution)/shard_map/ppermute | solution.py:465
  32.5 6.4 %collective-permute-start.8 = (bf16[16,64,128]{2,1,0:T(8,128)(2,1)S(1)}, bf16[16,64,128]{2,1,0:T(8,128)(2,1)S(1)}, u32[]{:S(2)}, u32[]{:S(2)}) collective-permute-start(bf16[16,64,128]{2,1,0:T(8,128)(2,1)S(1)} %ordered.4), channel_id=1, source_target_pairs={{0,16},{8,24},{16,0},{24,8},{1,17},{9,25},{17,1},{25,9},{2,18},{10... | collective-permute-start | bytes 786440 | tf_op jit(solution)/shard_map/ppermute | solution.py:462
  34.0 11.6 %collective-permute-start.2 = (f32[64,128]{1,0:T(8,128)S(1)}, f32[64,128]{1,0:T(8,128)S(1)}, u32[]{:S(2)}, u32[]{:S(2)}) collective-permute-start(f32[64,128]{1,0:T(8,128)S(1)} %copy-done.44), channel_id=1, source_target_pairs={{0,4},{1,5},{2,6},{3,7},{4,0},{5,1},{6,2},{7,3},{8,12},{9,13},{10,... | collective-permute-start | bytes 98312 | tf_op jit(solution)/shard_map/ppermute | solution.py:465
  45.0 15.1 %collective-permute-start.12 = (bf16[16,64,256]{2,1,0:T(8,128)(2,1)}, bf16[16,64,256]{2,1,0:T(8,128)(2,1)S(1)}, u32[]{:S(2)}, u32[]{:S(2)}) collective-permute-start(bf16[16,64,256]{2,1,0:T(8,128)(2,1)} %ordered.5.refs_0_), channel_id=1, source_target_pairs={{0,1},{1,0},{2,3},{3,2},{4,5},{5,4},{6,7},{7,6},{8,9},{9,8},{10,11... | collective-permute-start | bytes 1572872 | tf_op jit(solution)/shard_map/ppermute | solution.py:465
  45.6 6.1 %collective-permute-start.3 = (f32[2,32,128]{2,1,0:T(8,128)S(1)}, f32[2,32,128]{2,1,0:T(8,128)S(1)}, u32[]{:S(2)}, u32[]{:S(2)}) collective-permute-start(f32[2,32,128]{2,1,0:T(8,128)S(1)} %get-tuple-element.96), channel_id=1, source_target_pairs={{0,8},{8,0},{16,24},{24,16},{1,9},{9,1},{17,25},{25,17},{2,10},{10... | collective-permute-start | bytes 98312 | tf_op jit(solution)/shard_map/ppermute | solution.py:459
  46.7 8.5 %collective-permute-start.9 = (bf16[256,256]{1,0:T(8,128)(2,1)S(1)}, bf16[256,256]{1,0:T(8,128)(2,1)S(1)}, u32[]{:S(2)}, u32[]{:S(2)}) collective-permute-start(bf16[256,256]{1,0:T(8,128)(2,1)S(1)} %get-tuple-element.50), channel_id=1, source_target_pairs={{0,2},{1,3},{2,0},{3,1},{4,6},{5,7},{6,4},{7,5},{8,10},{9,11},{10,... | collective-permute-start | bytes 393224 | tf_op jit(solution)/shard_map/ppermute | solution.py:465
  47.2 8.0 %collective-permute-start.10 = (bf16[256,256]{1,0:T(8,128)(2,1)S(1)}, bf16[256,256]{1,0:T(8,128)(2,1)S(1)}, u32[]{:S(2)}, u32[]{:S(2)}) collective-permute-start(bf16[256,256]{1,0:T(8,128)(2,1)S(1)} %get-tuple-element.51), channel_id=1, source_target_pairs={{0,4},{1,5},{2,6},{3,7},{4,0},{5,1},{6,2},{7,3},{8,12},{9,13},{10,... | collective-permute-start | bytes 393224 | tf_op jit(solution)/shard_map/ppermute | solution.py:465
  49.8 10.3 %collective-permute-start.11 = (bf16[256,256]{1,0:T(8,128)(2,1)S(1)}, bf16[256,256]{1,0:T(8,128)(2,1)S(1)}, u32[]{:S(2)}, u32[]{:S(2)}) collective-permute-start(bf16[256,256]{1,0:T(8,128)(2,1)S(1)} %get-tuple-element.52), channel_id=1, source_target_pairs={{0,6},{1,7},{2,4},{3,5},{4,2},{5,3},{6,0},{7,1},{8,14},{9,15},{10,... | collective-permute-start | bytes 393224 | tf_op jit(solution)/shard_map/ppermute | solution.py:465
  61.5 6.9 %collective-permute-start.21 = (bf16[256,256]{1,0:T(8,128)(2,1)S(1)}, bf16[256,256]{1,0:T(8,128)(2,1)S(1)}, u32[]{:S(2)}, u32[]{:S(2)}) collective-permute-start(bf16[256,256]{1,0:T(8,128)(2,1)S(1)} %get-tuple-element.60.refs_0_), channel_id=1, source_target_pairs={{0,6},{1,7},{2,4},{3,5},{4,2},{5,3},{6,0},{7,1},{8,14},{9,15},{10,... | collective-permute-start | bytes 393224 | tf_op jit(solution)/shard_map/ppermute | solution.py:465
  64.4 12.0 %collective-permute-start.20 = (bf16[256,256]{1,0:T(8,128)(2,1)S(1)}, bf16[256,256]{1,0:T(8,128)(2,1)S(1)}, u32[]{:S(2)}, u32[]{:S(2)}) collective-permute-start(bf16[256,256]{1,0:T(8,128)(2,1)S(1)} %get-tuple-element.60.refs_0_), channel_id=1, source_target_pairs={{0,4},{1,5},{2,6},{3,7},{4,0},{5,1},{6,2},{7,3},{8,12},{9,13},{10,... | collective-permute-start | bytes 393224 | tf_op jit(solution)/shard_map/ppermute | solution.py:465
  65.9 10.5 %collective-permute-start.19 = (bf16[256,256]{1,0:T(8,128)(2,1)S(1)}, bf16[256,256]{1,0:T(8,128)(2,1)S(1)}, u32[]{:S(2)}, u32[]{:S(2)}) collective-permute-start(bf16[256,256]{1,0:T(8,128)(2,1)S(1)} %get-tuple-element.60.refs_0_), channel_id=1, source_target_pairs={{0,2},{1,3},{2,0},{3,1},{4,6},{5,7},{6,4},{7,5},{8,10},{9,11},{10,... | collective-permute-start | bytes 393224 | tf_op jit(solution)/shard_map/ppermute | solution.py:465
  77.1 14.0 %collective-permute-start.22 = (bf16[16,64,256]{2,1,0:T(8,128)(2,1)S(1)}, bf16[16,64,256]{2,1,0:T(8,128)(2,1)S(1)}, u32[]{:S(2)}, u32[]{:S(2)}) collective-permute-start(bf16[16,64,256]{2,1,0:T(8,128)(2,1)S(1)} %bitcast.51), channel_id=1, source_target_pairs={{0,1},{1,0},{2,3},{3,2},{4,5},{5,4},{6,7},{7,6},{8,9},{9,8},{10,11... | collective-permute-start | bytes 1572872 | tf_op jit(solution)/shard_map/ppermute | solution.py:465
  79.6 19.6 %collective-permute-start.13 = (bf16[256,256]{1,0:T(8,128)(2,1)S(1)}, bf16[256,256]{1,0:T(8,128)(2,1)S(1)}, u32[]{:S(2)}, u32[]{:S(2)}) collective-permute-start(bf16[256,256]{1,0:T(8,128)(2,1)S(1)} %get-tuple-element.56), channel_id=1, source_target_pairs={{0,2},{1,3},{2,0},{3,1},{4,6},{5,7},{6,4},{7,5},{8,10},{9,11},{10,... | collective-permute-start | bytes 393224 | tf_op jit(solution)/shard_map/ppermute | solution.py:465
  79.7 19.5 %collective-permute-start.14 = (bf16[256,256]{1,0:T(8,128)(2,1)S(1)}, bf16[256,256]{1,0:T(8,128)(2,1)S(1)}, u32[]{:S(2)}, u32[]{:S(2)}) collective-permute-start(bf16[256,256]{1,0:T(8,128)(2,1)S(1)} %get-tuple-element.57), channel_id=1, source_target_pairs={{0,4},{1,5},{2,6},{3,7},{4,0},{5,1},{6,2},{7,3},{8,12},{9,13},{10,... | collective-permute-start | bytes 393224 | tf_op jit(solution)/shard_map/ppermute | solution.py:465
  82.9 16.3 %collective-permute-start.15 = (bf16[256,256]{1,0:T(8,128)(2,1)S(1)}, bf16[256,256]{1,0:T(8,128)(2,1)S(1)}, u32[]{:S(2)}, u32[]{:S(2)}) collective-permute-start(bf16[256,256]{1,0:T(8,128)(2,1)S(1)} %get-tuple-element.58), channel_id=1, source_target_pairs={{0,6},{1,7},{2,4},{3,5},{4,2},{5,3},{6,0},{7,1},{8,14},{9,15},{10,... | collective-permute-start | bytes 393224 | tf_op jit(solution)/shard_map/ppermute | solution.py:465
  97.1 19.7 %collective-permute-start.23 = (bf16[2,16,64,128]{3,2,1,0:T(8,128)(2,1)}, bf16[2,16,64,128]{3,2,1,0:T(8,128)(2,1)S(1)}, u32[]{:S(2)}, u32[]{:S(2)}) collective-permute-start(bf16[2,16,64,128]{3,2,1,0:T(8,128)(2,1)} %adjoint.4.one_ref.mine_ref.refs_4_), channel_id=1, source_target_pairs={{0,16},{8,24},{16,0},{24,8},{1,17},{9,25},{17,1},{25,9},{2,18},{10... | collective-permute-start | bytes 1572872 | tf_op jit(solution)/shard_map/ppermute | solution.py:462
  99.9 14.5 %collective-permute-start.33 = (bf16[256,256]{1,0:T(8,128)(2,1)S(1)}, bf16[256,256]{1,0:T(8,128)(2,1)S(1)}, u32[]{:S(2)}, u32[]{:S(2)}) collective-permute-start(bf16[256,256]{1,0:T(8,128)(2,1)S(1)} %get-tuple-element.71.refs_0_), channel_id=1, source_target_pairs={{0,6},{1,7},{2,4},{3,5},{4,2},{5,3},{6,0},{7,1},{8,14},{9,15},{10,... | collective-permute-start | bytes 393224 | tf_op jit(solution)/shard_map/ppermute | solution.py:465
  102.5 11.9 %collective-permute-start.32 = (bf16[256,256]{1,0:T(8,128)(2,1)S(1)}, bf16[256,256]{1,0:T(8,128)(2,1)S(1)}, u32[]{:S(2)}, u32[]{:S(2)}) collective-permute-start(bf16[256,256]{1,0:T(8,128)(2,1)S(1)} %get-tuple-element.71.refs_0_), channel_id=1, source_target_pairs={{0,4},{1,5},{2,6},{3,7},{4,0},{5,1},{6,2},{7,3},{8,12},{9,13},{10,... | collective-permute-start | bytes 393224 | tf_op jit(solution)/shard_map/ppermute | solution.py:465
  102.5 11.9 %collective-permute-start.31 = (bf16[256,256]{1,0:T(8,128)(2,1)S(1)}, bf16[256,256]{1,0:T(8,128)(2,1)S(1)}, u32[]{:S(2)}, u32[]{:S(2)}) collective-permute-start(bf16[256,256]{1,0:T(8,128)(2,1)S(1)} %get-tuple-element.71.refs_0_), channel_id=1, source_target_pairs={{0,2},{1,3},{2,0},{3,1},{4,6},{5,7},{6,4},{7,5},{8,10},{9,11},{10,... | collective-permute-start | bytes 393224 | tf_op jit(solution)/shard_map/ppermute | solution.py:465
  105.5 5.2 %collective-permute-start.17 = (f32[24,128]{1,0:T(8,128)S(1)}, f32[24,128]{1,0:T(8,128)S(1)}, u32[]{:S(2)}, u32[]{:S(2)}) collective-permute-start(f32[24,128]{1,0:T(8,128)S(1)} %add.103), channel_id=1, source_target_pairs={{0,16},{8,24},{16,0},{24,8},{1,17},{9,25},{17,1},{25,9},{2,18},{10... | collective-permute-start | bytes 36872 | tf_op jit(solution)/shard_map/ppermute | solution.py:462
  115.0 17.1 %collective-permute-start.34 = (bf16[16,64,256]{2,1,0:T(8,128)(2,1)S(1)}, bf16[16,64,256]{2,1,0:T(8,128)(2,1)S(1)}, u32[]{:S(2)}, u32[]{:S(2)}) collective-permute-start(bf16[16,64,256]{2,1,0:T(8,128)(2,1)S(1)} %bitcast.54), channel_id=1, source_target_pairs={{0,1},{1,0},{2,3},{3,2},{4,5},{5,4},{6,7},{7,6},{8,9},{9,8},{10,11... | collective-permute-start | bytes 1572872 | tf_op jit(solution)/shard_map/ppermute | solution.py:465
  126.8 4.6 %collective-permute-start.25 = (f32[24,128]{1,0:T(8,128)S(1)}, f32[24,128]{1,0:T(8,128)S(1)}, u32[]{:S(2)}, u32[]{:S(2)}) collective-permute-start(f32[24,128]{1,0:T(8,128)S(1)} %add.106), channel_id=1, source_target_pairs={{0,4},{1,5},{2,6},{3,7},{4,0},{5,1},{6,2},{7,3},{8,12},{9,13},{10,... | collective-permute-start | bytes 36872 | tf_op jit(solution)/shard_map/ppermute | solution.py:465
  127.7 12.6 %collective-permute-start.27 = (bf16[16,64,256]{2,1,0:T(8,128)(2,1)}, bf16[16,64,256]{2,1,0:T(8,128)(2,1)S(1)}, u32[]{:S(2)}, u32[]{:S(2)}) collective-permute-start(bf16[16,64,256]{2,1,0:T(8,128)(2,1)} %get-tuple-element.61.refs_1_.refs_0_), channel_id=1, source_target_pairs={{0,1},{1,0},{2,3},{3,2},{4,5},{5,4},{6,7},{7,6},{8,9},{9,8},{10,11... | collective-permute-start | bytes 1572872 | tf_op jit(solution)/shard_map/ppermute | solution.py:465
  138.2 9.5 %collective-permute-start.35 = (bf16[2,16,64,128]{3,2,1,0:T(8,128)(2,1)}, bf16[2,16,64,128]{3,2,1,0:T(8,128)(2,1)S(1)}, u32[]{:S(2)}, u32[]{:S(2)}) collective-permute-start(bf16[2,16,64,128]{3,2,1,0:T(8,128)(2,1)} %adjoint.5.mine_ref.one_ref), channel_id=1, source_target_pairs={{0,16},{8,24},{16,0},{24,8},{1,17},{9,25},{17,1},{25,9},{2,18},{10... | collective-permute-start | bytes 1572872 | tf_op jit(solution)/shard_map/ppermute | solution.py:462
  139.7 14.6 %collective-permute-start.26 = (f32[32]{0:T(128)S(1)}, f32[32]{0:T(128)S(1)}, u32[]{:S(2)}, u32[]{:S(2)}) collective-permute-start(f32[32]{0:T(128)S(1)} %copy-done.38), channel_id=1, source_target_pairs={{0,16},{8,24},{16,0},{24,8},{1,17},{9,25},{17,1},{25,9},{2,18},{10... | collective-permute-start | bytes 392 | tf_op jit(solution)/shard_map/ppermute | solution.py:462
  142.3 15.1 %collective-permute-start.28 = (bf16[256,256]{1,0:T(8,128)(2,1)}, bf16[256,256]{1,0:T(8,128)(2,1)}, u32[]{:S(2)}, u32[]{:S(2)}) collective-permute-start(bf16[256,256]{1,0:T(8,128)(2,1)} %get-tuple-element.66), channel_id=1, source_target_pairs={{0,2},{1,3},{2,0},{3,1},{4,6},{5,7},{6,4},{7,5},{8,10},{9,11},{10,... | collective-permute-start | bytes 393224 | tf_op jit(solution)/shard_map/ppermute | solution.py:465
  142.4 15.0 %collective-permute-start.29 = (bf16[256,256]{1,0:T(8,128)(2,1)}, bf16[256,256]{1,0:T(8,128)(2,1)}, u32[]{:S(2)}, u32[]{:S(2)}) collective-permute-start(bf16[256,256]{1,0:T(8,128)(2,1)} %get-tuple-element.67), channel_id=1, source_target_pairs={{0,4},{1,5},{2,6},{3,7},{4,0},{5,1},{6,2},{7,3},{8,12},{9,13},{10,... | collective-permute-start | bytes 393224 | tf_op jit(solution)/shard_map/ppermute | solution.py:465
  145.3 12.1 %collective-permute-start.30 = (bf16[256,256]{1,0:T(8,128)(2,1)}, bf16[256,256]{1,0:T(8,128)(2,1)}, u32[]{:S(2)}, u32[]{:S(2)}) collective-permute-start(bf16[256,256]{1,0:T(8,128)(2,1)} %get-tuple-element.68), channel_id=1, source_target_pairs={{0,6},{1,7},{2,4},{3,5},{4,2},{5,3},{6,0},{7,1},{8,14},{9,15},{10,... | collective-permute-start | bytes 393224 | tf_op jit(solution)/shard_map/ppermute | solution.py:465
  153.9 20.3 %collective-permute-start.36 = (bf16[16,64,256]{2,1,0:T(8,128)(2,1)}, bf16[16,64,256]{2,1,0:T(8,128)(2,1)}, u32[]{:S(2)}, u32[]{:S(2)}) collective-permute-start(bf16[16,64,256]{2,1,0:T(8,128)(2,1)} %ordered.7), channel_id=1, source_target_pairs={{0,1},{1,0},{2,3},{3,2},{4,5},{5,4},{6,7},{7,6},{8,9},{9,8},{10,11... | collective-permute-start | bytes 1572872 | tf_op jit(solution)/shard_map/ppermute | solution.py:465
  160.7 6.9 %collective-permute-start.47 = (bf16[256,256]{1,0:T(8,128)(2,1)S(1)}, bf16[256,256]{1,0:T(8,128)(2,1)S(1)}, u32[]{:S(2)}, u32[]{:S(2)}) collective-permute-start(bf16[256,256]{1,0:T(8,128)(2,1)S(1)} %get-tuple-element.82.refs_0_), channel_id=1, source_target_pairs={{0,6},{1,7},{2,4},{3,5},{4,2},{5,3},{6,0},{7,1},{8,14},{9,15},{10,... | collective-permute-start | bytes 393224 | tf_op jit(solution)/shard_map/ppermute | solution.py:465
  162.9 7.4 %collective-permute-start.46 = (bf16[256,256]{1,0:T(8,128)(2,1)S(1)}, bf16[256,256]{1,0:T(8,128)(2,1)S(1)}, u32[]{:S(2)}, u32[]{:S(2)}) collective-permute-start(bf16[256,256]{1,0:T(8,128)(2,1)S(1)} %get-tuple-element.82.refs_0_), channel_id=1, source_target_pairs={{0,4},{1,5},{2,6},{3,7},{4,0},{5,1},{6,2},{7,3},{8,12},{9,13},{10,... | collective-permute-start | bytes 393224 | tf_op jit(solution)/shard_map/ppermute | solution.py:465
  162.9 7.4 %collective-permute-start.45 = (bf16[256,256]{1,0:T(8,128)(2,1)S(1)}, bf16[256,256]{1,0:T(8,128)(2,1)S(1)}, u32[]{:S(2)}, u32[]{:S(2)}) collective-permute-start(bf16[256,256]{1,0:T(8,128)(2,1)S(1)} %get-tuple-element.82.refs_0_), channel_id=1, source_target_pairs={{0,2},{1,3},{2,0},{3,1},{4,6},{5,7},{6,4},{7,5},{8,10},{9,11},{10,... | collective-permute-start | bytes 393224 | tf_op jit(solution)/shard_map/ppermute | solution.py:465
  170.9 32.0 %collective-permute-start.48 = (bf16[16,64,256]{2,1,0:T(8,128)(2,1)S(1)}, bf16[16,64,256]{2,1,0:T(8,128)(2,1)S(1)}, u32[]{:S(2)}, u32[]{:S(2)}) collective-permute-start(bf16[16,64,256]{2,1,0:T(8,128)(2,1)S(1)} %bitcast.48), channel_id=1, source_target_pairs={{0,1},{1,0},{2,3},{3,2},{4,5},{5,4},{6,7},{7,6},{8,9},{9,8},{10,11... | collective-permute-start | bytes 1572872 | tf_op jit(solution)/shard_map/ppermute | solution.py:465
  176.4 7.5 %collective-permute-start.37 = (bf16[256,256]{1,0:T(8,128)(2,1)S(1)}, bf16[256,256]{1,0:T(8,128)(2,1)S(1)}, u32[]{:S(2)}, u32[]{:S(2)}) collective-permute-start(bf16[256,256]{1,0:T(8,128)(2,1)S(1)} %get-tuple-element.76), channel_id=1, source_target_pairs={{0,2},{1,3},{2,0},{3,1},{4,6},{5,7},{6,4},{7,5},{8,10},{9,11},{10,... | collective-permute-start | bytes 393224 | tf_op jit(solution)/shard_map/ppermute | solution.py:465
  177.0 12.2 %collective-permute-start.38 = (bf16[256,256]{1,0:T(8,128)(2,1)S(1)}, bf16[256,256]{1,0:T(8,128)(2,1)S(1)}, u32[]{:S(2)}, u32[]{:S(2)}) collective-permute-start(bf16[256,256]{1,0:T(8,128)(2,1)S(1)} %get-tuple-element.77), channel_id=1, source_target_pairs={{0,4},{1,5},{2,6},{3,7},{4,0},{5,1},{6,2},{7,3},{8,12},{9,13},{10,... | collective-permute-start | bytes 393224 | tf_op jit(solution)/shard_map/ppermute | solution.py:465
  179.8 9.5 %collective-permute-start.39 = (bf16[256,256]{1,0:T(8,128)(2,1)S(1)}, bf16[256,256]{1,0:T(8,128)(2,1)S(1)}, u32[]{:S(2)}, u32[]{:S(2)}) collective-permute-start(bf16[256,256]{1,0:T(8,128)(2,1)S(1)} %get-tuple-element.78), channel_id=1, source_target_pairs={{0,6},{1,7},{2,4},{3,5},{4,2},{5,3},{6,0},{7,1},{8,14},{9,15},{10,... | collective-permute-start | bytes 393224 | tf_op jit(solution)/shard_map/ppermute | solution.py:465
  189.9 19.2 %collective-permute-start.52 = (bf16[256,256]{1,0:T(8,128)(2,1)S(1)}, bf16[256,256]{1,0:T(8,128)(2,1)S(1)}, u32[]{:S(2)}, u32[]{:S(2)}) collective-permute-start(bf16[256,256]{1,0:T(8,128)(2,1)S(1)} %get-tuple-element.85.refs_0_), channel_id=1, source_target_pairs={{0,6},{1,7},{2,4},{3,5},{4,2},{5,3},{6,0},{7,1},{8,14},{9,15},{10,... | collective-permute-start | bytes 393224 | tf_op jit(solution)/shard_map/ppermute | solution.py:465
  192.3 16.8 %collective-permute-start.51 = (bf16[256,256]{1,0:T(8,128)(2,1)S(1)}, bf16[256,256]{1,0:T(8,128)(2,1)S(1)}, u32[]{:S(2)}, u32[]{:S(2)}) collective-permute-start(bf16[256,256]{1,0:T(8,128)(2,1)S(1)} %get-tuple-element.85.refs_0_), channel_id=1, source_target_pairs={{0,4},{1,5},{2,6},{3,7},{4,0},{5,1},{6,2},{7,3},{8,12},{9,13},{10,... | collective-permute-start | bytes 393224 | tf_op jit(solution)/shard_map/ppermute | solution.py:465
  194.2 15.0 %collective-permute-start.50 = (bf16[256,256]{1,0:T(8,128)(2,1)S(1)}, bf16[256,256]{1,0:T(8,128)(2,1)S(1)}, u32[]{:S(2)}, u32[]{:S(2)}) collective-permute-start(bf16[256,256]{1,0:T(8,128)(2,1)S(1)} %get-tuple-element.85.refs_0_), channel_id=1, source_target_pairs={{0,2},{1,3},{2,0},{3,1},{4,6},{5,7},{6,4},{7,5},{8,10},{9,11},{10,... | collective-permute-start | bytes 393224 | tf_op jit(solution)/shard_map/ppermute | solution.py:465
  210.7 12.2 %collective-permute-start.53 = (bf16[16,64,256]{2,1,0:T(8,128)(2,1)S(1)}, bf16[16,64,256]{2,1,0:T(8,128)(2,1)}, u32[]{:S(2)}, u32[]{:S(2)}) collective-permute-start(bf16[16,64,256]{2,1,0:T(8,128)(2,1)S(1)} %bitcast.45), channel_id=1, source_target_pairs={{0,1},{1,0},{2,3},{3,2},{4,5},{5,4},{6,7},{7,6},{8,9},{9,8},{10,11... | collective-permute-start | bytes 1572872 | tf_op jit(solution)/shard_map/ppermute | solution.py:465
  211.5 10.7 %collective-permute-start.49 = (bf16[16,64,128]{2,1,0:T(8,128)(2,1)S(1)}, bf16[16,64,128]{2,1,0:T(8,128)(2,1)S(1)}, u32[]{:S(2)}, u32[]{:S(2)}) collective-permute-start(bf16[16,64,128]{2,1,0:T(8,128)(2,1)S(1)} %copy-done.33), channel_id=1, source_target_pairs={{0,16},{8,24},{16,0},{24,8},{1,17},{9,25},{17,1},{25,9},{2,18},{10... | collective-permute-start | bytes 786440 | tf_op jit(solution)/shard_map/ppermute | solution.py:462
  216.7 4.6 %collective-permute-start.44 = (f32[24,128]{1,0:T(8,128)S(1)}, f32[24,128]{1,0:T(8,128)S(1)}, u32[]{:S(2)}, u32[]{:S(2)}) collective-permute-start(f32[24,128]{1,0:T(8,128)S(1)} %add.112), channel_id=1, source_target_pairs={{0,4},{1,5},{2,6},{3,7},{4,0},{5,1},{6,2},{7,3},{8,12},{9,13},{10,... | collective-permute-start | bytes 36872 | tf_op jit(solution)/shard_map/ppermute | solution.py:465
  228.2 6.9 %collective-permute-start.54 = (bf16[16,64,128]{2,1,0:T(8,128)(2,1)}, bf16[16,64,128]{2,1,0:T(8,128)(2,1)S(1)}, u32[]{:S(2)}, u32[]{:S(2)}) collective-permute-start(bf16[16,64,128]{2,1,0:T(8,128)(2,1)} %get-tuple-element.87), channel_id=1, source_target_pairs={{0,16},{8,24},{16,0},{24,8},{1,17},{9,25},{17,1},{25,9},{2,18},{10... | collective-permute-start | bytes 786440 | tf_op jit(solution)/shard_map/ppermute | solution.py:462
  (53 other events, 370.6 us)

commit v2 on v1

--- a/solution.py
+++ b/solution.py
@@ -69,56 +69,54 @@
     def __init__(self, plan, chunk, m, blk_of, refs):
         (whole, far), (near_buf, far_buf, sems) = refs
         self.buffers, self.copies = (near_buf, far_buf), {}
+        high = plan.step * 2 * plan.sensors
         for phase in range(2):
             for t in range(plan.steps):
                 slot = phase * plan.steps + t
                 side = m[0] ^ blk_of(phase, m)
-                rows = pl.ds(t * plan.step, plan.step)
-                near_rows = pl.ds(chunk * plan.part + t * plan.step, plan.step)
+                near_rows = pl.ds((chunk * plan.steps + t) * high, high)
                 self.copies[phase, t] = [
                     pltpu.make_async_copy(ref, buffer.at[slot], sems.at[slot, place])
                     for place, (ref, buffer) in enumerate((
                         (whole.at[side, m[1], near_rows], near_buf),
-                        (far.at[side, rows], far_buf),
+                        (far.at[side, pl.ds(t * high, high)], far_buf),
                     ))
                 ]
-        self.order = list(self.copies)
-        for slot in self.order[:2]:
-            self.start(slot)
-
-    def start(self, slot):
-        for copy in self.copies[slot]:
-            copy.start()
+        for copies in self.copies.values():
+            for copy in copies:
+                copy.start()
 
     def get(self, plan, phase, t):
         for copy in self.copies[phase, t]:
             copy.wait()
-        slot = phase * plan.steps + t
-        for later in self.order[slot + 2:slot + 3]:
-            self.start(later)
+        slot, high = phase * plan.steps + t, plan.sensors
         return [
-            tuple(tuple(buffer[slot, f, c] for c in range(2)) for buffer in self.buffers)
+            tuple(
+                tuple(buffer[slot, pl.ds((2 * f + c) * high, high)] for c in range(2))
+                for buffer in self.buffers
+            )
             for f in range(plan.step)
         ]
 
     @staticmethod
     def scratch(plan):
-        buffer = pltpu.VMEM((2 * plan.steps, plan.step, 2, plan.sensors, plan.sources), BF16)
+        buffer = pltpu.VMEM((2 * plan.steps, plan.step * 2 * plan.sensors, plan.sources), BF16)
         return [buffer, buffer, pltpu.SemaphoreType.DMA((2 * plan.steps, 2))]
 
 
 def cut_call(plan, chunk, meta, whole, wait=()):
     def kernel(m, whole_ref, *refs):
         out_ref, buffer, sems = refs[len(wait):]
+        high = plan.step * 2 * plan.sensors
         slots = [(side, t) for side in range(plan.pairs) for t in range(plan.steps)]
         ins, outs = [], []
         for slot, (side, t) in enumerate(slots):
-            rows = pl.ds(chunk * plan.part + t * plan.step, plan.step)
+            rows = pl.ds((chunk * plan.steps + t) * high, high)
             ins.append(pltpu.make_async_copy(
                 whole_ref.at[side, 1 - m[1], rows], buffer.at[slot], sems.at[0, slot]
             ))
             outs.append(pltpu.make_async_copy(
-                buffer.at[slot], out_ref.at[side, pl.ds(t * plan.step, plan.step)], sems.at[1, slot]
+                buffer.at[slot], out_ref.at[side, pl.ds(t * high, high)], sems.at[1, slot]
             ))
         for copy in ins:
             copy.start()
@@ -128,14 +126,14 @@
         for copy in outs:
             copy.wait()
 
-    shape = (plan.pairs, plan.part, 2, plan.sensors, plan.sources)
+    shape = (plan.pairs, plan.part * 2 * plan.sensors, plan.sources)
     return pl.pallas_call(
         kernel,
         in_specs=[pl.BlockSpec(memory_space=pltpu.SMEM), ANYWHERE] + [ANYWHERE] * len(wait),
         out_specs=ANYWHERE,
         out_shape=jax.ShapeDtypeStruct(shape, BF16),
         scratch_shapes=[
-            pltpu.VMEM((plan.pairs * plan.steps, plan.step) + shape[2:], BF16),
+            pltpu.VMEM((plan.pairs * plan.steps, shape[1] // plan.steps, plan.sources), BF16),
             pltpu.SemaphoreType.DMA((2, plan.pairs * plan.steps)),
         ],
         cost_estimate=cost(0, 8 * plan.part * plan.sensors * plan.sources),
@@ -487,7 +485,7 @@
         low = (src >> level) % 2 == 0
         return jnp.concatenate([jnp.where(low, table, other), jnp.where(low, other, table)], axis=0)
 
-    whole = operator.reshape(plan.pairs, 2, block, 2, plan.sensors, plan.sources)
+    whole = operator.reshape(plan.pairs, 2, block * 2 * plan.sensors, plan.sources)
     start = right_side.reshape(block, rows, plan.sources)
 
     casts = [cast_call(plan, k, start) for k in chunks]
@@ -518,11 +516,11 @@
     def to_half(array):
         return to_src(array, 1)
 
-    def both_products(scaled, near_sums, last, then):
+    def both_products(scaled, near_sums, last, then, received):
         outs, wait, sums = [], (), None
         for k in chunks:
             pieces = [scaled[k]] + [to_src(scaled[k], step) for step in steps]
-            own = place_call(plan, meta, pieces, wait)
+            own = place_call(plan, meta, pieces, wait + tuple(sum(received[k + 1:k + 2], [])))
             halves = (own, to_half(own))
             if k == 1:
                 after = outs[0][1][0]
@@ -550,7 +548,7 @@
         send, keep = forward_call(plan, k, meta, whole, far[k], False, (back, got))
         return send, keep, got
 
-    outs, sums = both_products(scaled, near_0, False, go_on)
+    outs, sums = both_products(scaled, near_0, False, go_on, [each[1:] for each in pieces])
     norm_0, curve_0 = sums[0], sums[1]
     alpha_0 = (norm_0 / curve_0)[None]
     back = [out for out, _ in outs]
@@ -565,7 +563,7 @@
         for k in chunks
     ])
     near_1 = total_near(sum(stats))
-    outs, sums = both_products(scaled, near_1, True, lambda k, out: (to_pair(out[0]),))
+    outs, sums = both_products(scaled, near_1, True, lambda k, out: (to_pair(out[0]),), [each[1:] for each in pieces])
     norm_1 = sums[0]
     beta = norm_1 / norm_0
     curve_1 = sums[1] + 2.0 * beta * sums[2] + beta * beta * curve_0

time: 239 us -> 252 us (1.054)
  waiting for transfers between devices: 72.2 us -> 88 us
  Pallas kernels: 60.9 us -> 57.4 us
    ppermute x41, waiting for transfers between devices: 55.3 us -> 65.1 us  [to_src(): return lax.ppermute(array, 'src', [(j, j ^ step) for j in range(n_src)])]
    ppermute x9, waiting for transfers between devices: 14.5 us -> 20.5 us  [to_pair(): return lax.ppermute(array, 'sens', [(i, i ^ 2) for i in range(n_sens)])]
    pallas_call x4, Pallas kernels: 21 us -> 18.4 us  [adjoint_call(): pl.pallas_call(kernel, grid=(1,), in_specs=[pl.BlockSpec(memory_space=plt...]
    unnamed x92 -> x88, local copies, waits for them, and re-layouts: 15.7 us -> 15.6 us
  transfers between devices with their start and end apart: 55 -> 55, of which waited for: 24 -> 23; matrix products, arithmetic and copies ran while one was open for 2% -> 2% of each run, Pallas kernels for 21% -> 15%
where the time goes in v2:
time: 252 us; the launch traced here: 251 us
  waiting for transfers between devices  88 us (35%)
  starting transfers between devices  74.6 us (30%)
  Pallas kernels  57.4 us (23%)
  local copies, waits for them, and re-layouts  17.1 us (7%)
  other arithmetic  7.14 us (3%)
  between operations  6.4 us (3%)
    ppermute x41, waiting for transfers between devices, to_src(): return lax.ppermute(array, 'src', [(j, j ^ step) for j in range(n_src)])  65.1 us
    ppermute x41, starting transfers between devices, to_src(): return lax.ppermute(array, 'src', [(j, j ^ step) for j in range(n_src)])  63 us
    ppermute x9, waiting for transfers between devices, to_pair(): return lax.ppermute(array, 'sens', [(i, i ^ 2) for i in range(n_sens)])  20.5 us
    pallas_call x4, Pallas kernels, forward_call(): pl.pallas_call(kernel, grid=(1,), in_specs=[pl.BlockSpec(memory_space=plt...  20.1 us
    pallas_call x4, Pallas kernels, adjoint_call(): pl.pallas_call(kernel, grid=(1,), in_specs=[pl.BlockSpec(memory_space=plt...  18.4 us
    unnamed x88, local copies, waits for them, and re-layouts  15.6 us
    ppermute x9, starting transfers between devices, to_pair(): return lax.ppermute(array, 'sens', [(i, i ^ 2) for i in range(n_sens)])  10.8 us
    pallas_call x2, Pallas kernels, cut_call(): pl.pallas_call(kernel, in_specs=[pl.BlockSpec(memory_space=pltpu.SMEM), A...  6.24 us
  transfers between devices with their start and end apart: 55, of which 23 were waited for; matrix products, arithmetic and copies ran while one was open for 2% of the time, Pallas kernels for 15%

profile of v2, /device:TPU:0, one launch (start us, length us, event | category | flops | bytes accessed | tf_op | source)
XLA Modules:
  0.0 250.7 jit_solution(9426013902838332445)
XLA Ops:
  3.3 3.2 %cut.2 = bf16[2,4096,128]{2,1,0:T(8,128)(2,1)} custom-call(s32[4]{0:T(128)} %pad_add_fusion.m, bf16[2,2,8192,128]{3,2,1,0:T(8,128)(2,1)} %bitcast.64, bf16[16,64,128]{2,1,0:T(8,128)(2,1)} %copy-done.6), custom_call_target="tpu_custom_call" | custom-call | bytes 2097 | tf_op jit(solution)/shard_map/cut/pallas_call | solution.py:130
  7.0 3.1 %cut.3.refs_1_ = bf16[2,4096,128]{2,1,0:T(8,128)(2,1)} custom-call(s32[4]{0:T(128)} %pad_add_fusion.m, bf16[2,2,8192,128]{3,2,1,0:T(8,128)(2,1)} %bitcast.65, bf16[16,64,128]{2,1,0:T(8,128)(2,1)} %copy-done.6), custom_call_target="tpu_custom_call" | custom-call | bytes 2097 | tf_op jit(solution)/shard_map/cut/pallas_call | solution.py:130
  10.4 2.8 %collective-permute-start = (f32[16,128]{1,0:T(8,128)S(1)}, f32[16,128]{1,0:T(8,128)S(1)}, u32[]{:S(2)}, u32[]{:S(2)}) collective-permute-start(f32[16,128]{1,0:T(8,128)S(1)} %copy-done.43), channel_id=1, source_target_pairs={{0,1},{1,0},{2,3},{3,2},{4,5},{5,4},{6,7},{7,6},{8,9},{9,8},{10,11... | collective-permute-start | bytes 24584 | tf_op jit(solution)/shard_map/ppermute | solution.py:463
  14.9 2.1 collective-permute-start.1
  19.9 4.0 %collective-permute-done.5.two_ref.refs_1_ = bf16[16,64,128]{2,1,0:T(8,128)(2,1)S(1)} collective-permute-done((bf16[16,64,128]{2,1,0:T(8,128)(2,1)S(1)}, bf16[16,64,128]{2,1,0:T(8,128)(2,1)S(1)}, u32[]{:S(2)}, u32[]{:S(2)}) %collective-permute-start.5) | collective-permute-done | bytes 262176 | tf_op jit(solution)/shard_map/ppermute | solution.py:460
  24.6 5.0 %forward.4 = (bf16[16,64,256]{2,1,0:T(8,128)(2,1)}, bf16[16,64,256]{2,1,0:T(8,128)(2,1)}) custom-call(s32[4]{0:T(128)} %pad_add_fusion.m, bf16[2,2,8192,128]{3,2,1,0:T(8,128)(2,1)} %bitcast.66, bf16[2,4096,128]{2,1,0:T(8,128)(2,1)} %collective-permute-done.4.far, f32[32,64,128]{2,1,0:T(8,128)} %bitcast.37, bf16[16,64,128]{2,1,0:T(8,128)(2,1)} %copy-done.20, ...), custom_call_target="tpu_custom_call" | custom-call | flops 536870 | bytes 4194 | tf_op jit(solution)/shard_map/forward/pallas_call | solution.py:194
  33.6 2.6 %collective-permute-start.2 = (f32[64,128]{1,0:T(8,128)S(1)}, f32[64,128]{1,0:T(8,128)S(1)}, u32[]{:S(2)}, u32[]{:S(2)}) collective-permute-start(f32[64,128]{1,0:T(8,128)S(1)} %copy-done.42), channel_id=1, source_target_pairs={{0,4},{1,5},{2,6},{3,7},{4,0},{5,1},{6,2},{7,3},{8,12},{9,13},{10,... | collective-permute-start | bytes 98312 | tf_op jit(solution)/shard_map/ppermute | solution.py:463
  36.2 2.3 collective-permute-done.8.two_ref
  39.2 5.0 %forward.5 = (bf16[16,64,256]{2,1,0:T(8,128)(2,1)}, bf16[16,64,256]{2,1,0:T(8,128)(2,1)}) custom-call(s32[4]{0:T(128)} %pad_add_fusion.m, bf16[2,2,8192,128]{3,2,1,0:T(8,128)(2,1)} %bitcast.67, bf16[2,4096,128]{2,1,0:T(8,128)(2,1)} %collective-permute-done.7.far, f32[32,64,128]{2,1,0:T(8,128)} %bitcast.38, bf16[16,64,128]{2,1,0:T(8,128)(2,1)} %copy-done.41), custom_call_target="tpu_custom_call" | custom-call | flops 536870 | bytes 4194 | tf_op jit(solution)/shard_map/forward/pallas_call | solution.py:194
  46.5 2.6 %collective-permute-start.10 = (bf16[256,256]{1,0:T(8,128)(2,1)}, bf16[256,256]{1,0:T(8,128)(2,1)S(1)}, u32[]{:S(2)}, u32[]{:S(2)}) collective-permute-start(bf16[256,256]{1,0:T(8,128)(2,1)} %get-tuple-element.51), channel_id=1, source_target_pairs={{0,4},{1,5},{2,6},{3,7},{4,0},{5,1},{6,2},{7,3},{8,12},{9,13},{10,... | collective-permute-start | bytes 393224 | tf_op jit(solution)/shard_map/ppermute | solution.py:463
  50.6 8.2 %collective-permute-done.10.refs_4_ = bf16[256,256]{1,0:T(8,128)(2,1)S(1)} collective-permute-done((bf16[256,256]{1,0:T(8,128)(2,1)}, bf16[256,256]{1,0:T(8,128)(2,1)S(1)}, u32[]{:S(2)}, u32[]{:S(2)}) %collective-permute-start.10) | collective-permute-done | bytes 131104 | tf_op jit(solution)/shard_map/ppermute | solution.py:463
  60.6 2.2 collective-permute-start.19
  67.1 2.2 collective-permute-start.14
  70.6 5.2 %collective-permute-done.20.refs_2_ = bf16[256,256]{1,0:T(8,128)(2,1)S(1)} collective-permute-done((bf16[256,256]{1,0:T(8,128)(2,1)S(1)}, bf16[256,256]{1,0:T(8,128)(2,1)S(1)}, u32[]{:S(2)}, u32[]{:S(2)}) %collective-permute-start.20) | collective-permute-done | bytes 131104 | tf_op jit(solution)/shard_map/ppermute | solution.py:463
  75.8 10.9 %collective-permute-done.14.refs_4_.refs_5_ = bf16[256,256]{1,0:T(8,128)(2,1)S(1)} collective-permute-done((bf16[256,256]{1,0:T(8,128)(2,1)S(1)}, bf16[256,256]{1,0:T(8,128)(2,1)S(1)}, u32[]{:S(2)}, u32[]{:S(2)}) %collective-permute-start.14) | collective-permute-done | bytes 131104 | tf_op jit(solution)/shard_map/ppermute | solution.py:463
  87.3 1.9 collective-permute-start.22
  89.2 10.3 %collective-permute-done.22.got_ref = bf16[16,64,256]{2,1,0:T(8,128)(2,1)S(1)} collective-permute-done((bf16[16,64,256]{2,1,0:T(8,128)(2,1)S(1)}, bf16[16,64,256]{2,1,0:T(8,128)(2,1)S(1)}, u32[]{:S(2)}, u32[]{:S(2)}) %collective-permute-start.22) | collective-permute-done | bytes 524320 | tf_op jit(solution)/shard_map/ppermute | solution.py:463
  100.3 4.5 %adjoint.4.one_ref.mine_ref.refs_4_ = bf16[2,16,64,128]{3,2,1,0:T(8,128)(2,1)} custom-call(s32[4]{0:T(128)} %pad_add_fusion.m, bf16[2,2,8192,128]{3,2,1,0:T(8,128)(2,1)} %bitcast.68, bf16[2,4096,128]{2,1,0:T(8,128)(2,1)} %collective-permute-done.4.far, bf16[16,64,256]{2,1,0:T(8,128)(2,1)} %bitcast.51, bf16[16,64,256]{2,1,0:T(8,128)(2,1)} %copy-done.39), custom_call_target="tpu_custom_call" | custom-call | flops 536870 | bytes 4194 | tf_op jit(solution)/shard_map/adjoint/pallas_call | solution.py:235
  107.7 3.4 %collective-permute-start.31 = (bf16[256,256]{1,0:T(8,128)(2,1)S(1)}, bf16[256,256]{1,0:T(8,128)(2,1)S(1)}, u32[]{:S(2)}, u32[]{:S(2)}) collective-permute-start(bf16[256,256]{1,0:T(8,128)(2,1)S(1)} %get-tuple-element.71.refs_0_), channel_id=1, source_target_pairs={{0,2},{1,3},{2,0},{3,1},{4,6},{5,7},{6,4},{7,5},{8,10},{9,11},{10,... | collective-permute-start | bytes 393224 | tf_op jit(solution)/shard_map/ppermute | solution.py:463
  111.4 2.2 collective-permute-start.33
  115.2 3.2 %collective-permute-done.17 = f32[24,128]{1,0:T(8,128)S(1)} collective-permute-done((f32[24,128]{1,0:T(8,128)S(1)}, f32[24,128]{1,0:T(8,128)S(1)}, u32[]{:S(2)}, u32[]{:S(2)}) %collective-permute-start.17) | collective-permute-done | bytes 12320 | tf_op jit(solution)/shard_map/ppermute | solution.py:460
  119.8 2.3 collective-permute-done.18
  125.0 5.1 %forward.6 = (bf16[16,64,256]{2,1,0:T(8,128)(2,1)}, bf16[16,64,256]{2,1,0:T(8,128)(2,1)}) custom-call(s32[4]{0:T(128)} %pad_add_fusion.m, bf16[2,2,8192,128]{3,2,1,0:T(8,128)(2,1)} %bitcast.69, bf16[2,4096,128]{2,1,0:T(8,128)(2,1)} %collective-permute-done.4.far, bf16[2,16,64,128]{3,2,1,0:T(8,128)(2,1)} %adjoint.4.one_ref.mine_ref.refs_4_, ...), custom_call_target="tpu_custom_call" | custom-call | flops 536870 | bytes 4194 | tf_op jit(solution)/shard_map/forward/pallas_call | solution.py:194
  131.2 2.3 collective-permute-start.24
  133.5 1.7 collective-permute-done.24
  135.2 2.4 collective-permute-start.25
  137.5 2.2 collective-permute-done.25
  141.3 4.6 %adjoint.5.mine_ref.one_ref = bf16[2,16,64,128]{3,2,1,0:T(8,128)(2,1)} custom-call(s32[4]{0:T(128)} %pad_add_fusion.m, bf16[2,2,8192,128]{3,2,1,0:T(8,128)(2,1)} %bitcast.70, bf16[2,4096,128]{2,1,0:T(8,128)(2,1)} %collective-permute-done.7.far, bf16[16,64,256]{2,1,0:T(8,128)(2,1)} %bitcast.55, bf16[16,64,256]{2,1,0:T(8,128)(2,1)} %copy-done.40, ...), custom_call_target="tpu_custom_call" | custom-call | flops 536870 | bytes 4194 | tf_op jit(solution)/shard_map/adjoint/pallas_call | solution.py:235
  148.4 8.2 %collective-permute-done.35.got_ref.two_ref = bf16[2,16,64,128]{3,2,1,0:T(8,128)(2,1)S(1)} collective-permute-done((bf16[2,16,64,128]{3,2,1,0:T(8,128)(2,1)}, bf16[2,16,64,128]{3,2,1,0:T(8,128)(2,1)S(1)}, u32[]{:S(2)}, u32[]{:S(2)}) %collective-permute-start.35) | collective-permute-done | bytes 524320 | tf_op jit(solution)/shard_map/ppermute | solution.py:460
  157.3 5.1 %forward.7 = (bf16[16,64,256]{2,1,0:T(8,128)(2,1)}, bf16[16,64,256]{2,1,0:T(8,128)(2,1)}) custom-call(s32[4]{0:T(128)} %pad_add_fusion.m, bf16[2,2,8192,128]{3,2,1,0:T(8,128)(2,1)} %bitcast.71, bf16[2,4096,128]{2,1,0:T(8,128)(2,1)} %collective-permute-done.7.far, bf16[2,16,64,128]{3,2,1,0:T(8,128)(2,1)} %adjoint.5.mine_ref.one_ref, ...), custom_call_target="tpu_custom_call" | custom-call | flops 536870 | bytes 4194 | tf_op jit(solution)/shard_map/forward/pallas_call | solution.py:194
  167.3 1.7 collective-permute-start.28
  169.3 2.4 collective-permute-start.30
  174.7 3.1 %collective-permute-done.29.refs_7_ = bf16[256,256]{1,0:T(8,128)(2,1)} collective-permute-done((bf16[256,256]{1,0:T(8,128)(2,1)}, bf16[256,256]{1,0:T(8,128)(2,1)}, u32[]{:S(2)}, u32[]{:S(2)}) %collective-permute-start.29) | collective-permute-done | bytes 131104 | tf_op jit(solution)/shard_map/ppermute | solution.py:463
  179.9 2.0 collective-permute-start.45
  181.9 2.5 collective-permute-start.47
  188.6 2.5 collective-permute-start.39
  191.1 6.0 %collective-permute-done.46.refs_2_ = bf16[256,256]{1,0:T(8,128)(2,1)S(1)} collective-permute-done((bf16[256,256]{1,0:T(8,128)(2,1)S(1)}, bf16[256,256]{1,0:T(8,128)(2,1)S(1)}, u32[]{:S(2)}, u32[]{:S(2)}) %collective-permute-start.46) | collective-permute-done | bytes 131104 | tf_op jit(solution)/shard_map/ppermute | solution.py:463
  197.1 3.5 %collective-permute-done.38.refs_7_.refs_5_ = bf16[256,256]{1,0:T(8,128)(2,1)S(1)} collective-permute-done((bf16[256,256]{1,0:T(8,128)(2,1)S(1)}, bf16[256,256]{1,0:T(8,128)(2,1)S(1)}, u32[]{:S(2)}, u32[]{:S(2)}) %collective-permute-start.38) | collective-permute-done | bytes 131104 | tf_op jit(solution)/shard_map/ppermute | solution.py:463
  204.3 2.0 collective-permute-start.50
  206.9 1.9 collective-permute-start.52
  211.2 2.4 collective-permute-done.41
  214.8 2.5 collective-permute-done.42
  218.1 4.7 %adjoint.6 = (bf16[16,64,128]{2,1,0:T(8,128)(2,1)}, f32[16,64,128]{2,1,0:T(8,128)}) custom-call(s32[4]{0:T(128)} %pad_add_fusion.m, bf16[2,2,8192,128]{3,2,1,0:T(8,128)(2,1)} %bitcast.72, bf16[2,4096,128]{2,1,0:T(8,128)(2,1)} %collective-permute-done.4.far, bf16[16,64,256]{2,1,0:T(8,128)(2,1)} %bitcast.49, bf16[16,64,256]{2,1,0:T(8,128)(2,1)} %copy-done.38), custom_call_target="tpu_custom_call" | custom-call | flops 536870 | bytes 4194 | tf_op jit(solution)/shard_map/adjoint/pallas_call | solution.py:235
  224.8 1.8 collective-permute-start.49
  227.6 2.6 %collective-permute-done.43 = f32[24,128]{1,0:T(8,128)S(1)} collective-permute-done((f32[24,128]{1,0:T(8,128)S(1)}, f32[24,128]{1,0:T(8,128)S(1)}, u32[]{:S(2)}, u32[]{:S(2)}) %collective-permute-start.43) | collective-permute-done | bytes 12320 | tf_op jit(solution)/shard_map/ppermute | solution.py:463
  231.1 3.8 %collective-permute-done.44 = f32[24,128]{1,0:T(8,128)S(1)} collective-permute-done((f32[24,128]{1,0:T(8,128)S(1)}, f32[24,128]{1,0:T(8,128)S(1)}, u32[]{:S(2)}, u32[]{:S(2)}) %collective-permute-start.44) | collective-permute-done | bytes 12320 | tf_op jit(solution)/shard_map/ppermute | solution.py:463
  236.5 4.5 %adjoint.7 = (bf16[16,64,128]{2,1,0:T(8,128)(2,1)}, f32[16,64,128]{2,1,0:T(8,128)}) custom-call(s32[4]{0:T(128)} %pad_add_fusion.m, bf16[2,2,8192,128]{3,2,1,0:T(8,128)(2,1)} %bitcast.73, bf16[2,4096,128]{2,1,0:T(8,128)(2,1)} %collective-permute-done.7.far, bf16[16,64,256]{2,1,0:T(8,128)(2,1)} %bitcast.46, ...), custom_call_target="tpu_custom_call" | custom-call | flops 536870 | bytes 4194 | tf_op jit(solution)/shard_map/adjoint/pallas_call | solution.py:235
  248.8 1.9 fusion.2
  (213 shorter events, 71.9 us)
Async XLA Ops:
  6.5 17.4 %collective-permute-start.4 = (bf16[2,4096,128]{2,1,0:T(8,128)(2,1)}, bf16[2,4096,128]{2,1,0:T(8,128)(2,1)}, u32[]{:S(2)}, u32[]{:S(2)}) collective-permute-start(bf16[2,4096,128]{2,1,0:T(8,128)(2,1)} %cut.2), channel_id=1, source_target_pairs={{0,8},{8,0},{16,24},{24,16},{1,9},{9,1},{17,25},{25,17},{2,10},{10... | collective-permute-start | bytes 6291464 | tf_op jit(solution)/shard_map/ppermute | solution.py:457
  10.1 26.1 %collective-permute-start.7 = (bf16[2,4096,128]{2,1,0:T(8,128)(2,1)}, bf16[2,4096,128]{2,1,0:T(8,128)(2,1)}, u32[]{:S(2)}, u32[]{:S(2)}) collective-permute-start(bf16[2,4096,128]{2,1,0:T(8,128)(2,1)} %cut.3.refs_1_), channel_id=1, source_target_pairs={{0,8},{8,0},{16,24},{24,16},{1,9},{9,1},{17,25},{25,17},{2,10},{10... | collective-permute-start | bytes 6291464 | tf_op jit(solution)/shard_map/ppermute | solution.py:457
  10.4 4.5 %collective-permute-start = (f32[16,128]{1,0:T(8,128)S(1)}, f32[16,128]{1,0:T(8,128)S(1)}, u32[]{:S(2)}, u32[]{:S(2)}) collective-permute-start(f32[16,128]{1,0:T(8,128)S(1)} %copy-done.43), channel_id=1, source_target_pairs={{0,1},{1,0},{2,3},{3,2},{4,5},{5,4},{6,7},{7,6},{8,9},{9,8},{10,11... | collective-permute-start | bytes 24584 | tf_op jit(solution)/shard_map/ppermute | solution.py:463
  14.9 4.4 %collective-permute-start.1 = (f32[32,128]{1,0:T(8,128)S(1)}, f32[32,128]{1,0:T(8,128)S(1)}, u32[]{:S(2)}, u32[]{:S(2)}) collective-permute-start(f32[32,128]{1,0:T(8,128)S(1)} %pad_maximum_fusion.3), channel_id=1, source_target_pairs={{0,2},{1,3},{2,0},{3,1},{4,6},{5,7},{6,4},{7,5},{8,10},{9,11},{10,... | collective-permute-start | bytes 49160 | tf_op jit(solution)/shard_map/ppermute | solution.py:463
  17.0 6.9 %collective-permute-start.5 = (bf16[16,64,128]{2,1,0:T(8,128)(2,1)S(1)}, bf16[16,64,128]{2,1,0:T(8,128)(2,1)S(1)}, u32[]{:S(2)}, u32[]{:S(2)}) collective-permute-start(bf16[16,64,128]{2,1,0:T(8,128)(2,1)S(1)} %copy-done.7), channel_id=1, source_target_pairs={{0,16},{8,24},{16,0},{24,8},{1,17},{9,25},{17,1},{25,9},{2,18},{10... | collective-permute-start | bytes 786440 | tf_op jit(solution)/shard_map/ppermute | solution.py:460
  29.6 14.7 %collective-permute-start.6 = (bf16[16,64,256]{2,1,0:T(8,128)(2,1)}, bf16[16,64,256]{2,1,0:T(8,128)(2,1)S(1)}, u32[]{:S(2)}, u32[]{:S(2)}) collective-permute-start(bf16[16,64,256]{2,1,0:T(8,128)(2,1)} %get-tuple-element.47), channel_id=1, source_target_pairs={{0,1},{1,0},{2,3},{3,2},{4,5},{5,4},{6,7},{7,6},{8,9},{9,8},{10,11... | collective-permute-start | bytes 1572872 | tf_op jit(solution)/shard_map/ppermute | solution.py:463
  32.1 6.4 %collective-permute-start.8 = (bf16[16,64,128]{2,1,0:T(8,128)(2,1)S(1)}, bf16[16,64,128]{2,1,0:T(8,128)(2,1)S(1)}, u32[]{:S(2)}, u32[]{:S(2)}) collective-permute-start(bf16[16,64,128]{2,1,0:T(8,128)(2,1)S(1)} %ordered.4), channel_id=1, source_target_pairs={{0,16},{8,24},{16,0},{24,8},{1,17},{9,25},{17,1},{25,9},{2,18},{10... | collective-permute-start | bytes 786440 | tf_op jit(solution)/shard_map/ppermute | solution.py:460
  33.6 11.2 %collective-permute-start.2 = (f32[64,128]{1,0:T(8,128)S(1)}, f32[64,128]{1,0:T(8,128)S(1)}, u32[]{:S(2)}, u32[]{:S(2)}) collective-permute-start(f32[64,128]{1,0:T(8,128)S(1)} %copy-done.42), channel_id=1, source_target_pairs={{0,4},{1,5},{2,6},{3,7},{4,0},{5,1},{6,2},{7,3},{8,12},{9,13},{10,... | collective-permute-start | bytes 98312 | tf_op jit(solution)/shard_map/ppermute | solution.py:463
  44.3 15.7 %collective-permute-start.12 = (bf16[16,64,256]{2,1,0:T(8,128)(2,1)}, bf16[16,64,256]{2,1,0:T(8,128)(2,1)S(1)}, u32[]{:S(2)}, u32[]{:S(2)}) collective-permute-start(bf16[16,64,256]{2,1,0:T(8,128)(2,1)} %ordered.5.refs_0_), channel_id=1, source_target_pairs={{0,1},{1,0},{2,3},{3,2},{4,5},{5,4},{6,7},{7,6},{8,9},{9,8},{10,11... | collective-permute-start | bytes 1572872 | tf_op jit(solution)/shard_map/ppermute | solution.py:463
  44.9 5.7 %collective-permute-start.3 = (f32[2,32,128]{2,1,0:T(8,128)S(1)}, f32[2,32,128]{2,1,0:T(8,128)S(1)}, u32[]{:S(2)}, u32[]{:S(2)}) collective-permute-start(f32[2,32,128]{2,1,0:T(8,128)S(1)} %get-tuple-element.96), channel_id=1, source_target_pairs={{0,8},{8,0},{16,24},{24,16},{1,9},{9,1},{17,25},{25,17},{2,10},{10... | collective-permute-start | bytes 98312 | tf_op jit(solution)/shard_map/ppermute | solution.py:457
  46.5 12.3 %collective-permute-start.10 = (bf16[256,256]{1,0:T(8,128)(2,1)}, bf16[256,256]{1,0:T(8,128)(2,1)S(1)}, u32[]{:S(2)}, u32[]{:S(2)}) collective-permute-start(bf16[256,256]{1,0:T(8,128)(2,1)} %get-tuple-element.51), channel_id=1, source_target_pairs={{0,4},{1,5},{2,6},{3,7},{4,0},{5,1},{6,2},{7,3},{8,12},{9,13},{10,... | collective-permute-start | bytes 393224 | tf_op jit(solution)/shard_map/ppermute | solution.py:463
  49.1 9.7 %collective-permute-start.11 = (bf16[256,256]{1,0:T(8,128)(2,1)S(1)}, bf16[256,256]{1,0:T(8,128)(2,1)S(1)}, u32[]{:S(2)}, u32[]{:S(2)}) collective-permute-start(bf16[256,256]{1,0:T(8,128)(2,1)S(1)} %get-tuple-element.52), channel_id=1, source_target_pairs={{0,6},{1,7},{2,4},{3,5},{4,2},{5,3},{6,0},{7,1},{8,14},{9,15},{10,... | collective-permute-start | bytes 393224 | tf_op jit(solution)/shard_map/ppermute | solution.py:463
  49.3 10.6 %collective-permute-start.9 = (bf16[256,256]{1,0:T(8,128)(2,1)S(1)}, bf16[256,256]{1,0:T(8,128)(2,1)S(1)}, u32[]{:S(2)}, u32[]{:S(2)}) collective-permute-start(bf16[256,256]{1,0:T(8,128)(2,1)S(1)} %get-tuple-element.50), channel_id=1, source_target_pairs={{0,2},{1,3},{2,0},{3,1},{4,6},{5,7},{6,4},{7,5},{8,10},{9,11},{10,... | collective-permute-start | bytes 393224 | tf_op jit(solution)/shard_map/ppermute | solution.py:463
  60.6 8.6 %collective-permute-start.19 = (bf16[256,256]{1,0:T(8,128)(2,1)S(1)}, bf16[256,256]{1,0:T(8,128)(2,1)S(1)}, u32[]{:S(2)}, u32[]{:S(2)}) collective-permute-start(bf16[256,256]{1,0:T(8,128)(2,1)S(1)} %get-tuple-element.60.refs_0_), channel_id=1, source_target_pairs={{0,2},{1,3},{2,0},{3,1},{4,6},{5,7},{6,4},{7,5},{8,10},{9,11},{10,... | collective-permute-start | bytes 393224 | tf_op jit(solution)/shard_map/ppermute | solution.py:463
  62.8 12.9 %collective-permute-start.20 = (bf16[256,256]{1,0:T(8,128)(2,1)S(1)}, bf16[256,256]{1,0:T(8,128)(2,1)S(1)}, u32[]{:S(2)}, u32[]{:S(2)}) collective-permute-start(bf16[256,256]{1,0:T(8,128)(2,1)S(1)} %get-tuple-element.60.refs_0_), channel_id=1, source_target_pairs={{0,4},{1,5},{2,6},{3,7},{4,0},{5,1},{6,2},{7,3},{8,12},{9,13},{10,... | collective-permute-start | bytes 393224 | tf_op jit(solution)/shard_map/ppermute | solution.py:463
  64.1 11.7 %collective-permute-start.21 = (bf16[256,256]{1,0:T(8,128)(2,1)S(1)}, bf16[256,256]{1,0:T(8,128)(2,1)S(1)}, u32[]{:S(2)}, u32[]{:S(2)}) collective-permute-start(bf16[256,256]{1,0:T(8,128)(2,1)S(1)} %get-tuple-element.60.refs_0_), channel_id=1, source_target_pairs={{0,6},{1,7},{2,4},{3,5},{4,2},{5,3},{6,0},{7,1},{8,14},{9,15},{10,... | collective-permute-start | bytes 393224 | tf_op jit(solution)/shard_map/ppermute | solution.py:463
  66.2 9.6 %collective-permute-start.13 = (bf16[256,256]{1,0:T(8,128)(2,1)S(1)}, bf16[256,256]{1,0:T(8,128)(2,1)S(1)}, u32[]{:S(2)}, u32[]{:S(2)}) collective-permute-start(bf16[256,256]{1,0:T(8,128)(2,1)S(1)} %get-tuple-element.56), channel_id=1, source_target_pairs={{0,2},{1,3},{2,0},{3,1},{4,6},{5,7},{6,4},{7,5},{8,10},{9,11},{10,... | collective-permute-start | bytes 393224 | tf_op jit(solution)/shard_map/ppermute | solution.py:463
  67.1 19.6 %collective-permute-start.14 = (bf16[256,256]{1,0:T(8,128)(2,1)S(1)}, bf16[256,256]{1,0:T(8,128)(2,1)S(1)}, u32[]{:S(2)}, u32[]{:S(2)}) collective-permute-start(bf16[256,256]{1,0:T(8,128)(2,1)S(1)} %get-tuple-element.57), channel_id=1, source_target_pairs={{0,4},{1,5},{2,6},{3,7},{4,0},{5,1},{6,2},{7,3},{8,12},{9,13},{10,... | collective-permute-start | bytes 393224 | tf_op jit(solution)/shard_map/ppermute | solution.py:463
  69.2 17.4 %collective-permute-start.15 = (bf16[256,256]{1,0:T(8,128)(2,1)S(1)}, bf16[256,256]{1,0:T(8,128)(2,1)S(1)}, u32[]{:S(2)}, u32[]{:S(2)}) collective-permute-start(bf16[256,256]{1,0:T(8,128)(2,1)S(1)} %get-tuple-element.58), channel_id=1, source_target_pairs={{0,6},{1,7},{2,4},{3,5},{4,2},{5,3},{6,0},{7,1},{8,14},{9,15},{10,... | collective-permute-start | bytes 393224 | tf_op jit(solution)/shard_map/ppermute | solution.py:463
  87.3 12.2 %collective-permute-start.22 = (bf16[16,64,256]{2,1,0:T(8,128)(2,1)S(1)}, bf16[16,64,256]{2,1,0:T(8,128)(2,1)S(1)}, u32[]{:S(2)}, u32[]{:S(2)}) collective-permute-start(bf16[16,64,256]{2,1,0:T(8,128)(2,1)S(1)} %bitcast.50), channel_id=1, source_target_pairs={{0,1},{1,0},{2,3},{3,2},{4,5},{5,4},{6,7},{7,6},{8,9},{9,8},{10,11... | collective-permute-start | bytes 1572872 | tf_op jit(solution)/shard_map/ppermute | solution.py:463
  104.8 19.4 %collective-permute-start.23 = (bf16[2,16,64,128]{3,2,1,0:T(8,128)(2,1)}, bf16[2,16,64,128]{3,2,1,0:T(8,128)(2,1)S(1)}, u32[]{:S(2)}, u32[]{:S(2)}) collective-permute-start(bf16[2,16,64,128]{3,2,1,0:T(8,128)(2,1)} %adjoint.4.one_ref.mine_ref.refs_4_), channel_id=1, source_target_pairs={{0,16},{8,24},{16,0},{24,8},{1,17},{9,25},{17,1},{25,9},{2,18},{10... | collective-permute-start | bytes 1572872 | tf_op jit(solution)/shard_map/ppermute | solution.py:460
  107.7 14.5 %collective-permute-start.31 = (bf16[256,256]{1,0:T(8,128)(2,1)S(1)}, bf16[256,256]{1,0:T(8,128)(2,1)S(1)}, u32[]{:S(2)}, u32[]{:S(2)}) collective-permute-start(bf16[256,256]{1,0:T(8,128)(2,1)S(1)} %get-tuple-element.71.refs_0_), channel_id=1, source_target_pairs={{0,2},{1,3},{2,0},{3,1},{4,6},{5,7},{6,4},{7,5},{8,10},{9,11},{10,... | collective-permute-start | bytes 393224 | tf_op jit(solution)/shard_map/ppermute | solution.py:463
  111.1 11.0 %collective-permute-start.32 = (bf16[256,256]{1,0:T(8,128)(2,1)S(1)}, bf16[256,256]{1,0:T(8,128)(2,1)S(1)}, u32[]{:S(2)}, u32[]{:S(2)}) collective-permute-start(bf16[256,256]{1,0:T(8,128)(2,1)S(1)} %get-tuple-element.71.refs_0_), channel_id=1, source_target_pairs={{0,4},{1,5},{2,6},{3,7},{4,0},{5,1},{6,2},{7,3},{8,12},{9,13},{10,... | collective-permute-start | bytes 393224 | tf_op jit(solution)/shard_map/ppermute | solution.py:463
  111.4 10.8 %collective-permute-start.33 = (bf16[256,256]{1,0:T(8,128)(2,1)S(1)}, bf16[256,256]{1,0:T(8,128)(2,1)S(1)}, u32[]{:S(2)}, u32[]{:S(2)}) collective-permute-start(bf16[256,256]{1,0:T(8,128)(2,1)S(1)} %get-tuple-element.71.refs_0_), channel_id=1, source_target_pairs={{0,6},{1,7},{2,4},{3,5},{4,2},{5,3},{6,0},{7,1},{8,14},{9,15},{10,... | collective-permute-start | bytes 393224 | tf_op jit(solution)/shard_map/ppermute | solution.py:463
  122.8 17.7 %collective-permute-start.34 = (bf16[16,64,256]{2,1,0:T(8,128)(2,1)S(1)}, bf16[16,64,256]{2,1,0:T(8,128)(2,1)S(1)}, u32[]{:S(2)}, u32[]{:S(2)}) collective-permute-start(bf16[16,64,256]{2,1,0:T(8,128)(2,1)S(1)} %bitcast.54), channel_id=1, source_target_pairs={{0,1},{1,0},{2,3},{3,2},{4,5},{5,4},{6,7},{7,6},{8,9},{9,8},{10,11... | collective-permute-start | bytes 1572872 | tf_op jit(solution)/shard_map/ppermute | solution.py:463
  131.2 4.0 %collective-permute-start.24 = (f32[24,128]{1,0:T(8,128)S(1)}, f32[24,128]{1,0:T(8,128)S(1)}, u32[]{:S(2)}, u32[]{:S(2)}) collective-permute-start(f32[24,128]{1,0:T(8,128)S(1)} %ordered.6), channel_id=1, source_target_pairs={{0,2},{1,3},{2,0},{3,1},{4,6},{5,7},{6,4},{7,5},{8,10},{9,11},{10,... | collective-permute-start | bytes 36872 | tf_op jit(solution)/shard_map/ppermute | solution.py:463
  135.2 4.6 %collective-permute-start.25 = (f32[24,128]{1,0:T(8,128)S(1)}, f32[24,128]{1,0:T(8,128)S(1)}, u32[]{:S(2)}, u32[]{:S(2)}) collective-permute-start(f32[24,128]{1,0:T(8,128)S(1)} %add.106), channel_id=1, source_target_pairs={{0,4},{1,5},{2,6},{3,7},{4,0},{5,1},{6,2},{7,3},{8,12},{9,13},{10,... | collective-permute-start | bytes 36872 | tf_op jit(solution)/shard_map/ppermute | solution.py:463
  145.9 10.6 %collective-permute-start.35 = (bf16[2,16,64,128]{3,2,1,0:T(8,128)(2,1)}, bf16[2,16,64,128]{3,2,1,0:T(8,128)(2,1)S(1)}, u32[]{:S(2)}, u32[]{:S(2)}) collective-permute-start(bf16[2,16,64,128]{3,2,1,0:T(8,128)(2,1)} %adjoint.5.mine_ref.one_ref), channel_id=1, source_target_pairs={{0,16},{8,24},{16,0},{24,8},{1,17},{9,25},{17,1},{25,9},{2,18},{10... | collective-permute-start | bytes 1572872 | tf_op jit(solution)/shard_map/ppermute | solution.py:460
  147.5 14.9 %collective-permute-start.27 = (bf16[16,64,256]{2,1,0:T(8,128)(2,1)S(1)}, bf16[16,64,256]{2,1,0:T(8,128)(2,1)S(1)}, u32[]{:S(2)}, u32[]{:S(2)}) collective-permute-start(bf16[16,64,256]{2,1,0:T(8,128)(2,1)S(1)} %copy-done.18), channel_id=1, source_target_pairs={{0,1},{1,0},{2,3},{3,2},{4,5},{5,4},{6,7},{7,6},{8,9},{9,8},{10,11... | collective-permute-start | bytes 1572872 | tf_op jit(solution)/shard_map/ppermute | solution.py:463
  162.4 22.0 %collective-permute-start.36 = (bf16[16,64,256]{2,1,0:T(8,128)(2,1)}, bf16[16,64,256]{2,1,0:T(8,128)(2,1)}, u32[]{:S(2)}, u32[]{:S(2)}) collective-permute-start(bf16[16,64,256]{2,1,0:T(8,128)(2,1)} %ordered.7), channel_id=1, source_target_pairs={{0,1},{1,0},{2,3},{3,2},{4,5},{5,4},{6,7},{7,6},{8,9},{9,8},{10,11... | collective-permute-start | bytes 1572872 | tf_op jit(solution)/shard_map/ppermute | solution.py:463
  163.8 7.9 %collective-permute-start.26 = (f32[32]{0:T(128)S(1)}, f32[32]{0:T(128)S(1)}, u32[]{:S(2)}, u32[]{:S(2)}) collective-permute-start(f32[32]{0:T(128)S(1)} %copy-done.36), channel_id=1, source_target_pairs={{0,16},{8,24},{16,0},{24,8},{1,17},{9,25},{17,1},{25,9},{2,18},{10... | collective-permute-start | bytes 392 | tf_op jit(solution)/shard_map/ppermute | solution.py:460
  167.3 7.4 %collective-permute-start.28 = (bf16[256,256]{1,0:T(8,128)(2,1)}, bf16[256,256]{1,0:T(8,128)(2,1)}, u32[]{:S(2)}, u32[]{:S(2)}) collective-permute-start(bf16[256,256]{1,0:T(8,128)(2,1)} %get-tuple-element.66), channel_id=1, source_target_pairs={{0,2},{1,3},{2,0},{3,1},{4,6},{5,7},{6,4},{7,5},{8,10},{9,11},{10,... | collective-permute-start | bytes 393224 | tf_op jit(solution)/shard_map/ppermute | solution.py:463
  169.0 8.8 %collective-permute-start.29 = (bf16[256,256]{1,0:T(8,128)(2,1)}, bf16[256,256]{1,0:T(8,128)(2,1)}, u32[]{:S(2)}, u32[]{:S(2)}) collective-permute-start(bf16[256,256]{1,0:T(8,128)(2,1)} %get-tuple-element.67), channel_id=1, source_target_pairs={{0,4},{1,5},{2,6},{3,7},{4,0},{5,1},{6,2},{7,3},{8,12},{9,13},{10,... | collective-permute-start | bytes 393224 | tf_op jit(solution)/shard_map/ppermute | solution.py:463
  169.3 8.5 %collective-permute-start.30 = (bf16[256,256]{1,0:T(8,128)(2,1)}, bf16[256,256]{1,0:T(8,128)(2,1)}, u32[]{:S(2)}, u32[]{:S(2)}) collective-permute-start(bf16[256,256]{1,0:T(8,128)(2,1)} %get-tuple-element.68), channel_id=1, source_target_pairs={{0,6},{1,7},{2,4},{3,5},{4,2},{5,3},{6,0},{7,1},{8,14},{9,15},{10,... | collective-permute-start | bytes 393224 | tf_op jit(solution)/shard_map/ppermute | solution.py:463
  179.9 8.7 %collective-permute-start.45 = (bf16[256,256]{1,0:T(8,128)(2,1)S(1)}, bf16[256,256]{1,0:T(8,128)(2,1)S(1)}, u32[]{:S(2)}, u32[]{:S(2)}) collective-permute-start(bf16[256,256]{1,0:T(8,128)(2,1)S(1)} %get-tuple-element.82.refs_0_), channel_id=1, source_target_pairs={{0,2},{1,3},{2,0},{3,1},{4,6},{5,7},{6,4},{7,5},{8,10},{9,11},{10,... | collective-permute-start | bytes 393224 | tf_op jit(solution)/shard_map/ppermute | solution.py:463
  181.9 15.1 %collective-permute-start.46 = (bf16[256,256]{1,0:T(8,128)(2,1)S(1)}, bf16[256,256]{1,0:T(8,128)(2,1)S(1)}, u32[]{:S(2)}, u32[]{:S(2)}) collective-permute-start(bf16[256,256]{1,0:T(8,128)(2,1)S(1)} %get-tuple-element.82.refs_0_), channel_id=1, source_target_pairs={{0,4},{1,5},{2,6},{3,7},{4,0},{5,1},{6,2},{7,3},{8,12},{9,13},{10,... | collective-permute-start | bytes 393224 | tf_op jit(solution)/shard_map/ppermute | solution.py:463
  181.9 15.1 %collective-permute-start.47 = (bf16[256,256]{1,0:T(8,128)(2,1)S(1)}, bf16[256,256]{1,0:T(8,128)(2,1)S(1)}, u32[]{:S(2)}, u32[]{:S(2)}) collective-permute-start(bf16[256,256]{1,0:T(8,128)(2,1)S(1)} %get-tuple-element.82.refs_0_), channel_id=1, source_target_pairs={{0,6},{1,7},{2,4},{3,5},{4,2},{5,3},{6,0},{7,1},{8,14},{9,15},{10,... | collective-permute-start | bytes 393224 | tf_op jit(solution)/shard_map/ppermute | solution.py:463
  186.6 10.4 %collective-permute-start.37 = (bf16[256,256]{1,0:T(8,128)(2,1)S(1)}, bf16[256,256]{1,0:T(8,128)(2,1)S(1)}, u32[]{:S(2)}, u32[]{:S(2)}) collective-permute-start(bf16[256,256]{1,0:T(8,128)(2,1)S(1)} %get-tuple-element.76), channel_id=1, source_target_pairs={{0,2},{1,3},{2,0},{3,1},{4,6},{5,7},{6,4},{7,5},{8,10},{9,11},{10,... | collective-permute-start | bytes 393224 | tf_op jit(solution)/shard_map/ppermute | solution.py:463
  187.7 12.8 %collective-permute-start.38 = (bf16[256,256]{1,0:T(8,128)(2,1)S(1)}, bf16[256,256]{1,0:T(8,128)(2,1)S(1)}, u32[]{:S(2)}, u32[]{:S(2)}) collective-permute-start(bf16[256,256]{1,0:T(8,128)(2,1)S(1)} %get-tuple-element.77), channel_id=1, source_target_pairs={{0,4},{1,5},{2,6},{3,7},{4,0},{5,1},{6,2},{7,3},{8,12},{9,13},{10,... | collective-permute-start | bytes 393224 | tf_op jit(solution)/shard_map/ppermute | solution.py:463
  188.6 11.9 %collective-permute-start.39 = (bf16[256,256]{1,0:T(8,128)(2,1)S(1)}, bf16[256,256]{1,0:T(8,128)(2,1)S(1)}, u32[]{:S(2)}, u32[]{:S(2)}) collective-permute-start(bf16[256,256]{1,0:T(8,128)(2,1)S(1)} %get-tuple-element.78), channel_id=1, source_target_pairs={{0,6},{1,7},{2,4},{3,5},{4,2},{5,3},{6,0},{7,1},{8,14},{9,15},{10,... | collective-permute-start | bytes 393224 | tf_op jit(solution)/shard_map/ppermute | solution.py:463
  201.1 16.2 %collective-permute-start.48 = (bf16[16,64,256]{2,1,0:T(8,128)(2,1)S(1)}, bf16[16,64,256]{2,1,0:T(8,128)(2,1)S(1)}, u32[]{:S(2)}, u32[]{:S(2)}) collective-permute-start(bf16[16,64,256]{2,1,0:T(8,128)(2,1)S(1)} %bitcast.48), channel_id=1, source_target_pairs={{0,1},{1,0},{2,3},{3,2},{4,5},{5,4},{6,7},{7,6},{8,9},{9,8},{10,11... | collective-permute-start | bytes 1572872 | tf_op jit(solution)/shard_map/ppermute | solution.py:463
  204.3 18.6 %collective-permute-start.50 = (bf16[256,256]{1,0:T(8,128)(2,1)S(1)}, bf16[256,256]{1,0:T(8,128)(2,1)S(1)}, u32[]{:S(2)}, u32[]{:S(2)}) collective-permute-start(bf16[256,256]{1,0:T(8,128)(2,1)S(1)} %get-tuple-element.85.refs_0_), channel_id=1, source_target_pairs={{0,2},{1,3},{2,0},{3,1},{4,6},{5,7},{6,4},{7,5},{8,10},{9,11},{10,... | collective-permute-start | bytes 393224 | tf_op jit(solution)/shard_map/ppermute | solution.py:463
  206.3 16.6 %collective-permute-start.51 = (bf16[256,256]{1,0:T(8,128)(2,1)S(1)}, bf16[256,256]{1,0:T(8,128)(2,1)S(1)}, u32[]{:S(2)}, u32[]{:S(2)}) collective-permute-start(bf16[256,256]{1,0:T(8,128)(2,1)S(1)} %get-tuple-element.85.refs_0_), channel_id=1, source_target_pairs={{0,4},{1,5},{2,6},{3,7},{4,0},{5,1},{6,2},{7,3},{8,12},{9,13},{10,... | collective-permute-start | bytes 393224 | tf_op jit(solution)/shard_map/ppermute | solution.py:463
  206.9 16.0 %collective-permute-start.52 = (bf16[256,256]{1,0:T(8,128)(2,1)S(1)}, bf16[256,256]{1,0:T(8,128)(2,1)S(1)}, u32[]{:S(2)}, u32[]{:S(2)}) collective-permute-start(bf16[256,256]{1,0:T(8,128)(2,1)S(1)} %get-tuple-element.85.refs_0_), channel_id=1, source_target_pairs={{0,6},{1,7},{2,4},{3,5},{4,2},{5,3},{6,0},{7,1},{8,14},{9,15},{10,... | collective-permute-start | bytes 393224 | tf_op jit(solution)/shard_map/ppermute | solution.py:463
  223.5 12.3 %collective-permute-start.53 = (bf16[16,64,256]{2,1,0:T(8,128)(2,1)S(1)}, bf16[16,64,256]{2,1,0:T(8,128)(2,1)}, u32[]{:S(2)}, u32[]{:S(2)}) collective-permute-start(bf16[16,64,256]{2,1,0:T(8,128)(2,1)S(1)} %bitcast.45), channel_id=1, source_target_pairs={{0,1},{1,0},{2,3},{3,2},{4,5},{5,4},{6,7},{7,6},{8,9},{9,8},{10,11... | collective-permute-start | bytes 1572872 | tf_op jit(solution)/shard_map/ppermute | solution.py:463
  224.8 11.0 %collective-permute-start.49 = (bf16[16,64,128]{2,1,0:T(8,128)(2,1)}, bf16[16,64,128]{2,1,0:T(8,128)(2,1)S(1)}, u32[]{:S(2)}, u32[]{:S(2)}) collective-permute-start(bf16[16,64,128]{2,1,0:T(8,128)(2,1)} %get-tuple-element.84.refs_4_), channel_id=1, source_target_pairs={{0,16},{8,24},{16,0},{24,8},{1,17},{9,25},{17,1},{25,9},{2,18},{10... | collective-permute-start | bytes 786440 | tf_op jit(solution)/shard_map/ppermute | solution.py:460
  230.3 4.6 %collective-permute-start.44 = (f32[24,128]{1,0:T(8,128)S(1)}, f32[24,128]{1,0:T(8,128)S(1)}, u32[]{:S(2)}, u32[]{:S(2)}) collective-permute-start(f32[24,128]{1,0:T(8,128)S(1)} %add.112), channel_id=1, source_target_pairs={{0,4},{1,5},{2,6},{3,7},{4,0},{5,1},{6,2},{7,3},{8,12},{9,13},{10,... | collective-permute-start | bytes 36872 | tf_op jit(solution)/shard_map/ppermute | solution.py:463
  241.0 6.6 %collective-permute-start.54 = (bf16[16,64,128]{2,1,0:T(8,128)(2,1)}, bf16[16,64,128]{2,1,0:T(8,128)(2,1)S(1)}, u32[]{:S(2)}, u32[]{:S(2)}) collective-permute-start(bf16[16,64,128]{2,1,0:T(8,128)(2,1)} %get-tuple-element.87), channel_id=1, source_target_pairs={{0,16},{8,24},{16,0},{24,8},{1,17},{9,25},{17,1},{25,9},{2,18},{10... | collective-permute-start | bytes 786440 | tf_op jit(solution)/shard_map/ppermute | solution.py:460
  (51 other events, 370.7 us)

commit v3 on v2

--- a/solution.py
+++ b/solution.py
@@ -444,6 +444,35 @@
     )(alpha, damping, start, mine, got)
 
 
+def update_call(plan, chunk, scalars, damping, start, residual, image, mine, got, outs):
+    block = (plan.part, plan.rows, plan.sources)
+
+    def kernel(scalars_ref, damp_ref, start_ref, residual_ref, image_ref, mine_ref, got_ref, *refs):
+        solution_ref, out_ref = refs[len(outs):]
+        alpha_0, alpha_1, beta = scalars_ref[0], scalars_ref[1], scalars_ref[2]
+        for f in range(plan.part):
+            begin, rest = start_ref[f], residual_ref[f]
+            second = mine_ref[f] + got_ref[f].astype(F32) + damp_ref[chunk * plan.part + f] * rest
+            second = second + beta * image_ref[f]
+            solution_ref[f] = alpha_0 * begin + alpha_1 * (rest + beta * begin)
+            out_ref[f] = rest - alpha_1 * second
+
+    here = pl.BlockSpec(block, lambda i: (chunk, 0, 0))
+    alone = pl.BlockSpec(block, lambda i: (0, 0, 0))
+    values = pl.BlockSpec(memory_space=pltpu.SMEM)
+    return pl.pallas_call(
+        kernel,
+        grid=(1,),
+        in_specs=[values, values, here, alone, alone, alone, alone] + [ANYWHERE] * len(outs),
+        out_specs=[here, here],
+        out_shape=[jax.ShapeDtypeStruct(start.shape, F32)] * 2,
+        input_output_aliases={7 + i: i for i in range(len(outs))},
+        cost_estimate=cost(8 * start.size, 16 * start.size),
+        compiler_params=pltpu.CompilerParams(vmem_limit_bytes=KERNEL_BYTES),
+        name="update",
+    )(scalars, damping, start, residual, image, mine, got, *outs)
+
+
 def body(n_sens, n_src, operator, right_side, noise_weights, damping):
     plan = Plan(operator, right_side, n_sens, n_src, CHUNKS)
     sens, src = lax.axis_index("sens"), lax.axis_index("src")
@@ -518,17 +547,18 @@
 
     def both_products(scaled, near_sums, last, then, received):
         outs, wait, sums = [], (), None
+        pieces = [[one] + [to_src(one, step) for step in steps] for one in scaled]
         for k in chunks:
-            pieces = [scaled[k]] + [to_src(scaled[k], step) for step in steps]
-            own = place_call(plan, meta, pieces, wait + tuple(sum(received[k + 1:k + 2], [])))
+            own = place_call(plan, meta, pieces[k], wait + tuple(sum(received[k + 1:k + 2], [])))
             halves = (own, to_half(own))
+            if k == 0:
+                wait = tuple(sum(pieces[1:2], [])) if received else ()
             if k == 1:
-                after = outs[0][1][0]
-                far_sums, sums = total_far(near_sums if last else ordered(near_sums, after))
-                wait = (after, far_sums)
-            out = adjoint_call(plan, k, meta, whole, far[k], halves, last, wait if k > 0 else ())
+                far_sums, sums = total_far(near_sums)
+                wait = (outs[0][1][0], far_sums)
+            out = adjoint_call(plan, k, meta, whole, far[k], halves, last, wait)
             outs.append((out, then(k, out)))
-            wait = (out[0] if last else out, near_sums)
+            wait = (out,) if received else (out[0] if last else out, near_sums)
         return outs, total_far(near_sums)[1] if sums is None else sums
 
     sends = [send for send, _ in pairs]
@@ -563,18 +593,20 @@
         for k in chunks
     ])
     near_1 = total_near(sum(stats))
-    outs, sums = both_products(scaled, near_1, True, lambda k, out: (to_pair(out[0]),), [each[1:] for each in pieces])
+    outs, sums = both_products(scaled, near_1, True, lambda k, out: (to_pair(out[0]),), [])
     norm_1 = sums[0]
     beta = norm_1 / norm_0
     curve_1 = sums[1] + 2.0 * beta * sums[2] + beta * beta * curve_0
     alpha_1 = norm_1 / curve_1
 
-    final = [out[1] + rest[0].astype(F32) for out, rest in outs]
-    residual, image_0 = jnp.concatenate(residual), jnp.concatenate(image_0)
-    image_1 = jnp.concatenate(final) + damping[:, None, None] * residual + beta * image_0
-    solution = alpha_0 * start + alpha_1 * (residual + beta * start)
-    residual = residual - alpha_1 * image_1
-    return solution.reshape(right_side.shape), residual.reshape(right_side.shape)
+    scalars = jnp.stack([alpha_0[0], alpha_1, beta])
+    results = ()
+    for k in chunks:
+        (_, mine), (got,) = outs[k]
+        results = update_call(
+            plan, k, scalars, damping, start, residual[k], image_0[k], mine, got, results
+        )
+    return tuple(result.reshape(right_side.shape) for result in results)
 
 
 def solution(mesh):

time: 252 us -> 250 us (level)
  waiting for transfers between devices: 88 us -> 73.8 us
  local copies, waits for them, and re-layouts: 17.1 us -> 25.8 us
  Pallas kernels: 57.4 us -> 61.8 us
  other arithmetic: 7.14 us -> 3.04 us
  starting transfers between devices: 74.6 us -> 78.2 us
    ppermute x41, waiting for transfers between devices: 65.1 us -> 55.3 us  [to_src(): return lax.ppermute(array, 'src', [(j, j ^ step) for j in range(n_src)])]
    unnamed x88 -> x134, local copies, waits for them, and re-layouts: 15.6 us -> 24.4 us
    ppermute x41, starting transfers between devices: 63 us -> 68.3 us  [to_src(): return lax.ppermute(array, 'src', [(j, j ^ step) for j in range(n_src)])]
    ppermute x9, waiting for transfers between devices: 20.5 us -> 16.2 us  [to_pair(): return lax.ppermute(array, 'sens', [(i, i ^ 2) for i in range(n_sens)])]
    pallas_call x0 -> x2, Pallas kernels: none -> 3.51 us  [update_call(): pl.pallas_call(kernel, grid=(1,), in_specs=[values, values, here, alone,...]
  transfers between devices with their start and end apart: 55 -> 55, of which waited for: 23 -> 23; matrix products, arithmetic and copies ran while one was open for 2% -> 2% of each run, Pallas kernels for 15% -> 19%
where the time goes in v3:
time: 250 us; the launch traced here: 249 us
  starting transfers between devices  78.2 us (31%)
  waiting for transfers between devices  73.8 us (30%)
  Pallas kernels  61.8 us (25%)
  local copies, waits for them, and re-layouts  25.8 us (10%)
  between operations  6.38 us (3%)
  other arithmetic  3.04 us (1%)
    ppermute x41, starting transfers between devices, to_src(): return lax.ppermute(array, 'src', [(j, j ^ step) for j in range(n_src)])  68.3 us
    ppermute x41, waiting for transfers between devices, to_src(): return lax.ppermute(array, 'src', [(j, j ^ step) for j in range(n_src)])  55.3 us
    unnamed x134, local copies, waits for them, and re-layouts  24.4 us
    pallas_call x4, Pallas kernels, forward_call(): pl.pallas_call(kernel, grid=(1,), in_specs=[pl.BlockSpec(memory_space=plt...  20.1 us
    pallas_call x4, Pallas kernels, adjoint_call(): pl.pallas_call(kernel, grid=(1,), in_specs=[pl.BlockSpec(memory_space=plt...  18.6 us
    ppermute x9, waiting for transfers between devices, to_pair(): return lax.ppermute(array, 'sens', [(i, i ^ 2) for i in range(n_sens)])  16.2 us
    ppermute x9, starting transfers between devices, to_pair(): return lax.ppermute(array, 'sens', [(i, i ^ 2) for i in range(n_sens)])  9.03 us
    pallas_call x2, Pallas kernels, cut_call(): pl.pallas_call(kernel, in_specs=[pl.BlockSpec(memory_space=pltpu.SMEM), A...  6.27 us
  transfers between devices with their start and end apart: 55, of which 23 were waited for; matrix products, arithmetic and copies ran while one was open for 2% of the time, Pallas kernels for 19%

profile of v3, /device:TPU:0, one launch (start us, length us, event | category | flops | bytes accessed | tf_op | source)
XLA Modules:
  0.0 249.0 jit_solution(6882477904644183905)
XLA Ops:
  3.3 3.1 %cut.2 = bf16[2,4096,128]{2,1,0:T(8,128)(2,1)} custom-call(s32[4]{0:T(128)} %pad_add_fusion.m, bf16[2,2,8192,128]{3,2,1,0:T(8,128)(2,1)} %bitcast.60, bf16[16,64,128]{2,1,0:T(8,128)(2,1)} %copy-done.6), custom_call_target="tpu_custom_call" | custom-call | bytes 2097 | tf_op jit(solution)/shard_map/cut/pallas_call | solution.py:130
  7.0 3.1 %cut.3.refs_1_ = bf16[2,4096,128]{2,1,0:T(8,128)(2,1)} custom-call(s32[4]{0:T(128)} %pad_add_fusion.m, bf16[2,2,8192,128]{3,2,1,0:T(8,128)(2,1)} %bitcast.61, bf16[16,64,128]{2,1,0:T(8,128)(2,1)} %copy-done.6), custom_call_target="tpu_custom_call" | custom-call | bytes 2097 | tf_op jit(solution)/shard_map/cut/pallas_call | solution.py:130
  10.4 2.8 %collective-permute-start = (f32[16,128]{1,0:T(8,128)S(1)}, f32[16,128]{1,0:T(8,128)S(1)}, u32[]{:S(2)}, u32[]{:S(2)}) collective-permute-start(f32[16,128]{1,0:T(8,128)S(1)} %copy-done.66), channel_id=1, source_target_pairs={{0,1},{1,0},{2,3},{3,2},{4,5},{5,4},{6,7},{7,6},{8,9},{9,8},{10,11... | collective-permute-start | bytes 24584 | tf_op jit(solution)/shard_map/ppermute | solution.py:492
  13.2 1.6 collective-permute-done
  14.9 2.1 collective-permute-start.1
  19.9 4.0 %collective-permute-done.5.two_ref.refs_1_ = bf16[16,64,128]{2,1,0:T(8,128)(2,1)S(1)} collective-permute-done((bf16[16,64,128]{2,1,0:T(8,128)(2,1)S(1)}, bf16[16,64,128]{2,1,0:T(8,128)(2,1)S(1)}, u32[]{:S(2)}, u32[]{:S(2)}) %collective-permute-start.5) | collective-permute-done | bytes 262176 | tf_op jit(solution)/shard_map/ppermute | solution.py:489
  24.6 5.0 %forward.4 = (bf16[16,64,256]{2,1,0:T(8,128)(2,1)}, bf16[16,64,256]{2,1,0:T(8,128)(2,1)}) custom-call(s32[4]{0:T(128)} %pad_add_fusion.m, bf16[2,2,8192,128]{3,2,1,0:T(8,128)(2,1)} %bitcast.62, bf16[2,4096,128]{2,1,0:T(8,128)(2,1)} %collective-permute-done.4.far, f32[32,64,128]{2,1,0:T(8,128)} %bitcast.35, bf16[16,64,128]{2,1,0:T(8,128)(2,1)} %copy-done.18, ...), custom_call_target="tpu_custom_call" | custom-call | flops 536870 | bytes 4194 | tf_op jit(solution)/shard_map/forward/pallas_call | solution.py:194
  33.6 4.9 %collective-permute-done.8.two_ref = bf16[16,64,128]{2,1,0:T(8,128)(2,1)S(1)} collective-permute-done((bf16[16,64,128]{2,1,0:T(8,128)(2,1)S(1)}, bf16[16,64,128]{2,1,0:T(8,128)(2,1)S(1)}, u32[]{:S(2)}, u32[]{:S(2)}) %collective-permute-start.8) | collective-permute-done | bytes 262176 | tf_op jit(solution)/shard_map/ppermute | solution.py:489
  39.2 5.0 %forward.5 = (bf16[16,64,256]{2,1,0:T(8,128)(2,1)}, bf16[16,64,256]{2,1,0:T(8,128)(2,1)}) custom-call(s32[4]{0:T(128)} %pad_add_fusion.m, bf16[2,2,8192,128]{3,2,1,0:T(8,128)(2,1)} %bitcast.63, bf16[2,4096,128]{2,1,0:T(8,128)(2,1)} %collective-permute-done.7.far, f32[32,64,128]{2,1,0:T(8,128)} %bitcast.36, bf16[16,64,128]{2,1,0:T(8,128)(2,1)} %copy-done.64), custom_call_target="tpu_custom_call" | custom-call | flops 536870 | bytes 4194 | tf_op jit(solution)/shard_map/forward/pallas_call | solution.py:194
  44.8 2.6 %collective-permute-start.2 = (f32[64,128]{1,0:T(8,128)S(1)}, f32[64,128]{1,0:T(8,128)S(1)}, u32[]{:S(2)}, u32[]{:S(2)}) collective-permute-start(f32[64,128]{1,0:T(8,128)S(1)} %copy-done.65), channel_id=1, source_target_pairs={{0,4},{1,5},{2,6},{3,7},{4,0},{5,1},{6,2},{7,3},{8,12},{9,13},{10,... | collective-permute-start | bytes 98312 | tf_op jit(solution)/shard_map/ppermute | solution.py:492
  47.4 2.4 collective-permute-done.2
  51.5 2.7 %collective-permute-start.10 = (bf16[256,256]{1,0:T(8,128)(2,1)}, bf16[256,256]{1,0:T(8,128)(2,1)S(1)}, u32[]{:S(2)}, u32[]{:S(2)}) collective-permute-start(bf16[256,256]{1,0:T(8,128)(2,1)} %get-tuple-element.55), channel_id=1, source_target_pairs={{0,4},{1,5},{2,6},{3,7},{4,0},{5,1},{6,2},{7,3},{8,12},{9,13},{10,... | collective-permute-start | bytes 393224 | tf_op jit(solution)/shard_map/ppermute | solution.py:492
  57.6 2.9 %collective-permute-start.14 = (bf16[256,256]{1,0:T(8,128)(2,1)}, bf16[256,256]{1,0:T(8,128)(2,1)S(1)}, u32[]{:S(2)}, u32[]{:S(2)}) collective-permute-start(bf16[256,256]{1,0:T(8,128)(2,1)} %get-tuple-element.61), channel_id=1, source_target_pairs={{0,4},{1,5},{2,6},{3,7},{4,0},{5,1},{6,2},{7,3},{8,12},{9,13},{10,... | collective-permute-start | bytes 393224 | tf_op jit(solution)/shard_map/ppermute | solution.py:492
  62.0 3.3 %collective-permute-done.11.refs_5_ = bf16[256,256]{1,0:T(8,128)(2,1)S(1)} collective-permute-done((bf16[256,256]{1,0:T(8,128)(2,1)}, bf16[256,256]{1,0:T(8,128)(2,1)S(1)}, u32[]{:S(2)}, u32[]{:S(2)}) %collective-permute-start.11) | collective-permute-done | bytes 131104 | tf_op jit(solution)/shard_map/ppermute | solution.py:492
  66.9 3.0 %collective-permute-start.24 = (bf16[256,256]{1,0:T(8,128)(2,1)S(1)}, bf16[256,256]{1,0:T(8,128)(2,1)S(1)}, u32[]{:S(2)}, u32[]{:S(2)}) collective-permute-start(bf16[256,256]{1,0:T(8,128)(2,1)S(1)} %get-tuple-element.65.refs_0_), channel_id=1, source_target_pairs={{0,6},{1,7},{2,4},{3,5},{4,2},{5,3},{6,0},{7,1},{8,14},{9,15},{10,... | collective-permute-start | bytes 393224 | tf_op jit(solution)/shard_map/ppermute | solution.py:492
  69.9 10.1 %collective-permute-start.23 = (bf16[256,256]{1,0:T(8,128)(2,1)S(1)}, bf16[256,256]{1,0:T(8,128)(2,1)S(1)}, u32[]{:S(2)}, u32[]{:S(2)}) collective-permute-start(bf16[256,256]{1,0:T(8,128)(2,1)S(1)} %get-tuple-element.65.refs_0_), channel_id=1, source_target_pairs={{0,4},{1,5},{2,6},{3,7},{4,0},{5,1},{6,2},{7,3},{8,12},{9,13},{10,... | collective-permute-start | bytes 393224 | tf_op jit(solution)/shard_map/ppermute | solution.py:492
  80.5 8.7 %collective-permute-done.23.refs_2_ = bf16[256,256]{1,0:T(8,128)(2,1)S(1)} collective-permute-done((bf16[256,256]{1,0:T(8,128)(2,1)S(1)}, bf16[256,256]{1,0:T(8,128)(2,1)S(1)}, u32[]{:S(2)}, u32[]{:S(2)}) %collective-permute-start.23) | collective-permute-done | bytes 131104 | tf_op jit(solution)/shard_map/ppermute | solution.py:492
  89.8 1.7 collective-permute-start.25
  93.4 3.5 %collective-permute-start.28 = (bf16[256,256]{1,0:T(8,128)(2,1)S(1)}, bf16[256,256]{1,0:T(8,128)(2,1)S(1)}, u32[]{:S(2)}, u32[]{:S(2)}) collective-permute-start(bf16[256,256]{1,0:T(8,128)(2,1)S(1)} %get-tuple-element.66.refs_0_), channel_id=1, source_target_pairs={{0,6},{1,7},{2,4},{3,5},{4,2},{5,3},{6,0},{7,1},{8,14},{9,15},{10,... | collective-permute-start | bytes 393224 | tf_op jit(solution)/shard_map/ppermute | solution.py:492
  97.8 3.8 %collective-permute-done.28.refs_3_ = bf16[256,256]{1,0:T(8,128)(2,1)S(1)} collective-permute-done((bf16[256,256]{1,0:T(8,128)(2,1)S(1)}, bf16[256,256]{1,0:T(8,128)(2,1)S(1)}, u32[]{:S(2)}, u32[]{:S(2)}) %collective-permute-start.28) | collective-permute-done | bytes 131104 | tf_op jit(solution)/shard_map/ppermute | solution.py:492
  101.7 5.3 %collective-permute-done.27.refs_2_ = bf16[256,256]{1,0:T(8,128)(2,1)S(1)} collective-permute-done((bf16[256,256]{1,0:T(8,128)(2,1)S(1)}, bf16[256,256]{1,0:T(8,128)(2,1)S(1)}, u32[]{:S(2)}, u32[]{:S(2)}) %collective-permute-start.27) | collective-permute-done | bytes 131104 | tf_op jit(solution)/shard_map/ppermute | solution.py:492
  108.5 4.5 %adjoint.4.mine_ref.one_ref.refs_4_ = bf16[2,16,64,128]{3,2,1,0:T(8,128)(2,1)} custom-call(s32[4]{0:T(128)} %pad_add_fusion.m, bf16[2,2,8192,128]{3,2,1,0:T(8,128)(2,1)} %bitcast.64, bf16[2,4096,128]{2,1,0:T(8,128)(2,1)} %collective-permute-done.4.far, bf16[16,64,256]{2,1,0:T(8,128)(2,1)} %bitcast.49, bf16[16,64,256]{2,1,0:T(8,128)(2,1)} %copy-done.62, ...), custom_call_target="tpu_custom_call" | custom-call | flops 536870 | bytes 4194 | tf_op jit(solution)/shard_map/adjoint/pallas_call | solution.py:235
  122.2 4.1 %collective-permute-done.17 = f32[24,128]{1,0:T(8,128)S(1)} collective-permute-done((f32[24,128]{1,0:T(8,128)S(1)}, f32[24,128]{1,0:T(8,128)S(1)}, u32[]{:S(2)}, u32[]{:S(2)}) %collective-permute-start.17) | collective-permute-done | bytes 12320 | tf_op jit(solution)/shard_map/ppermute | solution.py:489
  126.8 5.8 %collective-permute-done.18 = f32[24,128]{1,0:T(8,128)S(1)} collective-permute-done((f32[24,128]{1,0:T(8,128)S(1)}, f32[24,128]{1,0:T(8,128)S(1)}, u32[]{:S(2)}, u32[]{:S(2)}) %collective-permute-start.18) | collective-permute-done | bytes 12320 | tf_op jit(solution)/shard_map/ppermute | solution.py:492
  132.7 3.6 %collective-permute-done.19 = f32[24,128]{1,0:T(8,128)S(1)} collective-permute-done((f32[24,128]{1,0:T(8,128)S(1)}, f32[24,128]{1,0:T(8,128)S(1)}, u32[]{:S(2)}, u32[]{:S(2)}) %collective-permute-start.19) | collective-permute-done | bytes 12320 | tf_op jit(solution)/shard_map/ppermute | solution.py:492
  137.2 5.1 %forward.6 = (bf16[16,64,256]{2,1,0:T(8,128)(2,1)}, bf16[16,64,256]{2,1,0:T(8,128)(2,1)}) custom-call(s32[4]{0:T(128)} %pad_add_fusion.m, bf16[2,2,8192,128]{3,2,1,0:T(8,128)(2,1)} %bitcast.65, bf16[2,4096,128]{2,1,0:T(8,128)(2,1)} %collective-permute-done.4.far, bf16[2,16,64,128]{3,2,1,0:T(8,128)(2,1)} %adjoint.4.mine_ref.one_ref.refs_4_, ...), custom_call_target="tpu_custom_call" | custom-call | flops 536870 | bytes 4194 | tf_op jit(solution)/shard_map/forward/pallas_call | solution.py:194
  144.4 4.6 %adjoint.5.mine_ref.one_ref = bf16[2,16,64,128]{3,2,1,0:T(8,128)(2,1)} custom-call(s32[4]{0:T(128)} %pad_add_fusion.m, bf16[2,2,8192,128]{3,2,1,0:T(8,128)(2,1)} %bitcast.66, bf16[2,4096,128]{2,1,0:T(8,128)(2,1)} %collective-permute-done.7.far, bf16[16,64,256]{2,1,0:T(8,128)(2,1)} %bitcast.55, bf16[16,64,256]{2,1,0:T(8,128)(2,1)} %copy-done.63, ...), custom_call_target="tpu_custom_call" | custom-call | flops 536870 | bytes 4194 | tf_op jit(solution)/shard_map/adjoint/pallas_call | solution.py:235
  151.1 1.8 collective-permute-done.30.refs_1_
  160.1 5.1 %forward.7 = (bf16[16,64,256]{2,1,0:T(8,128)(2,1)}, bf16[16,64,256]{2,1,0:T(8,128)(2,1)}) custom-call(s32[4]{0:T(128)} %pad_add_fusion.m, bf16[2,2,8192,128]{3,2,1,0:T(8,128)(2,1)} %bitcast.67, bf16[2,4096,128]{2,1,0:T(8,128)(2,1)} %collective-permute-done.7.far, bf16[2,16,64,128]{3,2,1,0:T(8,128)(2,1)} %adjoint.5.mine_ref.one_ref, ...), custom_call_target="tpu_custom_call" | custom-call | flops 536870 | bytes 4194 | tf_op jit(solution)/shard_map/forward/pallas_call | solution.py:194
  174.7 2.4 collective-permute-start.50
  179.2 2.5 %collective-permute-done.50.refs_3_ = bf16[256,256]{1,0:T(8,128)(2,1)S(1)} collective-permute-done((bf16[256,256]{1,0:T(8,128)(2,1)S(1)}, bf16[256,256]{1,0:T(8,128)(2,1)S(1)}, u32[]{:S(2)}, u32[]{:S(2)}) %collective-permute-start.50) | collective-permute-done | bytes 131104 | tf_op jit(solution)/shard_map/ppermute | solution.py:492
  181.7 3.3 %collective-permute-done.49.refs_2_ = bf16[256,256]{1,0:T(8,128)(2,1)S(1)} collective-permute-done((bf16[256,256]{1,0:T(8,128)(2,1)S(1)}, bf16[256,256]{1,0:T(8,128)(2,1)S(1)}, u32[]{:S(2)}, u32[]{:S(2)}) %collective-permute-start.49) | collective-permute-done | bytes 131104 | tf_op jit(solution)/shard_map/ppermute | solution.py:492
  188.4 3.1 %collective-permute-start.38 = (bf16[256,256]{1,0:T(8,128)(2,1)S(1)}, bf16[256,256]{1,0:T(8,128)(2,1)S(1)}, u32[]{:S(2)}, u32[]{:S(2)}) collective-permute-start(bf16[256,256]{1,0:T(8,128)(2,1)S(1)} %get-tuple-element.81), channel_id=1, source_target_pairs={{0,4},{1,5},{2,6},{3,7},{4,0},{5,1},{6,2},{7,3},{8,12},{9,13},{10,... | collective-permute-start | bytes 393224 | tf_op jit(solution)/shard_map/ppermute | solution.py:492
  194.7 5.5 %collective-permute-done.38.refs_7_ = bf16[256,256]{1,0:T(8,128)(2,1)S(1)} collective-permute-done((bf16[256,256]{1,0:T(8,128)(2,1)S(1)}, bf16[256,256]{1,0:T(8,128)(2,1)S(1)}, u32[]{:S(2)}, u32[]{:S(2)}) %collective-permute-start.38) | collective-permute-done | bytes 131104 | tf_op jit(solution)/shard_map/ppermute | solution.py:492
  200.9 2.3 collective-permute-start.47
  203.2 2.6 %collective-permute-start.46 = (bf16[256,256]{1,0:T(8,128)(2,1)S(1)}, bf16[256,256]{1,0:T(8,128)(2,1)S(1)}, u32[]{:S(2)}, u32[]{:S(2)}) collective-permute-start(bf16[256,256]{1,0:T(8,128)(2,1)S(1)} %get-tuple-element.86.refs_0_), channel_id=1, source_target_pairs={{0,4},{1,5},{2,6},{3,7},{4,0},{5,1},{6,2},{7,3},{8,12},{9,13},{10,... | collective-permute-start | bytes 393224 | tf_op jit(solution)/shard_map/ppermute | solution.py:492
  207.5 3.1 %collective-permute-done.41 = f32[24,128]{1,0:T(8,128)S(1)} collective-permute-done((f32[24,128]{1,0:T(8,128)S(1)}, f32[24,128]{1,0:T(8,128)S(1)}, u32[]{:S(2)}, u32[]{:S(2)}) %collective-permute-start.41) | collective-permute-done | bytes 12320 | tf_op jit(solution)/shard_map/ppermute | solution.py:489
  210.7 1.6 collective-permute-start.42
  212.3 2.1 collective-permute-done.42
  215.2 4.8 %adjoint.6 = (bf16[16,64,128]{2,1,0:T(8,128)(2,1)}, f32[16,64,128]{2,1,0:T(8,128)}) custom-call(s32[4]{0:T(128)} %pad_add_fusion.m, bf16[2,2,8192,128]{3,2,1,0:T(8,128)(2,1)} %bitcast.68, bf16[2,4096,128]{2,1,0:T(8,128)(2,1)} %collective-permute-done.4.far, bf16[16,64,256]{2,1,0:T(8,128)(2,1)} %bitcast.51, bf16[16,64,256]{2,1,0:T(8,128)(2,1)} %copy-done.60), custom_call_target="tpu_custom_call" | custom-call | flops 536870 | bytes 4194 | tf_op jit(solution)/shard_map/adjoint/pallas_call | solution.py:235
  221.5 1.7 collective-permute-start.52
  223.7 2.0 collective-permute-start.43
  225.7 1.7 collective-permute-done.43
  227.4 2.9 %collective-permute-start.44 = (f32[24,128]{1,0:T(8,128)S(1)}, f32[24,128]{1,0:T(8,128)S(1)}, u32[]{:S(2)}, u32[]{:S(2)}) collective-permute-start(f32[24,128]{1,0:T(8,128)S(1)} %add.90), channel_id=1, source_target_pairs={{0,4},{1,5},{2,6},{3,7},{4,0},{5,1},{6,2},{7,3},{8,12},{9,13},{10,... | collective-permute-start | bytes 36872 | tf_op jit(solution)/shard_map/ppermute | solution.py:492
  230.3 1.7 collective-permute-done.44
  234.4 4.7 %adjoint.7 = (bf16[16,64,128]{2,1,0:T(8,128)(2,1)}, f32[16,64,128]{2,1,0:T(8,128)}) custom-call(s32[4]{0:T(128)} %pad_add_fusion.m, bf16[2,2,8192,128]{3,2,1,0:T(8,128)(2,1)} %bitcast.69, bf16[2,4096,128]{2,1,0:T(8,128)(2,1)} %collective-permute-done.7.far, bf16[16,64,256]{2,1,0:T(8,128)(2,1)} %bitcast.46, bf16[16,64,256]{2,1,0:T(8,128)(2,1)} %copy-done.61, ...), custom_call_target="tpu_custom_call" | custom-call | flops 536870 | bytes 4194 | tf_op jit(solution)/shard_map/adjoint/pallas_call | solution.py:235
  245.5 1.7 update.2
  247.2 1.8 update.3
  (258 shorter events, 74.8 us)
Async XLA Ops:
  6.5 17.4 %collective-permute-start.4 = (bf16[2,4096,128]{2,1,0:T(8,128)(2,1)}, bf16[2,4096,128]{2,1,0:T(8,128)(2,1)}, u32[]{:S(2)}, u32[]{:S(2)}) collective-permute-start(bf16[2,4096,128]{2,1,0:T(8,128)(2,1)} %cut.2), channel_id=1, source_target_pairs={{0,8},{8,0},{16,24},{24,16},{1,9},{9,1},{17,25},{25,17},{2,10},{10... | collective-permute-start | bytes 6291464 | tf_op jit(solution)/shard_map/ppermute | solution.py:486
  10.1 23.5 %collective-permute-start.7 = (bf16[2,4096,128]{2,1,0:T(8,128)(2,1)}, bf16[2,4096,128]{2,1,0:T(8,128)(2,1)}, u32[]{:S(2)}, u32[]{:S(2)}) collective-permute-start(bf16[2,4096,128]{2,1,0:T(8,128)(2,1)} %cut.3.refs_1_), channel_id=1, source_target_pairs={{0,8},{8,0},{16,24},{24,16},{1,9},{9,1},{17,25},{25,17},{2,10},{10... | collective-permute-start | bytes 6291464 | tf_op jit(solution)/shard_map/ppermute | solution.py:486
  10.4 4.5 %collective-permute-start = (f32[16,128]{1,0:T(8,128)S(1)}, f32[16,128]{1,0:T(8,128)S(1)}, u32[]{:S(2)}, u32[]{:S(2)}) collective-permute-start(f32[16,128]{1,0:T(8,128)S(1)} %copy-done.66), channel_id=1, source_target_pairs={{0,1},{1,0},{2,3},{3,2},{4,5},{5,4},{6,7},{7,6},{8,9},{9,8},{10,11... | collective-permute-start | bytes 24584 | tf_op jit(solution)/shard_map/ppermute | solution.py:492
  17.0 6.9 %collective-permute-start.5 = (bf16[16,64,128]{2,1,0:T(8,128)(2,1)S(1)}, bf16[16,64,128]{2,1,0:T(8,128)(2,1)S(1)}, u32[]{:S(2)}, u32[]{:S(2)}) collective-permute-start(bf16[16,64,128]{2,1,0:T(8,128)(2,1)S(1)} %copy-done.7), channel_id=1, source_target_pairs={{0,16},{8,24},{16,0},{24,8},{1,17},{9,25},{17,1},{25,9},{2,18},{10... | collective-permute-start | bytes 786440 | tf_op jit(solution)/shard_map/ppermute | solution.py:489
  29.6 14.6 %collective-permute-start.6 = (bf16[16,64,256]{2,1,0:T(8,128)(2,1)}, bf16[16,64,256]{2,1,0:T(8,128)(2,1)S(1)}, u32[]{:S(2)}, u32[]{:S(2)}) collective-permute-start(bf16[16,64,256]{2,1,0:T(8,128)(2,1)} %get-tuple-element.51), channel_id=1, source_target_pairs={{0,1},{1,0},{2,3},{3,2},{4,5},{5,4},{6,7},{7,6},{8,9},{9,8},{10,11... | collective-permute-start | bytes 1572872 | tf_op jit(solution)/shard_map/ppermute | solution.py:492
  32.1 6.4 %collective-permute-start.8 = (bf16[16,64,128]{2,1,0:T(8,128)(2,1)S(1)}, bf16[16,64,128]{2,1,0:T(8,128)(2,1)S(1)}, u32[]{:S(2)}, u32[]{:S(2)}) collective-permute-start(bf16[16,64,128]{2,1,0:T(8,128)(2,1)S(1)} %ordered.3), channel_id=1, source_target_pairs={{0,16},{8,24},{16,0},{24,8},{1,17},{9,25},{17,1},{25,9},{2,18},{10... | collective-permute-start | bytes 786440 | tf_op jit(solution)/shard_map/ppermute | solution.py:489
  44.2 11.4 %collective-permute-start.12 = (bf16[16,64,256]{2,1,0:T(8,128)(2,1)}, bf16[16,64,256]{2,1,0:T(8,128)(2,1)S(1)}, u32[]{:S(2)}, u32[]{:S(2)}) collective-permute-start(bf16[16,64,256]{2,1,0:T(8,128)(2,1)} %ordered.4.refs_0_), channel_id=1, source_target_pairs={{0,1},{1,0},{2,3},{3,2},{4,5},{5,4},{6,7},{7,6},{8,9},{9,8},{10,11... | collective-permute-start | bytes 1572872 | tf_op jit(solution)/shard_map/ppermute | solution.py:492
  44.8 5.0 %collective-permute-start.2 = (f32[64,128]{1,0:T(8,128)S(1)}, f32[64,128]{1,0:T(8,128)S(1)}, u32[]{:S(2)}, u32[]{:S(2)}) collective-permute-start(f32[64,128]{1,0:T(8,128)S(1)} %copy-done.65), channel_id=1, source_target_pairs={{0,4},{1,5},{2,6},{3,7},{4,0},{5,1},{6,2},{7,3},{8,12},{9,13},{10,... | collective-permute-start | bytes 98312 | tf_op jit(solution)/shard_map/ppermute | solution.py:492
  49.8 7.8 %collective-permute-start.3 = (f32[2,32,128]{2,1,0:T(8,128)S(1)}, f32[2,32,128]{2,1,0:T(8,128)S(1)}, u32[]{:S(2)}, u32[]{:S(2)}) collective-permute-start(f32[2,32,128]{2,1,0:T(8,128)S(1)} %get-tuple-element.102), channel_id=1, source_target_pairs={{0,8},{8,0},{16,24},{24,16},{1,9},{9,1},{17,25},{25,17},{2,10},{10... | collective-permute-start | bytes 98312 | tf_op jit(solution)/shard_map/ppermute | solution.py:486
  51.2 9.3 %collective-permute-start.9 = (bf16[256,256]{1,0:T(8,128)(2,1)}, bf16[256,256]{1,0:T(8,128)(2,1)S(1)}, u32[]{:S(2)}, u32[]{:S(2)}) collective-permute-start(bf16[256,256]{1,0:T(8,128)(2,1)} %get-tuple-element.54), channel_id=1, source_target_pairs={{0,2},{1,3},{2,0},{3,1},{4,6},{5,7},{6,4},{7,5},{8,10},{9,11},{10,... | collective-permute-start | bytes 393224 | tf_op jit(solution)/shard_map/ppermute | solution.py:492
  51.5 10.6 %collective-permute-start.10 = (bf16[256,256]{1,0:T(8,128)(2,1)}, bf16[256,256]{1,0:T(8,128)(2,1)S(1)}, u32[]{:S(2)}, u32[]{:S(2)}) collective-permute-start(bf16[256,256]{1,0:T(8,128)(2,1)} %get-tuple-element.55), channel_id=1, source_target_pairs={{0,4},{1,5},{2,6},{3,7},{4,0},{5,1},{6,2},{7,3},{8,12},{9,13},{10,... | collective-permute-start | bytes 393224 | tf_op jit(solution)/shard_map/ppermute | solution.py:492
  54.1 11.2 %collective-permute-start.11 = (bf16[256,256]{1,0:T(8,128)(2,1)}, bf16[256,256]{1,0:T(8,128)(2,1)S(1)}, u32[]{:S(2)}, u32[]{:S(2)}) collective-permute-start(bf16[256,256]{1,0:T(8,128)(2,1)} %get-tuple-element.56), channel_id=1, source_target_pairs={{0,6},{1,7},{2,4},{3,5},{4,2},{5,3},{6,0},{7,1},{8,14},{9,15},{10,... | collective-permute-start | bytes 393224 | tf_op jit(solution)/shard_map/ppermute | solution.py:492
  56.9 23.1 %collective-permute-start.13 = (bf16[256,256]{1,0:T(8,128)(2,1)}, bf16[256,256]{1,0:T(8,128)(2,1)S(1)}, u32[]{:S(2)}, u32[]{:S(2)}) collective-permute-start(bf16[256,256]{1,0:T(8,128)(2,1)} %get-tuple-element.60), channel_id=1, source_target_pairs={{0,2},{1,3},{2,0},{3,1},{4,6},{5,7},{6,4},{7,5},{8,10},{9,11},{10,... | collective-permute-start | bytes 393224 | tf_op jit(solution)/shard_map/ppermute | solution.py:492
  57.6 22.8 %collective-permute-start.14 = (bf16[256,256]{1,0:T(8,128)(2,1)}, bf16[256,256]{1,0:T(8,128)(2,1)S(1)}, u32[]{:S(2)}, u32[]{:S(2)}) collective-permute-start(bf16[256,256]{1,0:T(8,128)(2,1)} %get-tuple-element.61), channel_id=1, source_target_pairs={{0,4},{1,5},{2,6},{3,7},{4,0},{5,1},{6,2},{7,3},{8,12},{9,13},{10,... | collective-permute-start | bytes 393224 | tf_op jit(solution)/shard_map/ppermute | solution.py:492
  60.5 19.9 %collective-permute-start.15 = (bf16[256,256]{1,0:T(8,128)(2,1)S(1)}, bf16[256,256]{1,0:T(8,128)(2,1)S(1)}, u32[]{:S(2)}, u32[]{:S(2)}) collective-permute-start(bf16[256,256]{1,0:T(8,128)(2,1)S(1)} %get-tuple-element.62), channel_id=1, source_target_pairs={{0,6},{1,7},{2,4},{3,5},{4,2},{5,3},{6,0},{7,1},{8,14},{9,15},{10,... | collective-permute-start | bytes 393224 | tf_op jit(solution)/shard_map/ppermute | solution.py:492
  66.9 13.5 %collective-permute-start.24 = (bf16[256,256]{1,0:T(8,128)(2,1)S(1)}, bf16[256,256]{1,0:T(8,128)(2,1)S(1)}, u32[]{:S(2)}, u32[]{:S(2)}) collective-permute-start(bf16[256,256]{1,0:T(8,128)(2,1)S(1)} %get-tuple-element.65.refs_0_), channel_id=1, source_target_pairs={{0,6},{1,7},{2,4},{3,5},{4,2},{5,3},{6,0},{7,1},{8,14},{9,15},{10,... | collective-permute-start | bytes 393224 | tf_op jit(solution)/shard_map/ppermute | solution.py:492
  69.9 19.3 %collective-permute-start.23 = (bf16[256,256]{1,0:T(8,128)(2,1)S(1)}, bf16[256,256]{1,0:T(8,128)(2,1)S(1)}, u32[]{:S(2)}, u32[]{:S(2)}) collective-permute-start(bf16[256,256]{1,0:T(8,128)(2,1)S(1)} %get-tuple-element.65.refs_0_), channel_id=1, source_target_pairs={{0,4},{1,5},{2,6},{3,7},{4,0},{5,1},{6,2},{7,3},{8,12},{9,13},{10,... | collective-permute-start | bytes 393224 | tf_op jit(solution)/shard_map/ppermute | solution.py:492
  80.0 9.2 %collective-permute-start.22 = (bf16[256,256]{1,0:T(8,128)(2,1)S(1)}, bf16[256,256]{1,0:T(8,128)(2,1)S(1)}, u32[]{:S(2)}, u32[]{:S(2)}) collective-permute-start(bf16[256,256]{1,0:T(8,128)(2,1)S(1)} %get-tuple-element.65.refs_0_), channel_id=1, source_target_pairs={{0,2},{1,3},{2,0},{3,1},{4,6},{5,7},{6,4},{7,5},{8,10},{9,11},{10,... | collective-permute-start | bytes 393224 | tf_op jit(solution)/shard_map/ppermute | solution.py:492
  89.8 17.2 %collective-permute-start.25 = (bf16[16,64,256]{2,1,0:T(8,128)(2,1)S(1)}, bf16[16,64,256]{2,1,0:T(8,128)(2,1)S(1)}, u32[]{:S(2)}, u32[]{:S(2)}) collective-permute-start(bf16[16,64,256]{2,1,0:T(8,128)(2,1)S(1)} %bitcast.48), channel_id=1, source_target_pairs={{0,1},{1,0},{2,3},{3,2},{4,5},{5,4},{6,7},{7,6},{8,9},{9,8},{10,11... | collective-permute-start | bytes 1572872 | tf_op jit(solution)/shard_map/ppermute | solution.py:492
  93.4 8.2 %collective-permute-start.28 = (bf16[256,256]{1,0:T(8,128)(2,1)S(1)}, bf16[256,256]{1,0:T(8,128)(2,1)S(1)}, u32[]{:S(2)}, u32[]{:S(2)}) collective-permute-start(bf16[256,256]{1,0:T(8,128)(2,1)S(1)} %get-tuple-element.66.refs_0_), channel_id=1, source_target_pairs={{0,6},{1,7},{2,4},{3,5},{4,2},{5,3},{6,0},{7,1},{8,14},{9,15},{10,... | collective-permute-start | bytes 393224 | tf_op jit(solution)/shard_map/ppermute | solution.py:492
  97.0 10.0 %collective-permute-start.27 = (bf16[256,256]{1,0:T(8,128)(2,1)S(1)}, bf16[256,256]{1,0:T(8,128)(2,1)S(1)}, u32[]{:S(2)}, u32[]{:S(2)}) collective-permute-start(bf16[256,256]{1,0:T(8,128)(2,1)S(1)} %get-tuple-element.66.refs_0_), channel_id=1, source_target_pairs={{0,4},{1,5},{2,6},{3,7},{4,0},{5,1},{6,2},{7,3},{8,12},{9,13},{10,... | collective-permute-start | bytes 393224 | tf_op jit(solution)/shard_map/ppermute | solution.py:492
  97.0 10.0 %collective-permute-start.26 = (bf16[256,256]{1,0:T(8,128)(2,1)S(1)}, bf16[256,256]{1,0:T(8,128)(2,1)S(1)}, u32[]{:S(2)}, u32[]{:S(2)}) collective-permute-start(bf16[256,256]{1,0:T(8,128)(2,1)S(1)} %get-tuple-element.66.refs_0_), channel_id=1, source_target_pairs={{0,2},{1,3},{2,0},{3,1},{4,6},{5,7},{6,4},{7,5},{8,10},{9,11},{10,... | collective-permute-start | bytes 393224 | tf_op jit(solution)/shard_map/ppermute | solution.py:492
  113.0 23.3 %collective-permute-start.29 = (bf16[2,16,64,128]{3,2,1,0:T(8,128)(2,1)}, bf16[2,16,64,128]{3,2,1,0:T(8,128)(2,1)S(1)}, u32[]{:S(2)}, u32[]{:S(2)}) collective-permute-start(bf16[2,16,64,128]{3,2,1,0:T(8,128)(2,1)} %adjoint.4.mine_ref.one_ref.refs_4_), channel_id=1, source_target_pairs={{0,16},{8,24},{16,0},{24,8},{1,17},{9,25},{17,1},{25,9},{2,18},{10... | collective-permute-start | bytes 1572872 | tf_op jit(solution)/shard_map/ppermute | solution.py:489
  119.9 23.7 %collective-permute-start.34 = (bf16[16,64,256]{2,1,0:T(8,128)(2,1)S(1)}, bf16[16,64,256]{2,1,0:T(8,128)(2,1)S(1)}, u32[]{:S(2)}, u32[]{:S(2)}) collective-permute-start(bf16[16,64,256]{2,1,0:T(8,128)(2,1)S(1)} %bitcast.54), channel_id=1, source_target_pairs={{0,1},{1,0},{2,3},{3,2},{4,5},{5,4},{6,7},{7,6},{8,9},{9,8},{10,11... | collective-permute-start | bytes 1572872 | tf_op jit(solution)/shard_map/ppermute | solution.py:492
  121.6 4.7 %collective-permute-start.17 = (f32[24,128]{1,0:T(8,128)S(1)}, f32[24,128]{1,0:T(8,128)S(1)}, u32[]{:S(2)}, u32[]{:S(2)}) collective-permute-start(f32[24,128]{1,0:T(8,128)S(1)} %add.81), channel_id=1, source_target_pairs={{0,16},{8,24},{16,0},{24,8},{1,17},{9,25},{17,1},{25,9},{2,18},{10... | collective-permute-start | bytes 36872 | tf_op jit(solution)/shard_map/ppermute | solution.py:489
  126.3 6.3 %collective-permute-start.18 = (f32[24,128]{1,0:T(8,128)S(1)}, f32[24,128]{1,0:T(8,128)S(1)}, u32[]{:S(2)}, u32[]{:S(2)}) collective-permute-start(f32[24,128]{1,0:T(8,128)S(1)} %add.82), channel_id=1, source_target_pairs={{0,1},{1,0},{2,3},{3,2},{4,5},{5,4},{6,7},{7,6},{8,9},{9,8},{10,11... | collective-permute-start | bytes 36872 | tf_op jit(solution)/shard_map/ppermute | solution.py:492
  136.4 6.5 %collective-permute-start.20 = (f32[24,128]{1,0:T(8,128)S(1)}, f32[24,128]{1,0:T(8,128)S(1)}, u32[]{:S(2)}, u32[]{:S(2)}) collective-permute-start(f32[24,128]{1,0:T(8,128)S(1)} %add.84), channel_id=1, source_target_pairs={{0,4},{1,5},{2,6},{3,7},{4,0},{5,1},{6,2},{7,3},{8,12},{9,13},{10,... | collective-permute-start | bytes 36872 | tf_op jit(solution)/shard_map/ppermute | solution.py:492
  142.2 10.7 %collective-permute-start.30 = (bf16[16,64,256]{2,1,0:T(8,128)(2,1)}, bf16[16,64,256]{2,1,0:T(8,128)(2,1)S(1)}, u32[]{:S(2)}, u32[]{:S(2)}) collective-permute-start(bf16[16,64,256]{2,1,0:T(8,128)(2,1)} %get-tuple-element.69.refs_0_), channel_id=1, source_target_pairs={{0,1},{1,0},{2,3},{3,2},{4,5},{5,4},{6,7},{7,6},{8,9},{9,8},{10,11... | collective-permute-start | bytes 1572872 | tf_op jit(solution)/shard_map/ppermute | solution.py:492
  149.0 10.4 %collective-permute-start.35 = (bf16[2,16,64,128]{3,2,1,0:T(8,128)(2,1)}, bf16[2,16,64,128]{3,2,1,0:T(8,128)(2,1)S(1)}, u32[]{:S(2)}, u32[]{:S(2)}) collective-permute-start(bf16[2,16,64,128]{3,2,1,0:T(8,128)(2,1)} %adjoint.5.mine_ref.one_ref), channel_id=1, source_target_pairs={{0,16},{8,24},{16,0},{24,8},{1,17},{9,25},{17,1},{25,9},{2,18},{10... | collective-permute-start | bytes 1572872 | tf_op jit(solution)/shard_map/ppermute | solution.py:489
  149.6 18.3 %collective-permute-start.21 = (f32[32]{0:T(128)S(1)}, f32[32]{0:T(128)S(1)}, u32[]{:S(2)}, u32[]{:S(2)}) collective-permute-start(f32[32]{0:T(128)S(1)} %copy-done.59), channel_id=1, source_target_pairs={{0,16},{8,24},{16,0},{24,8},{1,17},{9,25},{17,1},{25,9},{2,18},{10... | collective-permute-start | bytes 392 | tf_op jit(solution)/shard_map/ppermute | solution.py:489
  154.9 16.6 %collective-permute-start.31 = (bf16[256,256]{1,0:T(8,128)(2,1)}, bf16[256,256]{1,0:T(8,128)(2,1)S(1)}, u32[]{:S(2)}, u32[]{:S(2)}) collective-permute-start(bf16[256,256]{1,0:T(8,128)(2,1)} %get-tuple-element.71), channel_id=1, source_target_pairs={{0,2},{1,3},{2,0},{3,1},{4,6},{5,7},{6,4},{7,5},{8,10},{9,11},{10,... | collective-permute-start | bytes 393224 | tf_op jit(solution)/shard_map/ppermute | solution.py:492
  156.5 15.0 %collective-permute-start.32 = (bf16[256,256]{1,0:T(8,128)(2,1)}, bf16[256,256]{1,0:T(8,128)(2,1)S(1)}, u32[]{:S(2)}, u32[]{:S(2)}) collective-permute-start(bf16[256,256]{1,0:T(8,128)(2,1)} %get-tuple-element.72), channel_id=1, source_target_pairs={{0,4},{1,5},{2,6},{3,7},{4,0},{5,1},{6,2},{7,3},{8,12},{9,13},{10,... | collective-permute-start | bytes 393224 | tf_op jit(solution)/shard_map/ppermute | solution.py:492
  157.9 13.7 %collective-permute-start.33 = (bf16[256,256]{1,0:T(8,128)(2,1)}, bf16[256,256]{1,0:T(8,128)(2,1)}, u32[]{:S(2)}, u32[]{:S(2)}) collective-permute-start(bf16[256,256]{1,0:T(8,128)(2,1)} %get-tuple-element.73), channel_id=1, source_target_pairs={{0,6},{1,7},{2,4},{3,5},{4,2},{5,3},{6,0},{7,1},{8,14},{9,15},{10,... | collective-permute-start | bytes 393224 | tf_op jit(solution)/shard_map/ppermute | solution.py:492
  166.3 19.8 %collective-permute-start.36 = (bf16[16,64,256]{2,1,0:T(8,128)(2,1)S(1)}, bf16[16,64,256]{2,1,0:T(8,128)(2,1)}, u32[]{:S(2)}, u32[]{:S(2)}) collective-permute-start(bf16[16,64,256]{2,1,0:T(8,128)(2,1)S(1)} %ordered.5), channel_id=1, source_target_pairs={{0,1},{1,0},{2,3},{3,2},{4,5},{5,4},{6,7},{7,6},{8,9},{9,8},{10,11... | collective-permute-start | bytes 1572872 | tf_op jit(solution)/shard_map/ppermute | solution.py:492
  174.7 7.0 %collective-permute-start.50 = (bf16[256,256]{1,0:T(8,128)(2,1)S(1)}, bf16[256,256]{1,0:T(8,128)(2,1)S(1)}, u32[]{:S(2)}, u32[]{:S(2)}) collective-permute-start(bf16[256,256]{1,0:T(8,128)(2,1)S(1)} %get-tuple-element.87.refs_0_), channel_id=1, source_target_pairs={{0,6},{1,7},{2,4},{3,5},{4,2},{5,3},{6,0},{7,1},{8,14},{9,15},{10,... | collective-permute-start | bytes 393224 | tf_op jit(solution)/shard_map/ppermute | solution.py:492
  177.1 7.9 %collective-permute-start.49 = (bf16[256,256]{1,0:T(8,128)(2,1)S(1)}, bf16[256,256]{1,0:T(8,128)(2,1)S(1)}, u32[]{:S(2)}, u32[]{:S(2)}) collective-permute-start(bf16[256,256]{1,0:T(8,128)(2,1)S(1)} %get-tuple-element.87.refs_0_), channel_id=1, source_target_pairs={{0,4},{1,5},{2,6},{3,7},{4,0},{5,1},{6,2},{7,3},{8,12},{9,13},{10,... | collective-permute-start | bytes 393224 | tf_op jit(solution)/shard_map/ppermute | solution.py:492
  177.8 7.2 %collective-permute-start.48 = (bf16[256,256]{1,0:T(8,128)(2,1)S(1)}, bf16[256,256]{1,0:T(8,128)(2,1)S(1)}, u32[]{:S(2)}, u32[]{:S(2)}) collective-permute-start(bf16[256,256]{1,0:T(8,128)(2,1)S(1)} %get-tuple-element.87.refs_0_), channel_id=1, source_target_pairs={{0,2},{1,3},{2,0},{3,1},{4,6},{5,7},{6,4},{7,5},{8,10},{9,11},{10,... | collective-permute-start | bytes 393224 | tf_op jit(solution)/shard_map/ppermute | solution.py:492
  185.6 28.8 %collective-permute-start.51 = (bf16[16,64,256]{2,1,0:T(8,128)(2,1)S(1)}, bf16[16,64,256]{2,1,0:T(8,128)(2,1)S(1)}, u32[]{:S(2)}, u32[]{:S(2)}) collective-permute-start(bf16[16,64,256]{2,1,0:T(8,128)(2,1)S(1)} %bitcast.50), channel_id=1, source_target_pairs={{0,1},{1,0},{2,3},{3,2},{4,5},{5,4},{6,7},{7,6},{8,9},{9,8},{10,11... | collective-permute-start | bytes 1572872 | tf_op jit(solution)/shard_map/ppermute | solution.py:492
  188.3 6.4 %collective-permute-start.37 = (bf16[256,256]{1,0:T(8,128)(2,1)S(1)}, bf16[256,256]{1,0:T(8,128)(2,1)S(1)}, u32[]{:S(2)}, u32[]{:S(2)}) collective-permute-start(bf16[256,256]{1,0:T(8,128)(2,1)S(1)} %get-tuple-element.80), channel_id=1, source_target_pairs={{0,2},{1,3},{2,0},{3,1},{4,6},{5,7},{6,4},{7,5},{8,10},{9,11},{10,... | collective-permute-start | bytes 393224 | tf_op jit(solution)/shard_map/ppermute | solution.py:492
  188.4 11.8 %collective-permute-start.38 = (bf16[256,256]{1,0:T(8,128)(2,1)S(1)}, bf16[256,256]{1,0:T(8,128)(2,1)S(1)}, u32[]{:S(2)}, u32[]{:S(2)}) collective-permute-start(bf16[256,256]{1,0:T(8,128)(2,1)S(1)} %get-tuple-element.81), channel_id=1, source_target_pairs={{0,4},{1,5},{2,6},{3,7},{4,0},{5,1},{6,2},{7,3},{8,12},{9,13},{10,... | collective-permute-start | bytes 393224 | tf_op jit(solution)/shard_map/ppermute | solution.py:492
  191.5 8.7 %collective-permute-start.39 = (bf16[256,256]{1,0:T(8,128)(2,1)S(1)}, bf16[256,256]{1,0:T(8,128)(2,1)S(1)}, u32[]{:S(2)}, u32[]{:S(2)}) collective-permute-start(bf16[256,256]{1,0:T(8,128)(2,1)S(1)} %get-tuple-element.82), channel_id=1, source_target_pairs={{0,6},{1,7},{2,4},{3,5},{4,2},{5,3},{6,0},{7,1},{8,14},{9,15},{10,... | collective-permute-start | bytes 393224 | tf_op jit(solution)/shard_map/ppermute | solution.py:492
  200.9 19.1 %collective-permute-start.47 = (bf16[256,256]{1,0:T(8,128)(2,1)S(1)}, bf16[256,256]{1,0:T(8,128)(2,1)S(1)}, u32[]{:S(2)}, u32[]{:S(2)}) collective-permute-start(bf16[256,256]{1,0:T(8,128)(2,1)S(1)} %get-tuple-element.86.refs_0_), channel_id=1, source_target_pairs={{0,6},{1,7},{2,4},{3,5},{4,2},{5,3},{6,0},{7,1},{8,14},{9,15},{10,... | collective-permute-start | bytes 393224 | tf_op jit(solution)/shard_map/ppermute | solution.py:492
  203.2 16.8 %collective-permute-start.46 = (bf16[256,256]{1,0:T(8,128)(2,1)S(1)}, bf16[256,256]{1,0:T(8,128)(2,1)S(1)}, u32[]{:S(2)}, u32[]{:S(2)}) collective-permute-start(bf16[256,256]{1,0:T(8,128)(2,1)S(1)} %get-tuple-element.86.refs_0_), channel_id=1, source_target_pairs={{0,4},{1,5},{2,6},{3,7},{4,0},{5,1},{6,2},{7,3},{8,12},{9,13},{10,... | collective-permute-start | bytes 393224 | tf_op jit(solution)/shard_map/ppermute | solution.py:492
  205.8 14.2 %collective-permute-start.45 = (bf16[256,256]{1,0:T(8,128)(2,1)S(1)}, bf16[256,256]{1,0:T(8,128)(2,1)S(1)}, u32[]{:S(2)}, u32[]{:S(2)}) collective-permute-start(bf16[256,256]{1,0:T(8,128)(2,1)S(1)} %get-tuple-element.86.refs_0_), channel_id=1, source_target_pairs={{0,2},{1,3},{2,0},{3,1},{4,6},{5,7},{6,4},{7,5},{8,10},{9,11},{10,... | collective-permute-start | bytes 393224 | tf_op jit(solution)/shard_map/ppermute | solution.py:492
  221.5 12.1 %collective-permute-start.52 = (bf16[16,64,256]{2,1,0:T(8,128)(2,1)S(1)}, bf16[16,64,256]{2,1,0:T(8,128)(2,1)S(1)}, u32[]{:S(2)}, u32[]{:S(2)}) collective-permute-start(bf16[16,64,256]{2,1,0:T(8,128)(2,1)S(1)} %bitcast.45), channel_id=1, source_target_pairs={{0,1},{1,0},{2,3},{3,2},{4,5},{5,4},{6,7},{7,6},{8,9},{9,8},{10,11... | collective-permute-start | bytes 1572872 | tf_op jit(solution)/shard_map/ppermute | solution.py:492
  223.2 9.5 %collective-permute-start.53 = (bf16[16,64,128]{2,1,0:T(8,128)(2,1)S(1)}, bf16[16,64,128]{2,1,0:T(8,128)(2,1)S(1)}, u32[]{:S(2)}, u32[]{:S(2)}) collective-permute-start(bf16[16,64,128]{2,1,0:T(8,128)(2,1)S(1)} %copy-done.50), channel_id=1, source_target_pairs={{0,16},{8,24},{16,0},{24,8},{1,17},{9,25},{17,1},{25,9},{2,18},{10... | collective-permute-start | bytes 786440 | tf_op jit(solution)/shard_map/ppermute | solution.py:489
  227.4 4.6 %collective-permute-start.44 = (f32[24,128]{1,0:T(8,128)S(1)}, f32[24,128]{1,0:T(8,128)S(1)}, u32[]{:S(2)}, u32[]{:S(2)}) collective-permute-start(f32[24,128]{1,0:T(8,128)S(1)} %add.90), channel_id=1, source_target_pairs={{0,4},{1,5},{2,6},{3,7},{4,0},{5,1},{6,2},{7,3},{8,12},{9,13},{10,... | collective-permute-start | bytes 36872 | tf_op jit(solution)/shard_map/ppermute | solution.py:492
  239.1 8.1 %collective-permute-start.54 = (bf16[16,64,128]{2,1,0:T(8,128)(2,1)}, bf16[16,64,128]{2,1,0:T(8,128)(2,1)S(1)}, u32[]{:S(2)}, u32[]{:S(2)}) collective-permute-start(bf16[16,64,128]{2,1,0:T(8,128)(2,1)} %get-tuple-element.90), channel_id=1, source_target_pairs={{0,16},{8,24},{16,0},{24,8},{1,17},{9,25},{17,1},{25,9},{2,18},{10... | collective-permute-start | bytes 786440 | tf_op jit(solution)/shard_map/ppermute | solution.py:489
  (74 other events, 545.4 us)

commit v4 on v3

--- a/solution.py
+++ b/solution.py
@@ -66,20 +66,22 @@
 
 
 class Parts:
-    def __init__(self, plan, chunk, m, blk_of, refs):
-        (whole, far), (near_buf, far_buf, sems) = refs
+    def __init__(self, plan, chunk, m, blk_of, refs, whole):
+        (near, far), (near_buf, far_buf, sems) = refs
         self.buffers, self.copies = (near_buf, far_buf), {}
         high = plan.step * 2 * plan.sensors
         for phase in range(2):
             for t in range(plan.steps):
                 slot = phase * plan.steps + t
                 side = m[0] ^ blk_of(phase, m)
+                rows = pl.ds(t * high, high)
                 near_rows = pl.ds((chunk * plan.steps + t) * high, high)
+                source = near.at[side, m[1], near_rows] if whole else near.at[side, rows]
                 self.copies[phase, t] = [
                     pltpu.make_async_copy(ref, buffer.at[slot], sems.at[slot, place])
                     for place, (ref, buffer) in enumerate((
-                        (whole.at[side, m[1], near_rows], near_buf),
-                        (far.at[side, pl.ds(t * high, high)], far_buf),
+                        (source, near_buf),
+                        (far.at[side, rows], far_buf),
                     ))
                 ]
         for copies in self.copies.values():
@@ -165,22 +167,35 @@
     )(start, *wait)
 
 
-def forward_call(plan, chunk, meta, whole, far, first, vectors, wait=()):
+def forward_call(plan, chunk, meta, near, far, first, vectors, wait=()):
+    n_out = 3 if first else 2
     blk_of = lambda p, m: 1 - (m[2] ^ p)
 
-    def kernel(m, whole, far, one_ref, two_ref, *refs):
-        outs, scratch = refs[len(wait):len(wait) + 2], refs[len(wait) + 2:]
-        parts = Parts(plan, chunk, m, blk_of, ((whole, far), scratch))
+    def kernel(m, near, far, one_ref, two_ref, *refs):
+        outs, scratch = refs[len(wait):len(wait) + n_out], refs[len(wait) + n_out:]
+        parts = Parts(plan, chunk, m, blk_of, ((near, far), scratch[:3]), first)
+        saves = []
         for phase in range(2):
             blk = blk_of(phase, m)
             for t in range(plan.steps):
-                for i, (near_part, far_part) in enumerate(parts.get(plan, phase, t)):
+                blocks = parts.get(plan, phase, t)
+                if first:
+                    slot, high = phase * plan.steps + t, plan.step * 2 * plan.sensors
+                    saves.append(pltpu.make_async_copy(
+                        scratch[0].at[slot],
+                        outs[2].at[m[0] ^ blk, pl.ds(t * high, high)],
+                        scratch[3].at[slot],
+                    ))
+                    saves[-1].start()
+                for i, (near_part, far_part) in enumerate(blocks):
                     f = t * plan.step + i
                     if first:
                         vector = jnp.where(blk == 0, one_ref[f].astype(BF16), two_ref[f])
                     else:
                         vector = one_ref[blk, f].astype(F32) + two_ref[1 - blk, f].astype(F32)
                     outs[phase][f] = forward_rows(vector.astype(BF16), near_part, far_part).astype(BF16)
+        for save in saves:
+            save.wait()
 
     size = (plan.part, plan.rows, plan.sources)
     if first:
@@ -196,22 +211,23 @@
         grid=(1,),
         in_specs=[pl.BlockSpec(memory_space=pltpu.SMEM)] + [ANYWHERE] * 2 + vec_specs
         + [ANYWHERE] * len(wait),
-        out_specs=[pl.BlockSpec(shape, lambda i: (0, 0, 0))] * 2,
-        out_shape=[jax.ShapeDtypeStruct(shape, BF16)] * 2,
-        scratch_shapes=Parts.scratch(plan),
+        out_specs=[pl.BlockSpec(shape, lambda i: (0, 0, 0))] * 2 + [ANYWHERE] * (n_out - 2),
+        out_shape=[jax.ShapeDtypeStruct(shape, BF16)] * 2
+        + [jax.ShapeDtypeStruct(far.shape, BF16)] * (n_out - 2),
+        scratch_shapes=Parts.scratch(plan) + [pltpu.SemaphoreType.DMA((2 * plan.steps,))],
         cost_estimate=cost(plan.flops, 16 * plan.part * plan.sensors * plan.sources),
-        compiler_params=pltpu.CompilerParams(vmem_limit_bytes=PRODUCT_BYTES),
+        compiler_params=pltpu.CompilerParams(vmem_limit_bytes=PRODUCT_BYTES if first else KERNEL_BYTES),
         name="forward",
-    )(meta, whole, far, *vectors, *wait)
-
-
-def adjoint_call(plan, chunk, meta, whole, far, halves, last, wait=()):
+    )(meta, near, far, *vectors, *wait)
+
+
+def adjoint_call(plan, chunk, meta, near, far, halves, last, wait=()):
     blk_of = lambda p, m: 1 - p
     n_out = 2 if last else 1
 
-    def kernel(m, whole, far, own_ref, got_ref, *refs):
+    def kernel(m, near, far, own_ref, got_ref, *refs):
         outs, scratch = refs[len(wait):len(wait) + n_out], refs[len(wait) + n_out:]
-        parts = Parts(plan, chunk, m, blk_of, ((whole, far), scratch))
+        parts = Parts(plan, chunk, m, blk_of, ((near, far), scratch), False)
         for phase in range(2):
             blk = blk_of(phase, m)
             for t in range(plan.steps):
@@ -241,9 +257,9 @@
         out_shape=out_shape,
         scratch_shapes=Parts.scratch(plan),
         cost_estimate=cost(plan.flops, 16 * plan.part * plan.sensors * plan.sources),
-        compiler_params=pltpu.CompilerParams(vmem_limit_bytes=PRODUCT_BYTES),
+        compiler_params=pltpu.CompilerParams(vmem_limit_bytes=KERNEL_BYTES),
         name="adjoint",
-    )(meta, whole, far, *halves, *wait)
+    )(meta, near, far, *halves, *wait)
 
 
 def split_call(plan, meta, keep, got, wait=()):
@@ -545,23 +561,22 @@
     def to_half(array):
         return to_src(array, 1)
 
-    def both_products(scaled, near_sums, last, then, received):
+    def both_products(scaled, near_sums, last, then):
         outs, wait, sums = [], (), None
-        pieces = [[one] + [to_src(one, step) for step in steps] for one in scaled]
         for k in chunks:
-            own = place_call(plan, meta, pieces[k], wait + tuple(sum(received[k + 1:k + 2], [])))
+            pieces = [scaled[k]] + [to_src(scaled[k], step) for step in steps]
+            own = place_call(plan, meta, pieces, wait)
             halves = (own, to_half(own))
-            if k == 0:
-                wait = tuple(sum(pieces[1:2], [])) if received else ()
             if k == 1:
-                far_sums, sums = total_far(near_sums)
-                wait = (outs[0][1][0], far_sums)
-            out = adjoint_call(plan, k, meta, whole, far[k], halves, last, wait)
+                after = outs[0][1][0]
+                far_sums, sums = total_far(near_sums if last else ordered(near_sums, after))
+                wait = (after, far_sums)
+            out = adjoint_call(plan, k, meta, near[k], far[k], halves, last, wait if k > 0 else ())
             outs.append((out, then(k, out)))
-            wait = (out,) if received else (out[0] if last else out, near_sums)
+            wait = (out[0] if last else out, near_sums)
         return outs, total_far(near_sums)[1] if sums is None else sums
 
-    sends = [send for send, _ in pairs]
+    sends, near = [each[0] for each in pairs], [each[2] for each in pairs]
     got = in_turn(sends, to_half)
     pieces = [reduce_field(pairs[k][1], got[k], tuple(sends[k + 1:k + 2])) for k in chunks]
     scaled, field, stats = zip(*[
@@ -575,10 +590,10 @@
 
     def go_on(k, back):
         got = to_pair(back)
-        send, keep = forward_call(plan, k, meta, whole, far[k], False, (back, got))
+        send, keep = forward_call(plan, k, meta, near[k], far[k], False, (back, got))
         return send, keep, got
 
-    outs, sums = both_products(scaled, near_0, False, go_on, [each[1:] for each in pieces])
+    outs, sums = both_products(scaled, near_0, False, go_on)
     norm_0, curve_0 = sums[0], sums[1]
     alpha_0 = (norm_0 / curve_0)[None]
     back = [out for out, _ in outs]
@@ -593,7 +608,7 @@
         for k in chunks
     ])
     near_1 = total_near(sum(stats))
-    outs, sums = both_products(scaled, near_1, True, lambda k, out: (to_pair(out[0]),), [])
+    outs, sums = both_products(scaled, near_1, True, lambda k, out: (to_pair(out[0]),))
     norm_1 = sums[0]
     beta = norm_1 / norm_0
     curve_1 = sums[1] + 2.0 * beta * sums[2] + beta * beta * curve_0

time: 250 us -> 236 us (0.944)
  starting transfers between devices: 78.2 us -> 70 us
  Pallas kernels: 61.8 us -> 55.9 us
  waiting for transfers between devices: 73.8 us -> 78.1 us
  local copies, waits for them, and re-layouts: 25.8 us -> 21.7 us
    ppermute x41, starting transfers between devices: 68.3 us -> 60.3 us  [to_src(): return lax.ppermute(array, 'src', [(j, j ^ step) for j in range(n_src)])]
    ppermute x41, waiting for transfers between devices: 55.3 us -> 62.4 us  [to_src(): return lax.ppermute(array, 'src', [(j, j ^ step) for j in range(n_src)])]
    pallas_call x4, Pallas kernels: 18.6 us -> 11.6 us  [adjoint_call(): pl.pallas_call(kernel, grid=(1,), in_specs=[pl.BlockSpec(memory_space=plt...]
    unnamed x134 -> x100, local copies, waits for them, and re-layouts: 24.4 us -> 20.3 us
    ppermute x9, waiting for transfers between devices: 16.2 us -> 13.4 us  [to_pair(): return lax.ppermute(array, 'sens', [(i, i ^ 2) for i in range(n_sens)])]
  transfers between devices with their start and end apart: 55 -> 55, of which waited for: 23 -> 23; matrix products, arithmetic and copies ran while one was open for 2% -> 1% of each run, Pallas kernels for 19% -> 20%
where the time goes in v4:
time: 236 us; the launch traced here: 235 us
  waiting for transfers between devices  78.1 us (33%)
  starting transfers between devices  70 us (30%)
  Pallas kernels  55.9 us (24%)
  local copies, waits for them, and re-layouts  21.7 us (9%)
  between operations  6.43 us (3%)
  other arithmetic  2.58 us (1%)
    ppermute x41, waiting for transfers between devices, to_src(): return lax.ppermute(array, 'src', [(j, j ^ step) for j in range(n_src)])  62.4 us
    ppermute x41, starting transfers between devices, to_src(): return lax.ppermute(array, 'src', [(j, j ^ step) for j in range(n_src)])  60.3 us
    unnamed x100, local copies, waits for them, and re-layouts  20.3 us
    pallas_call x4, Pallas kernels, forward_call(): pl.pallas_call(kernel, grid=(1,), in_specs=[pl.BlockSpec(memory_space=plt...  19.4 us
    ppermute x9, waiting for transfers between devices, to_pair(): return lax.ppermute(array, 'sens', [(i, i ^ 2) for i in range(n_sens)])  13.4 us
    pallas_call x4, Pallas kernels, adjoint_call(): pl.pallas_call(kernel, grid=(1,), in_specs=[pl.BlockSpec(memory_space=plt...  11.6 us
    ppermute x9, starting transfers between devices, to_pair(): return lax.ppermute(array, 'sens', [(i, i ^ 2) for i in range(n_sens)])  8.79 us
    pallas_call x2, Pallas kernels, cut_call(): pl.pallas_call(kernel, in_specs=[pl.BlockSpec(memory_space=pltpu.SMEM), A...  6.22 us
  transfers between devices with their start and end apart: 55, of which 23 were waited for; matrix products, arithmetic and copies ran while one was open for 1% of the time, Pallas kernels for 20%

profile of v4, /device:TPU:0, one launch (start us, length us, event | category | flops | bytes accessed | tf_op | source)
XLA Modules:
  0.0 234.7 jit_solution(11660475767756059611)
XLA Ops:
  3.3 3.1 %cut.2 = bf16[2,4096,128]{2,1,0:T(8,128)(2,1)} custom-call(s32[4]{0:T(128)} %pad_add_fusion.m, bf16[2,2,8192,128]{3,2,1,0:T(8,128)(2,1)} %bitcast.57, bf16[16,64,128]{2,1,0:T(8,128)(2,1)} %copy-done.13), custom_call_target="tpu_custom_call" | custom-call | bytes 2097 | tf_op jit(solution)/shard_map/cut/pallas_call | solution.py:132
  7.0 3.1 %cut.3.refs_1_ = bf16[2,4096,128]{2,1,0:T(8,128)(2,1)} custom-call(s32[4]{0:T(128)} %pad_add_fusion.m, bf16[2,2,8192,128]{3,2,1,0:T(8,128)(2,1)} %bitcast.58, bf16[16,64,128]{2,1,0:T(8,128)(2,1)} %copy-done.13), custom_call_target="tpu_custom_call" | custom-call | bytes 2097 | tf_op jit(solution)/shard_map/cut/pallas_call | solution.py:132
  10.3 2.8 %collective-permute-start = (f32[16,128]{1,0:T(8,128)S(1)}, f32[16,128]{1,0:T(8,128)S(1)}, u32[]{:S(2)}, u32[]{:S(2)}) collective-permute-start(f32[16,128]{1,0:T(8,128)S(1)} %copy-done.49), channel_id=1, source_target_pairs={{0,1},{1,0},{2,3},{3,2},{4,5},{5,4},{6,7},{7,6},{8,9},{9,8},{10,11... | collective-permute-start | bytes 24584 | tf_op jit(solution)/shard_map/ppermute | solution.py:508
  14.8 2.1 collective-permute-start.1
  19.8 4.1 %collective-permute-done.5.two_ref.refs_1_ = bf16[16,64,128]{2,1,0:T(8,128)(2,1)} collective-permute-done((bf16[16,64,128]{2,1,0:T(8,128)(2,1)S(1)}, bf16[16,64,128]{2,1,0:T(8,128)(2,1)}, u32[]{:S(2)}, u32[]{:S(2)}) %collective-permute-start.5) | collective-permute-done | bytes 262176 | tf_op jit(solution)/shard_map/ppermute | solution.py:505
  23.9 5.5 %forward.4 = (bf16[16,64,256]{2,1,0:T(8,128)(2,1)}, bf16[16,64,256]{2,1,0:T(8,128)(2,1)}, bf16[2,4096,128]{2,1,0:T(8,128)(2,1)}) custom-call(s32[4]{0:T(128)} %pad_add_fusion.m, bf16[2,2,8192,128]{3,2,1,0:T(8,128)(2,1)} %bitcast.59, bf16[2,4096,128]{2,1,0:T(8,128)(2,1)} %collective-permute-done.4.far, f32[32,64,128]{2,1,0:T(8,128)} %bitcast.35, ...), custom_call_target="tpu_custom_call" | custom-call | flops 536870 | bytes 4194 | tf_op jit(solution)/shard_map/forward/pallas_call | solution.py:209
  32.6 2.6 %collective-permute-start.2 = (f32[64,128]{1,0:T(8,128)S(1)}, f32[64,128]{1,0:T(8,128)}, u32[]{:S(2)}, u32[]{:S(2)}) collective-permute-start(f32[64,128]{1,0:T(8,128)S(1)} %copy-done.48), channel_id=1, source_target_pairs={{0,4},{1,5},{2,6},{3,7},{4,0},{5,1},{6,2},{7,3},{8,12},{9,13},{10,... | collective-permute-start | bytes 98312 | tf_op jit(solution)/shard_map/ppermute | solution.py:508
  35.1 2.3 collective-permute-done.8.two_ref
  38.1 5.5 %forward.5 = (bf16[16,64,256]{2,1,0:T(8,128)(2,1)}, bf16[16,64,256]{2,1,0:T(8,128)(2,1)}, bf16[2,4096,128]{2,1,0:T(8,128)(2,1)}) custom-call(s32[4]{0:T(128)} %pad_add_fusion.m, bf16[2,2,8192,128]{3,2,1,0:T(8,128)(2,1)} %bitcast.60, bf16[2,4096,128]{2,1,0:T(8,128)(2,1)} %copy-done.3, f32[32,64,128]{2,1,0:T(8,128)} %bitcast.36, bf16[16,64,128]{2,1,0:T(8,128)(2,1)} %copy-done.47), custom_call_target="tpu_custom_call" | custom-call | flops 536870 | bytes 4194 | tf_op jit(solution)/shard_map/forward/pallas_call | solution.py:209
  45.2 1.8 split.4
  48.1 2.7 %collective-permute-start.10 = (bf16[256,256]{1,0:T(8,128)(2,1)}, bf16[256,256]{1,0:T(8,128)(2,1)S(1)}, u32[]{:S(2)}, u32[]{:S(2)}) collective-permute-start(bf16[256,256]{1,0:T(8,128)(2,1)} %get-tuple-element.57), channel_id=1, source_target_pairs={{0,4},{1,5},{2,6},{3,7},{4,0},{5,1},{6,2},{7,3},{8,12},{9,13},{10,... | collective-permute-start | bytes 393224 | tf_op jit(solution)/shard_map/ppermute | solution.py:508
  52.8 3.9 %collective-permute-done.9.refs_3_ = bf16[256,256]{1,0:T(8,128)(2,1)S(1)} collective-permute-done((bf16[256,256]{1,0:T(8,128)(2,1)}, bf16[256,256]{1,0:T(8,128)(2,1)S(1)}, u32[]{:S(2)}, u32[]{:S(2)}) %collective-permute-start.9) | collective-permute-done | bytes 131104 | tf_op jit(solution)/shard_map/ppermute | solution.py:508
  56.6 5.0 %collective-permute-done.11.refs_5_ = bf16[256,256]{1,0:T(8,128)(2,1)} collective-permute-done((bf16[256,256]{1,0:T(8,128)(2,1)}, bf16[256,256]{1,0:T(8,128)(2,1)}, u32[]{:S(2)}, u32[]{:S(2)}) %collective-permute-start.11) | collective-permute-done | bytes 131104 | tf_op jit(solution)/shard_map/ppermute | solution.py:508
  63.6 2.9 %collective-permute-start.21 = (bf16[256,256]{1,0:T(8,128)(2,1)S(1)}, bf16[256,256]{1,0:T(8,128)(2,1)S(1)}, u32[]{:S(2)}, u32[]{:S(2)}) collective-permute-start(bf16[256,256]{1,0:T(8,128)(2,1)S(1)} %get-tuple-element.67.refs_0_), channel_id=1, source_target_pairs={{0,6},{1,7},{2,4},{3,5},{4,2},{5,3},{6,0},{7,1},{8,14},{9,15},{10,... | collective-permute-start | bytes 393224 | tf_op jit(solution)/shard_map/ppermute | solution.py:508
  68.7 2.0 collective-permute-done.21.refs_3_
  70.7 8.3 %collective-permute-done.20.refs_2_ = bf16[256,256]{1,0:T(8,128)(2,1)S(1)} collective-permute-done((bf16[256,256]{1,0:T(8,128)(2,1)S(1)}, bf16[256,256]{1,0:T(8,128)(2,1)S(1)}, u32[]{:S(2)}, u32[]{:S(2)}) %collective-permute-start.20) | collective-permute-done | bytes 131104 | tf_op jit(solution)/shard_map/ppermute | solution.py:508
  82.4 3.1 %collective-permute-start.14 = (bf16[256,256]{1,0:T(8,128)(2,1)S(1)}, bf16[256,256]{1,0:T(8,128)(2,1)S(1)}, u32[]{:S(2)}, u32[]{:S(2)}) collective-permute-start(bf16[256,256]{1,0:T(8,128)(2,1)S(1)} %get-tuple-element.63), channel_id=1, source_target_pairs={{0,4},{1,5},{2,6},{3,7},{4,0},{5,1},{6,2},{7,3},{8,12},{9,13},{10,... | collective-permute-start | bytes 393224 | tf_op jit(solution)/shard_map/ppermute | solution.py:508
  86.8 6.7 %collective-permute-done.22.got_ref = bf16[16,64,256]{2,1,0:T(8,128)(2,1)S(1)} collective-permute-done((bf16[16,64,256]{2,1,0:T(8,128)(2,1)S(1)}, bf16[16,64,256]{2,1,0:T(8,128)(2,1)S(1)}, u32[]{:S(2)}, u32[]{:S(2)}) %collective-permute-start.22) | collective-permute-done | bytes 524320 | tf_op jit(solution)/shard_map/ppermute | solution.py:508
  93.5 3.0 %adjoint.4.one_ref.mine_ref.refs_4_ = bf16[2,16,64,128]{3,2,1,0:T(8,128)(2,1)S(1)} custom-call(s32[4]{0:T(128)S(1)} %copy-done.37, bf16[2,4096,128]{2,1,0:T(8,128)(2,1)S(1)} %copy-done.5, bf16[2,4096,128]{2,1,0:T(8,128)(2,1)} %collective-permute-done.4.far, bf16[16,64,256]{2,1,0:T(8,128)(2,1)S(1)} %bitcast.50, ...), custom_call_target="tpu_custom_call" | custom-call | flops 536870 | bytes 4194 | tf_op jit(solution)/shard_map/adjoint/pallas_call | solution.py:251
  100.0 2.4 %collective-permute-start.33 = (bf16[256,256]{1,0:T(8,128)(2,1)S(1)}, bf16[256,256]{1,0:T(8,128)(2,1)S(1)}, u32[]{:S(2)}, u32[]{:S(2)}) collective-permute-start(bf16[256,256]{1,0:T(8,128)(2,1)S(1)} %get-tuple-element.79.refs_0_), channel_id=1, source_target_pairs={{0,6},{1,7},{2,4},{3,5},{4,2},{5,3},{6,0},{7,1},{8,14},{9,15},{10,... | collective-permute-start | bytes 393224 | tf_op jit(solution)/shard_map/ppermute | solution.py:508
  102.4 2.0 collective-permute-start.31
  106.1 3.7 %collective-permute-done.17 = f32[24,128]{1,0:T(8,128)S(1)} collective-permute-done((f32[24,128]{1,0:T(8,128)S(1)}, f32[24,128]{1,0:T(8,128)S(1)}, u32[]{:S(2)}, u32[]{:S(2)}) %collective-permute-start.17) | collective-permute-done | bytes 12320 | tf_op jit(solution)/shard_map/ppermute | solution.py:505
  111.3 2.2 collective-permute-done.18
  115.7 4.2 %forward.6 = (bf16[16,64,256]{2,1,0:T(8,128)(2,1)}, bf16[16,64,256]{2,1,0:T(8,128)(2,1)S(1)}) custom-call(s32[4]{0:T(128)S(1)} %copy-done.37, bf16[2,4096,128]{2,1,0:T(8,128)(2,1)S(1)} %copy-done.6, bf16[2,4096,128]{2,1,0:T(8,128)(2,1)} %collective-permute-done.4.far, bf16[2,16,64,128]{3,2,1,0:T(8,128)(2,1)S(1)} %adjoint.4.one_ref.mine_ref.refs_4_, ...), custom_call_target="tpu_custom_call" | custom-call | flops 536870 | bytes 4194 | tf_op jit(solution)/shard_map/forward/pallas_call | solution.py:209
  120.0 3.7 %collective-permute-done.24 = f32[24,128]{1,0:T(8,128)S(1)} collective-permute-done((f32[24,128]{1,0:T(8,128)S(1)}, f32[24,128]{1,0:T(8,128)S(1)}, u32[]{:S(2)}, u32[]{:S(2)}) %collective-permute-start.24) | collective-permute-done | bytes 12320 | tf_op jit(solution)/shard_map/ppermute | solution.py:508
  125.3 3.0 %collective-permute-done.25 = f32[24,128]{1,0:T(8,128)S(1)} collective-permute-done((f32[24,128]{1,0:T(8,128)S(1)}, f32[24,128]{1,0:T(8,128)S(1)}, u32[]{:S(2)}, u32[]{:S(2)}) %collective-permute-start.25) | collective-permute-done | bytes 12320 | tf_op jit(solution)/shard_map/ppermute | solution.py:508
  128.5 3.0 %adjoint.5.mine_ref.one_ref = bf16[2,16,64,128]{3,2,1,0:T(8,128)(2,1)} custom-call(s32[4]{0:T(128)S(1)} %copy-done.37, bf16[2,4096,128]{2,1,0:T(8,128)(2,1)S(1)} %copy-done.8, bf16[2,4096,128]{2,1,0:T(8,128)(2,1)S(1)} %copy-done.4, bf16[16,64,256]{2,1,0:T(8,128)(2,1)S(1)} %bitcast.48, bf16[16,64,256]{2,1,0:T(8,128)(2,1)S(1)} %collective-permute-done.34.got_ref, ...), custom_call_target="tpu_custom_call" | custom-call | flops 536870 | bytes 4194 | tf_op jit(solution)/shard_map/adjoint/pallas_call | solution.py:251
  133.6 4.2 %collective-permute-done.27.refs_1_ = bf16[16,64,256]{2,1,0:T(8,128)(2,1)} collective-permute-done((bf16[16,64,256]{2,1,0:T(8,128)(2,1)}, bf16[16,64,256]{2,1,0:T(8,128)(2,1)}, u32[]{:S(2)}, u32[]{:S(2)}) %collective-permute-start.27) | collective-permute-done | bytes 524320 | tf_op jit(solution)/shard_map/ppermute | solution.py:508
  138.9 1.8 split.6
  141.4 2.8 %collective-permute-start.29 = (bf16[256,256]{1,0:T(8,128)(2,1)}, bf16[256,256]{1,0:T(8,128)(2,1)S(1)}, u32[]{:S(2)}, u32[]{:S(2)}) collective-permute-start(bf16[256,256]{1,0:T(8,128)(2,1)} %get-tuple-element.74), channel_id=1, source_target_pairs={{0,4},{1,5},{2,6},{3,7},{4,0},{5,1},{6,2},{7,3},{8,12},{9,13},{10,... | collective-permute-start | bytes 393224 | tf_op jit(solution)/shard_map/ppermute | solution.py:508
  147.4 4.2 %forward.7 = (bf16[16,64,256]{2,1,0:T(8,128)(2,1)}, bf16[16,64,256]{2,1,0:T(8,128)(2,1)S(1)}) custom-call(s32[4]{0:T(128)S(1)} %copy-done.37, bf16[2,4096,128]{2,1,0:T(8,128)(2,1)S(1)} %copy-done.9, bf16[2,4096,128]{2,1,0:T(8,128)(2,1)S(1)} %copy-done.4, bf16[2,16,64,128]{3,2,1,0:T(8,128)(2,1)} %adjoint.5.mine_ref.one_ref, ...), custom_call_target="tpu_custom_call" | custom-call | flops 536870 | bytes 4194 | tf_op jit(solution)/shard_map/forward/pallas_call | solution.py:209
  162.0 2.1 collective-permute-start.50
  164.1 2.3 collective-permute-start.48
  166.4 2.6 %collective-permute-done.50.refs_3_ = bf16[256,256]{1,0:T(8,128)(2,1)S(1)} collective-permute-done((bf16[256,256]{1,0:T(8,128)(2,1)S(1)}, bf16[256,256]{1,0:T(8,128)(2,1)S(1)}, u32[]{:S(2)}, u32[]{:S(2)}) %collective-permute-start.50) | collective-permute-done | bytes 131104 | tf_op jit(solution)/shard_map/ppermute | solution.py:508
  169.0 3.8 %collective-permute-done.49.refs_2_ = bf16[256,256]{1,0:T(8,128)(2,1)S(1)} collective-permute-done((bf16[256,256]{1,0:T(8,128)(2,1)S(1)}, bf16[256,256]{1,0:T(8,128)(2,1)S(1)}, u32[]{:S(2)}, u32[]{:S(2)}) %collective-permute-start.49) | collective-permute-done | bytes 131104 | tf_op jit(solution)/shard_map/ppermute | solution.py:508
  175.9 2.3 collective-permute-start.38
  178.2 2.1 collective-permute-start.39
  181.6 5.9 %collective-permute-done.38.refs_7_ = bf16[256,256]{1,0:T(8,128)(2,1)S(1)} collective-permute-done((bf16[256,256]{1,0:T(8,128)(2,1)S(1)}, bf16[256,256]{1,0:T(8,128)(2,1)S(1)}, u32[]{:S(2)}, u32[]{:S(2)}) %collective-permute-start.38) | collective-permute-done | bytes 131104 | tf_op jit(solution)/shard_map/ppermute | solution.py:508
  188.2 1.8 collective-permute-start.47
  189.9 2.0 collective-permute-start.46
  194.3 3.3 %collective-permute-done.41 = f32[24,128]{1,0:T(8,128)S(1)} collective-permute-done((f32[24,128]{1,0:T(8,128)S(1)}, f32[24,128]{1,0:T(8,128)S(1)}, u32[]{:S(2)}, u32[]{:S(2)}) %collective-permute-start.41) | collective-permute-done | bytes 12320 | tf_op jit(solution)/shard_map/ppermute | solution.py:505
  198.5 2.7 %collective-permute-done.42 = f32[24,128]{1,0:T(8,128)S(1)} collective-permute-done((f32[24,128]{1,0:T(8,128)S(1)}, f32[24,128]{1,0:T(8,128)S(1)}, u32[]{:S(2)}, u32[]{:S(2)}) %collective-permute-start.42) | collective-permute-done | bytes 12320 | tf_op jit(solution)/shard_map/ppermute | solution.py:508
  201.3 3.0 %adjoint.6 = (bf16[16,64,128]{2,1,0:T(8,128)(2,1)S(1)}, f32[16,64,128]{2,1,0:T(8,128)S(1)}) custom-call(s32[4]{0:T(128)S(1)} %copy-done.37, bf16[2,4096,128]{2,1,0:T(8,128)(2,1)S(1)} %copy-done.7, bf16[2,4096,128]{2,1,0:T(8,128)(2,1)} %collective-permute-done.4.far, bf16[16,64,256]{2,1,0:T(8,128)(2,1)S(1)} %bitcast.52, ...), custom_call_target="tpu_custom_call" | custom-call | flops 536870 | bytes 4194 | tf_op jit(solution)/shard_map/adjoint/pallas_call | solution.py:251
  207.9 2.5 %collective-permute-done.43 = f32[24,128]{1,0:T(8,128)S(1)} collective-permute-done((f32[24,128]{1,0:T(8,128)S(1)}, f32[24,128]{1,0:T(8,128)S(1)}, u32[]{:S(2)}, u32[]{:S(2)}) %collective-permute-start.43) | collective-permute-done | bytes 12320 | tf_op jit(solution)/shard_map/ppermute | solution.py:508
  210.5 2.6 %collective-permute-start.44 = (f32[24,128]{1,0:T(8,128)S(1)}, f32[24,128]{1,0:T(8,128)S(1)}, u32[]{:S(2)}, u32[]{:S(2)}) collective-permute-start(f32[24,128]{1,0:T(8,128)S(1)} %add.90), channel_id=1, source_target_pairs={{0,4},{1,5},{2,6},{3,7},{4,0},{5,1},{6,2},{7,3},{8,12},{9,13},{10,... | collective-permute-start | bytes 36872 | tf_op jit(solution)/shard_map/ppermute | solution.py:508
  213.0 2.0 collective-permute-done.44
  215.2 2.2 collective-permute-done.52.got_ref
  217.3 2.6 %adjoint.7 = (bf16[16,64,128]{2,1,0:T(8,128)(2,1)}, f32[16,64,128]{2,1,0:T(8,128)S(1)}) custom-call(s32[4]{0:T(128)S(1)} %copy-done.37, bf16[2,4096,128]{2,1,0:T(8,128)(2,1)S(1)} %copy-done.10, bf16[2,4096,128]{2,1,0:T(8,128)(2,1)S(1)} %copy-done.4, bf16[16,64,256]{2,1,0:T(8,128)(2,1)S(1)} %bitcast.46, ...), custom_call_target="tpu_custom_call" | custom-call | flops 536870 | bytes 4194 | tf_op jit(solution)/shard_map/adjoint/pallas_call | solution.py:251
  (225 shorter events, 74.8 us)
Async XLA Ops:
  6.4 17.5 %collective-permute-start.4 = (bf16[2,4096,128]{2,1,0:T(8,128)(2,1)}, bf16[2,4096,128]{2,1,0:T(8,128)(2,1)}, u32[]{:S(2)}, u32[]{:S(2)}) collective-permute-start(bf16[2,4096,128]{2,1,0:T(8,128)(2,1)} %cut.2), channel_id=1, source_target_pairs={{0,8},{8,0},{16,24},{24,16},{1,9},{9,1},{17,25},{25,17},{2,10},{10... | collective-permute-start | bytes 6291464 | tf_op jit(solution)/shard_map/ppermute | solution.py:502
  10.1 25.1 %collective-permute-start.7 = (bf16[2,4096,128]{2,1,0:T(8,128)(2,1)}, bf16[2,4096,128]{2,1,0:T(8,128)(2,1)S(1)}, u32[]{:S(2)}, u32[]{:S(2)}) collective-permute-start(bf16[2,4096,128]{2,1,0:T(8,128)(2,1)} %cut.3.refs_1_), channel_id=1, source_target_pairs={{0,8},{8,0},{16,24},{24,16},{1,9},{9,1},{17,25},{25,17},{2,10},{10... | collective-permute-start | bytes 6291464 | tf_op jit(solution)/shard_map/ppermute | solution.py:502
  10.3 4.5 %collective-permute-start = (f32[16,128]{1,0:T(8,128)S(1)}, f32[16,128]{1,0:T(8,128)S(1)}, u32[]{:S(2)}, u32[]{:S(2)}) collective-permute-start(f32[16,128]{1,0:T(8,128)S(1)} %copy-done.49), channel_id=1, source_target_pairs={{0,1},{1,0},{2,3},{3,2},{4,5},{5,4},{6,7},{7,6},{8,9},{9,8},{10,11... | collective-permute-start | bytes 24584 | tf_op jit(solution)/shard_map/ppermute | solution.py:508
  14.8 4.4 %collective-permute-start.1 = (f32[32,128]{1,0:T(8,128)S(1)}, f32[32,128]{1,0:T(8,128)S(1)}, u32[]{:S(2)}, u32[]{:S(2)}) collective-permute-start(f32[32,128]{1,0:T(8,128)S(1)} %pad_maximum_fusion.2), channel_id=1, source_target_pairs={{0,2},{1,3},{2,0},{3,1},{4,6},{5,7},{6,4},{7,5},{8,10},{9,11},{10,... | collective-permute-start | bytes 49160 | tf_op jit(solution)/shard_map/ppermute | solution.py:508
  16.9 7.0 %collective-permute-start.5 = (bf16[16,64,128]{2,1,0:T(8,128)(2,1)S(1)}, bf16[16,64,128]{2,1,0:T(8,128)(2,1)}, u32[]{:S(2)}, u32[]{:S(2)}) collective-permute-start(bf16[16,64,128]{2,1,0:T(8,128)(2,1)S(1)} %copy-done.14), channel_id=1, source_target_pairs={{0,16},{8,24},{16,0},{24,8},{1,17},{9,25},{17,1},{25,9},{2,18},{10... | collective-permute-start | bytes 786440 | tf_op jit(solution)/shard_map/ppermute | solution.py:505
  29.5 14.2 %collective-permute-start.6 = (bf16[16,64,256]{2,1,0:T(8,128)(2,1)}, bf16[16,64,256]{2,1,0:T(8,128)(2,1)}, u32[]{:S(2)}, u32[]{:S(2)}) collective-permute-start(bf16[16,64,256]{2,1,0:T(8,128)(2,1)} %get-tuple-element.53), channel_id=1, source_target_pairs={{0,1},{1,0},{2,3},{3,2},{4,5},{5,4},{6,7},{7,6},{8,9},{9,8},{10,11... | collective-permute-start | bytes 1572872 | tf_op jit(solution)/shard_map/ppermute | solution.py:508
  31.0 6.4 %collective-permute-start.8 = (bf16[16,64,128]{2,1,0:T(8,128)(2,1)S(1)}, bf16[16,64,128]{2,1,0:T(8,128)(2,1)S(1)}, u32[]{:S(2)}, u32[]{:S(2)}) collective-permute-start(bf16[16,64,128]{2,1,0:T(8,128)(2,1)S(1)} %ordered.4), channel_id=1, source_target_pairs={{0,16},{8,24},{16,0},{24,8},{1,17},{9,25},{17,1},{25,9},{2,18},{10... | collective-permute-start | bytes 786440 | tf_op jit(solution)/shard_map/ppermute | solution.py:505
  32.6 11.7 %collective-permute-start.2 = (f32[64,128]{1,0:T(8,128)S(1)}, f32[64,128]{1,0:T(8,128)}, u32[]{:S(2)}, u32[]{:S(2)}) collective-permute-start(f32[64,128]{1,0:T(8,128)S(1)} %copy-done.48), channel_id=1, source_target_pairs={{0,4},{1,5},{2,6},{3,7},{4,0},{5,1},{6,2},{7,3},{8,12},{9,13},{10,... | collective-permute-start | bytes 98312 | tf_op jit(solution)/shard_map/ppermute | solution.py:508
  43.7 18.0 %collective-permute-start.12 = (bf16[16,64,256]{2,1,0:T(8,128)(2,1)}, bf16[16,64,256]{2,1,0:T(8,128)(2,1)}, u32[]{:S(2)}, u32[]{:S(2)}) collective-permute-start(bf16[16,64,256]{2,1,0:T(8,128)(2,1)} %ordered.5.refs_0_), channel_id=1, source_target_pairs={{0,1},{1,0},{2,3},{3,2},{4,5},{5,4},{6,7},{7,6},{8,9},{9,8},{10,11... | collective-permute-start | bytes 1572872 | tf_op jit(solution)/shard_map/ppermute | solution.py:508
  45.1 7.6 %collective-permute-start.3 = (f32[2,32,128]{2,1,0:T(8,128)S(1)}, f32[2,32,128]{2,1,0:T(8,128)S(1)}, u32[]{:S(2)}, u32[]{:S(2)}) collective-permute-start(f32[2,32,128]{2,1,0:T(8,128)S(1)} %get-tuple-element.106), channel_id=1, source_target_pairs={{0,8},{8,0},{16,24},{24,16},{1,9},{9,1},{17,25},{25,17},{2,10},{10... | collective-permute-start | bytes 98312 | tf_op jit(solution)/shard_map/ppermute | solution.py:502
  47.7 8.9 %collective-permute-start.9 = (bf16[256,256]{1,0:T(8,128)(2,1)}, bf16[256,256]{1,0:T(8,128)(2,1)S(1)}, u32[]{:S(2)}, u32[]{:S(2)}) collective-permute-start(bf16[256,256]{1,0:T(8,128)(2,1)} %get-tuple-element.56), channel_id=1, source_target_pairs={{0,2},{1,3},{2,0},{3,1},{4,6},{5,7},{6,4},{7,5},{8,10},{9,11},{10,... | collective-permute-start | bytes 393224 | tf_op jit(solution)/shard_map/ppermute | solution.py:508
  48.1 8.5 %collective-permute-start.10 = (bf16[256,256]{1,0:T(8,128)(2,1)}, bf16[256,256]{1,0:T(8,128)(2,1)S(1)}, u32[]{:S(2)}, u32[]{:S(2)}) collective-permute-start(bf16[256,256]{1,0:T(8,128)(2,1)} %get-tuple-element.57), channel_id=1, source_target_pairs={{0,4},{1,5},{2,6},{3,7},{4,0},{5,1},{6,2},{7,3},{8,12},{9,13},{10,... | collective-permute-start | bytes 393224 | tf_op jit(solution)/shard_map/ppermute | solution.py:508
  50.8 10.9 %collective-permute-start.11 = (bf16[256,256]{1,0:T(8,128)(2,1)}, bf16[256,256]{1,0:T(8,128)(2,1)}, u32[]{:S(2)}, u32[]{:S(2)}) collective-permute-start(bf16[256,256]{1,0:T(8,128)(2,1)} %get-tuple-element.58), channel_id=1, source_target_pairs={{0,6},{1,7},{2,4},{3,5},{4,2},{5,3},{6,0},{7,1},{8,14},{9,15},{10,... | collective-permute-start | bytes 393224 | tf_op jit(solution)/shard_map/ppermute | solution.py:508
  63.6 7.0 %collective-permute-start.21 = (bf16[256,256]{1,0:T(8,128)(2,1)S(1)}, bf16[256,256]{1,0:T(8,128)(2,1)S(1)}, u32[]{:S(2)}, u32[]{:S(2)}) collective-permute-start(bf16[256,256]{1,0:T(8,128)(2,1)S(1)} %get-tuple-element.67.refs_0_), channel_id=1, source_target_pairs={{0,6},{1,7},{2,4},{3,5},{4,2},{5,3},{6,0},{7,1},{8,14},{9,15},{10,... | collective-permute-start | bytes 393224 | tf_op jit(solution)/shard_map/ppermute | solution.py:508
  66.5 12.5 %collective-permute-start.20 = (bf16[256,256]{1,0:T(8,128)(2,1)S(1)}, bf16[256,256]{1,0:T(8,128)(2,1)S(1)}, u32[]{:S(2)}, u32[]{:S(2)}) collective-permute-start(bf16[256,256]{1,0:T(8,128)(2,1)S(1)} %get-tuple-element.67.refs_0_), channel_id=1, source_target_pairs={{0,4},{1,5},{2,6},{3,7},{4,0},{5,1},{6,2},{7,3},{8,12},{9,13},{10,... | collective-permute-start | bytes 393224 | tf_op jit(solution)/shard_map/ppermute | solution.py:508
  68.2 10.8 %collective-permute-start.19 = (bf16[256,256]{1,0:T(8,128)(2,1)S(1)}, bf16[256,256]{1,0:T(8,128)(2,1)S(1)}, u32[]{:S(2)}, u32[]{:S(2)}) collective-permute-start(bf16[256,256]{1,0:T(8,128)(2,1)S(1)} %get-tuple-element.67.refs_0_), channel_id=1, source_target_pairs={{0,2},{1,3},{2,0},{3,1},{4,6},{5,7},{6,4},{7,5},{8,10},{9,11},{10,... | collective-permute-start | bytes 393224 | tf_op jit(solution)/shard_map/ppermute | solution.py:508
  79.6 13.9 %collective-permute-start.22 = (bf16[16,64,256]{2,1,0:T(8,128)(2,1)S(1)}, bf16[16,64,256]{2,1,0:T(8,128)(2,1)S(1)}, u32[]{:S(2)}, u32[]{:S(2)}) collective-permute-start(bf16[16,64,256]{2,1,0:T(8,128)(2,1)S(1)} %bitcast.49), channel_id=1, source_target_pairs={{0,1},{1,0},{2,3},{3,2},{4,5},{5,4},{6,7},{7,6},{8,9},{9,8},{10,11... | collective-permute-start | bytes 1572872 | tf_op jit(solution)/shard_map/ppermute | solution.py:508
  82.3 16.3 %collective-permute-start.13 = (bf16[256,256]{1,0:T(8,128)(2,1)S(1)}, bf16[256,256]{1,0:T(8,128)(2,1)S(1)}, u32[]{:S(2)}, u32[]{:S(2)}) collective-permute-start(bf16[256,256]{1,0:T(8,128)(2,1)S(1)} %get-tuple-element.62), channel_id=1, source_target_pairs={{0,2},{1,3},{2,0},{3,1},{4,6},{5,7},{6,4},{7,5},{8,10},{9,11},{10,... | collective-permute-start | bytes 393224 | tf_op jit(solution)/shard_map/ppermute | solution.py:508
  82.4 16.2 %collective-permute-start.14 = (bf16[256,256]{1,0:T(8,128)(2,1)S(1)}, bf16[256,256]{1,0:T(8,128)(2,1)S(1)}, u32[]{:S(2)}, u32[]{:S(2)}) collective-permute-start(bf16[256,256]{1,0:T(8,128)(2,1)S(1)} %get-tuple-element.63), channel_id=1, source_target_pairs={{0,4},{1,5},{2,6},{3,7},{4,0},{5,1},{6,2},{7,3},{8,12},{9,13},{10,... | collective-permute-start | bytes 393224 | tf_op jit(solution)/shard_map/ppermute | solution.py:508
  85.5 13.1 %collective-permute-start.15 = (bf16[256,256]{1,0:T(8,128)(2,1)S(1)}, bf16[256,256]{1,0:T(8,128)(2,1)S(1)}, u32[]{:S(2)}, u32[]{:S(2)}) collective-permute-start(bf16[256,256]{1,0:T(8,128)(2,1)S(1)} %get-tuple-element.64), channel_id=1, source_target_pairs={{0,6},{1,7},{2,4},{3,5},{4,2},{5,3},{6,0},{7,1},{8,14},{9,15},{10,... | collective-permute-start | bytes 393224 | tf_op jit(solution)/shard_map/ppermute | solution.py:508
  96.5 19.3 %collective-permute-start.23 = (bf16[2,16,64,128]{3,2,1,0:T(8,128)(2,1)S(1)}, bf16[2,16,64,128]{3,2,1,0:T(8,128)(2,1)S(1)}, u32[]{:S(2)}, u32[]{:S(2)}) collective-permute-start(bf16[2,16,64,128]{3,2,1,0:T(8,128)(2,1)S(1)} %adjoint.4.one_ref.mine_ref.refs_4_), channel_id=1, source_target_pairs={{0,16},{8,24},{16,0},{24,8},{1,17},{9,25},{17,1},{25,9},{2,18},{10... | collective-permute-start | bytes 1572872 | tf_op jit(solution)/shard_map/ppermute | solution.py:505
  100.0 13.5 %collective-permute-start.33 = (bf16[256,256]{1,0:T(8,128)(2,1)S(1)}, bf16[256,256]{1,0:T(8,128)(2,1)S(1)}, u32[]{:S(2)}, u32[]{:S(2)}) collective-permute-start(bf16[256,256]{1,0:T(8,128)(2,1)S(1)} %get-tuple-element.79.refs_0_), channel_id=1, source_target_pairs={{0,6},{1,7},{2,4},{3,5},{4,2},{5,3},{6,0},{7,1},{8,14},{9,15},{10,... | collective-permute-start | bytes 393224 | tf_op jit(solution)/shard_map/ppermute | solution.py:508
  102.4 11.1 %collective-permute-start.32 = (bf16[256,256]{1,0:T(8,128)(2,1)S(1)}, bf16[256,256]{1,0:T(8,128)(2,1)S(1)}, u32[]{:S(2)}, u32[]{:S(2)}) collective-permute-start(bf16[256,256]{1,0:T(8,128)(2,1)S(1)} %get-tuple-element.79.refs_0_), channel_id=1, source_target_pairs={{0,4},{1,5},{2,6},{3,7},{4,0},{5,1},{6,2},{7,3},{8,12},{9,13},{10,... | collective-permute-start | bytes 393224 | tf_op jit(solution)/shard_map/ppermute | solution.py:508
  102.4 11.1 %collective-permute-start.31 = (bf16[256,256]{1,0:T(8,128)(2,1)S(1)}, bf16[256,256]{1,0:T(8,128)(2,1)S(1)}, u32[]{:S(2)}, u32[]{:S(2)}) collective-permute-start(bf16[256,256]{1,0:T(8,128)(2,1)S(1)} %get-tuple-element.79.refs_0_), channel_id=1, source_target_pairs={{0,2},{1,3},{2,0},{3,1},{4,6},{5,7},{6,4},{7,5},{8,10},{9,11},{10,... | collective-permute-start | bytes 393224 | tf_op jit(solution)/shard_map/ppermute | solution.py:508
  105.6 4.2 %collective-permute-start.17 = (f32[24,128]{1,0:T(8,128)S(1)}, f32[24,128]{1,0:T(8,128)S(1)}, u32[]{:S(2)}, u32[]{:S(2)}) collective-permute-start(f32[24,128]{1,0:T(8,128)S(1)} %add.81), channel_id=1, source_target_pairs={{0,16},{8,24},{16,0},{24,8},{1,17},{9,25},{17,1},{25,9},{2,18},{10... | collective-permute-start | bytes 36872 | tf_op jit(solution)/shard_map/ppermute | solution.py:505
  114.1 14.3 %collective-permute-start.34 = (bf16[16,64,256]{2,1,0:T(8,128)(2,1)S(1)}, bf16[16,64,256]{2,1,0:T(8,128)(2,1)S(1)}, u32[]{:S(2)}, u32[]{:S(2)}) collective-permute-start(bf16[16,64,256]{2,1,0:T(8,128)(2,1)S(1)} %bitcast.47), channel_id=1, source_target_pairs={{0,1},{1,0},{2,3},{3,2},{4,5},{5,4},{6,7},{7,6},{8,9},{9,8},{10,11... | collective-permute-start | bytes 1572872 | tf_op jit(solution)/shard_map/ppermute | solution.py:508
  123.7 4.6 %collective-permute-start.25 = (f32[24,128]{1,0:T(8,128)S(1)}, f32[24,128]{1,0:T(8,128)S(1)}, u32[]{:S(2)}, u32[]{:S(2)}) collective-permute-start(f32[24,128]{1,0:T(8,128)S(1)} %add.84), channel_id=1, source_target_pairs={{0,4},{1,5},{2,6},{3,7},{4,0},{5,1},{6,2},{7,3},{8,12},{9,13},{10,... | collective-permute-start | bytes 36872 | tf_op jit(solution)/shard_map/ppermute | solution.py:508
  124.5 13.3 %collective-permute-start.27 = (bf16[16,64,256]{2,1,0:T(8,128)(2,1)}, bf16[16,64,256]{2,1,0:T(8,128)(2,1)}, u32[]{:S(2)}, u32[]{:S(2)}) collective-permute-start(bf16[16,64,256]{2,1,0:T(8,128)(2,1)} %get-tuple-element.68.refs_1_.refs_0_), channel_id=1, source_target_pairs={{0,1},{1,0},{2,3},{3,2},{4,5},{5,4},{6,7},{7,6},{8,9},{9,8},{10,11... | collective-permute-start | bytes 1572872 | tf_op jit(solution)/shard_map/ppermute | solution.py:508
  131.5 14.3 %collective-permute-start.35 = (bf16[2,16,64,128]{3,2,1,0:T(8,128)(2,1)}, bf16[2,16,64,128]{3,2,1,0:T(8,128)(2,1)}, u32[]{:S(2)}, u32[]{:S(2)}) collective-permute-start(bf16[2,16,64,128]{3,2,1,0:T(8,128)(2,1)} %adjoint.5.mine_ref.one_ref), channel_id=1, source_target_pairs={{0,16},{8,24},{16,0},{24,8},{1,17},{9,25},{17,1},{25,9},{2,18},{10... | collective-permute-start | bytes 1572872 | tf_op jit(solution)/shard_map/ppermute | solution.py:505
  133.1 20.8 %collective-permute-start.26 = (f32[32]{0:T(128)S(1)}, f32[32]{0:T(128)S(1)}, u32[]{:S(2)}, u32[]{:S(2)}) collective-permute-start(f32[32]{0:T(128)S(1)} %copy-done.46), channel_id=1, source_target_pairs={{0,16},{8,24},{16,0},{24,8},{1,17},{9,25},{17,1},{25,9},{2,18},{10... | collective-permute-start | bytes 392 | tf_op jit(solution)/shard_map/ppermute | solution.py:505
  141.4 17.4 %collective-permute-start.28 = (bf16[256,256]{1,0:T(8,128)(2,1)}, bf16[256,256]{1,0:T(8,128)(2,1)S(1)}, u32[]{:S(2)}, u32[]{:S(2)}) collective-permute-start(bf16[256,256]{1,0:T(8,128)(2,1)} %get-tuple-element.73), channel_id=1, source_target_pairs={{0,2},{1,3},{2,0},{3,1},{4,6},{5,7},{6,4},{7,5},{8,10},{9,11},{10,... | collective-permute-start | bytes 393224 | tf_op jit(solution)/shard_map/ppermute | solution.py:508
  141.4 17.4 %collective-permute-start.29 = (bf16[256,256]{1,0:T(8,128)(2,1)}, bf16[256,256]{1,0:T(8,128)(2,1)S(1)}, u32[]{:S(2)}, u32[]{:S(2)}) collective-permute-start(bf16[256,256]{1,0:T(8,128)(2,1)} %get-tuple-element.74), channel_id=1, source_target_pairs={{0,4},{1,5},{2,6},{3,7},{4,0},{5,1},{6,2},{7,3},{8,12},{9,13},{10,... | collective-permute-start | bytes 393224 | tf_op jit(solution)/shard_map/ppermute | solution.py:508
  144.2 14.6 %collective-permute-start.30 = (bf16[256,256]{1,0:T(8,128)(2,1)}, bf16[256,256]{1,0:T(8,128)(2,1)}, u32[]{:S(2)}, u32[]{:S(2)}) collective-permute-start(bf16[256,256]{1,0:T(8,128)(2,1)} %get-tuple-element.75), channel_id=1, source_target_pairs={{0,6},{1,7},{2,4},{3,5},{4,2},{5,3},{6,0},{7,1},{8,14},{9,15},{10,... | collective-permute-start | bytes 393224 | tf_op jit(solution)/shard_map/ppermute | solution.py:508
  152.4 22.1 %collective-permute-start.36 = (bf16[16,64,256]{2,1,0:T(8,128)(2,1)}, bf16[16,64,256]{2,1,0:T(8,128)(2,1)}, u32[]{:S(2)}, u32[]{:S(2)}) collective-permute-start(bf16[16,64,256]{2,1,0:T(8,128)(2,1)} %ordered.7), channel_id=1, source_target_pairs={{0,1},{1,0},{2,3},{3,2},{4,5},{5,4},{6,7},{7,6},{8,9},{9,8},{10,11... | collective-permute-start | bytes 1572872 | tf_op jit(solution)/shard_map/ppermute | solution.py:508
  162.0 7.0 %collective-permute-start.50 = (bf16[256,256]{1,0:T(8,128)(2,1)S(1)}, bf16[256,256]{1,0:T(8,128)(2,1)S(1)}, u32[]{:S(2)}, u32[]{:S(2)}) collective-permute-start(bf16[256,256]{1,0:T(8,128)(2,1)S(1)} %get-tuple-element.91.refs_0_), channel_id=1, source_target_pairs={{0,6},{1,7},{2,4},{3,5},{4,2},{5,3},{6,0},{7,1},{8,14},{9,15},{10,... | collective-permute-start | bytes 393224 | tf_op jit(solution)/shard_map/ppermute | solution.py:508
  164.1 8.7 %collective-permute-start.49 = (bf16[256,256]{1,0:T(8,128)(2,1)S(1)}, bf16[256,256]{1,0:T(8,128)(2,1)S(1)}, u32[]{:S(2)}, u32[]{:S(2)}) collective-permute-start(bf16[256,256]{1,0:T(8,128)(2,1)S(1)} %get-tuple-element.91.refs_0_), channel_id=1, source_target_pairs={{0,4},{1,5},{2,6},{3,7},{4,0},{5,1},{6,2},{7,3},{8,12},{9,13},{10,... | collective-permute-start | bytes 393224 | tf_op jit(solution)/shard_map/ppermute | solution.py:508
  164.1 8.7 %collective-permute-start.48 = (bf16[256,256]{1,0:T(8,128)(2,1)S(1)}, bf16[256,256]{1,0:T(8,128)(2,1)S(1)}, u32[]{:S(2)}, u32[]{:S(2)}) collective-permute-start(bf16[256,256]{1,0:T(8,128)(2,1)S(1)} %get-tuple-element.91.refs_0_), channel_id=1, source_target_pairs={{0,2},{1,3},{2,0},{3,1},{4,6},{5,7},{6,4},{7,5},{8,10},{9,11},{10,... | collective-permute-start | bytes 393224 | tf_op jit(solution)/shard_map/ppermute | solution.py:508
  173.4 27.8 %collective-permute-start.51 = (bf16[16,64,256]{2,1,0:T(8,128)(2,1)S(1)}, bf16[16,64,256]{2,1,0:T(8,128)(2,1)S(1)}, u32[]{:S(2)}, u32[]{:S(2)}) collective-permute-start(bf16[16,64,256]{2,1,0:T(8,128)(2,1)S(1)} %bitcast.51), channel_id=1, source_target_pairs={{0,1},{1,0},{2,3},{3,2},{4,5},{5,4},{6,7},{7,6},{8,9},{9,8},{10,11... | collective-permute-start | bytes 1572872 | tf_op jit(solution)/shard_map/ppermute | solution.py:508
  175.9 5.7 %collective-permute-start.37 = (bf16[256,256]{1,0:T(8,128)(2,1)S(1)}, bf16[256,256]{1,0:T(8,128)(2,1)S(1)}, u32[]{:S(2)}, u32[]{:S(2)}) collective-permute-start(bf16[256,256]{1,0:T(8,128)(2,1)S(1)} %get-tuple-element.84), channel_id=1, source_target_pairs={{0,2},{1,3},{2,0},{3,1},{4,6},{5,7},{6,4},{7,5},{8,10},{9,11},{10,... | collective-permute-start | bytes 393224 | tf_op jit(solution)/shard_map/ppermute | solution.py:508
  175.9 11.6 %collective-permute-start.38 = (bf16[256,256]{1,0:T(8,128)(2,1)S(1)}, bf16[256,256]{1,0:T(8,128)(2,1)S(1)}, u32[]{:S(2)}, u32[]{:S(2)}) collective-permute-start(bf16[256,256]{1,0:T(8,128)(2,1)S(1)} %get-tuple-element.85), channel_id=1, source_target_pairs={{0,4},{1,5},{2,6},{3,7},{4,0},{5,1},{6,2},{7,3},{8,12},{9,13},{10,... | collective-permute-start | bytes 393224 | tf_op jit(solution)/shard_map/ppermute | solution.py:508
  178.2 9.3 %collective-permute-start.39 = (bf16[256,256]{1,0:T(8,128)(2,1)S(1)}, bf16[256,256]{1,0:T(8,128)(2,1)S(1)}, u32[]{:S(2)}, u32[]{:S(2)}) collective-permute-start(bf16[256,256]{1,0:T(8,128)(2,1)S(1)} %get-tuple-element.86), channel_id=1, source_target_pairs={{0,6},{1,7},{2,4},{3,5},{4,2},{5,3},{6,0},{7,1},{8,14},{9,15},{10,... | collective-permute-start | bytes 393224 | tf_op jit(solution)/shard_map/ppermute | solution.py:508
  188.2 16.1 %collective-permute-start.47 = (bf16[256,256]{1,0:T(8,128)(2,1)S(1)}, bf16[256,256]{1,0:T(8,128)(2,1)S(1)}, u32[]{:S(2)}, u32[]{:S(2)}) collective-permute-start(bf16[256,256]{1,0:T(8,128)(2,1)S(1)} %get-tuple-element.90.refs_0_), channel_id=1, source_target_pairs={{0,6},{1,7},{2,4},{3,5},{4,2},{5,3},{6,0},{7,1},{8,14},{9,15},{10,... | collective-permute-start | bytes 393224 | tf_op jit(solution)/shard_map/ppermute | solution.py:508
  189.9 14.4 %collective-permute-start.46 = (bf16[256,256]{1,0:T(8,128)(2,1)S(1)}, bf16[256,256]{1,0:T(8,128)(2,1)S(1)}, u32[]{:S(2)}, u32[]{:S(2)}) collective-permute-start(bf16[256,256]{1,0:T(8,128)(2,1)S(1)} %get-tuple-element.90.refs_0_), channel_id=1, source_target_pairs={{0,4},{1,5},{2,6},{3,7},{4,0},{5,1},{6,2},{7,3},{8,12},{9,13},{10,... | collective-permute-start | bytes 393224 | tf_op jit(solution)/shard_map/ppermute | solution.py:508
  191.9 12.4 %collective-permute-start.45 = (bf16[256,256]{1,0:T(8,128)(2,1)S(1)}, bf16[256,256]{1,0:T(8,128)(2,1)S(1)}, u32[]{:S(2)}, u32[]{:S(2)}) collective-permute-start(bf16[256,256]{1,0:T(8,128)(2,1)S(1)} %get-tuple-element.90.refs_0_), channel_id=1, source_target_pairs={{0,2},{1,3},{2,0},{3,1},{4,6},{5,7},{6,4},{7,5},{8,10},{9,11},{10,... | collective-permute-start | bytes 393224 | tf_op jit(solution)/shard_map/ppermute | solution.py:508
  205.1 12.3 %collective-permute-start.52 = (bf16[16,64,256]{2,1,0:T(8,128)(2,1)S(1)}, bf16[16,64,256]{2,1,0:T(8,128)(2,1)S(1)}, u32[]{:S(2)}, u32[]{:S(2)}) collective-permute-start(bf16[16,64,256]{2,1,0:T(8,128)(2,1)S(1)} %bitcast.45), channel_id=1, source_target_pairs={{0,1},{1,0},{2,3},{3,2},{4,5},{5,4},{6,7},{7,6},{8,9},{9,8},{10,11... | collective-permute-start | bytes 1572872 | tf_op jit(solution)/shard_map/ppermute | solution.py:508
  206.0 9.1 %collective-permute-start.53 = (bf16[16,64,128]{2,1,0:T(8,128)(2,1)S(1)}, bf16[16,64,128]{2,1,0:T(8,128)(2,1)S(1)}, u32[]{:S(2)}, u32[]{:S(2)}) collective-permute-start(bf16[16,64,128]{2,1,0:T(8,128)(2,1)S(1)} %get-tuple-element.92.refs_4_), channel_id=1, source_target_pairs={{0,16},{8,24},{16,0},{24,8},{1,17},{9,25},{17,1},{25,9},{2,18},{10... | collective-permute-start | bytes 786440 | tf_op jit(solution)/shard_map/ppermute | solution.py:505
  210.5 4.6 %collective-permute-start.44 = (f32[24,128]{1,0:T(8,128)S(1)}, f32[24,128]{1,0:T(8,128)S(1)}, u32[]{:S(2)}, u32[]{:S(2)}) collective-permute-start(f32[24,128]{1,0:T(8,128)S(1)} %add.90), channel_id=1, source_target_pairs={{0,4},{1,5},{2,6},{3,7},{4,0},{5,1},{6,2},{7,3},{8,12},{9,13},{10,... | collective-permute-start | bytes 36872 | tf_op jit(solution)/shard_map/ppermute | solution.py:508
  220.8 10.1 %collective-permute-start.54 = (bf16[16,64,128]{2,1,0:T(8,128)(2,1)}, bf16[16,64,128]{2,1,0:T(8,128)(2,1)S(1)}, u32[]{:S(2)}, u32[]{:S(2)}) collective-permute-start(bf16[16,64,128]{2,1,0:T(8,128)(2,1)} %get-tuple-element.94), channel_id=1, source_target_pairs={{0,16},{8,24},{16,0},{24,8},{1,17},{9,25},{17,1},{25,9},{2,18},{10... | collective-permute-start | bytes 786440 | tf_op jit(solution)/shard_map/ppermute | solution.py:505
  (57 other events, 455.7 us)

commit v5 on v4

--- a/solution.py
+++ b/solution.py
@@ -460,35 +460,6 @@
     )(alpha, damping, start, mine, got)
 
 
-def update_call(plan, chunk, scalars, damping, start, residual, image, mine, got, outs):
-    block = (plan.part, plan.rows, plan.sources)
-
-    def kernel(scalars_ref, damp_ref, start_ref, residual_ref, image_ref, mine_ref, got_ref, *refs):
-        solution_ref, out_ref = refs[len(outs):]
-        alpha_0, alpha_1, beta = scalars_ref[0], scalars_ref[1], scalars_ref[2]
-        for f in range(plan.part):
-            begin, rest = start_ref[f], residual_ref[f]
-            second = mine_ref[f] + got_ref[f].astype(F32) + damp_ref[chunk * plan.part + f] * rest
-            second = second + beta * image_ref[f]
-            solution_ref[f] = alpha_0 * begin + alpha_1 * (rest + beta * begin)
-            out_ref[f] = rest - alpha_1 * second
-
-    here = pl.BlockSpec(block, lambda i: (chunk, 0, 0))
-    alone = pl.BlockSpec(block, lambda i: (0, 0, 0))
-    values = pl.BlockSpec(memory_space=pltpu.SMEM)
-    return pl.pallas_call(
-        kernel,
-        grid=(1,),
-        in_specs=[values, values, here, alone, alone, alone, alone] + [ANYWHERE] * len(outs),
-        out_specs=[here, here],
-        out_shape=[jax.ShapeDtypeStruct(start.shape, F32)] * 2,
-        input_output_aliases={7 + i: i for i in range(len(outs))},
-        cost_estimate=cost(8 * start.size, 16 * start.size),
-        compiler_params=pltpu.CompilerParams(vmem_limit_bytes=KERNEL_BYTES),
-        name="update",
-    )(scalars, damping, start, residual, image, mine, got, *outs)
-
-
 def body(n_sens, n_src, operator, right_side, noise_weights, damping):
     plan = Plan(operator, right_side, n_sens, n_src, CHUNKS)
     sens, src = lax.axis_index("sens"), lax.axis_index("src")
@@ -602,7 +573,7 @@
     image_0, residual, norms = zip(*[
         residual_call(plan, k, alpha_0, damping, start, back[k], got_back[k]) for k in chunks
     ])
-    pieces = [reduce_field(keeps[k], got[k]) for k in chunks]
+    pieces = [reduce_field(keeps[k], got[k], (norms[k],)) for k in chunks]
     scaled, stats = zip(*[
         sensor_call(plan, k, meta, weights, pieces[k], norms[k], alpha_0, damping_row, field[k])
         for k in chunks
@@ -614,14 +585,12 @@
     curve_1 = sums[1] + 2.0 * beta * sums[2] + beta * beta * curve_0
     alpha_1 = norm_1 / curve_1
 
-    scalars = jnp.stack([alpha_0[0], alpha_1, beta])
-    results = ()
-    for k in chunks:
-        (_, mine), (got,) = outs[k]
-        results = update_call(
-            plan, k, scalars, damping, start, residual[k], image_0[k], mine, got, results
-        )
-    return tuple(result.reshape(right_side.shape) for result in results)
+    final = [mine + rest[0].astype(F32) for (_, mine), rest in outs]
+    residual, image_0 = jnp.concatenate(residual), jnp.concatenate(image_0)
+    image_1 = jnp.concatenate(final) + damping[:, None, None] * residual + beta * image_0
+    solution = alpha_0 * start + alpha_1 * (residual + beta * start)
+    residual = residual - alpha_1 * image_1
+    return solution.reshape(right_side.shape), residual.reshape(right_side.shape)
 
 
 def solution(mesh):

time: 236 us -> 230 us (0.975)
  local copies, waits for them, and re-layouts: 21.7 us -> 13 us
  Pallas kernels: 55.9 us -> 52 us
  other arithmetic: 2.58 us -> 5.98 us
  starting transfers between devices: 70 us -> 73.2 us
    unnamed x100 -> x84, local copies, waits for them, and re-layouts: 20.3 us -> 10.9 us
    ppermute x41, starting transfers between devices: 60.3 us -> 64.6 us  [to_src(): return lax.ppermute(array, 'src', [(j, j ^ step) for j in range(n_src)])]
    pallas_call x2 -> x0, Pallas kernels: 3.49 us -> none  [update_call(): pl.pallas_call(kernel, grid=(1,), in_specs=[values, values, here, alone,...]
  transfers between devices with their start and end apart: 55 -> 55, of which waited for: 23 -> 26; matrix products, arithmetic and copies ran while one was open for 1% -> 2% of each run, Pallas kernels for 20% -> 19%
where the time goes in v5:
time: 230 us; the launch traced here: 229 us
  waiting for transfers between devices  78.7 us (34%)
  starting transfers between devices  73.2 us (32%)
  Pallas kernels  52 us (23%)
  local copies, waits for them, and re-layouts  13 us (6%)
  between operations  6.55 us (3%)
  other arithmetic  5.98 us (3%)
    ppermute x41, starting transfers between devices, to_src(): return lax.ppermute(array, 'src', [(j, j ^ step) for j in range(n_src)])  64.6 us
    ppermute x41, waiting for transfers between devices, to_src(): return lax.ppermute(array, 'src', [(j, j ^ step) for j in range(n_src)])  62.1 us
    pallas_call x4, Pallas kernels, forward_call(): pl.pallas_call(kernel, grid=(1,), in_specs=[pl.BlockSpec(memory_space=plt...  18.8 us
    ppermute x9, waiting for transfers between devices, to_pair(): return lax.ppermute(array, 'sens', [(i, i ^ 2) for i in range(n_sens)])  14.3 us
    pallas_call x4, Pallas kernels, adjoint_call(): pl.pallas_call(kernel, grid=(1,), in_specs=[pl.BlockSpec(memory_space=plt...  12.6 us
    unnamed x84, local copies, waits for them, and re-layouts  10.9 us
    ppermute x9, starting transfers between devices, to_pair(): return lax.ppermute(array, 'sens', [(i, i ^ 2) for i in range(n_sens)])  7.83 us
    pallas_call x2, Pallas kernels, cut_call(): pl.pallas_call(kernel, in_specs=[pl.BlockSpec(memory_space=pltpu.SMEM), A...  6.22 us
  transfers between devices with their start and end apart: 55, of which 26 were waited for; matrix products, arithmetic and copies ran while one was open for 2% of the time, Pallas kernels for 19%

profile of v5, /device:TPU:0, one launch (start us, length us, event | category | flops | bytes accessed | tf_op | source)
XLA Modules:
  0.0 229.4 jit_solution(10644911617533381859)
XLA Ops:
  3.3 3.1 %cut.2 = bf16[2,4096,128]{2,1,0:T(8,128)(2,1)} custom-call(s32[4]{0:T(128)} %pad_add_fusion.m, bf16[2,2,8192,128]{3,2,1,0:T(8,128)(2,1)} %bitcast.60, bf16[16,64,128]{2,1,0:T(8,128)(2,1)} %copy-done.13), custom_call_target="tpu_custom_call" | custom-call | bytes 2097 | tf_op jit(solution)/shard_map/cut/pallas_call | solution.py:132
  7.0 3.1 %cut.3.refs_1_ = bf16[2,4096,128]{2,1,0:T(8,128)(2,1)} custom-call(s32[4]{0:T(128)} %pad_add_fusion.m, bf16[2,2,8192,128]{3,2,1,0:T(8,128)(2,1)} %bitcast.61, bf16[16,64,128]{2,1,0:T(8,128)(2,1)} %copy-done.13), custom_call_target="tpu_custom_call" | custom-call | bytes 2097 | tf_op jit(solution)/shard_map/cut/pallas_call | solution.py:132
  10.4 2.8 %collective-permute-start = (f32[16,128]{1,0:T(8,128)S(1)}, f32[16,128]{1,0:T(8,128)S(1)}, u32[]{:S(2)}, u32[]{:S(2)}) collective-permute-start(f32[16,128]{1,0:T(8,128)S(1)} %copy-done.41), channel_id=1, source_target_pairs={{0,1},{1,0},{2,3},{3,2},{4,5},{5,4},{6,7},{7,6},{8,9},{9,8},{10,11... | collective-permute-start | bytes 24584 | tf_op jit(solution)/shard_map/ppermute | solution.py:479
  14.9 2.1 collective-permute-start.1
  19.9 4.1 %collective-permute-done.5.two_ref.refs_1_ = bf16[16,64,128]{2,1,0:T(8,128)(2,1)} collective-permute-done((bf16[16,64,128]{2,1,0:T(8,128)(2,1)S(1)}, bf16[16,64,128]{2,1,0:T(8,128)(2,1)}, u32[]{:S(2)}, u32[]{:S(2)}) %collective-permute-start.5) | collective-permute-done | bytes 262176 | tf_op jit(solution)/shard_map/ppermute | solution.py:476
  24.0 5.6 %forward.4 = (bf16[16,64,256]{2,1,0:T(8,128)(2,1)}, bf16[16,64,256]{2,1,0:T(8,128)(2,1)}, bf16[2,4096,128]{2,1,0:T(8,128)(2,1)}) custom-call(s32[4]{0:T(128)} %pad_add_fusion.m, bf16[2,2,8192,128]{3,2,1,0:T(8,128)(2,1)} %bitcast.62, bf16[2,4096,128]{2,1,0:T(8,128)(2,1)} %collective-permute-done.4.far, f32[32,64,128]{2,1,0:T(8,128)} %bitcast.37, ...), custom_call_target="tpu_custom_call" | custom-call | flops 536870 | bytes 4194 | tf_op jit(solution)/shard_map/forward/pallas_call | solution.py:209
  32.6 2.6 %collective-permute-start.2 = (f32[64,128]{1,0:T(8,128)S(1)}, f32[64,128]{1,0:T(8,128)S(1)}, u32[]{:S(2)}, u32[]{:S(2)}) collective-permute-start(f32[64,128]{1,0:T(8,128)S(1)} %copy-done.40), channel_id=1, source_target_pairs={{0,4},{1,5},{2,6},{3,7},{4,0},{5,1},{6,2},{7,3},{8,12},{9,13},{10,... | collective-permute-start | bytes 98312 | tf_op jit(solution)/shard_map/ppermute | solution.py:479
  35.2 2.3 %collective-permute-done.8.two_ref = bf16[16,64,128]{2,1,0:T(8,128)(2,1)S(1)} collective-permute-done((bf16[16,64,128]{2,1,0:T(8,128)(2,1)S(1)}, bf16[16,64,128]{2,1,0:T(8,128)(2,1)S(1)}, u32[]{:S(2)}, u32[]{:S(2)}) %collective-permute-start.8) | collective-permute-done | bytes 262176 | tf_op jit(solution)/shard_map/ppermute | solution.py:476
  38.2 5.5 %forward.5 = (bf16[16,64,256]{2,1,0:T(8,128)(2,1)}, bf16[16,64,256]{2,1,0:T(8,128)(2,1)}, bf16[2,4096,128]{2,1,0:T(8,128)(2,1)}) custom-call(s32[4]{0:T(128)} %pad_add_fusion.m, bf16[2,2,8192,128]{3,2,1,0:T(8,128)(2,1)} %bitcast.63, bf16[2,4096,128]{2,1,0:T(8,128)(2,1)} %copy-done.3, f32[32,64,128]{2,1,0:T(8,128)} %bitcast.38, bf16[16,64,128]{2,1,0:T(8,128)(2,1)} %copy-done.39), custom_call_target="tpu_custom_call" | custom-call | flops 536870 | bytes 4194 | tf_op jit(solution)/shard_map/forward/pallas_call | solution.py:209
  45.0 1.8 split.4
  46.9 2.6 %collective-permute-start.10 = (bf16[256,256]{1,0:T(8,128)(2,1)}, bf16[256,256]{1,0:T(8,128)(2,1)}, u32[]{:S(2)}, u32[]{:S(2)}) collective-permute-start(bf16[256,256]{1,0:T(8,128)(2,1)} %get-tuple-element.53), channel_id=1, source_target_pairs={{0,4},{1,5},{2,6},{3,7},{4,0},{5,1},{6,2},{7,3},{8,12},{9,13},{10,... | collective-permute-start | bytes 393224 | tf_op jit(solution)/shard_map/ppermute | solution.py:479
  51.0 8.5 %collective-permute-done.10.refs_4_ = bf16[256,256]{1,0:T(8,128)(2,1)} collective-permute-done((bf16[256,256]{1,0:T(8,128)(2,1)}, bf16[256,256]{1,0:T(8,128)(2,1)}, u32[]{:S(2)}, u32[]{:S(2)}) %collective-permute-start.10) | collective-permute-done | bytes 131104 | tf_op jit(solution)/shard_map/ppermute | solution.py:479
  62.8 1.9 collective-permute-start.19
  67.4 2.6 %collective-permute-done.19.refs_1_ = bf16[256,256]{1,0:T(8,128)(2,1)S(1)} collective-permute-done((bf16[256,256]{1,0:T(8,128)(2,1)S(1)}, bf16[256,256]{1,0:T(8,128)(2,1)S(1)}, u32[]{:S(2)}, u32[]{:S(2)}) %collective-permute-start.19) | collective-permute-done | bytes 131104 | tf_op jit(solution)/shard_map/ppermute | solution.py:479
  70.0 7.6 %collective-permute-done.20.refs_2_ = bf16[256,256]{1,0:T(8,128)(2,1)S(1)} collective-permute-done((bf16[256,256]{1,0:T(8,128)(2,1)S(1)}, bf16[256,256]{1,0:T(8,128)(2,1)S(1)}, u32[]{:S(2)}, u32[]{:S(2)}) %collective-permute-start.20) | collective-permute-done | bytes 131104 | tf_op jit(solution)/shard_map/ppermute | solution.py:479
  81.0 2.3 %collective-permute-start.13 = (bf16[256,256]{1,0:T(8,128)(2,1)S(1)}, bf16[256,256]{1,0:T(8,128)(2,1)S(1)}, u32[]{:S(2)}, u32[]{:S(2)}) collective-permute-start(bf16[256,256]{1,0:T(8,128)(2,1)S(1)} %get-tuple-element.58), channel_id=1, source_target_pairs={{0,2},{1,3},{2,0},{3,1},{4,6},{5,7},{6,4},{7,5},{8,10},{9,11},{10,... | collective-permute-start | bytes 393224 | tf_op jit(solution)/shard_map/ppermute | solution.py:479
  85.8 3.6 %collective-permute-done.22.got_ref = bf16[16,64,256]{2,1,0:T(8,128)(2,1)S(1)} collective-permute-done((bf16[16,64,256]{2,1,0:T(8,128)(2,1)S(1)}, bf16[16,64,256]{2,1,0:T(8,128)(2,1)S(1)}, u32[]{:S(2)}, u32[]{:S(2)}) %collective-permute-start.22) | collective-permute-done | bytes 524320 | tf_op jit(solution)/shard_map/ppermute | solution.py:479
  89.4 3.0 %adjoint.4.one_ref.mine_ref.refs_4_ = bf16[2,16,64,128]{3,2,1,0:T(8,128)(2,1)S(1)} custom-call(s32[4]{0:T(128)S(1)} %copy-done.33, bf16[2,4096,128]{2,1,0:T(8,128)(2,1)S(1)} %copy-done.5, bf16[2,4096,128]{2,1,0:T(8,128)(2,1)} %collective-permute-done.4.far, bf16[16,64,256]{2,1,0:T(8,128)(2,1)S(1)} %bitcast.48, ...), custom_call_target="tpu_custom_call" | custom-call | flops 536870 | bytes 4194 | tf_op jit(solution)/shard_map/adjoint/pallas_call | solution.py:251
  96.3 3.6 %collective-permute-start.31 = (bf16[256,256]{1,0:T(8,128)(2,1)S(1)}, bf16[256,256]{1,0:T(8,128)(2,1)S(1)}, u32[]{:S(2)}, u32[]{:S(2)}) collective-permute-start(bf16[256,256]{1,0:T(8,128)(2,1)S(1)} %get-tuple-element.75.refs_0_), channel_id=1, source_target_pairs={{0,2},{1,3},{2,0},{3,1},{4,6},{5,7},{6,4},{7,5},{8,10},{9,11},{10,... | collective-permute-start | bytes 393224 | tf_op jit(solution)/shard_map/ppermute | solution.py:479
  100.5 1.8 collective-permute-start.33
  103.9 3.3 %collective-permute-done.17 = f32[24,128]{1,0:T(8,128)S(1)} collective-permute-done((f32[24,128]{1,0:T(8,128)S(1)}, f32[24,128]{1,0:T(8,128)S(1)}, u32[]{:S(2)}, u32[]{:S(2)}) %collective-permute-start.17) | collective-permute-done | bytes 12320 | tf_op jit(solution)/shard_map/ppermute | solution.py:476
  108.7 2.2 collective-permute-done.18
  113.1 4.2 %forward.6 = (bf16[16,64,256]{2,1,0:T(8,128)(2,1)}, bf16[16,64,256]{2,1,0:T(8,128)(2,1)S(1)}) custom-call(s32[4]{0:T(128)S(1)} %copy-done.33, bf16[2,4096,128]{2,1,0:T(8,128)(2,1)S(1)} %copy-done.6, bf16[2,4096,128]{2,1,0:T(8,128)(2,1)} %collective-permute-done.4.far, bf16[2,16,64,128]{3,2,1,0:T(8,128)(2,1)S(1)} %adjoint.4.one_ref.mine_ref.refs_4_, ...), custom_call_target="tpu_custom_call" | custom-call | flops 536870 | bytes 4194 | tf_op jit(solution)/shard_map/forward/pallas_call | solution.py:209
  117.3 1.9 collective-permute-start.24
  119.2 1.9 collective-permute-done.24
  121.0 2.3 collective-permute-start.25
  125.8 3.0 %adjoint.5.mine_ref.one_ref = bf16[2,16,64,128]{3,2,1,0:T(8,128)(2,1)} custom-call(s32[4]{0:T(128)S(1)} %copy-done.33, bf16[2,4096,128]{2,1,0:T(8,128)(2,1)S(1)} %copy-done.8, bf16[2,4096,128]{2,1,0:T(8,128)(2,1)S(1)} %copy-done.4, bf16[16,64,256]{2,1,0:T(8,128)(2,1)S(1)} %bitcast.46, bf16[16,64,256]{2,1,0:T(8,128)(2,1)S(1)} %collective-permute-done.34.got_ref, ...), custom_call_target="tpu_custom_call" | custom-call | flops 536870 | bytes 4194 | tf_op jit(solution)/shard_map/adjoint/pallas_call | solution.py:251
  138.7 2.5 %collective-permute-start.28 = (bf16[256,256]{1,0:T(8,128)(2,1)S(1)}, bf16[256,256]{1,0:T(8,128)(2,1)S(1)}, u32[]{:S(2)}, u32[]{:S(2)}) collective-permute-start(bf16[256,256]{1,0:T(8,128)(2,1)S(1)} %get-tuple-element.69), channel_id=1, source_target_pairs={{0,2},{1,3},{2,0},{3,1},{4,6},{5,7},{6,4},{7,5},{8,10},{9,11},{10,... | collective-permute-start | bytes 393224 | tf_op jit(solution)/shard_map/ppermute | solution.py:479
  141.6 2.1 collective-permute-start.30
  143.7 3.6 %forward.7 = (bf16[16,64,256]{2,1,0:T(8,128)(2,1)S(1)}, bf16[16,64,256]{2,1,0:T(8,128)(2,1)S(1)}) custom-call(s32[4]{0:T(128)S(1)} %copy-done.33, bf16[2,4096,128]{2,1,0:T(8,128)(2,1)S(1)} %copy-done.9, bf16[2,4096,128]{2,1,0:T(8,128)(2,1)S(1)} %copy-done.4, bf16[2,16,64,128]{3,2,1,0:T(8,128)(2,1)} %adjoint.5.mine_ref.one_ref, ...), custom_call_target="tpu_custom_call" | custom-call | flops 536870 | bytes 4194 | tf_op jit(solution)/shard_map/forward/pallas_call | solution.py:209
  148.9 2.0 collective-permute-done.29.refs_7_
  151.6 2.0 collective-permute-start.45
  154.1 2.0 collective-permute-start.47
  157.3 7.2 %collective-permute-done.46.refs_2_ = bf16[256,256]{1,0:T(8,128)(2,1)S(1)} collective-permute-done((bf16[256,256]{1,0:T(8,128)(2,1)S(1)}, bf16[256,256]{1,0:T(8,128)(2,1)S(1)}, u32[]{:S(2)}, u32[]{:S(2)}) %collective-permute-start.46) | collective-permute-done | bytes 131104 | tf_op jit(solution)/shard_map/ppermute | solution.py:479
  168.1 2.7 %collective-permute-start.37 = (bf16[256,256]{1,0:T(8,128)(2,1)S(1)}, bf16[256,256]{1,0:T(8,128)(2,1)S(1)}, u32[]{:S(2)}, u32[]{:S(2)}) collective-permute-start(bf16[256,256]{1,0:T(8,128)(2,1)S(1)} %get-tuple-element.80), channel_id=1, source_target_pairs={{0,2},{1,3},{2,0},{3,1},{4,6},{5,7},{6,4},{7,5},{8,10},{9,11},{10,... | collective-permute-start | bytes 393224 | tf_op jit(solution)/shard_map/ppermute | solution.py:479
  170.7 2.4 %collective-permute-start.39 = (bf16[256,256]{1,0:T(8,128)(2,1)S(1)}, bf16[256,256]{1,0:T(8,128)(2,1)S(1)}, u32[]{:S(2)}, u32[]{:S(2)}) collective-permute-start(bf16[256,256]{1,0:T(8,128)(2,1)S(1)} %get-tuple-element.82), channel_id=1, source_target_pairs={{0,6},{1,7},{2,4},{3,5},{4,2},{5,3},{6,0},{7,1},{8,14},{9,15},{10,... | collective-permute-start | bytes 393224 | tf_op jit(solution)/shard_map/ppermute | solution.py:479
  174.7 7.5 %collective-permute-done.38.refs_7_ = bf16[256,256]{1,0:T(8,128)(2,1)S(1)} collective-permute-done((bf16[256,256]{1,0:T(8,128)(2,1)S(1)}, bf16[256,256]{1,0:T(8,128)(2,1)S(1)}, u32[]{:S(2)}, u32[]{:S(2)}) %collective-permute-start.38) | collective-permute-done | bytes 131104 | tf_op jit(solution)/shard_map/ppermute | solution.py:479
  182.8 2.5 %collective-permute-start.50 = (bf16[256,256]{1,0:T(8,128)(2,1)S(1)}, bf16[256,256]{1,0:T(8,128)(2,1)S(1)}, u32[]{:S(2)}, u32[]{:S(2)}) collective-permute-start(bf16[256,256]{1,0:T(8,128)(2,1)S(1)} %get-tuple-element.89.refs_0_), channel_id=1, source_target_pairs={{0,2},{1,3},{2,0},{3,1},{4,6},{5,7},{6,4},{7,5},{8,10},{9,11},{10,... | collective-permute-start | bytes 393224 | tf_op jit(solution)/shard_map/ppermute | solution.py:479
  185.4 2.4 %collective-permute-start.52 = (bf16[256,256]{1,0:T(8,128)(2,1)S(1)}, bf16[256,256]{1,0:T(8,128)(2,1)S(1)}, u32[]{:S(2)}, u32[]{:S(2)}) collective-permute-start(bf16[256,256]{1,0:T(8,128)(2,1)S(1)} %get-tuple-element.89.refs_0_), channel_id=1, source_target_pairs={{0,6},{1,7},{2,4},{3,5},{4,2},{5,3},{6,0},{7,1},{8,14},{9,15},{10,... | collective-permute-start | bytes 393224 | tf_op jit(solution)/shard_map/ppermute | solution.py:479
  189.0 3.7 %collective-permute-done.41 = f32[24,128]{1,0:T(8,128)S(1)} collective-permute-done((f32[24,128]{1,0:T(8,128)S(1)}, f32[24,128]{1,0:T(8,128)S(1)}, u32[]{:S(2)}, u32[]{:S(2)}) %collective-permute-start.41) | collective-permute-done | bytes 12320 | tf_op jit(solution)/shard_map/ppermute | solution.py:476
  193.3 3.1 %collective-permute-done.42 = f32[24,128]{1,0:T(8,128)S(1)} collective-permute-done((f32[24,128]{1,0:T(8,128)S(1)}, f32[24,128]{1,0:T(8,128)S(1)}, u32[]{:S(2)}, u32[]{:S(2)}) %collective-permute-start.42) | collective-permute-done | bytes 12320 | tf_op jit(solution)/shard_map/ppermute | solution.py:479
  196.4 3.4 %adjoint.6 = (bf16[16,64,128]{2,1,0:T(8,128)(2,1)}, f32[16,64,128]{2,1,0:T(8,128)S(1)}) custom-call(s32[4]{0:T(128)S(1)} %copy-done.33, bf16[2,4096,128]{2,1,0:T(8,128)(2,1)S(1)} %copy-done.7, bf16[2,4096,128]{2,1,0:T(8,128)(2,1)} %collective-permute-done.4.far, bf16[16,64,256]{2,1,0:T(8,128)(2,1)S(1)} %bitcast.50, ...), custom_call_target="tpu_custom_call" | custom-call | flops 536870 | bytes 4194 | tf_op jit(solution)/shard_map/adjoint/pallas_call | solution.py:251
  203.4 2.6 %collective-permute-done.43 = f32[24,128]{1,0:T(8,128)S(1)} collective-permute-done((f32[24,128]{1,0:T(8,128)S(1)}, f32[24,128]{1,0:T(8,128)S(1)}, u32[]{:S(2)}, u32[]{:S(2)}) %collective-permute-start.43) | collective-permute-done | bytes 12320 | tf_op jit(solution)/shard_map/ppermute | solution.py:479
  206.0 2.0 collective-permute-start.44
  208.0 2.6 %collective-permute-done.44 = f32[24,128]{1,0:T(8,128)S(1)} collective-permute-done((f32[24,128]{1,0:T(8,128)S(1)}, f32[24,128]{1,0:T(8,128)S(1)}, u32[]{:S(2)}, u32[]{:S(2)}) %collective-permute-start.44) | collective-permute-done | bytes 12320 | tf_op jit(solution)/shard_map/ppermute | solution.py:479
  210.9 2.9 %collective-permute-done.53.got_ref = bf16[16,64,256]{2,1,0:T(8,128)(2,1)} collective-permute-done((bf16[16,64,256]{2,1,0:T(8,128)(2,1)}, bf16[16,64,256]{2,1,0:T(8,128)(2,1)}, u32[]{:S(2)}, u32[]{:S(2)}) %collective-permute-start.53) | collective-permute-done | bytes 524320 | tf_op jit(solution)/shard_map/ppermute | solution.py:479
  215.5 3.2 %adjoint.7 = (bf16[16,64,128]{2,1,0:T(8,128)(2,1)}, f32[16,64,128]{2,1,0:T(8,128)S(1)}) custom-call(s32[4]{0:T(128)S(1)} %copy-done.33, bf16[2,4096,128]{2,1,0:T(8,128)(2,1)S(1)} %copy-done.10, bf16[2,4096,128]{2,1,0:T(8,128)(2,1)S(1)} %copy-done.4, bf16[16,64,256]{2,1,0:T(8,128)(2,1)} %bitcast.30.own_ref, ...), custom_call_target="tpu_custom_call" | custom-call | flops 536870 | bytes 4194 | tf_op jit(solution)/shard_map/adjoint/pallas_call | solution.py:251
  227.5 1.9 fusion.2
  (209 shorter events, 69.1 us)
Async XLA Ops:
  6.5 17.5 %collective-permute-start.4 = (bf16[2,4096,128]{2,1,0:T(8,128)(2,1)}, bf16[2,4096,128]{2,1,0:T(8,128)(2,1)}, u32[]{:S(2)}, u32[]{:S(2)}) collective-permute-start(bf16[2,4096,128]{2,1,0:T(8,128)(2,1)} %cut.2), channel_id=1, source_target_pairs={{0,8},{8,0},{16,24},{24,16},{1,9},{9,1},{17,25},{25,17},{2,10},{10... | collective-permute-start | bytes 6291464 | tf_op jit(solution)/shard_map/ppermute | solution.py:473
  10.1 25.1 %collective-permute-start.7 = (bf16[2,4096,128]{2,1,0:T(8,128)(2,1)}, bf16[2,4096,128]{2,1,0:T(8,128)(2,1)S(1)}, u32[]{:S(2)}, u32[]{:S(2)}) collective-permute-start(bf16[2,4096,128]{2,1,0:T(8,128)(2,1)} %cut.3.refs_1_), channel_id=1, source_target_pairs={{0,8},{8,0},{16,24},{24,16},{1,9},{9,1},{17,25},{25,17},{2,10},{10... | collective-permute-start | bytes 6291464 | tf_op jit(solution)/shard_map/ppermute | solution.py:473
  10.4 4.5 %collective-permute-start = (f32[16,128]{1,0:T(8,128)S(1)}, f32[16,128]{1,0:T(8,128)S(1)}, u32[]{:S(2)}, u32[]{:S(2)}) collective-permute-start(f32[16,128]{1,0:T(8,128)S(1)} %copy-done.41), channel_id=1, source_target_pairs={{0,1},{1,0},{2,3},{3,2},{4,5},{5,4},{6,7},{7,6},{8,9},{9,8},{10,11... | collective-permute-start | bytes 24584 | tf_op jit(solution)/shard_map/ppermute | solution.py:479
  14.9 4.4 %collective-permute-start.1 = (f32[32,128]{1,0:T(8,128)S(1)}, f32[32,128]{1,0:T(8,128)S(1)}, u32[]{:S(2)}, u32[]{:S(2)}) collective-permute-start(f32[32,128]{1,0:T(8,128)S(1)} %pad_maximum_fusion.3), channel_id=1, source_target_pairs={{0,2},{1,3},{2,0},{3,1},{4,6},{5,7},{6,4},{7,5},{8,10},{9,11},{10,... | collective-permute-start | bytes 49160 | tf_op jit(solution)/shard_map/ppermute | solution.py:479
  16.9 7.0 %collective-permute-start.5 = (bf16[16,64,128]{2,1,0:T(8,128)(2,1)S(1)}, bf16[16,64,128]{2,1,0:T(8,128)(2,1)}, u32[]{:S(2)}, u32[]{:S(2)}) collective-permute-start(bf16[16,64,128]{2,1,0:T(8,128)(2,1)S(1)} %copy-done.14), channel_id=1, source_target_pairs={{0,16},{8,24},{16,0},{24,8},{1,17},{9,25},{17,1},{25,9},{2,18},{10... | collective-permute-start | bytes 786440 | tf_op jit(solution)/shard_map/ppermute | solution.py:476
  29.5 14.3 %collective-permute-start.6 = (bf16[16,64,256]{2,1,0:T(8,128)(2,1)}, bf16[16,64,256]{2,1,0:T(8,128)(2,1)}, u32[]{:S(2)}, u32[]{:S(2)}) collective-permute-start(bf16[16,64,256]{2,1,0:T(8,128)(2,1)} %get-tuple-element.49), channel_id=1, source_target_pairs={{0,1},{1,0},{2,3},{3,2},{4,5},{5,4},{6,7},{7,6},{8,9},{9,8},{10,11... | collective-permute-start | bytes 1572872 | tf_op jit(solution)/shard_map/ppermute | solution.py:479
  31.2 6.4 %collective-permute-start.8 = (bf16[16,64,128]{2,1,0:T(8,128)(2,1)S(1)}, bf16[16,64,128]{2,1,0:T(8,128)(2,1)S(1)}, u32[]{:S(2)}, u32[]{:S(2)}) collective-permute-start(bf16[16,64,128]{2,1,0:T(8,128)(2,1)S(1)} %ordered.4), channel_id=1, source_target_pairs={{0,16},{8,24},{16,0},{24,8},{1,17},{9,25},{17,1},{25,9},{2,18},{10... | collective-permute-start | bytes 786440 | tf_op jit(solution)/shard_map/ppermute | solution.py:476
  32.6 11.8 %collective-permute-start.2 = (f32[64,128]{1,0:T(8,128)S(1)}, f32[64,128]{1,0:T(8,128)S(1)}, u32[]{:S(2)}, u32[]{:S(2)}) collective-permute-start(f32[64,128]{1,0:T(8,128)S(1)} %copy-done.40), channel_id=1, source_target_pairs={{0,4},{1,5},{2,6},{3,7},{4,0},{5,1},{6,2},{7,3},{8,12},{9,13},{10,... | collective-permute-start | bytes 98312 | tf_op jit(solution)/shard_map/ppermute | solution.py:479
  43.8 17.1 %collective-permute-start.12 = (bf16[16,64,256]{2,1,0:T(8,128)(2,1)}, bf16[16,64,256]{2,1,0:T(8,128)(2,1)}, u32[]{:S(2)}, u32[]{:S(2)}) collective-permute-start(bf16[16,64,256]{2,1,0:T(8,128)(2,1)} %ordered.5.refs_0_), channel_id=1, source_target_pairs={{0,1},{1,0},{2,3},{3,2},{4,5},{5,4},{6,7},{7,6},{8,9},{9,8},{10,11... | collective-permute-start | bytes 1572872 | tf_op jit(solution)/shard_map/ppermute | solution.py:479
  45.0 6.0 %collective-permute-start.3 = (f32[2,32,128]{2,1,0:T(8,128)}, f32[2,32,128]{2,1,0:T(8,128)S(1)}, u32[]{:S(2)}, u32[]{:S(2)}) collective-permute-start(f32[2,32,128]{2,1,0:T(8,128)} %get-tuple-element.100), channel_id=1, source_target_pairs={{0,8},{8,0},{16,24},{24,16},{1,9},{9,1},{17,25},{25,17},{2,10},{10... | collective-permute-start | bytes 98312 | tf_op jit(solution)/shard_map/ppermute | solution.py:473
  46.9 12.7 %collective-permute-start.10 = (bf16[256,256]{1,0:T(8,128)(2,1)}, bf16[256,256]{1,0:T(8,128)(2,1)}, u32[]{:S(2)}, u32[]{:S(2)}) collective-permute-start(bf16[256,256]{1,0:T(8,128)(2,1)} %get-tuple-element.53), channel_id=1, source_target_pairs={{0,4},{1,5},{2,6},{3,7},{4,0},{5,1},{6,2},{7,3},{8,12},{9,13},{10,... | collective-permute-start | bytes 393224 | tf_op jit(solution)/shard_map/ppermute | solution.py:479
  49.5 10.1 %collective-permute-start.11 = (bf16[256,256]{1,0:T(8,128)(2,1)}, bf16[256,256]{1,0:T(8,128)(2,1)}, u32[]{:S(2)}, u32[]{:S(2)}) collective-permute-start(bf16[256,256]{1,0:T(8,128)(2,1)} %get-tuple-element.54), channel_id=1, source_target_pairs={{0,6},{1,7},{2,4},{3,5},{4,2},{5,3},{6,0},{7,1},{8,14},{9,15},{10,... | collective-permute-start | bytes 393224 | tf_op jit(solution)/shard_map/ppermute | solution.py:479
  49.6 11.3 %collective-permute-start.9 = (bf16[256,256]{1,0:T(8,128)(2,1)}, bf16[256,256]{1,0:T(8,128)(2,1)}, u32[]{:S(2)}, u32[]{:S(2)}) collective-permute-start(bf16[256,256]{1,0:T(8,128)(2,1)} %get-tuple-element.52), channel_id=1, source_target_pairs={{0,2},{1,3},{2,0},{3,1},{4,6},{5,7},{6,4},{7,5},{8,10},{9,11},{10,... | collective-permute-start | bytes 393224 | tf_op jit(solution)/shard_map/ppermute | solution.py:479
  62.8 7.2 %collective-permute-start.19 = (bf16[256,256]{1,0:T(8,128)(2,1)S(1)}, bf16[256,256]{1,0:T(8,128)(2,1)S(1)}, u32[]{:S(2)}, u32[]{:S(2)}) collective-permute-start(bf16[256,256]{1,0:T(8,128)(2,1)S(1)} %get-tuple-element.63.refs_0_), channel_id=1, source_target_pairs={{0,2},{1,3},{2,0},{3,1},{4,6},{5,7},{6,4},{7,5},{8,10},{9,11},{10,... | collective-permute-start | bytes 393224 | tf_op jit(solution)/shard_map/ppermute | solution.py:479
  64.7 12.9 %collective-permute-start.20 = (bf16[256,256]{1,0:T(8,128)(2,1)S(1)}, bf16[256,256]{1,0:T(8,128)(2,1)S(1)}, u32[]{:S(2)}, u32[]{:S(2)}) collective-permute-start(bf16[256,256]{1,0:T(8,128)(2,1)S(1)} %get-tuple-element.63.refs_0_), channel_id=1, source_target_pairs={{0,4},{1,5},{2,6},{3,7},{4,0},{5,1},{6,2},{7,3},{8,12},{9,13},{10,... | collective-permute-start | bytes 393224 | tf_op jit(solution)/shard_map/ppermute | solution.py:479
  65.9 11.7 %collective-permute-start.21 = (bf16[256,256]{1,0:T(8,128)(2,1)S(1)}, bf16[256,256]{1,0:T(8,128)(2,1)S(1)}, u32[]{:S(2)}, u32[]{:S(2)}) collective-permute-start(bf16[256,256]{1,0:T(8,128)(2,1)S(1)} %get-tuple-element.63.refs_0_), channel_id=1, source_target_pairs={{0,6},{1,7},{2,4},{3,5},{4,2},{5,3},{6,0},{7,1},{8,14},{9,15},{10,... | collective-permute-start | bytes 393224 | tf_op jit(solution)/shard_map/ppermute | solution.py:479
  78.2 11.2 %collective-permute-start.22 = (bf16[16,64,256]{2,1,0:T(8,128)(2,1)S(1)}, bf16[16,64,256]{2,1,0:T(8,128)(2,1)S(1)}, u32[]{:S(2)}, u32[]{:S(2)}) collective-permute-start(bf16[16,64,256]{2,1,0:T(8,128)(2,1)S(1)} %bitcast.47), channel_id=1, source_target_pairs={{0,1},{1,0},{2,3},{3,2},{4,5},{5,4},{6,7},{7,6},{8,9},{9,8},{10,11... | collective-permute-start | bytes 1572872 | tf_op jit(solution)/shard_map/ppermute | solution.py:479
  81.0 13.6 %collective-permute-start.13 = (bf16[256,256]{1,0:T(8,128)(2,1)S(1)}, bf16[256,256]{1,0:T(8,128)(2,1)S(1)}, u32[]{:S(2)}, u32[]{:S(2)}) collective-permute-start(bf16[256,256]{1,0:T(8,128)(2,1)S(1)} %get-tuple-element.58), channel_id=1, source_target_pairs={{0,2},{1,3},{2,0},{3,1},{4,6},{5,7},{6,4},{7,5},{8,10},{9,11},{10,... | collective-permute-start | bytes 393224 | tf_op jit(solution)/shard_map/ppermute | solution.py:479
  83.4 11.6 %collective-permute-start.14 = (bf16[256,256]{1,0:T(8,128)(2,1)S(1)}, bf16[256,256]{1,0:T(8,128)(2,1)S(1)}, u32[]{:S(2)}, u32[]{:S(2)}) collective-permute-start(bf16[256,256]{1,0:T(8,128)(2,1)S(1)} %get-tuple-element.59), channel_id=1, source_target_pairs={{0,4},{1,5},{2,6},{3,7},{4,0},{5,1},{6,2},{7,3},{8,12},{9,13},{10,... | collective-permute-start | bytes 393224 | tf_op jit(solution)/shard_map/ppermute | solution.py:479
  84.2 10.8 %collective-permute-start.15 = (bf16[256,256]{1,0:T(8,128)(2,1)S(1)}, bf16[256,256]{1,0:T(8,128)(2,1)S(1)}, u32[]{:S(2)}, u32[]{:S(2)}) collective-permute-start(bf16[256,256]{1,0:T(8,128)(2,1)S(1)} %get-tuple-element.60), channel_id=1, source_target_pairs={{0,6},{1,7},{2,4},{3,5},{4,2},{5,3},{6,0},{7,1},{8,14},{9,15},{10,... | collective-permute-start | bytes 393224 | tf_op jit(solution)/shard_map/ppermute | solution.py:479
  92.4 20.6 %collective-permute-start.23 = (bf16[2,16,64,128]{3,2,1,0:T(8,128)(2,1)S(1)}, bf16[2,16,64,128]{3,2,1,0:T(8,128)(2,1)S(1)}, u32[]{:S(2)}, u32[]{:S(2)}) collective-permute-start(bf16[2,16,64,128]{3,2,1,0:T(8,128)(2,1)S(1)} %adjoint.4.one_ref.mine_ref.refs_4_), channel_id=1, source_target_pairs={{0,16},{8,24},{16,0},{24,8},{1,17},{9,25},{17,1},{25,9},{2,18},{10... | collective-permute-start | bytes 1572872 | tf_op jit(solution)/shard_map/ppermute | solution.py:476
  96.3 14.6 %collective-permute-start.31 = (bf16[256,256]{1,0:T(8,128)(2,1)S(1)}, bf16[256,256]{1,0:T(8,128)(2,1)S(1)}, u32[]{:S(2)}, u32[]{:S(2)}) collective-permute-start(bf16[256,256]{1,0:T(8,128)(2,1)S(1)} %get-tuple-element.75.refs_0_), channel_id=1, source_target_pairs={{0,2},{1,3},{2,0},{3,1},{4,6},{5,7},{6,4},{7,5},{8,10},{9,11},{10,... | collective-permute-start | bytes 393224 | tf_op jit(solution)/shard_map/ppermute | solution.py:479
  99.9 11.0 %collective-permute-start.32 = (bf16[256,256]{1,0:T(8,128)(2,1)S(1)}, bf16[256,256]{1,0:T(8,128)(2,1)S(1)}, u32[]{:S(2)}, u32[]{:S(2)}) collective-permute-start(bf16[256,256]{1,0:T(8,128)(2,1)S(1)} %get-tuple-element.75.refs_0_), channel_id=1, source_target_pairs={{0,4},{1,5},{2,6},{3,7},{4,0},{5,1},{6,2},{7,3},{8,12},{9,13},{10,... | collective-permute-start | bytes 393224 | tf_op jit(solution)/shard_map/ppermute | solution.py:479
  100.5 10.4 %collective-permute-start.33 = (bf16[256,256]{1,0:T(8,128)(2,1)S(1)}, bf16[256,256]{1,0:T(8,128)(2,1)S(1)}, u32[]{:S(2)}, u32[]{:S(2)}) collective-permute-start(bf16[256,256]{1,0:T(8,128)(2,1)S(1)} %get-tuple-element.75.refs_0_), channel_id=1, source_target_pairs={{0,6},{1,7},{2,4},{3,5},{4,2},{5,3},{6,0},{7,1},{8,14},{9,15},{10,... | collective-permute-start | bytes 393224 | tf_op jit(solution)/shard_map/ppermute | solution.py:479
  111.5 14.2 %collective-permute-start.34 = (bf16[16,64,256]{2,1,0:T(8,128)(2,1)S(1)}, bf16[16,64,256]{2,1,0:T(8,128)(2,1)S(1)}, u32[]{:S(2)}, u32[]{:S(2)}) collective-permute-start(bf16[16,64,256]{2,1,0:T(8,128)(2,1)S(1)} %bitcast.45), channel_id=1, source_target_pairs={{0,1},{1,0},{2,3},{3,2},{4,5},{5,4},{6,7},{7,6},{8,9},{9,8},{10,11... | collective-permute-start | bytes 1572872 | tf_op jit(solution)/shard_map/ppermute | solution.py:479
  117.3 3.8 %collective-permute-start.24 = (f32[24,128]{1,0:T(8,128)S(1)}, f32[24,128]{1,0:T(8,128)S(1)}, u32[]{:S(2)}, u32[]{:S(2)}) collective-permute-start(f32[24,128]{1,0:T(8,128)S(1)} %ordered.6), channel_id=1, source_target_pairs={{0,2},{1,3},{2,0},{3,1},{4,6},{5,7},{6,4},{7,5},{8,10},{9,11},{10,... | collective-permute-start | bytes 36872 | tf_op jit(solution)/shard_map/ppermute | solution.py:479
  121.0 4.6 %collective-permute-start.25 = (f32[24,128]{1,0:T(8,128)S(1)}, f32[24,128]{1,0:T(8,128)S(1)}, u32[]{:S(2)}, u32[]{:S(2)}) collective-permute-start(f32[24,128]{1,0:T(8,128)S(1)} %add.106), channel_id=1, source_target_pairs={{0,4},{1,5},{2,6},{3,7},{4,0},{5,1},{6,2},{7,3},{8,12},{9,13},{10,... | collective-permute-start | bytes 36872 | tf_op jit(solution)/shard_map/ppermute | solution.py:479
  123.3 12.8 %collective-permute-start.27 = (bf16[16,64,256]{2,1,0:T(8,128)(2,1)}, bf16[16,64,256]{2,1,0:T(8,128)(2,1)}, u32[]{:S(2)}, u32[]{:S(2)}) collective-permute-start(bf16[16,64,256]{2,1,0:T(8,128)(2,1)} %get-tuple-element.64.refs_1_.refs_0_), channel_id=1, source_target_pairs={{0,1},{1,0},{2,3},{3,2},{4,5},{5,4},{6,7},{7,6},{8,9},{9,8},{10,11... | collective-permute-start | bytes 1572872 | tf_op jit(solution)/shard_map/ppermute | solution.py:479
  128.7 14.9 %collective-permute-start.35 = (bf16[2,16,64,128]{3,2,1,0:T(8,128)(2,1)}, bf16[2,16,64,128]{3,2,1,0:T(8,128)(2,1)}, u32[]{:S(2)}, u32[]{:S(2)}) collective-permute-start(bf16[2,16,64,128]{3,2,1,0:T(8,128)(2,1)} %adjoint.5.mine_ref.one_ref), channel_id=1, source_target_pairs={{0,16},{8,24},{16,0},{24,8},{1,17},{9,25},{17,1},{25,9},{2,18},{10... | collective-permute-start | bytes 1572872 | tf_op jit(solution)/shard_map/ppermute | solution.py:476
  129.7 19.2 %collective-permute-start.26 = (f32[32]{0:T(128)S(1)}, f32[32]{0:T(128)S(1)}, u32[]{:S(2)}, u32[]{:S(2)}) collective-permute-start(f32[32]{0:T(128)S(1)} %copy-done.38), channel_id=1, source_target_pairs={{0,16},{8,24},{16,0},{24,8},{1,17},{9,25},{17,1},{25,9},{2,18},{10... | collective-permute-start | bytes 392 | tf_op jit(solution)/shard_map/ppermute | solution.py:476
  138.7 10.2 %collective-permute-start.28 = (bf16[256,256]{1,0:T(8,128)(2,1)S(1)}, bf16[256,256]{1,0:T(8,128)(2,1)S(1)}, u32[]{:S(2)}, u32[]{:S(2)}) collective-permute-start(bf16[256,256]{1,0:T(8,128)(2,1)S(1)} %get-tuple-element.69), channel_id=1, source_target_pairs={{0,2},{1,3},{2,0},{3,1},{4,6},{5,7},{6,4},{7,5},{8,10},{9,11},{10,... | collective-permute-start | bytes 393224 | tf_op jit(solution)/shard_map/ppermute | solution.py:479
  141.2 9.6 %collective-permute-start.29 = (bf16[256,256]{1,0:T(8,128)(2,1)S(1)}, bf16[256,256]{1,0:T(8,128)(2,1)S(1)}, u32[]{:S(2)}, u32[]{:S(2)}) collective-permute-start(bf16[256,256]{1,0:T(8,128)(2,1)S(1)} %get-tuple-element.70), channel_id=1, source_target_pairs={{0,4},{1,5},{2,6},{3,7},{4,0},{5,1},{6,2},{7,3},{8,12},{9,13},{10,... | collective-permute-start | bytes 393224 | tf_op jit(solution)/shard_map/ppermute | solution.py:479
  141.6 9.3 %collective-permute-start.30 = (bf16[256,256]{1,0:T(8,128)(2,1)S(1)}, bf16[256,256]{1,0:T(8,128)(2,1)S(1)}, u32[]{:S(2)}, u32[]{:S(2)}) collective-permute-start(bf16[256,256]{1,0:T(8,128)(2,1)S(1)} %get-tuple-element.71), channel_id=1, source_target_pairs={{0,6},{1,7},{2,4},{3,5},{4,2},{5,3},{6,0},{7,1},{8,14},{9,15},{10,... | collective-permute-start | bytes 393224 | tf_op jit(solution)/shard_map/ppermute | solution.py:479
  147.3 20.1 %collective-permute-start.36 = (bf16[16,64,256]{2,1,0:T(8,128)(2,1)S(1)}, bf16[16,64,256]{2,1,0:T(8,128)(2,1)S(1)}, u32[]{:S(2)}, u32[]{:S(2)}) collective-permute-start(bf16[16,64,256]{2,1,0:T(8,128)(2,1)S(1)} %ordered.7), channel_id=1, source_target_pairs={{0,1},{1,0},{2,3},{3,2},{4,5},{5,4},{6,7},{7,6},{8,9},{9,8},{10,11... | collective-permute-start | bytes 1572872 | tf_op jit(solution)/shard_map/ppermute | solution.py:479
  151.6 5.7 %collective-permute-start.45 = (bf16[256,256]{1,0:T(8,128)(2,1)S(1)}, bf16[256,256]{1,0:T(8,128)(2,1)S(1)}, u32[]{:S(2)}, u32[]{:S(2)}) collective-permute-start(bf16[256,256]{1,0:T(8,128)(2,1)S(1)} %get-tuple-element.86.refs_0_), channel_id=1, source_target_pairs={{0,2},{1,3},{2,0},{3,1},{4,6},{5,7},{6,4},{7,5},{8,10},{9,11},{10,... | collective-permute-start | bytes 393224 | tf_op jit(solution)/shard_map/ppermute | solution.py:479
  153.6 10.9 %collective-permute-start.46 = (bf16[256,256]{1,0:T(8,128)(2,1)S(1)}, bf16[256,256]{1,0:T(8,128)(2,1)S(1)}, u32[]{:S(2)}, u32[]{:S(2)}) collective-permute-start(bf16[256,256]{1,0:T(8,128)(2,1)S(1)} %get-tuple-element.86.refs_0_), channel_id=1, source_target_pairs={{0,4},{1,5},{2,6},{3,7},{4,0},{5,1},{6,2},{7,3},{8,12},{9,13},{10,... | collective-permute-start | bytes 393224 | tf_op jit(solution)/shard_map/ppermute | solution.py:479
  154.1 10.4 %collective-permute-start.47 = (bf16[256,256]{1,0:T(8,128)(2,1)S(1)}, bf16[256,256]{1,0:T(8,128)(2,1)S(1)}, u32[]{:S(2)}, u32[]{:S(2)}) collective-permute-start(bf16[256,256]{1,0:T(8,128)(2,1)S(1)} %get-tuple-element.86.refs_0_), channel_id=1, source_target_pairs={{0,6},{1,7},{2,4},{3,5},{4,2},{5,3},{6,0},{7,1},{8,14},{9,15},{10,... | collective-permute-start | bytes 393224 | tf_op jit(solution)/shard_map/ppermute | solution.py:479
  165.1 31.3 %collective-permute-start.48 = (bf16[16,64,256]{2,1,0:T(8,128)(2,1)S(1)}, bf16[16,64,256]{2,1,0:T(8,128)(2,1)S(1)}, u32[]{:S(2)}, u32[]{:S(2)}) collective-permute-start(bf16[16,64,256]{2,1,0:T(8,128)(2,1)S(1)} %bitcast.49), channel_id=1, source_target_pairs={{0,1},{1,0},{2,3},{3,2},{4,5},{5,4},{6,7},{7,6},{8,9},{9,8},{10,11... | collective-permute-start | bytes 1572872 | tf_op jit(solution)/shard_map/ppermute | solution.py:479
  168.1 6.6 %collective-permute-start.37 = (bf16[256,256]{1,0:T(8,128)(2,1)S(1)}, bf16[256,256]{1,0:T(8,128)(2,1)S(1)}, u32[]{:S(2)}, u32[]{:S(2)}) collective-permute-start(bf16[256,256]{1,0:T(8,128)(2,1)S(1)} %get-tuple-element.80), channel_id=1, source_target_pairs={{0,2},{1,3},{2,0},{3,1},{4,6},{5,7},{6,4},{7,5},{8,10},{9,11},{10,... | collective-permute-start | bytes 393224 | tf_op jit(solution)/shard_map/ppermute | solution.py:479
  170.7 11.4 %collective-permute-start.38 = (bf16[256,256]{1,0:T(8,128)(2,1)S(1)}, bf16[256,256]{1,0:T(8,128)(2,1)S(1)}, u32[]{:S(2)}, u32[]{:S(2)}) collective-permute-start(bf16[256,256]{1,0:T(8,128)(2,1)S(1)} %get-tuple-element.81), channel_id=1, source_target_pairs={{0,4},{1,5},{2,6},{3,7},{4,0},{5,1},{6,2},{7,3},{8,12},{9,13},{10,... | collective-permute-start | bytes 393224 | tf_op jit(solution)/shard_map/ppermute | solution.py:479
  170.7 11.4 %collective-permute-start.39 = (bf16[256,256]{1,0:T(8,128)(2,1)S(1)}, bf16[256,256]{1,0:T(8,128)(2,1)S(1)}, u32[]{:S(2)}, u32[]{:S(2)}) collective-permute-start(bf16[256,256]{1,0:T(8,128)(2,1)S(1)} %get-tuple-element.82), channel_id=1, source_target_pairs={{0,6},{1,7},{2,4},{3,5},{4,2},{5,3},{6,0},{7,1},{8,14},{9,15},{10,... | collective-permute-start | bytes 393224 | tf_op jit(solution)/shard_map/ppermute | solution.py:479
  182.8 17.0 %collective-permute-start.50 = (bf16[256,256]{1,0:T(8,128)(2,1)S(1)}, bf16[256,256]{1,0:T(8,128)(2,1)S(1)}, u32[]{:S(2)}, u32[]{:S(2)}) collective-permute-start(bf16[256,256]{1,0:T(8,128)(2,1)S(1)} %get-tuple-element.89.refs_0_), channel_id=1, source_target_pairs={{0,2},{1,3},{2,0},{3,1},{4,6},{5,7},{6,4},{7,5},{8,10},{9,11},{10,... | collective-permute-start | bytes 393224 | tf_op jit(solution)/shard_map/ppermute | solution.py:479
  185.4 14.5 %collective-permute-start.51 = (bf16[256,256]{1,0:T(8,128)(2,1)S(1)}, bf16[256,256]{1,0:T(8,128)(2,1)S(1)}, u32[]{:S(2)}, u32[]{:S(2)}) collective-permute-start(bf16[256,256]{1,0:T(8,128)(2,1)S(1)} %get-tuple-element.89.refs_0_), channel_id=1, source_target_pairs={{0,4},{1,5},{2,6},{3,7},{4,0},{5,1},{6,2},{7,3},{8,12},{9,13},{10,... | collective-permute-start | bytes 393224 | tf_op jit(solution)/shard_map/ppermute | solution.py:479
  185.4 14.5 %collective-permute-start.52 = (bf16[256,256]{1,0:T(8,128)(2,1)S(1)}, bf16[256,256]{1,0:T(8,128)(2,1)S(1)}, u32[]{:S(2)}, u32[]{:S(2)}) collective-permute-start(bf16[256,256]{1,0:T(8,128)(2,1)S(1)} %get-tuple-element.89.refs_0_), channel_id=1, source_target_pairs={{0,6},{1,7},{2,4},{3,5},{4,2},{5,3},{6,0},{7,1},{8,14},{9,15},{10,... | collective-permute-start | bytes 393224 | tf_op jit(solution)/shard_map/ppermute | solution.py:479
  201.3 12.6 %collective-permute-start.53 = (bf16[16,64,256]{2,1,0:T(8,128)(2,1)}, bf16[16,64,256]{2,1,0:T(8,128)(2,1)}, u32[]{:S(2)}, u32[]{:S(2)}) collective-permute-start(bf16[16,64,256]{2,1,0:T(8,128)(2,1)} %bitcast.30.own_ref), channel_id=1, source_target_pairs={{0,1},{1,0},{2,3},{3,2},{4,5},{5,4},{6,7},{7,6},{8,9},{9,8},{10,11... | collective-permute-start | bytes 1572872 | tf_op jit(solution)/shard_map/ppermute | solution.py:479
  201.9 9.0 %collective-permute-start.49 = (bf16[16,64,128]{2,1,0:T(8,128)(2,1)}, bf16[16,64,128]{2,1,0:T(8,128)(2,1)S(1)}, u32[]{:S(2)}, u32[]{:S(2)}) collective-permute-start(bf16[16,64,128]{2,1,0:T(8,128)(2,1)} %get-tuple-element.88.refs_4_), channel_id=1, source_target_pairs={{0,16},{8,24},{16,0},{24,8},{1,17},{9,25},{17,1},{25,9},{2,18},{10... | collective-permute-start | bytes 786440 | tf_op jit(solution)/shard_map/ppermute | solution.py:476
  206.0 4.6 %collective-permute-start.44 = (f32[24,128]{1,0:T(8,128)S(1)}, f32[24,128]{1,0:T(8,128)S(1)}, u32[]{:S(2)}, u32[]{:S(2)}) collective-permute-start(f32[24,128]{1,0:T(8,128)S(1)} %add.112), channel_id=1, source_target_pairs={{0,4},{1,5},{2,6},{3,7},{4,0},{5,1},{6,2},{7,3},{8,12},{9,13},{10,... | collective-permute-start | bytes 36872 | tf_op jit(solution)/shard_map/ppermute | solution.py:479
  219.5 6.8 %collective-permute-start.54 = (bf16[16,64,128]{2,1,0:T(8,128)(2,1)}, bf16[16,64,128]{2,1,0:T(8,128)(2,1)}, u32[]{:S(2)}, u32[]{:S(2)}) collective-permute-start(bf16[16,64,128]{2,1,0:T(8,128)(2,1)} %get-tuple-element.91), channel_id=1, source_target_pairs={{0,16},{8,24},{16,0},{24,8},{1,17},{9,25},{17,1},{25,9},{2,18},{10... | collective-permute-start | bytes 786440 | tf_op jit(solution)/shard_map/ppermute | solution.py:476
  (49 other events, 469.4 us)

commit v6 on v5

--- a/solution.py
+++ b/solution.py
@@ -486,12 +486,14 @@
             moved.append(move(array))
         return moved
 
-    def total_near(sums):
-        sums = sums + to_core(sums)
+    def total_near(sums, last):
+        sums = sums + (to_src(sums, 1) if last else to_core(sums))
         sums = sums + to_pair(sums)
-        return sums + to_src(sums, 1)
-
-    def total_far(sums):
+        return sums if last else sums + to_src(sums, 1)
+
+    def total_far(sums, last):
+        if last:
+            sums = sums + to_core(sums)
         for level in levels[1:]:
             sums = sums + to_src(sums, 1 << level)
         return sums, jnp.sum(sums.reshape(-1, 8 * 128), axis=1)
@@ -540,12 +542,12 @@
             halves = (own, to_half(own))
             if k == 1:
                 after = outs[0][1][0]
-                far_sums, sums = total_far(near_sums if last else ordered(near_sums, after))
+                far_sums, sums = total_far(near_sums if last else ordered(near_sums, after), last)
                 wait = (after, far_sums)
             out = adjoint_call(plan, k, meta, near[k], far[k], halves, last, wait if k > 0 else ())
             outs.append((out, then(k, out)))
             wait = (out[0] if last else out, near_sums)
-        return outs, total_far(near_sums)[1] if sums is None else sums
+        return outs, total_far(near_sums, last)[1] if sums is None else sums
 
     sends, near = [each[0] for each in pairs], [each[2] for each in pairs]
     got = in_turn(sends, to_half)
@@ -557,7 +559,7 @@
         )
         for k in chunks
     ])
-    near_0 = total_near(sum(stats))
+    near_0 = total_near(sum(stats), False)
 
     def go_on(k, back):
         got = to_pair(back)
@@ -578,7 +580,7 @@
         sensor_call(plan, k, meta, weights, pieces[k], norms[k], alpha_0, damping_row, field[k])
         for k in chunks
     ])
-    near_1 = total_near(sum(stats))
+    near_1 = total_near(sum(stats), True)
     outs, sums = both_products(scaled, near_1, True, lambda k, out: (to_pair(out[0]),))
     norm_1 = sums[0]
     beta = norm_1 / norm_0

time: 230 us -> 228 us (level)
  no operation moved by 1% of the time
where the time goes in v6:
time: 228 us; the launch traced here: 227 us
  waiting for transfers between devices  76.7 us (34%)
  starting transfers between devices  72.7 us (32%)
  Pallas kernels  52 us (23%)
  local copies, waits for them, and re-layouts  13 us (6%)
  between operations  6.55 us (3%)
  other arithmetic  5.98 us (3%)
    ppermute x41, starting transfers between devices, to_src(): return lax.ppermute(array, 'src', [(j, j ^ step) for j in range(n_src)])  63.8 us
    ppermute x41, waiting for transfers between devices, to_src(): return lax.ppermute(array, 'src', [(j, j ^ step) for j in range(n_src)])  60.2 us
    pallas_call x4, Pallas kernels, forward_call(): pl.pallas_call(kernel, grid=(1,), in_specs=[pl.BlockSpec(memory_space=plt...  18.8 us
    ppermute x9, waiting for transfers between devices, to_pair(): return lax.ppermute(array, 'sens', [(i, i ^ 2) for i in range(n_sens)])  14.5 us
    pallas_call x4, Pallas kernels, adjoint_call(): pl.pallas_call(kernel, grid=(1,), in_specs=[pl.BlockSpec(memory_space=plt...  12.6 us
    unnamed x84, local copies, waits for them, and re-layouts  10.9 us
    ppermute x9, starting transfers between devices, to_pair(): return lax.ppermute(array, 'sens', [(i, i ^ 2) for i in range(n_sens)])  8.07 us
    pallas_call x2, Pallas kernels, cut_call(): pl.pallas_call(kernel, in_specs=[pl.BlockSpec(memory_space=pltpu.SMEM), A...  6.22 us
  transfers between devices with their start and end apart: 55, of which 26 were waited for; matrix products, arithmetic and copies ran while one was open for 2% of the time, Pallas kernels for 19%

profile of v6, /device:TPU:0, one launch (start us, length us, event | category | flops | bytes accessed | tf_op | source)
XLA Modules:
  0.0 226.8 jit_solution(1899539717983999532)
XLA Ops:
  3.3 3.1 %cut.2 = bf16[2,4096,128]{2,1,0:T(8,128)(2,1)} custom-call(s32[4]{0:T(128)} %pad_add_fusion.m, bf16[2,2,8192,128]{3,2,1,0:T(8,128)(2,1)} %bitcast.60, bf16[16,64,128]{2,1,0:T(8,128)(2,1)} %copy-done.13), custom_call_target="tpu_custom_call" | custom-call | bytes 2097 | tf_op jit(solution)/shard_map/cut/pallas_call | solution.py:132
  7.0 3.1 %cut.3.refs_1_ = bf16[2,4096,128]{2,1,0:T(8,128)(2,1)} custom-call(s32[4]{0:T(128)} %pad_add_fusion.m, bf16[2,2,8192,128]{3,2,1,0:T(8,128)(2,1)} %bitcast.61, bf16[16,64,128]{2,1,0:T(8,128)(2,1)} %copy-done.13), custom_call_target="tpu_custom_call" | custom-call | bytes 2097 | tf_op jit(solution)/shard_map/cut/pallas_call | solution.py:132
  10.4 2.8 %collective-permute-start = (f32[16,128]{1,0:T(8,128)S(1)}, f32[16,128]{1,0:T(8,128)S(1)}, u32[]{:S(2)}, u32[]{:S(2)}) collective-permute-start(f32[16,128]{1,0:T(8,128)S(1)} %copy-done.41), channel_id=1, source_target_pairs={{0,1},{1,0},{2,3},{3,2},{4,5},{5,4},{6,7},{7,6},{8,9},{9,8},{10,11... | collective-permute-start | bytes 24584 | tf_op jit(solution)/shard_map/ppermute | solution.py:479
  14.9 2.1 collective-permute-start.1
  19.9 4.1 %collective-permute-done.5.two_ref.refs_1_ = bf16[16,64,128]{2,1,0:T(8,128)(2,1)} collective-permute-done((bf16[16,64,128]{2,1,0:T(8,128)(2,1)S(1)}, bf16[16,64,128]{2,1,0:T(8,128)(2,1)}, u32[]{:S(2)}, u32[]{:S(2)}) %collective-permute-start.5) | collective-permute-done | bytes 262176 | tf_op jit(solution)/shard_map/ppermute | solution.py:476
  24.0 5.6 %forward.4 = (bf16[16,64,256]{2,1,0:T(8,128)(2,1)}, bf16[16,64,256]{2,1,0:T(8,128)(2,1)}, bf16[2,4096,128]{2,1,0:T(8,128)(2,1)}) custom-call(s32[4]{0:T(128)} %pad_add_fusion.m, bf16[2,2,8192,128]{3,2,1,0:T(8,128)(2,1)} %bitcast.62, bf16[2,4096,128]{2,1,0:T(8,128)(2,1)} %collective-permute-done.4.far, f32[32,64,128]{2,1,0:T(8,128)} %bitcast.37, ...), custom_call_target="tpu_custom_call" | custom-call | flops 536870 | bytes 4194 | tf_op jit(solution)/shard_map/forward/pallas_call | solution.py:209
  32.6 2.6 %collective-permute-start.2 = (f32[64,128]{1,0:T(8,128)S(1)}, f32[64,128]{1,0:T(8,128)S(1)}, u32[]{:S(2)}, u32[]{:S(2)}) collective-permute-start(f32[64,128]{1,0:T(8,128)S(1)} %copy-done.40), channel_id=1, source_target_pairs={{0,4},{1,5},{2,6},{3,7},{4,0},{5,1},{6,2},{7,3},{8,12},{9,13},{10,... | collective-permute-start | bytes 98312 | tf_op jit(solution)/shard_map/ppermute | solution.py:479
  35.2 2.3 %collective-permute-done.8.two_ref = bf16[16,64,128]{2,1,0:T(8,128)(2,1)S(1)} collective-permute-done((bf16[16,64,128]{2,1,0:T(8,128)(2,1)S(1)}, bf16[16,64,128]{2,1,0:T(8,128)(2,1)S(1)}, u32[]{:S(2)}, u32[]{:S(2)}) %collective-permute-start.8) | collective-permute-done | bytes 262176 | tf_op jit(solution)/shard_map/ppermute | solution.py:476
  38.2 5.5 %forward.5 = (bf16[16,64,256]{2,1,0:T(8,128)(2,1)}, bf16[16,64,256]{2,1,0:T(8,128)(2,1)}, bf16[2,4096,128]{2,1,0:T(8,128)(2,1)}) custom-call(s32[4]{0:T(128)} %pad_add_fusion.m, bf16[2,2,8192,128]{3,2,1,0:T(8,128)(2,1)} %bitcast.63, bf16[2,4096,128]{2,1,0:T(8,128)(2,1)} %copy-done.3, f32[32,64,128]{2,1,0:T(8,128)} %bitcast.38, bf16[16,64,128]{2,1,0:T(8,128)(2,1)} %copy-done.39), custom_call_target="tpu_custom_call" | custom-call | flops 536870 | bytes 4194 | tf_op jit(solution)/shard_map/forward/pallas_call | solution.py:209
  45.0 1.8 split.4
  46.9 2.6 %collective-permute-start.10 = (bf16[256,256]{1,0:T(8,128)(2,1)}, bf16[256,256]{1,0:T(8,128)(2,1)}, u32[]{:S(2)}, u32[]{:S(2)}) collective-permute-start(bf16[256,256]{1,0:T(8,128)(2,1)} %get-tuple-element.53), channel_id=1, source_target_pairs={{0,4},{1,5},{2,6},{3,7},{4,0},{5,1},{6,2},{7,3},{8,12},{9,13},{10,... | collective-permute-start | bytes 393224 | tf_op jit(solution)/shard_map/ppermute | solution.py:479
  51.0 8.5 %collective-permute-done.10.refs_4_ = bf16[256,256]{1,0:T(8,128)(2,1)} collective-permute-done((bf16[256,256]{1,0:T(8,128)(2,1)}, bf16[256,256]{1,0:T(8,128)(2,1)}, u32[]{:S(2)}, u32[]{:S(2)}) %collective-permute-start.10) | collective-permute-done | bytes 131104 | tf_op jit(solution)/shard_map/ppermute | solution.py:479
  62.8 1.9 collective-permute-start.19
  67.4 2.6 %collective-permute-done.19.refs_1_ = bf16[256,256]{1,0:T(8,128)(2,1)S(1)} collective-permute-done((bf16[256,256]{1,0:T(8,128)(2,1)S(1)}, bf16[256,256]{1,0:T(8,128)(2,1)S(1)}, u32[]{:S(2)}, u32[]{:S(2)}) %collective-permute-start.19) | collective-permute-done | bytes 131104 | tf_op jit(solution)/shard_map/ppermute | solution.py:479
  70.0 7.6 %collective-permute-done.20.refs_2_ = bf16[256,256]{1,0:T(8,128)(2,1)S(1)} collective-permute-done((bf16[256,256]{1,0:T(8,128)(2,1)S(1)}, bf16[256,256]{1,0:T(8,128)(2,1)S(1)}, u32[]{:S(2)}, u32[]{:S(2)}) %collective-permute-start.20) | collective-permute-done | bytes 131104 | tf_op jit(solution)/shard_map/ppermute | solution.py:479
  78.2 1.6 collective-permute-start.22
  81.0 2.3 %collective-permute-start.13 = (bf16[256,256]{1,0:T(8,128)(2,1)S(1)}, bf16[256,256]{1,0:T(8,128)(2,1)S(1)}, u32[]{:S(2)}, u32[]{:S(2)}) collective-permute-start(bf16[256,256]{1,0:T(8,128)(2,1)S(1)} %get-tuple-element.58), channel_id=1, source_target_pairs={{0,2},{1,3},{2,0},{3,1},{4,6},{5,7},{6,4},{7,5},{8,10},{9,11},{10,... | collective-permute-start | bytes 393224 | tf_op jit(solution)/shard_map/ppermute | solution.py:479
  84.2 1.6 collective-permute-start.15
  85.8 3.6 %collective-permute-done.22.got_ref = bf16[16,64,256]{2,1,0:T(8,128)(2,1)S(1)} collective-permute-done((bf16[16,64,256]{2,1,0:T(8,128)(2,1)S(1)}, bf16[16,64,256]{2,1,0:T(8,128)(2,1)S(1)}, u32[]{:S(2)}, u32[]{:S(2)}) %collective-permute-start.22) | collective-permute-done | bytes 524320 | tf_op jit(solution)/shard_map/ppermute | solution.py:479
  89.4 3.0 %adjoint.4.one_ref.mine_ref.refs_4_ = bf16[2,16,64,128]{3,2,1,0:T(8,128)(2,1)S(1)} custom-call(s32[4]{0:T(128)S(1)} %copy-done.33, bf16[2,4096,128]{2,1,0:T(8,128)(2,1)S(1)} %copy-done.8, bf16[2,4096,128]{2,1,0:T(8,128)(2,1)} %collective-permute-done.4.far, bf16[16,64,256]{2,1,0:T(8,128)(2,1)S(1)} %bitcast.48, ...), custom_call_target="tpu_custom_call" | custom-call | flops 536870 | bytes 4194 | tf_op jit(solution)/shard_map/adjoint/pallas_call | solution.py:251
  96.3 3.6 %collective-permute-start.31 = (bf16[256,256]{1,0:T(8,128)(2,1)S(1)}, bf16[256,256]{1,0:T(8,128)(2,1)S(1)}, u32[]{:S(2)}, u32[]{:S(2)}) collective-permute-start(bf16[256,256]{1,0:T(8,128)(2,1)S(1)} %get-tuple-element.75.refs_0_), channel_id=1, source_target_pairs={{0,2},{1,3},{2,0},{3,1},{4,6},{5,7},{6,4},{7,5},{8,10},{9,11},{10,... | collective-permute-start | bytes 393224 | tf_op jit(solution)/shard_map/ppermute | solution.py:479
  100.5 1.8 collective-permute-start.33
  103.9 3.3 %collective-permute-done.17 = f32[24,128]{1,0:T(8,128)S(1)} collective-permute-done((f32[24,128]{1,0:T(8,128)S(1)}, f32[24,128]{1,0:T(8,128)S(1)}, u32[]{:S(2)}, u32[]{:S(2)}) %collective-permute-start.17) | collective-permute-done | bytes 12320 | tf_op jit(solution)/shard_map/ppermute | solution.py:476
  108.7 2.2 collective-permute-done.18
  113.1 4.2 %forward.6 = (bf16[16,64,256]{2,1,0:T(8,128)(2,1)}, bf16[16,64,256]{2,1,0:T(8,128)(2,1)S(1)}) custom-call(s32[4]{0:T(128)S(1)} %copy-done.33, bf16[2,4096,128]{2,1,0:T(8,128)(2,1)S(1)} %copy-done.9, bf16[2,4096,128]{2,1,0:T(8,128)(2,1)} %collective-permute-done.4.far, bf16[2,16,64,128]{3,2,1,0:T(8,128)(2,1)S(1)} %adjoint.4.one_ref.mine_ref.refs_4_, ...), custom_call_target="tpu_custom_call" | custom-call | flops 536870 | bytes 4194 | tf_op jit(solution)/shard_map/forward/pallas_call | solution.py:209
  117.3 1.9 collective-permute-start.24
  119.2 1.9 collective-permute-done.24
  121.0 2.3 %collective-permute-start.25 = (f32[24,128]{1,0:T(8,128)S(1)}, f32[24,128]{1,0:T(8,128)S(1)}, u32[]{:S(2)}, u32[]{:S(2)}) collective-permute-start(f32[24,128]{1,0:T(8,128)S(1)} %add.106), channel_id=1, source_target_pairs={{0,4},{1,5},{2,6},{3,7},{4,0},{5,1},{6,2},{7,3},{8,12},{9,13},{10,... | collective-permute-start | bytes 36872 | tf_op jit(solution)/shard_map/ppermute | solution.py:479
  125.8 3.0 %adjoint.5.mine_ref.one_ref = bf16[2,16,64,128]{3,2,1,0:T(8,128)(2,1)} custom-call(s32[4]{0:T(128)S(1)} %copy-done.33, bf16[2,4096,128]{2,1,0:T(8,128)(2,1)S(1)} %copy-done.5, bf16[2,4096,128]{2,1,0:T(8,128)(2,1)S(1)} %copy-done.4, bf16[16,64,256]{2,1,0:T(8,128)(2,1)S(1)} %bitcast.46, bf16[16,64,256]{2,1,0:T(8,128)(2,1)S(1)} %collective-permute-done.34.got_ref, ...), custom_call_target="tpu_custom_call" | custom-call | flops 536870 | bytes 4194 | tf_op jit(solution)/shard_map/adjoint/pallas_call | solution.py:251
  138.7 2.5 %collective-permute-start.28 = (bf16[256,256]{1,0:T(8,128)(2,1)S(1)}, bf16[256,256]{1,0:T(8,128)(2,1)S(1)}, u32[]{:S(2)}, u32[]{:S(2)}) collective-permute-start(bf16[256,256]{1,0:T(8,128)(2,1)S(1)} %get-tuple-element.69), channel_id=1, source_target_pairs={{0,2},{1,3},{2,0},{3,1},{4,6},{5,7},{6,4},{7,5},{8,10},{9,11},{10,... | collective-permute-start | bytes 393224 | tf_op jit(solution)/shard_map/ppermute | solution.py:479
  141.6 2.1 collective-permute-start.30
  143.7 3.6 %forward.7 = (bf16[16,64,256]{2,1,0:T(8,128)(2,1)S(1)}, bf16[16,64,256]{2,1,0:T(8,128)(2,1)S(1)}) custom-call(s32[4]{0:T(128)S(1)} %copy-done.33, bf16[2,4096,128]{2,1,0:T(8,128)(2,1)S(1)} %copy-done.6, bf16[2,4096,128]{2,1,0:T(8,128)(2,1)S(1)} %copy-done.4, bf16[2,16,64,128]{3,2,1,0:T(8,128)(2,1)} %adjoint.5.mine_ref.one_ref, ...), custom_call_target="tpu_custom_call" | custom-call | flops 536870 | bytes 4194 | tf_op jit(solution)/shard_map/forward/pallas_call | solution.py:209
  148.9 2.0 collective-permute-done.29.refs_7_
  151.6 2.0 collective-permute-start.45
  154.1 2.0 collective-permute-start.47
  157.3 7.2 %collective-permute-done.46.refs_2_ = bf16[256,256]{1,0:T(8,128)(2,1)S(1)} collective-permute-done((bf16[256,256]{1,0:T(8,128)(2,1)S(1)}, bf16[256,256]{1,0:T(8,128)(2,1)S(1)}, u32[]{:S(2)}, u32[]{:S(2)}) %collective-permute-start.46) | collective-permute-done | bytes 131104 | tf_op jit(solution)/shard_map/ppermute | solution.py:479
  168.1 2.7 %collective-permute-start.37 = (bf16[256,256]{1,0:T(8,128)(2,1)S(1)}, bf16[256,256]{1,0:T(8,128)(2,1)S(1)}, u32[]{:S(2)}, u32[]{:S(2)}) collective-permute-start(bf16[256,256]{1,0:T(8,128)(2,1)S(1)} %get-tuple-element.80), channel_id=1, source_target_pairs={{0,2},{1,3},{2,0},{3,1},{4,6},{5,7},{6,4},{7,5},{8,10},{9,11},{10,... | collective-permute-start | bytes 393224 | tf_op jit(solution)/shard_map/ppermute | solution.py:479
  170.7 2.4 %collective-permute-start.39 = (bf16[256,256]{1,0:T(8,128)(2,1)S(1)}, bf16[256,256]{1,0:T(8,128)(2,1)S(1)}, u32[]{:S(2)}, u32[]{:S(2)}) collective-permute-start(bf16[256,256]{1,0:T(8,128)(2,1)S(1)} %get-tuple-element.82), channel_id=1, source_target_pairs={{0,6},{1,7},{2,4},{3,5},{4,2},{5,3},{6,0},{7,1},{8,14},{9,15},{10,... | collective-permute-start | bytes 393224 | tf_op jit(solution)/shard_map/ppermute | solution.py:479
  174.7 7.5 %collective-permute-done.38.refs_7_ = bf16[256,256]{1,0:T(8,128)(2,1)S(1)} collective-permute-done((bf16[256,256]{1,0:T(8,128)(2,1)S(1)}, bf16[256,256]{1,0:T(8,128)(2,1)S(1)}, u32[]{:S(2)}, u32[]{:S(2)}) %collective-permute-start.38) | collective-permute-done | bytes 131104 | tf_op jit(solution)/shard_map/ppermute | solution.py:479
  182.8 2.5 %collective-permute-start.50 = (bf16[256,256]{1,0:T(8,128)(2,1)S(1)}, bf16[256,256]{1,0:T(8,128)(2,1)S(1)}, u32[]{:S(2)}, u32[]{:S(2)}) collective-permute-start(bf16[256,256]{1,0:T(8,128)(2,1)S(1)} %get-tuple-element.89.refs_0_), channel_id=1, source_target_pairs={{0,2},{1,3},{2,0},{3,1},{4,6},{5,7},{6,4},{7,5},{8,10},{9,11},{10,... | collective-permute-start | bytes 393224 | tf_op jit(solution)/shard_map/ppermute | solution.py:479
  185.4 2.4 %collective-permute-start.52 = (bf16[256,256]{1,0:T(8,128)(2,1)S(1)}, bf16[256,256]{1,0:T(8,128)(2,1)S(1)}, u32[]{:S(2)}, u32[]{:S(2)}) collective-permute-start(bf16[256,256]{1,0:T(8,128)(2,1)S(1)} %get-tuple-element.89.refs_0_), channel_id=1, source_target_pairs={{0,6},{1,7},{2,4},{3,5},{4,2},{5,3},{6,0},{7,1},{8,14},{9,15},{10,... | collective-permute-start | bytes 393224 | tf_op jit(solution)/shard_map/ppermute | solution.py:479
  188.4 3.1 %collective-permute-done.40 = f32[24,128]{1,0:T(8,128)S(1)} collective-permute-done((f32[24,128]{1,0:T(8,128)S(1)}, f32[24,128]{1,0:T(8,128)S(1)}, u32[]{:S(2)}, u32[]{:S(2)}) %collective-permute-start.40) | collective-permute-done | bytes 12320 | tf_op jit(solution)/shard_map/ppermute | solution.py:479
  191.5 3.7 %collective-permute-done.41 = f32[24,128]{1,0:T(8,128)S(1)} collective-permute-done((f32[24,128]{1,0:T(8,128)S(1)}, f32[24,128]{1,0:T(8,128)S(1)}, u32[]{:S(2)}, u32[]{:S(2)}) %collective-permute-start.41) | collective-permute-done | bytes 12320 | tf_op jit(solution)/shard_map/ppermute | solution.py:476
  195.2 3.4 %adjoint.6 = (bf16[16,64,128]{2,1,0:T(8,128)(2,1)}, f32[16,64,128]{2,1,0:T(8,128)S(1)}) custom-call(s32[4]{0:T(128)S(1)} %copy-done.33, bf16[2,4096,128]{2,1,0:T(8,128)(2,1)S(1)} %copy-done.10, bf16[2,4096,128]{2,1,0:T(8,128)(2,1)} %collective-permute-done.4.far, bf16[16,64,256]{2,1,0:T(8,128)(2,1)S(1)} %bitcast.50, ...), custom_call_target="tpu_custom_call" | custom-call | flops 536870 | bytes 4194 | tf_op jit(solution)/shard_map/adjoint/pallas_call | solution.py:251
  202.9 2.6 %collective-permute-done.43 = f32[24,128]{1,0:T(8,128)S(1)} collective-permute-done((f32[24,128]{1,0:T(8,128)S(1)}, f32[24,128]{1,0:T(8,128)S(1)}, u32[]{:S(2)}, u32[]{:S(2)}) %collective-permute-start.43) | collective-permute-done | bytes 12320 | tf_op jit(solution)/shard_map/ppermute | solution.py:479
  206.9 3.3 %collective-permute-done.44 = f32[24,128]{1,0:T(8,128)S(1)} collective-permute-done((f32[24,128]{1,0:T(8,128)S(1)}, f32[24,128]{1,0:T(8,128)S(1)}, u32[]{:S(2)}, u32[]{:S(2)}) %collective-permute-start.44) | collective-permute-done | bytes 12320 | tf_op jit(solution)/shard_map/ppermute | solution.py:479
  212.4 3.2 %adjoint.7 = (bf16[16,64,128]{2,1,0:T(8,128)(2,1)}, f32[16,64,128]{2,1,0:T(8,128)S(1)}) custom-call(s32[4]{0:T(128)S(1)} %copy-done.33, bf16[2,4096,128]{2,1,0:T(8,128)(2,1)S(1)} %copy-done.7, bf16[2,4096,128]{2,1,0:T(8,128)(2,1)S(1)} %copy-done.4, bf16[16,64,256]{2,1,0:T(8,128)(2,1)} %bitcast.30.own_ref, ...), custom_call_target="tpu_custom_call" | custom-call | flops 536870 | bytes 4194 | tf_op jit(solution)/shard_map/adjoint/pallas_call | solution.py:251
  224.9 1.9 fusion.2
  (209 shorter events, 67.5 us)
Async XLA Ops:
  6.5 17.5 %collective-permute-start.4 = (bf16[2,4096,128]{2,1,0:T(8,128)(2,1)}, bf16[2,4096,128]{2,1,0:T(8,128)(2,1)}, u32[]{:S(2)}, u32[]{:S(2)}) collective-permute-start(bf16[2,4096,128]{2,1,0:T(8,128)(2,1)} %cut.2), channel_id=1, source_target_pairs={{0,8},{8,0},{16,24},{24,16},{1,9},{9,1},{17,25},{25,17},{2,10},{10... | collective-permute-start | bytes 6291464 | tf_op jit(solution)/shard_map/ppermute | solution.py:473
  10.1 25.1 %collective-permute-start.7 = (bf16[2,4096,128]{2,1,0:T(8,128)(2,1)}, bf16[2,4096,128]{2,1,0:T(8,128)(2,1)S(1)}, u32[]{:S(2)}, u32[]{:S(2)}) collective-permute-start(bf16[2,4096,128]{2,1,0:T(8,128)(2,1)} %cut.3.refs_1_), channel_id=1, source_target_pairs={{0,8},{8,0},{16,24},{24,16},{1,9},{9,1},{17,25},{25,17},{2,10},{10... | collective-permute-start | bytes 6291464 | tf_op jit(solution)/shard_map/ppermute | solution.py:473
  10.4 4.5 %collective-permute-start = (f32[16,128]{1,0:T(8,128)S(1)}, f32[16,128]{1,0:T(8,128)S(1)}, u32[]{:S(2)}, u32[]{:S(2)}) collective-permute-start(f32[16,128]{1,0:T(8,128)S(1)} %copy-done.41), channel_id=1, source_target_pairs={{0,1},{1,0},{2,3},{3,2},{4,5},{5,4},{6,7},{7,6},{8,9},{9,8},{10,11... | collective-permute-start | bytes 24584 | tf_op jit(solution)/shard_map/ppermute | solution.py:479
  14.9 4.4 %collective-permute-start.1 = (f32[32,128]{1,0:T(8,128)S(1)}, f32[32,128]{1,0:T(8,128)S(1)}, u32[]{:S(2)}, u32[]{:S(2)}) collective-permute-start(f32[32,128]{1,0:T(8,128)S(1)} %pad_maximum_fusion.3), channel_id=1, source_target_pairs={{0,2},{1,3},{2,0},{3,1},{4,6},{5,7},{6,4},{7,5},{8,10},{9,11},{10,... | collective-permute-start | bytes 49160 | tf_op jit(solution)/shard_map/ppermute | solution.py:479
  16.9 7.0 %collective-permute-start.5 = (bf16[16,64,128]{2,1,0:T(8,128)(2,1)S(1)}, bf16[16,64,128]{2,1,0:T(8,128)(2,1)}, u32[]{:S(2)}, u32[]{:S(2)}) collective-permute-start(bf16[16,64,128]{2,1,0:T(8,128)(2,1)S(1)} %copy-done.14), channel_id=1, source_target_pairs={{0,16},{8,24},{16,0},{24,8},{1,17},{9,25},{17,1},{25,9},{2,18},{10... | collective-permute-start | bytes 786440 | tf_op jit(solution)/shard_map/ppermute | solution.py:476
  29.5 14.3 %collective-permute-start.6 = (bf16[16,64,256]{2,1,0:T(8,128)(2,1)}, bf16[16,64,256]{2,1,0:T(8,128)(2,1)}, u32[]{:S(2)}, u32[]{:S(2)}) collective-permute-start(bf16[16,64,256]{2,1,0:T(8,128)(2,1)} %get-tuple-element.49), channel_id=1, source_target_pairs={{0,1},{1,0},{2,3},{3,2},{4,5},{5,4},{6,7},{7,6},{8,9},{9,8},{10,11... | collective-permute-start | bytes 1572872 | tf_op jit(solution)/shard_map/ppermute | solution.py:479
  31.2 6.4 %collective-permute-start.8 = (bf16[16,64,128]{2,1,0:T(8,128)(2,1)S(1)}, bf16[16,64,128]{2,1,0:T(8,128)(2,1)S(1)}, u32[]{:S(2)}, u32[]{:S(2)}) collective-permute-start(bf16[16,64,128]{2,1,0:T(8,128)(2,1)S(1)} %ordered.4), channel_id=1, source_target_pairs={{0,16},{8,24},{16,0},{24,8},{1,17},{9,25},{17,1},{25,9},{2,18},{10... | collective-permute-start | bytes 786440 | tf_op jit(solution)/shard_map/ppermute | solution.py:476
  32.6 11.8 %collective-permute-start.2 = (f32[64,128]{1,0:T(8,128)S(1)}, f32[64,128]{1,0:T(8,128)S(1)}, u32[]{:S(2)}, u32[]{:S(2)}) collective-permute-start(f32[64,128]{1,0:T(8,128)S(1)} %copy-done.40), channel_id=1, source_target_pairs={{0,4},{1,5},{2,6},{3,7},{4,0},{5,1},{6,2},{7,3},{8,12},{9,13},{10,... | collective-permute-start | bytes 98312 | tf_op jit(solution)/shard_map/ppermute | solution.py:479
  43.8 17.1 %collective-permute-start.12 = (bf16[16,64,256]{2,1,0:T(8,128)(2,1)}, bf16[16,64,256]{2,1,0:T(8,128)(2,1)}, u32[]{:S(2)}, u32[]{:S(2)}) collective-permute-start(bf16[16,64,256]{2,1,0:T(8,128)(2,1)} %ordered.5.refs_0_), channel_id=1, source_target_pairs={{0,1},{1,0},{2,3},{3,2},{4,5},{5,4},{6,7},{7,6},{8,9},{9,8},{10,11... | collective-permute-start | bytes 1572872 | tf_op jit(solution)/shard_map/ppermute | solution.py:479
  45.0 6.0 %collective-permute-start.3 = (f32[2,32,128]{2,1,0:T(8,128)}, f32[2,32,128]{2,1,0:T(8,128)S(1)}, u32[]{:S(2)}, u32[]{:S(2)}) collective-permute-start(f32[2,32,128]{2,1,0:T(8,128)} %get-tuple-element.100), channel_id=1, source_target_pairs={{0,8},{8,0},{16,24},{24,16},{1,9},{9,1},{17,25},{25,17},{2,10},{10... | collective-permute-start | bytes 98312 | tf_op jit(solution)/shard_map/ppermute | solution.py:473
  46.9 12.7 %collective-permute-start.10 = (bf16[256,256]{1,0:T(8,128)(2,1)}, bf16[256,256]{1,0:T(8,128)(2,1)}, u32[]{:S(2)}, u32[]{:S(2)}) collective-permute-start(bf16[256,256]{1,0:T(8,128)(2,1)} %get-tuple-element.53), channel_id=1, source_target_pairs={{0,4},{1,5},{2,6},{3,7},{4,0},{5,1},{6,2},{7,3},{8,12},{9,13},{10,... | collective-permute-start | bytes 393224 | tf_op jit(solution)/shard_map/ppermute | solution.py:479
  49.5 10.1 %collective-permute-start.11 = (bf16[256,256]{1,0:T(8,128)(2,1)}, bf16[256,256]{1,0:T(8,128)(2,1)}, u32[]{:S(2)}, u32[]{:S(2)}) collective-permute-start(bf16[256,256]{1,0:T(8,128)(2,1)} %get-tuple-element.54), channel_id=1, source_target_pairs={{0,6},{1,7},{2,4},{3,5},{4,2},{5,3},{6,0},{7,1},{8,14},{9,15},{10,... | collective-permute-start | bytes 393224 | tf_op jit(solution)/shard_map/ppermute | solution.py:479
  49.6 11.3 %collective-permute-start.9 = (bf16[256,256]{1,0:T(8,128)(2,1)}, bf16[256,256]{1,0:T(8,128)(2,1)}, u32[]{:S(2)}, u32[]{:S(2)}) collective-permute-start(bf16[256,256]{1,0:T(8,128)(2,1)} %get-tuple-element.52), channel_id=1, source_target_pairs={{0,2},{1,3},{2,0},{3,1},{4,6},{5,7},{6,4},{7,5},{8,10},{9,11},{10,... | collective-permute-start | bytes 393224 | tf_op jit(solution)/shard_map/ppermute | solution.py:479
  62.8 7.2 %collective-permute-start.19 = (bf16[256,256]{1,0:T(8,128)(2,1)S(1)}, bf16[256,256]{1,0:T(8,128)(2,1)S(1)}, u32[]{:S(2)}, u32[]{:S(2)}) collective-permute-start(bf16[256,256]{1,0:T(8,128)(2,1)S(1)} %get-tuple-element.63.refs_0_), channel_id=1, source_target_pairs={{0,2},{1,3},{2,0},{3,1},{4,6},{5,7},{6,4},{7,5},{8,10},{9,11},{10,... | collective-permute-start | bytes 393224 | tf_op jit(solution)/shard_map/ppermute | solution.py:479
  64.7 12.9 %collective-permute-start.20 = (bf16[256,256]{1,0:T(8,128)(2,1)S(1)}, bf16[256,256]{1,0:T(8,128)(2,1)S(1)}, u32[]{:S(2)}, u32[]{:S(2)}) collective-permute-start(bf16[256,256]{1,0:T(8,128)(2,1)S(1)} %get-tuple-element.63.refs_0_), channel_id=1, source_target_pairs={{0,4},{1,5},{2,6},{3,7},{4,0},{5,1},{6,2},{7,3},{8,12},{9,13},{10,... | collective-permute-start | bytes 393224 | tf_op jit(solution)/shard_map/ppermute | solution.py:479
  65.9 11.7 %collective-permute-start.21 = (bf16[256,256]{1,0:T(8,128)(2,1)S(1)}, bf16[256,256]{1,0:T(8,128)(2,1)S(1)}, u32[]{:S(2)}, u32[]{:S(2)}) collective-permute-start(bf16[256,256]{1,0:T(8,128)(2,1)S(1)} %get-tuple-element.63.refs_0_), channel_id=1, source_target_pairs={{0,6},{1,7},{2,4},{3,5},{4,2},{5,3},{6,0},{7,1},{8,14},{9,15},{10,... | collective-permute-start | bytes 393224 | tf_op jit(solution)/shard_map/ppermute | solution.py:479
  78.2 11.2 %collective-permute-start.22 = (bf16[16,64,256]{2,1,0:T(8,128)(2,1)S(1)}, bf16[16,64,256]{2,1,0:T(8,128)(2,1)S(1)}, u32[]{:S(2)}, u32[]{:S(2)}) collective-permute-start(bf16[16,64,256]{2,1,0:T(8,128)(2,1)S(1)} %bitcast.47), channel_id=1, source_target_pairs={{0,1},{1,0},{2,3},{3,2},{4,5},{5,4},{6,7},{7,6},{8,9},{9,8},{10,11... | collective-permute-start | bytes 1572872 | tf_op jit(solution)/shard_map/ppermute | solution.py:479
  81.0 13.6 %collective-permute-start.13 = (bf16[256,256]{1,0:T(8,128)(2,1)S(1)}, bf16[256,256]{1,0:T(8,128)(2,1)S(1)}, u32[]{:S(2)}, u32[]{:S(2)}) collective-permute-start(bf16[256,256]{1,0:T(8,128)(2,1)S(1)} %get-tuple-element.58), channel_id=1, source_target_pairs={{0,2},{1,3},{2,0},{3,1},{4,6},{5,7},{6,4},{7,5},{8,10},{9,11},{10,... | collective-permute-start | bytes 393224 | tf_op jit(solution)/shard_map/ppermute | solution.py:479
  83.4 11.6 %collective-permute-start.14 = (bf16[256,256]{1,0:T(8,128)(2,1)S(1)}, bf16[256,256]{1,0:T(8,128)(2,1)S(1)}, u32[]{:S(2)}, u32[]{:S(2)}) collective-permute-start(bf16[256,256]{1,0:T(8,128)(2,1)S(1)} %get-tuple-element.59), channel_id=1, source_target_pairs={{0,4},{1,5},{2,6},{3,7},{4,0},{5,1},{6,2},{7,3},{8,12},{9,13},{10,... | collective-permute-start | bytes 393224 | tf_op jit(solution)/shard_map/ppermute | solution.py:479
  84.2 10.8 %collective-permute-start.15 = (bf16[256,256]{1,0:T(8,128)(2,1)S(1)}, bf16[256,256]{1,0:T(8,128)(2,1)S(1)}, u32[]{:S(2)}, u32[]{:S(2)}) collective-permute-start(bf16[256,256]{1,0:T(8,128)(2,1)S(1)} %get-tuple-element.60), channel_id=1, source_target_pairs={{0,6},{1,7},{2,4},{3,5},{4,2},{5,3},{6,0},{7,1},{8,14},{9,15},{10,... | collective-permute-start | bytes 393224 | tf_op jit(solution)/shard_map/ppermute | solution.py:479
  92.4 20.6 %collective-permute-start.23 = (bf16[2,16,64,128]{3,2,1,0:T(8,128)(2,1)S(1)}, bf16[2,16,64,128]{3,2,1,0:T(8,128)(2,1)S(1)}, u32[]{:S(2)}, u32[]{:S(2)}) collective-permute-start(bf16[2,16,64,128]{3,2,1,0:T(8,128)(2,1)S(1)} %adjoint.4.one_ref.mine_ref.refs_4_), channel_id=1, source_target_pairs={{0,16},{8,24},{16,0},{24,8},{1,17},{9,25},{17,1},{25,9},{2,18},{10... | collective-permute-start | bytes 1572872 | tf_op jit(solution)/shard_map/ppermute | solution.py:476
  96.3 14.6 %collective-permute-start.31 = (bf16[256,256]{1,0:T(8,128)(2,1)S(1)}, bf16[256,256]{1,0:T(8,128)(2,1)S(1)}, u32[]{:S(2)}, u32[]{:S(2)}) collective-permute-start(bf16[256,256]{1,0:T(8,128)(2,1)S(1)} %get-tuple-element.75.refs_0_), channel_id=1, source_target_pairs={{0,2},{1,3},{2,0},{3,1},{4,6},{5,7},{6,4},{7,5},{8,10},{9,11},{10,... | collective-permute-start | bytes 393224 | tf_op jit(solution)/shard_map/ppermute | solution.py:479
  99.9 11.0 %collective-permute-start.32 = (bf16[256,256]{1,0:T(8,128)(2,1)S(1)}, bf16[256,256]{1,0:T(8,128)(2,1)S(1)}, u32[]{:S(2)}, u32[]{:S(2)}) collective-permute-start(bf16[256,256]{1,0:T(8,128)(2,1)S(1)} %get-tuple-element.75.refs_0_), channel_id=1, source_target_pairs={{0,4},{1,5},{2,6},{3,7},{4,0},{5,1},{6,2},{7,3},{8,12},{9,13},{10,... | collective-permute-start | bytes 393224 | tf_op jit(solution)/shard_map/ppermute | solution.py:479
  100.5 10.4 %collective-permute-start.33 = (bf16[256,256]{1,0:T(8,128)(2,1)S(1)}, bf16[256,256]{1,0:T(8,128)(2,1)S(1)}, u32[]{:S(2)}, u32[]{:S(2)}) collective-permute-start(bf16[256,256]{1,0:T(8,128)(2,1)S(1)} %get-tuple-element.75.refs_0_), channel_id=1, source_target_pairs={{0,6},{1,7},{2,4},{3,5},{4,2},{5,3},{6,0},{7,1},{8,14},{9,15},{10,... | collective-permute-start | bytes 393224 | tf_op jit(solution)/shard_map/ppermute | solution.py:479
  111.5 14.2 %collective-permute-start.34 = (bf16[16,64,256]{2,1,0:T(8,128)(2,1)S(1)}, bf16[16,64,256]{2,1,0:T(8,128)(2,1)S(1)}, u32[]{:S(2)}, u32[]{:S(2)}) collective-permute-start(bf16[16,64,256]{2,1,0:T(8,128)(2,1)S(1)} %bitcast.45), channel_id=1, source_target_pairs={{0,1},{1,0},{2,3},{3,2},{4,5},{5,4},{6,7},{7,6},{8,9},{9,8},{10,11... | collective-permute-start | bytes 1572872 | tf_op jit(solution)/shard_map/ppermute | solution.py:479
  117.3 3.8 %collective-permute-start.24 = (f32[24,128]{1,0:T(8,128)S(1)}, f32[24,128]{1,0:T(8,128)S(1)}, u32[]{:S(2)}, u32[]{:S(2)}) collective-permute-start(f32[24,128]{1,0:T(8,128)S(1)} %ordered.6), channel_id=1, source_target_pairs={{0,2},{1,3},{2,0},{3,1},{4,6},{5,7},{6,4},{7,5},{8,10},{9,11},{10,... | collective-permute-start | bytes 36872 | tf_op jit(solution)/shard_map/ppermute | solution.py:479
  121.0 4.6 %collective-permute-start.25 = (f32[24,128]{1,0:T(8,128)S(1)}, f32[24,128]{1,0:T(8,128)S(1)}, u32[]{:S(2)}, u32[]{:S(2)}) collective-permute-start(f32[24,128]{1,0:T(8,128)S(1)} %add.106), channel_id=1, source_target_pairs={{0,4},{1,5},{2,6},{3,7},{4,0},{5,1},{6,2},{7,3},{8,12},{9,13},{10,... | collective-permute-start | bytes 36872 | tf_op jit(solution)/shard_map/ppermute | solution.py:479
  123.3 12.8 %collective-permute-start.27 = (bf16[16,64,256]{2,1,0:T(8,128)(2,1)}, bf16[16,64,256]{2,1,0:T(8,128)(2,1)}, u32[]{:S(2)}, u32[]{:S(2)}) collective-permute-start(bf16[16,64,256]{2,1,0:T(8,128)(2,1)} %get-tuple-element.64.refs_1_.refs_0_), channel_id=1, source_target_pairs={{0,1},{1,0},{2,3},{3,2},{4,5},{5,4},{6,7},{7,6},{8,9},{9,8},{10,11... | collective-permute-start | bytes 1572872 | tf_op jit(solution)/shard_map/ppermute | solution.py:479
  128.7 14.9 %collective-permute-start.35 = (bf16[2,16,64,128]{3,2,1,0:T(8,128)(2,1)}, bf16[2,16,64,128]{3,2,1,0:T(8,128)(2,1)}, u32[]{:S(2)}, u32[]{:S(2)}) collective-permute-start(bf16[2,16,64,128]{3,2,1,0:T(8,128)(2,1)} %adjoint.5.mine_ref.one_ref), channel_id=1, source_target_pairs={{0,16},{8,24},{16,0},{24,8},{1,17},{9,25},{17,1},{25,9},{2,18},{10... | collective-permute-start | bytes 1572872 | tf_op jit(solution)/shard_map/ppermute | solution.py:476
  129.7 19.2 %collective-permute-start.26 = (f32[32]{0:T(128)S(1)}, f32[32]{0:T(128)S(1)}, u32[]{:S(2)}, u32[]{:S(2)}) collective-permute-start(f32[32]{0:T(128)S(1)} %copy-done.38), channel_id=1, source_target_pairs={{0,16},{8,24},{16,0},{24,8},{1,17},{9,25},{17,1},{25,9},{2,18},{10... | collective-permute-start | bytes 392 | tf_op jit(solution)/shard_map/ppermute | solution.py:476
  138.7 10.2 %collective-permute-start.28 = (bf16[256,256]{1,0:T(8,128)(2,1)S(1)}, bf16[256,256]{1,0:T(8,128)(2,1)S(1)}, u32[]{:S(2)}, u32[]{:S(2)}) collective-permute-start(bf16[256,256]{1,0:T(8,128)(2,1)S(1)} %get-tuple-element.69), channel_id=1, source_target_pairs={{0,2},{1,3},{2,0},{3,1},{4,6},{5,7},{6,4},{7,5},{8,10},{9,11},{10,... | collective-permute-start | bytes 393224 | tf_op jit(solution)/shard_map/ppermute | solution.py:479
  141.2 9.6 %collective-permute-start.29 = (bf16[256,256]{1,0:T(8,128)(2,1)S(1)}, bf16[256,256]{1,0:T(8,128)(2,1)S(1)}, u32[]{:S(2)}, u32[]{:S(2)}) collective-permute-start(bf16[256,256]{1,0:T(8,128)(2,1)S(1)} %get-tuple-element.70), channel_id=1, source_target_pairs={{0,4},{1,5},{2,6},{3,7},{4,0},{5,1},{6,2},{7,3},{8,12},{9,13},{10,... | collective-permute-start | bytes 393224 | tf_op jit(solution)/shard_map/ppermute | solution.py:479
  141.6 9.3 %collective-permute-start.30 = (bf16[256,256]{1,0:T(8,128)(2,1)S(1)}, bf16[256,256]{1,0:T(8,128)(2,1)S(1)}, u32[]{:S(2)}, u32[]{:S(2)}) collective-permute-start(bf16[256,256]{1,0:T(8,128)(2,1)S(1)} %get-tuple-element.71), channel_id=1, source_target_pairs={{0,6},{1,7},{2,4},{3,5},{4,2},{5,3},{6,0},{7,1},{8,14},{9,15},{10,... | collective-permute-start | bytes 393224 | tf_op jit(solution)/shard_map/ppermute | solution.py:479
  147.3 20.1 %collective-permute-start.36 = (bf16[16,64,256]{2,1,0:T(8,128)(2,1)S(1)}, bf16[16,64,256]{2,1,0:T(8,128)(2,1)S(1)}, u32[]{:S(2)}, u32[]{:S(2)}) collective-permute-start(bf16[16,64,256]{2,1,0:T(8,128)(2,1)S(1)} %ordered.7), channel_id=1, source_target_pairs={{0,1},{1,0},{2,3},{3,2},{4,5},{5,4},{6,7},{7,6},{8,9},{9,8},{10,11... | collective-permute-start | bytes 1572872 | tf_op jit(solution)/shard_map/ppermute | solution.py:479
  151.6 5.7 %collective-permute-start.45 = (bf16[256,256]{1,0:T(8,128)(2,1)S(1)}, bf16[256,256]{1,0:T(8,128)(2,1)S(1)}, u32[]{:S(2)}, u32[]{:S(2)}) collective-permute-start(bf16[256,256]{1,0:T(8,128)(2,1)S(1)} %get-tuple-element.86.refs_0_), channel_id=1, source_target_pairs={{0,2},{1,3},{2,0},{3,1},{4,6},{5,7},{6,4},{7,5},{8,10},{9,11},{10,... | collective-permute-start | bytes 393224 | tf_op jit(solution)/shard_map/ppermute | solution.py:479
  153.6 10.9 %collective-permute-start.46 = (bf16[256,256]{1,0:T(8,128)(2,1)S(1)}, bf16[256,256]{1,0:T(8,128)(2,1)S(1)}, u32[]{:S(2)}, u32[]{:S(2)}) collective-permute-start(bf16[256,256]{1,0:T(8,128)(2,1)S(1)} %get-tuple-element.86.refs_0_), channel_id=1, source_target_pairs={{0,4},{1,5},{2,6},{3,7},{4,0},{5,1},{6,2},{7,3},{8,12},{9,13},{10,... | collective-permute-start | bytes 393224 | tf_op jit(solution)/shard_map/ppermute | solution.py:479
  154.1 10.4 %collective-permute-start.47 = (bf16[256,256]{1,0:T(8,128)(2,1)S(1)}, bf16[256,256]{1,0:T(8,128)(2,1)S(1)}, u32[]{:S(2)}, u32[]{:S(2)}) collective-permute-start(bf16[256,256]{1,0:T(8,128)(2,1)S(1)} %get-tuple-element.86.refs_0_), channel_id=1, source_target_pairs={{0,6},{1,7},{2,4},{3,5},{4,2},{5,3},{6,0},{7,1},{8,14},{9,15},{10,... | collective-permute-start | bytes 393224 | tf_op jit(solution)/shard_map/ppermute | solution.py:479
  165.1 30.1 %collective-permute-start.48 = (bf16[16,64,256]{2,1,0:T(8,128)(2,1)S(1)}, bf16[16,64,256]{2,1,0:T(8,128)(2,1)S(1)}, u32[]{:S(2)}, u32[]{:S(2)}) collective-permute-start(bf16[16,64,256]{2,1,0:T(8,128)(2,1)S(1)} %bitcast.49), channel_id=1, source_target_pairs={{0,1},{1,0},{2,3},{3,2},{4,5},{5,4},{6,7},{7,6},{8,9},{9,8},{10,11... | collective-permute-start | bytes 1572872 | tf_op jit(solution)/shard_map/ppermute | solution.py:479
  168.1 6.6 %collective-permute-start.37 = (bf16[256,256]{1,0:T(8,128)(2,1)S(1)}, bf16[256,256]{1,0:T(8,128)(2,1)S(1)}, u32[]{:S(2)}, u32[]{:S(2)}) collective-permute-start(bf16[256,256]{1,0:T(8,128)(2,1)S(1)} %get-tuple-element.80), channel_id=1, source_target_pairs={{0,2},{1,3},{2,0},{3,1},{4,6},{5,7},{6,4},{7,5},{8,10},{9,11},{10,... | collective-permute-start | bytes 393224 | tf_op jit(solution)/shard_map/ppermute | solution.py:479
  170.7 11.4 %collective-permute-start.38 = (bf16[256,256]{1,0:T(8,128)(2,1)S(1)}, bf16[256,256]{1,0:T(8,128)(2,1)S(1)}, u32[]{:S(2)}, u32[]{:S(2)}) collective-permute-start(bf16[256,256]{1,0:T(8,128)(2,1)S(1)} %get-tuple-element.81), channel_id=1, source_target_pairs={{0,4},{1,5},{2,6},{3,7},{4,0},{5,1},{6,2},{7,3},{8,12},{9,13},{10,... | collective-permute-start | bytes 393224 | tf_op jit(solution)/shard_map/ppermute | solution.py:479
  170.7 11.4 %collective-permute-start.39 = (bf16[256,256]{1,0:T(8,128)(2,1)S(1)}, bf16[256,256]{1,0:T(8,128)(2,1)S(1)}, u32[]{:S(2)}, u32[]{:S(2)}) collective-permute-start(bf16[256,256]{1,0:T(8,128)(2,1)S(1)} %get-tuple-element.82), channel_id=1, source_target_pairs={{0,6},{1,7},{2,4},{3,5},{4,2},{5,3},{6,0},{7,1},{8,14},{9,15},{10,... | collective-permute-start | bytes 393224 | tf_op jit(solution)/shard_map/ppermute | solution.py:479
  182.8 15.8 %collective-permute-start.50 = (bf16[256,256]{1,0:T(8,128)(2,1)S(1)}, bf16[256,256]{1,0:T(8,128)(2,1)S(1)}, u32[]{:S(2)}, u32[]{:S(2)}) collective-permute-start(bf16[256,256]{1,0:T(8,128)(2,1)S(1)} %get-tuple-element.89.refs_0_), channel_id=1, source_target_pairs={{0,2},{1,3},{2,0},{3,1},{4,6},{5,7},{6,4},{7,5},{8,10},{9,11},{10,... | collective-permute-start | bytes 393224 | tf_op jit(solution)/shard_map/ppermute | solution.py:479
  185.4 13.3 %collective-permute-start.51 = (bf16[256,256]{1,0:T(8,128)(2,1)S(1)}, bf16[256,256]{1,0:T(8,128)(2,1)S(1)}, u32[]{:S(2)}, u32[]{:S(2)}) collective-permute-start(bf16[256,256]{1,0:T(8,128)(2,1)S(1)} %get-tuple-element.89.refs_0_), channel_id=1, source_target_pairs={{0,4},{1,5},{2,6},{3,7},{4,0},{5,1},{6,2},{7,3},{8,12},{9,13},{10,... | collective-permute-start | bytes 393224 | tf_op jit(solution)/shard_map/ppermute | solution.py:479
  185.4 13.3 %collective-permute-start.52 = (bf16[256,256]{1,0:T(8,128)(2,1)S(1)}, bf16[256,256]{1,0:T(8,128)(2,1)S(1)}, u32[]{:S(2)}, u32[]{:S(2)}) collective-permute-start(bf16[256,256]{1,0:T(8,128)(2,1)S(1)} %get-tuple-element.89.refs_0_), channel_id=1, source_target_pairs={{0,6},{1,7},{2,4},{3,5},{4,2},{5,3},{6,0},{7,1},{8,14},{9,15},{10,... | collective-permute-start | bytes 393224 | tf_op jit(solution)/shard_map/ppermute | solution.py:479
  200.1 10.8 %collective-permute-start.53 = (bf16[16,64,256]{2,1,0:T(8,128)(2,1)}, bf16[16,64,256]{2,1,0:T(8,128)(2,1)}, u32[]{:S(2)}, u32[]{:S(2)}) collective-permute-start(bf16[16,64,256]{2,1,0:T(8,128)(2,1)} %bitcast.30.own_ref), channel_id=1, source_target_pairs={{0,1},{1,0},{2,3},{3,2},{4,5},{5,4},{6,7},{7,6},{8,9},{9,8},{10,11... | collective-permute-start | bytes 1572872 | tf_op jit(solution)/shard_map/ppermute | solution.py:479
  200.7 9.8 %collective-permute-start.49 = (bf16[16,64,128]{2,1,0:T(8,128)(2,1)}, bf16[16,64,128]{2,1,0:T(8,128)(2,1)S(1)}, u32[]{:S(2)}, u32[]{:S(2)}) collective-permute-start(bf16[16,64,128]{2,1,0:T(8,128)(2,1)} %get-tuple-element.88.refs_4_), channel_id=1, source_target_pairs={{0,16},{8,24},{16,0},{24,8},{1,17},{9,25},{17,1},{25,9},{2,18},{10... | collective-permute-start | bytes 786440 | tf_op jit(solution)/shard_map/ppermute | solution.py:476
  205.6 4.6 %collective-permute-start.44 = (f32[24,128]{1,0:T(8,128)S(1)}, f32[24,128]{1,0:T(8,128)S(1)}, u32[]{:S(2)}, u32[]{:S(2)}) collective-permute-start(f32[24,128]{1,0:T(8,128)S(1)} %add.112), channel_id=1, source_target_pairs={{0,4},{1,5},{2,6},{3,7},{4,0},{5,1},{6,2},{7,3},{8,12},{9,13},{10,... | collective-permute-start | bytes 36872 | tf_op jit(solution)/shard_map/ppermute | solution.py:479
  216.5 7.2 %collective-permute-start.54 = (bf16[16,64,128]{2,1,0:T(8,128)(2,1)}, bf16[16,64,128]{2,1,0:T(8,128)(2,1)}, u32[]{:S(2)}, u32[]{:S(2)}) collective-permute-start(bf16[16,64,128]{2,1,0:T(8,128)(2,1)} %get-tuple-element.91), channel_id=1, source_target_pairs={{0,16},{8,24},{16,0},{24,8},{1,17},{9,25},{17,1},{25,9},{2,18},{10... | collective-permute-start | bytes 786440 | tf_op jit(solution)/shard_map/ppermute | solution.py:476
  (49 other events, 468.3 us)

commit v7 on v5

--- a/solution.py
+++ b/solution.py
@@ -487,11 +487,11 @@
         return moved
 
     def total_near(sums):
+        sums = sums + to_src(sums, 1)
+        return sums + to_pair(sums)
+
+    def total_far(sums):
         sums = sums + to_core(sums)
-        sums = sums + to_pair(sums)
-        return sums + to_src(sums, 1)
-
-    def total_far(sums):
         for level in levels[1:]:
             sums = sums + to_src(sums, 1 << level)
         return sums, jnp.sum(sums.reshape(-1, 8 * 128), axis=1)

time: 230 us -> 230 us (level)
  transfers between devices with their start and end apart: 55 -> 55, of which waited for: 26 -> 27; matrix products, arithmetic and copies ran while one was open for 2% -> 2% of each run, Pallas kernels for 19% -> 19%
where the time goes in v7:
time: 230 us; the launch traced here: 229 us
  waiting for transfers between devices  78.4 us (34%)
  starting transfers between devices  73.5 us (32%)
  Pallas kernels  52 us (23%)
  local copies, waits for them, and re-layouts  12.6 us (5%)
  between operations  6.55 us (3%)
  other arithmetic  5.98 us (3%)
    ppermute x41, starting transfers between devices, to_src(): return lax.ppermute(array, 'src', [(j, j ^ step) for j in range(n_src)])  63.6 us
    ppermute x41, waiting for transfers between devices, to_src(): return lax.ppermute(array, 'src', [(j, j ^ step) for j in range(n_src)])  62.6 us
    pallas_call x4, Pallas kernels, forward_call(): pl.pallas_call(kernel, grid=(1,), in_specs=[pl.BlockSpec(memory_space=plt...  18.8 us
    ppermute x9, waiting for transfers between devices, to_pair(): return lax.ppermute(array, 'sens', [(i, i ^ 2) for i in range(n_sens)])  14 us
    pallas_call x4, Pallas kernels, adjoint_call(): pl.pallas_call(kernel, grid=(1,), in_specs=[pl.BlockSpec(memory_space=plt...  12.6 us
    unnamed x84, local copies, waits for them, and re-layouts  10.5 us
    ppermute x9, starting transfers between devices, to_pair(): return lax.ppermute(array, 'sens', [(i, i ^ 2) for i in range(n_sens)])  9.03 us
    pallas_call x2, Pallas kernels, cut_call(): pl.pallas_call(kernel, in_specs=[pl.BlockSpec(memory_space=pltpu.SMEM), A...  6.22 us
  transfers between devices with their start and end apart: 55, of which 27 were waited for; matrix products, arithmetic and copies ran while one was open for 2% of the time, Pallas kernels for 19%

profile of v7, /device:TPU:0, one launch (start us, length us, event | category | flops | bytes accessed | tf_op | source)
XLA Modules:
  0.0 229.0 jit_solution(15253204414677942462)
XLA Ops:
  3.3 3.1 %cut.2 = bf16[2,4096,128]{2,1,0:T(8,128)(2,1)} custom-call(s32[4]{0:T(128)} %pad_add_fusion.m, bf16[2,2,8192,128]{3,2,1,0:T(8,128)(2,1)} %bitcast.60, bf16[16,64,128]{2,1,0:T(8,128)(2,1)} %copy-done.13), custom_call_target="tpu_custom_call" | custom-call | bytes 2097 | tf_op jit(solution)/shard_map/cut/pallas_call | solution.py:132
  7.0 3.1 %cut.3.refs_1_ = bf16[2,4096,128]{2,1,0:T(8,128)(2,1)} custom-call(s32[4]{0:T(128)} %pad_add_fusion.m, bf16[2,2,8192,128]{3,2,1,0:T(8,128)(2,1)} %bitcast.61, bf16[16,64,128]{2,1,0:T(8,128)(2,1)} %copy-done.13), custom_call_target="tpu_custom_call" | custom-call | bytes 2097 | tf_op jit(solution)/shard_map/cut/pallas_call | solution.py:132
  10.4 2.8 %collective-permute-start = (f32[16,128]{1,0:T(8,128)S(1)}, f32[16,128]{1,0:T(8,128)S(1)}, u32[]{:S(2)}, u32[]{:S(2)}) collective-permute-start(f32[16,128]{1,0:T(8,128)S(1)} %copy-done.41), channel_id=1, source_target_pairs={{0,1},{1,0},{2,3},{3,2},{4,5},{5,4},{6,7},{7,6},{8,9},{9,8},{10,11... | collective-permute-start | bytes 24584 | tf_op jit(solution)/shard_map/ppermute | solution.py:479
  14.9 2.1 collective-permute-start.1
  19.9 4.1 %collective-permute-done.5.two_ref.refs_1_ = bf16[16,64,128]{2,1,0:T(8,128)(2,1)} collective-permute-done((bf16[16,64,128]{2,1,0:T(8,128)(2,1)S(1)}, bf16[16,64,128]{2,1,0:T(8,128)(2,1)}, u32[]{:S(2)}, u32[]{:S(2)}) %collective-permute-start.5) | collective-permute-done | bytes 262176 | tf_op jit(solution)/shard_map/ppermute | solution.py:476
  24.0 5.6 %forward.4 = (bf16[16,64,256]{2,1,0:T(8,128)(2,1)}, bf16[16,64,256]{2,1,0:T(8,128)(2,1)}, bf16[2,4096,128]{2,1,0:T(8,128)(2,1)}) custom-call(s32[4]{0:T(128)} %pad_add_fusion.m, bf16[2,2,8192,128]{3,2,1,0:T(8,128)(2,1)} %bitcast.62, bf16[2,4096,128]{2,1,0:T(8,128)(2,1)} %collective-permute-done.4.far, f32[32,64,128]{2,1,0:T(8,128)} %bitcast.37, ...), custom_call_target="tpu_custom_call" | custom-call | flops 536870 | bytes 4194 | tf_op jit(solution)/shard_map/forward/pallas_call | solution.py:209
  32.6 2.6 %collective-permute-start.2 = (f32[64,128]{1,0:T(8,128)S(1)}, f32[64,128]{1,0:T(8,128)S(1)}, u32[]{:S(2)}, u32[]{:S(2)}) collective-permute-start(f32[64,128]{1,0:T(8,128)S(1)} %copy-done.40), channel_id=1, source_target_pairs={{0,4},{1,5},{2,6},{3,7},{4,0},{5,1},{6,2},{7,3},{8,12},{9,13},{10,... | collective-permute-start | bytes 98312 | tf_op jit(solution)/shard_map/ppermute | solution.py:479
  35.2 2.3 %collective-permute-done.8.two_ref = bf16[16,64,128]{2,1,0:T(8,128)(2,1)S(1)} collective-permute-done((bf16[16,64,128]{2,1,0:T(8,128)(2,1)S(1)}, bf16[16,64,128]{2,1,0:T(8,128)(2,1)S(1)}, u32[]{:S(2)}, u32[]{:S(2)}) %collective-permute-start.8) | collective-permute-done | bytes 262176 | tf_op jit(solution)/shard_map/ppermute | solution.py:476
  38.2 5.5 %forward.5 = (bf16[16,64,256]{2,1,0:T(8,128)(2,1)}, bf16[16,64,256]{2,1,0:T(8,128)(2,1)}, bf16[2,4096,128]{2,1,0:T(8,128)(2,1)}) custom-call(s32[4]{0:T(128)} %pad_add_fusion.m, bf16[2,2,8192,128]{3,2,1,0:T(8,128)(2,1)} %bitcast.63, bf16[2,4096,128]{2,1,0:T(8,128)(2,1)} %copy-done.3, f32[32,64,128]{2,1,0:T(8,128)} %bitcast.38, bf16[16,64,128]{2,1,0:T(8,128)(2,1)} %copy-done.39), custom_call_target="tpu_custom_call" | custom-call | flops 536870 | bytes 4194 | tf_op jit(solution)/shard_map/forward/pallas_call | solution.py:209
  45.0 1.8 split.4
  46.9 2.6 %collective-permute-start.10 = (bf16[256,256]{1,0:T(8,128)(2,1)}, bf16[256,256]{1,0:T(8,128)(2,1)}, u32[]{:S(2)}, u32[]{:S(2)}) collective-permute-start(bf16[256,256]{1,0:T(8,128)(2,1)} %get-tuple-element.53), channel_id=1, source_target_pairs={{0,4},{1,5},{2,6},{3,7},{4,0},{5,1},{6,2},{7,3},{8,12},{9,13},{10,... | collective-permute-start | bytes 393224 | tf_op jit(solution)/shard_map/ppermute | solution.py:479
  51.0 8.5 %collective-permute-done.10.refs_4_ = bf16[256,256]{1,0:T(8,128)(2,1)} collective-permute-done((bf16[256,256]{1,0:T(8,128)(2,1)}, bf16[256,256]{1,0:T(8,128)(2,1)}, u32[]{:S(2)}, u32[]{:S(2)}) %collective-permute-start.10) | collective-permute-done | bytes 131104 | tf_op jit(solution)/shard_map/ppermute | solution.py:479
  62.8 1.9 collective-permute-start.18
  67.4 2.6 %collective-permute-done.18.refs_1_ = bf16[256,256]{1,0:T(8,128)(2,1)S(1)} collective-permute-done((bf16[256,256]{1,0:T(8,128)(2,1)S(1)}, bf16[256,256]{1,0:T(8,128)(2,1)S(1)}, u32[]{:S(2)}, u32[]{:S(2)}) %collective-permute-start.18) | collective-permute-done | bytes 131104 | tf_op jit(solution)/shard_map/ppermute | solution.py:479
  70.0 7.6 %collective-permute-done.19.refs_2_ = bf16[256,256]{1,0:T(8,128)(2,1)S(1)} collective-permute-done((bf16[256,256]{1,0:T(8,128)(2,1)S(1)}, bf16[256,256]{1,0:T(8,128)(2,1)S(1)}, u32[]{:S(2)}, u32[]{:S(2)}) %collective-permute-start.19) | collective-permute-done | bytes 131104 | tf_op jit(solution)/shard_map/ppermute | solution.py:479
  78.2 1.6 collective-permute-start.21
  81.0 2.3 %collective-permute-start.13 = (bf16[256,256]{1,0:T(8,128)(2,1)S(1)}, bf16[256,256]{1,0:T(8,128)(2,1)S(1)}, u32[]{:S(2)}, u32[]{:S(2)}) collective-permute-start(bf16[256,256]{1,0:T(8,128)(2,1)S(1)} %get-tuple-element.58), channel_id=1, source_target_pairs={{0,2},{1,3},{2,0},{3,1},{4,6},{5,7},{6,4},{7,5},{8,10},{9,11},{10,... | collective-permute-start | bytes 393224 | tf_op jit(solution)/shard_map/ppermute | solution.py:479
  84.2 1.6 collective-permute-start.15
  85.8 3.6 %collective-permute-done.21.got_ref = bf16[16,64,256]{2,1,0:T(8,128)(2,1)S(1)} collective-permute-done((bf16[16,64,256]{2,1,0:T(8,128)(2,1)S(1)}, bf16[16,64,256]{2,1,0:T(8,128)(2,1)S(1)}, u32[]{:S(2)}, u32[]{:S(2)}) %collective-permute-start.21) | collective-permute-done | bytes 524320 | tf_op jit(solution)/shard_map/ppermute | solution.py:479
  89.4 3.0 %adjoint.4.one_ref.mine_ref.refs_4_ = bf16[2,16,64,128]{3,2,1,0:T(8,128)(2,1)S(1)} custom-call(s32[4]{0:T(128)S(1)} %copy-done.33, bf16[2,4096,128]{2,1,0:T(8,128)(2,1)S(1)} %copy-done.8, bf16[2,4096,128]{2,1,0:T(8,128)(2,1)} %collective-permute-done.4.far, bf16[16,64,256]{2,1,0:T(8,128)(2,1)S(1)} %bitcast.48, ...), custom_call_target="tpu_custom_call" | custom-call | flops 536870 | bytes 4194 | tf_op jit(solution)/shard_map/adjoint/pallas_call | solution.py:251
  96.3 3.6 %collective-permute-start.31 = (bf16[256,256]{1,0:T(8,128)(2,1)S(1)}, bf16[256,256]{1,0:T(8,128)(2,1)S(1)}, u32[]{:S(2)}, u32[]{:S(2)}) collective-permute-start(bf16[256,256]{1,0:T(8,128)(2,1)S(1)} %get-tuple-element.75.refs_0_), channel_id=1, source_target_pairs={{0,2},{1,3},{2,0},{3,1},{4,6},{5,7},{6,4},{7,5},{8,10},{9,11},{10,... | collective-permute-start | bytes 393224 | tf_op jit(solution)/shard_map/ppermute | solution.py:479
  100.5 1.8 collective-permute-start.33
  103.8 2.2 collective-permute-done.16
  106.4 3.3 %collective-permute-done.17 = f32[24,128]{1,0:T(8,128)S(1)} collective-permute-done((f32[24,128]{1,0:T(8,128)S(1)}, f32[24,128]{1,0:T(8,128)S(1)}, u32[]{:S(2)}, u32[]{:S(2)}) %collective-permute-start.17) | collective-permute-done | bytes 12320 | tf_op jit(solution)/shard_map/ppermute | solution.py:476
  112.7 4.2 %forward.6 = (bf16[16,64,256]{2,1,0:T(8,128)(2,1)}, bf16[16,64,256]{2,1,0:T(8,128)(2,1)S(1)}) custom-call(s32[4]{0:T(128)S(1)} %copy-done.33, bf16[2,4096,128]{2,1,0:T(8,128)(2,1)S(1)} %copy-done.9, bf16[2,4096,128]{2,1,0:T(8,128)(2,1)} %collective-permute-done.4.far, bf16[2,16,64,128]{3,2,1,0:T(8,128)(2,1)S(1)} %adjoint.4.one_ref.mine_ref.refs_4_, ...), custom_call_target="tpu_custom_call" | custom-call | flops 536870 | bytes 4194 | tf_op jit(solution)/shard_map/forward/pallas_call | solution.py:209
  118.2 2.2 collective-permute-start.24
  120.4 1.7 collective-permute-done.24
  122.0 2.5 %collective-permute-start.25 = (f32[24,128]{1,0:T(8,128)S(1)}, f32[24,128]{1,0:T(8,128)S(1)}, u32[]{:S(2)}, u32[]{:S(2)}) collective-permute-start(f32[24,128]{1,0:T(8,128)S(1)} %add.106), channel_id=1, source_target_pairs={{0,4},{1,5},{2,6},{3,7},{4,0},{5,1},{6,2},{7,3},{8,12},{9,13},{10,... | collective-permute-start | bytes 36872 | tf_op jit(solution)/shard_map/ppermute | solution.py:479
  126.8 3.0 %adjoint.5.mine_ref.one_ref = bf16[2,16,64,128]{3,2,1,0:T(8,128)(2,1)} custom-call(s32[4]{0:T(128)S(1)} %copy-done.33, bf16[2,4096,128]{2,1,0:T(8,128)(2,1)S(1)} %copy-done.5, bf16[2,4096,128]{2,1,0:T(8,128)(2,1)S(1)} %copy-done.4, bf16[16,64,256]{2,1,0:T(8,128)(2,1)S(1)} %bitcast.46, bf16[16,64,256]{2,1,0:T(8,128)(2,1)S(1)} %collective-permute-done.34.got_ref, ...), custom_call_target="tpu_custom_call" | custom-call | flops 536870 | bytes 4194 | tf_op jit(solution)/shard_map/adjoint/pallas_call | solution.py:251
  139.9 1.9 collective-permute-start.28
  142.4 1.9 collective-permute-start.30
  144.4 3.6 %forward.7 = (bf16[16,64,256]{2,1,0:T(8,128)(2,1)S(1)}, bf16[16,64,256]{2,1,0:T(8,128)(2,1)S(1)}) custom-call(s32[4]{0:T(128)S(1)} %copy-done.33, bf16[2,4096,128]{2,1,0:T(8,128)(2,1)S(1)} %copy-done.6, bf16[2,4096,128]{2,1,0:T(8,128)(2,1)S(1)} %copy-done.4, bf16[2,16,64,128]{3,2,1,0:T(8,128)(2,1)} %adjoint.5.mine_ref.one_ref, ...), custom_call_target="tpu_custom_call" | custom-call | flops 536870 | bytes 4194 | tf_op jit(solution)/shard_map/forward/pallas_call | solution.py:209
  148.8 3.4 %collective-permute-done.29.refs_7_ = bf16[256,256]{1,0:T(8,128)(2,1)S(1)} collective-permute-done((bf16[256,256]{1,0:T(8,128)(2,1)S(1)}, bf16[256,256]{1,0:T(8,128)(2,1)S(1)}, u32[]{:S(2)}, u32[]{:S(2)}) %collective-permute-start.29) | collective-permute-done | bytes 131104 | tf_op jit(solution)/shard_map/ppermute | solution.py:479
  153.0 2.2 collective-permute-start.45
  155.7 1.9 collective-permute-start.47
  159.1 7.8 %collective-permute-done.46.refs_2_ = bf16[256,256]{1,0:T(8,128)(2,1)S(1)} collective-permute-done((bf16[256,256]{1,0:T(8,128)(2,1)S(1)}, bf16[256,256]{1,0:T(8,128)(2,1)S(1)}, u32[]{:S(2)}, u32[]{:S(2)}) %collective-permute-start.46) | collective-permute-done | bytes 131104 | tf_op jit(solution)/shard_map/ppermute | solution.py:479
  170.3 2.2 collective-permute-start.37
  173.1 1.9 collective-permute-start.39
  176.5 7.6 %collective-permute-done.38.refs_7_ = bf16[256,256]{1,0:T(8,128)(2,1)S(1)} collective-permute-done((bf16[256,256]{1,0:T(8,128)(2,1)S(1)}, bf16[256,256]{1,0:T(8,128)(2,1)S(1)}, u32[]{:S(2)}, u32[]{:S(2)}) %collective-permute-start.38) | collective-permute-done | bytes 131104 | tf_op jit(solution)/shard_map/ppermute | solution.py:479
  184.8 2.2 collective-permute-start.50
  187.5 1.9 collective-permute-start.52
  190.6 2.5 %collective-permute-done.40 = f32[24,128]{1,0:T(8,128)S(1)} collective-permute-done((f32[24,128]{1,0:T(8,128)S(1)}, f32[24,128]{1,0:T(8,128)S(1)}, u32[]{:S(2)}, u32[]{:S(2)}) %collective-permute-start.40) | collective-permute-done | bytes 12320 | tf_op jit(solution)/shard_map/ppermute | solution.py:479
  193.6 3.2 %collective-permute-done.41 = f32[24,128]{1,0:T(8,128)S(1)} collective-permute-done((f32[24,128]{1,0:T(8,128)S(1)}, f32[24,128]{1,0:T(8,128)S(1)}, u32[]{:S(2)}, u32[]{:S(2)}) %collective-permute-start.41) | collective-permute-done | bytes 12320 | tf_op jit(solution)/shard_map/ppermute | solution.py:476
  196.8 3.4 %adjoint.6 = (bf16[16,64,128]{2,1,0:T(8,128)(2,1)}, f32[16,64,128]{2,1,0:T(8,128)S(1)}) custom-call(s32[4]{0:T(128)S(1)} %copy-done.33, bf16[2,4096,128]{2,1,0:T(8,128)(2,1)S(1)} %copy-done.10, bf16[2,4096,128]{2,1,0:T(8,128)(2,1)} %collective-permute-done.4.far, bf16[16,64,256]{2,1,0:T(8,128)(2,1)S(1)} %bitcast.50, ...), custom_call_target="tpu_custom_call" | custom-call | flops 536870 | bytes 4194 | tf_op jit(solution)/shard_map/adjoint/pallas_call | solution.py:251
  205.1 2.6 %collective-permute-done.43 = f32[24,128]{1,0:T(8,128)S(1)} collective-permute-done((f32[24,128]{1,0:T(8,128)S(1)}, f32[24,128]{1,0:T(8,128)S(1)}, u32[]{:S(2)}, u32[]{:S(2)}) %collective-permute-start.43) | collective-permute-done | bytes 12320 | tf_op jit(solution)/shard_map/ppermute | solution.py:479
  209.3 3.1 %collective-permute-done.44 = f32[24,128]{1,0:T(8,128)S(1)} collective-permute-done((f32[24,128]{1,0:T(8,128)S(1)}, f32[24,128]{1,0:T(8,128)S(1)}, u32[]{:S(2)}, u32[]{:S(2)}) %collective-permute-start.44) | collective-permute-done | bytes 12320 | tf_op jit(solution)/shard_map/ppermute | solution.py:479
  214.3 3.2 %adjoint.7 = (bf16[16,64,128]{2,1,0:T(8,128)(2,1)}, f32[16,64,128]{2,1,0:T(8,128)S(1)}) custom-call(s32[4]{0:T(128)S(1)} %copy-done.33, bf16[2,4096,128]{2,1,0:T(8,128)(2,1)S(1)} %copy-done.7, bf16[2,4096,128]{2,1,0:T(8,128)(2,1)S(1)} %copy-done.4, bf16[16,64,256]{2,1,0:T(8,128)(2,1)} %bitcast.30.own_ref, ...), custom_call_target="tpu_custom_call" | custom-call | flops 536870 | bytes 4194 | tf_op jit(solution)/shard_map/adjoint/pallas_call | solution.py:251
  227.1 1.9 fusion.2
  (209 shorter events, 71.1 us)
Async XLA Ops:
  6.5 17.5 %collective-permute-start.4 = (bf16[2,4096,128]{2,1,0:T(8,128)(2,1)}, bf16[2,4096,128]{2,1,0:T(8,128)(2,1)}, u32[]{:S(2)}, u32[]{:S(2)}) collective-permute-start(bf16[2,4096,128]{2,1,0:T(8,128)(2,1)} %cut.2), channel_id=1, source_target_pairs={{0,8},{8,0},{16,24},{24,16},{1,9},{9,1},{17,25},{25,17},{2,10},{10... | collective-permute-start | bytes 6291464 | tf_op jit(solution)/shard_map/ppermute | solution.py:473
  10.1 25.1 %collective-permute-start.7 = (bf16[2,4096,128]{2,1,0:T(8,128)(2,1)}, bf16[2,4096,128]{2,1,0:T(8,128)(2,1)S(1)}, u32[]{:S(2)}, u32[]{:S(2)}) collective-permute-start(bf16[2,4096,128]{2,1,0:T(8,128)(2,1)} %cut.3.refs_1_), channel_id=1, source_target_pairs={{0,8},{8,0},{16,24},{24,16},{1,9},{9,1},{17,25},{25,17},{2,10},{10... | collective-permute-start | bytes 6291464 | tf_op jit(solution)/shard_map/ppermute | solution.py:473
  10.4 4.5 %collective-permute-start = (f32[16,128]{1,0:T(8,128)S(1)}, f32[16,128]{1,0:T(8,128)S(1)}, u32[]{:S(2)}, u32[]{:S(2)}) collective-permute-start(f32[16,128]{1,0:T(8,128)S(1)} %copy-done.41), channel_id=1, source_target_pairs={{0,1},{1,0},{2,3},{3,2},{4,5},{5,4},{6,7},{7,6},{8,9},{9,8},{10,11... | collective-permute-start | bytes 24584 | tf_op jit(solution)/shard_map/ppermute | solution.py:479
  14.9 4.4 %collective-permute-start.1 = (f32[32,128]{1,0:T(8,128)S(1)}, f32[32,128]{1,0:T(8,128)S(1)}, u32[]{:S(2)}, u32[]{:S(2)}) collective-permute-start(f32[32,128]{1,0:T(8,128)S(1)} %pad_maximum_fusion.3), channel_id=1, source_target_pairs={{0,2},{1,3},{2,0},{3,1},{4,6},{5,7},{6,4},{7,5},{8,10},{9,11},{10,... | collective-permute-start | bytes 49160 | tf_op jit(solution)/shard_map/ppermute | solution.py:479
  16.9 7.0 %collective-permute-start.5 = (bf16[16,64,128]{2,1,0:T(8,128)(2,1)S(1)}, bf16[16,64,128]{2,1,0:T(8,128)(2,1)}, u32[]{:S(2)}, u32[]{:S(2)}) collective-permute-start(bf16[16,64,128]{2,1,0:T(8,128)(2,1)S(1)} %copy-done.14), channel_id=1, source_target_pairs={{0,16},{8,24},{16,0},{24,8},{1,17},{9,25},{17,1},{25,9},{2,18},{10... | collective-permute-start | bytes 786440 | tf_op jit(solution)/shard_map/ppermute | solution.py:476
  29.5 14.3 %collective-permute-start.6 = (bf16[16,64,256]{2,1,0:T(8,128)(2,1)}, bf16[16,64,256]{2,1,0:T(8,128)(2,1)}, u32[]{:S(2)}, u32[]{:S(2)}) collective-permute-start(bf16[16,64,256]{2,1,0:T(8,128)(2,1)} %get-tuple-element.49), channel_id=1, source_target_pairs={{0,1},{1,0},{2,3},{3,2},{4,5},{5,4},{6,7},{7,6},{8,9},{9,8},{10,11... | collective-permute-start | bytes 1572872 | tf_op jit(solution)/shard_map/ppermute | solution.py:479
  31.2 6.4 %collective-permute-start.8 = (bf16[16,64,128]{2,1,0:T(8,128)(2,1)S(1)}, bf16[16,64,128]{2,1,0:T(8,128)(2,1)S(1)}, u32[]{:S(2)}, u32[]{:S(2)}) collective-permute-start(bf16[16,64,128]{2,1,0:T(8,128)(2,1)S(1)} %ordered.4), channel_id=1, source_target_pairs={{0,16},{8,24},{16,0},{24,8},{1,17},{9,25},{17,1},{25,9},{2,18},{10... | collective-permute-start | bytes 786440 | tf_op jit(solution)/shard_map/ppermute | solution.py:476
  32.6 11.8 %collective-permute-start.2 = (f32[64,128]{1,0:T(8,128)S(1)}, f32[64,128]{1,0:T(8,128)S(1)}, u32[]{:S(2)}, u32[]{:S(2)}) collective-permute-start(f32[64,128]{1,0:T(8,128)S(1)} %copy-done.40), channel_id=1, source_target_pairs={{0,4},{1,5},{2,6},{3,7},{4,0},{5,1},{6,2},{7,3},{8,12},{9,13},{10,... | collective-permute-start | bytes 98312 | tf_op jit(solution)/shard_map/ppermute | solution.py:479
  43.8 17.1 %collective-permute-start.12 = (bf16[16,64,256]{2,1,0:T(8,128)(2,1)}, bf16[16,64,256]{2,1,0:T(8,128)(2,1)}, u32[]{:S(2)}, u32[]{:S(2)}) collective-permute-start(bf16[16,64,256]{2,1,0:T(8,128)(2,1)} %ordered.5.refs_0_), channel_id=1, source_target_pairs={{0,1},{1,0},{2,3},{3,2},{4,5},{5,4},{6,7},{7,6},{8,9},{9,8},{10,11... | collective-permute-start | bytes 1572872 | tf_op jit(solution)/shard_map/ppermute | solution.py:479
  45.0 6.0 %collective-permute-start.3 = (f32[2,32,128]{2,1,0:T(8,128)}, f32[2,32,128]{2,1,0:T(8,128)S(1)}, u32[]{:S(2)}, u32[]{:S(2)}) collective-permute-start(f32[2,32,128]{2,1,0:T(8,128)} %get-tuple-element.100), channel_id=1, source_target_pairs={{0,8},{8,0},{16,24},{24,16},{1,9},{9,1},{17,25},{25,17},{2,10},{10... | collective-permute-start | bytes 98312 | tf_op jit(solution)/shard_map/ppermute | solution.py:473
  46.9 12.7 %collective-permute-start.10 = (bf16[256,256]{1,0:T(8,128)(2,1)}, bf16[256,256]{1,0:T(8,128)(2,1)}, u32[]{:S(2)}, u32[]{:S(2)}) collective-permute-start(bf16[256,256]{1,0:T(8,128)(2,1)} %get-tuple-element.53), channel_id=1, source_target_pairs={{0,4},{1,5},{2,6},{3,7},{4,0},{5,1},{6,2},{7,3},{8,12},{9,13},{10,... | collective-permute-start | bytes 393224 | tf_op jit(solution)/shard_map/ppermute | solution.py:479
  49.5 10.1 %collective-permute-start.11 = (bf16[256,256]{1,0:T(8,128)(2,1)}, bf16[256,256]{1,0:T(8,128)(2,1)}, u32[]{:S(2)}, u32[]{:S(2)}) collective-permute-start(bf16[256,256]{1,0:T(8,128)(2,1)} %get-tuple-element.54), channel_id=1, source_target_pairs={{0,6},{1,7},{2,4},{3,5},{4,2},{5,3},{6,0},{7,1},{8,14},{9,15},{10,... | collective-permute-start | bytes 393224 | tf_op jit(solution)/shard_map/ppermute | solution.py:479
  49.6 11.3 %collective-permute-start.9 = (bf16[256,256]{1,0:T(8,128)(2,1)}, bf16[256,256]{1,0:T(8,128)(2,1)}, u32[]{:S(2)}, u32[]{:S(2)}) collective-permute-start(bf16[256,256]{1,0:T(8,128)(2,1)} %get-tuple-element.52), channel_id=1, source_target_pairs={{0,2},{1,3},{2,0},{3,1},{4,6},{5,7},{6,4},{7,5},{8,10},{9,11},{10,... | collective-permute-start | bytes 393224 | tf_op jit(solution)/shard_map/ppermute | solution.py:479
  62.8 7.2 %collective-permute-start.18 = (bf16[256,256]{1,0:T(8,128)(2,1)S(1)}, bf16[256,256]{1,0:T(8,128)(2,1)S(1)}, u32[]{:S(2)}, u32[]{:S(2)}) collective-permute-start(bf16[256,256]{1,0:T(8,128)(2,1)S(1)} %get-tuple-element.63.refs_0_), channel_id=1, source_target_pairs={{0,2},{1,3},{2,0},{3,1},{4,6},{5,7},{6,4},{7,5},{8,10},{9,11},{10,... | collective-permute-start | bytes 393224 | tf_op jit(solution)/shard_map/ppermute | solution.py:479
  64.7 12.9 %collective-permute-start.19 = (bf16[256,256]{1,0:T(8,128)(2,1)S(1)}, bf16[256,256]{1,0:T(8,128)(2,1)S(1)}, u32[]{:S(2)}, u32[]{:S(2)}) collective-permute-start(bf16[256,256]{1,0:T(8,128)(2,1)S(1)} %get-tuple-element.63.refs_0_), channel_id=1, source_target_pairs={{0,4},{1,5},{2,6},{3,7},{4,0},{5,1},{6,2},{7,3},{8,12},{9,13},{10,... | collective-permute-start | bytes 393224 | tf_op jit(solution)/shard_map/ppermute | solution.py:479
  65.9 11.7 %collective-permute-start.20 = (bf16[256,256]{1,0:T(8,128)(2,1)S(1)}, bf16[256,256]{1,0:T(8,128)(2,1)S(1)}, u32[]{:S(2)}, u32[]{:S(2)}) collective-permute-start(bf16[256,256]{1,0:T(8,128)(2,1)S(1)} %get-tuple-element.63.refs_0_), channel_id=1, source_target_pairs={{0,6},{1,7},{2,4},{3,5},{4,2},{5,3},{6,0},{7,1},{8,14},{9,15},{10,... | collective-permute-start | bytes 393224 | tf_op jit(solution)/shard_map/ppermute | solution.py:479
  78.2 11.2 %collective-permute-start.21 = (bf16[16,64,256]{2,1,0:T(8,128)(2,1)S(1)}, bf16[16,64,256]{2,1,0:T(8,128)(2,1)S(1)}, u32[]{:S(2)}, u32[]{:S(2)}) collective-permute-start(bf16[16,64,256]{2,1,0:T(8,128)(2,1)S(1)} %bitcast.47), channel_id=1, source_target_pairs={{0,1},{1,0},{2,3},{3,2},{4,5},{5,4},{6,7},{7,6},{8,9},{9,8},{10,11... | collective-permute-start | bytes 1572872 | tf_op jit(solution)/shard_map/ppermute | solution.py:479
  81.0 13.6 %collective-permute-start.13 = (bf16[256,256]{1,0:T(8,128)(2,1)S(1)}, bf16[256,256]{1,0:T(8,128)(2,1)S(1)}, u32[]{:S(2)}, u32[]{:S(2)}) collective-permute-start(bf16[256,256]{1,0:T(8,128)(2,1)S(1)} %get-tuple-element.58), channel_id=1, source_target_pairs={{0,2},{1,3},{2,0},{3,1},{4,6},{5,7},{6,4},{7,5},{8,10},{9,11},{10,... | collective-permute-start | bytes 393224 | tf_op jit(solution)/shard_map/ppermute | solution.py:479
  83.4 11.6 %collective-permute-start.14 = (bf16[256,256]{1,0:T(8,128)(2,1)S(1)}, bf16[256,256]{1,0:T(8,128)(2,1)S(1)}, u32[]{:S(2)}, u32[]{:S(2)}) collective-permute-start(bf16[256,256]{1,0:T(8,128)(2,1)S(1)} %get-tuple-element.59), channel_id=1, source_target_pairs={{0,4},{1,5},{2,6},{3,7},{4,0},{5,1},{6,2},{7,3},{8,12},{9,13},{10,... | collective-permute-start | bytes 393224 | tf_op jit(solution)/shard_map/ppermute | solution.py:479
  84.2 10.8 %collective-permute-start.15 = (bf16[256,256]{1,0:T(8,128)(2,1)S(1)}, bf16[256,256]{1,0:T(8,128)(2,1)S(1)}, u32[]{:S(2)}, u32[]{:S(2)}) collective-permute-start(bf16[256,256]{1,0:T(8,128)(2,1)S(1)} %get-tuple-element.60), channel_id=1, source_target_pairs={{0,6},{1,7},{2,4},{3,5},{4,2},{5,3},{6,0},{7,1},{8,14},{9,15},{10,... | collective-permute-start | bytes 393224 | tf_op jit(solution)/shard_map/ppermute | solution.py:479
  92.4 20.3 %collective-permute-start.22 = (bf16[2,16,64,128]{3,2,1,0:T(8,128)(2,1)S(1)}, bf16[2,16,64,128]{3,2,1,0:T(8,128)(2,1)S(1)}, u32[]{:S(2)}, u32[]{:S(2)}) collective-permute-start(bf16[2,16,64,128]{3,2,1,0:T(8,128)(2,1)S(1)} %adjoint.4.one_ref.mine_ref.refs_4_), channel_id=1, source_target_pairs={{0,16},{8,24},{16,0},{24,8},{1,17},{9,25},{17,1},{25,9},{2,18},{10... | collective-permute-start | bytes 1572872 | tf_op jit(solution)/shard_map/ppermute | solution.py:476
  96.3 13.4 %collective-permute-start.31 = (bf16[256,256]{1,0:T(8,128)(2,1)S(1)}, bf16[256,256]{1,0:T(8,128)(2,1)S(1)}, u32[]{:S(2)}, u32[]{:S(2)}) collective-permute-start(bf16[256,256]{1,0:T(8,128)(2,1)S(1)} %get-tuple-element.75.refs_0_), channel_id=1, source_target_pairs={{0,2},{1,3},{2,0},{3,1},{4,6},{5,7},{6,4},{7,5},{8,10},{9,11},{10,... | collective-permute-start | bytes 393224 | tf_op jit(solution)/shard_map/ppermute | solution.py:479
  99.9 10.6 %collective-permute-start.32 = (bf16[256,256]{1,0:T(8,128)(2,1)S(1)}, bf16[256,256]{1,0:T(8,128)(2,1)S(1)}, u32[]{:S(2)}, u32[]{:S(2)}) collective-permute-start(bf16[256,256]{1,0:T(8,128)(2,1)S(1)} %get-tuple-element.75.refs_0_), channel_id=1, source_target_pairs={{0,4},{1,5},{2,6},{3,7},{4,0},{5,1},{6,2},{7,3},{8,12},{9,13},{10,... | collective-permute-start | bytes 393224 | tf_op jit(solution)/shard_map/ppermute | solution.py:479
  100.5 10.0 %collective-permute-start.33 = (bf16[256,256]{1,0:T(8,128)(2,1)S(1)}, bf16[256,256]{1,0:T(8,128)(2,1)S(1)}, u32[]{:S(2)}, u32[]{:S(2)}) collective-permute-start(bf16[256,256]{1,0:T(8,128)(2,1)S(1)} %get-tuple-element.75.refs_0_), channel_id=1, source_target_pairs={{0,6},{1,7},{2,4},{3,5},{4,2},{5,3},{6,0},{7,1},{8,14},{9,15},{10,... | collective-permute-start | bytes 393224 | tf_op jit(solution)/shard_map/ppermute | solution.py:479
  111.1 15.6 %collective-permute-start.34 = (bf16[16,64,256]{2,1,0:T(8,128)(2,1)S(1)}, bf16[16,64,256]{2,1,0:T(8,128)(2,1)S(1)}, u32[]{:S(2)}, u32[]{:S(2)}) collective-permute-start(bf16[16,64,256]{2,1,0:T(8,128)(2,1)S(1)} %bitcast.45), channel_id=1, source_target_pairs={{0,1},{1,0},{2,3},{3,2},{4,5},{5,4},{6,7},{7,6},{8,9},{9,8},{10,11... | collective-permute-start | bytes 1572872 | tf_op jit(solution)/shard_map/ppermute | solution.py:479
  118.2 3.9 %collective-permute-start.24 = (f32[24,128]{1,0:T(8,128)S(1)}, f32[24,128]{1,0:T(8,128)S(1)}, u32[]{:S(2)}, u32[]{:S(2)}) collective-permute-start(f32[24,128]{1,0:T(8,128)S(1)} %add.105), channel_id=1, source_target_pairs={{0,2},{1,3},{2,0},{3,1},{4,6},{5,7},{6,4},{7,5},{8,10},{9,11},{10,... | collective-permute-start | bytes 36872 | tf_op jit(solution)/shard_map/ppermute | solution.py:479
  122.0 4.6 %collective-permute-start.25 = (f32[24,128]{1,0:T(8,128)S(1)}, f32[24,128]{1,0:T(8,128)S(1)}, u32[]{:S(2)}, u32[]{:S(2)}) collective-permute-start(f32[24,128]{1,0:T(8,128)S(1)} %add.106), channel_id=1, source_target_pairs={{0,4},{1,5},{2,6},{3,7},{4,0},{5,1},{6,2},{7,3},{8,12},{9,13},{10,... | collective-permute-start | bytes 36872 | tf_op jit(solution)/shard_map/ppermute | solution.py:479
  124.5 13.2 %collective-permute-start.27 = (bf16[16,64,256]{2,1,0:T(8,128)(2,1)}, bf16[16,64,256]{2,1,0:T(8,128)(2,1)}, u32[]{:S(2)}, u32[]{:S(2)}) collective-permute-start(bf16[16,64,256]{2,1,0:T(8,128)(2,1)} %get-tuple-element.64.refs_1_.refs_0_), channel_id=1, source_target_pairs={{0,1},{1,0},{2,3},{3,2},{4,5},{5,4},{6,7},{7,6},{8,9},{9,8},{10,11... | collective-permute-start | bytes 1572872 | tf_op jit(solution)/shard_map/ppermute | solution.py:479
  129.7 14.6 %collective-permute-start.35 = (bf16[2,16,64,128]{3,2,1,0:T(8,128)(2,1)}, bf16[2,16,64,128]{3,2,1,0:T(8,128)(2,1)}, u32[]{:S(2)}, u32[]{:S(2)}) collective-permute-start(bf16[2,16,64,128]{3,2,1,0:T(8,128)(2,1)} %adjoint.5.mine_ref.one_ref), channel_id=1, source_target_pairs={{0,16},{8,24},{16,0},{24,8},{1,17},{9,25},{17,1},{25,9},{2,18},{10... | collective-permute-start | bytes 1572872 | tf_op jit(solution)/shard_map/ppermute | solution.py:476
  130.4 18.5 %collective-permute-start.26 = (f32[32]{0:T(128)S(1)}, f32[32]{0:T(128)S(1)}, u32[]{:S(2)}, u32[]{:S(2)}) collective-permute-start(f32[32]{0:T(128)S(1)} %copy-done.38), channel_id=1, source_target_pairs={{0,16},{8,24},{16,0},{24,8},{1,17},{9,25},{17,1},{25,9},{2,18},{10... | collective-permute-start | bytes 392 | tf_op jit(solution)/shard_map/ppermute | solution.py:476
  139.9 8.9 %collective-permute-start.28 = (bf16[256,256]{1,0:T(8,128)(2,1)S(1)}, bf16[256,256]{1,0:T(8,128)(2,1)S(1)}, u32[]{:S(2)}, u32[]{:S(2)}) collective-permute-start(bf16[256,256]{1,0:T(8,128)(2,1)S(1)} %get-tuple-element.69), channel_id=1, source_target_pairs={{0,2},{1,3},{2,0},{3,1},{4,6},{5,7},{6,4},{7,5},{8,10},{9,11},{10,... | collective-permute-start | bytes 393224 | tf_op jit(solution)/shard_map/ppermute | solution.py:479
  141.8 10.5 %collective-permute-start.29 = (bf16[256,256]{1,0:T(8,128)(2,1)S(1)}, bf16[256,256]{1,0:T(8,128)(2,1)S(1)}, u32[]{:S(2)}, u32[]{:S(2)}) collective-permute-start(bf16[256,256]{1,0:T(8,128)(2,1)S(1)} %get-tuple-element.70), channel_id=1, source_target_pairs={{0,4},{1,5},{2,6},{3,7},{4,0},{5,1},{6,2},{7,3},{8,12},{9,13},{10,... | collective-permute-start | bytes 393224 | tf_op jit(solution)/shard_map/ppermute | solution.py:479
  142.4 9.8 %collective-permute-start.30 = (bf16[256,256]{1,0:T(8,128)(2,1)S(1)}, bf16[256,256]{1,0:T(8,128)(2,1)S(1)}, u32[]{:S(2)}, u32[]{:S(2)}) collective-permute-start(bf16[256,256]{1,0:T(8,128)(2,1)S(1)} %get-tuple-element.71), channel_id=1, source_target_pairs={{0,6},{1,7},{2,4},{3,5},{4,2},{5,3},{6,0},{7,1},{8,14},{9,15},{10,... | collective-permute-start | bytes 393224 | tf_op jit(solution)/shard_map/ppermute | solution.py:479
  148.0 21.7 %collective-permute-start.36 = (bf16[16,64,256]{2,1,0:T(8,128)(2,1)S(1)}, bf16[16,64,256]{2,1,0:T(8,128)(2,1)S(1)}, u32[]{:S(2)}, u32[]{:S(2)}) collective-permute-start(bf16[16,64,256]{2,1,0:T(8,128)(2,1)S(1)} %ordered.7), channel_id=1, source_target_pairs={{0,1},{1,0},{2,3},{3,2},{4,5},{5,4},{6,7},{7,6},{8,9},{9,8},{10,11... | collective-permute-start | bytes 1572872 | tf_op jit(solution)/shard_map/ppermute | solution.py:479
  153.0 6.2 %collective-permute-start.45 = (bf16[256,256]{1,0:T(8,128)(2,1)S(1)}, bf16[256,256]{1,0:T(8,128)(2,1)S(1)}, u32[]{:S(2)}, u32[]{:S(2)}) collective-permute-start(bf16[256,256]{1,0:T(8,128)(2,1)S(1)} %get-tuple-element.86.refs_0_), channel_id=1, source_target_pairs={{0,2},{1,3},{2,0},{3,1},{4,6},{5,7},{6,4},{7,5},{8,10},{9,11},{10,... | collective-permute-start | bytes 393224 | tf_op jit(solution)/shard_map/ppermute | solution.py:479
  155.2 11.7 %collective-permute-start.46 = (bf16[256,256]{1,0:T(8,128)(2,1)S(1)}, bf16[256,256]{1,0:T(8,128)(2,1)S(1)}, u32[]{:S(2)}, u32[]{:S(2)}) collective-permute-start(bf16[256,256]{1,0:T(8,128)(2,1)S(1)} %get-tuple-element.86.refs_0_), channel_id=1, source_target_pairs={{0,4},{1,5},{2,6},{3,7},{4,0},{5,1},{6,2},{7,3},{8,12},{9,13},{10,... | collective-permute-start | bytes 393224 | tf_op jit(solution)/shard_map/ppermute | solution.py:479
  155.7 11.2 %collective-permute-start.47 = (bf16[256,256]{1,0:T(8,128)(2,1)S(1)}, bf16[256,256]{1,0:T(8,128)(2,1)S(1)}, u32[]{:S(2)}, u32[]{:S(2)}) collective-permute-start(bf16[256,256]{1,0:T(8,128)(2,1)S(1)} %get-tuple-element.86.refs_0_), channel_id=1, source_target_pairs={{0,6},{1,7},{2,4},{3,5},{4,2},{5,3},{6,0},{7,1},{8,14},{9,15},{10,... | collective-permute-start | bytes 393224 | tf_op jit(solution)/shard_map/ppermute | solution.py:479
  167.5 29.3 %collective-permute-start.48 = (bf16[16,64,256]{2,1,0:T(8,128)(2,1)S(1)}, bf16[16,64,256]{2,1,0:T(8,128)(2,1)S(1)}, u32[]{:S(2)}, u32[]{:S(2)}) collective-permute-start(bf16[16,64,256]{2,1,0:T(8,128)(2,1)S(1)} %bitcast.49), channel_id=1, source_target_pairs={{0,1},{1,0},{2,3},{3,2},{4,5},{5,4},{6,7},{7,6},{8,9},{9,8},{10,11... | collective-permute-start | bytes 1572872 | tf_op jit(solution)/shard_map/ppermute | solution.py:479
  170.3 6.2 %collective-permute-start.37 = (bf16[256,256]{1,0:T(8,128)(2,1)S(1)}, bf16[256,256]{1,0:T(8,128)(2,1)S(1)}, u32[]{:S(2)}, u32[]{:S(2)}) collective-permute-start(bf16[256,256]{1,0:T(8,128)(2,1)S(1)} %get-tuple-element.80), channel_id=1, source_target_pairs={{0,2},{1,3},{2,0},{3,1},{4,6},{5,7},{6,4},{7,5},{8,10},{9,11},{10,... | collective-permute-start | bytes 393224 | tf_op jit(solution)/shard_map/ppermute | solution.py:479
  172.5 11.6 %collective-permute-start.38 = (bf16[256,256]{1,0:T(8,128)(2,1)S(1)}, bf16[256,256]{1,0:T(8,128)(2,1)S(1)}, u32[]{:S(2)}, u32[]{:S(2)}) collective-permute-start(bf16[256,256]{1,0:T(8,128)(2,1)S(1)} %get-tuple-element.81), channel_id=1, source_target_pairs={{0,4},{1,5},{2,6},{3,7},{4,0},{5,1},{6,2},{7,3},{8,12},{9,13},{10,... | collective-permute-start | bytes 393224 | tf_op jit(solution)/shard_map/ppermute | solution.py:479
  173.1 11.0 %collective-permute-start.39 = (bf16[256,256]{1,0:T(8,128)(2,1)S(1)}, bf16[256,256]{1,0:T(8,128)(2,1)S(1)}, u32[]{:S(2)}, u32[]{:S(2)}) collective-permute-start(bf16[256,256]{1,0:T(8,128)(2,1)S(1)} %get-tuple-element.82), channel_id=1, source_target_pairs={{0,6},{1,7},{2,4},{3,5},{4,2},{5,3},{6,0},{7,1},{8,14},{9,15},{10,... | collective-permute-start | bytes 393224 | tf_op jit(solution)/shard_map/ppermute | solution.py:479
  184.8 15.5 %collective-permute-start.50 = (bf16[256,256]{1,0:T(8,128)(2,1)S(1)}, bf16[256,256]{1,0:T(8,128)(2,1)S(1)}, u32[]{:S(2)}, u32[]{:S(2)}) collective-permute-start(bf16[256,256]{1,0:T(8,128)(2,1)S(1)} %get-tuple-element.89.refs_0_), channel_id=1, source_target_pairs={{0,2},{1,3},{2,0},{3,1},{4,6},{5,7},{6,4},{7,5},{8,10},{9,11},{10,... | collective-permute-start | bytes 393224 | tf_op jit(solution)/shard_map/ppermute | solution.py:479
  187.0 13.3 %collective-permute-start.51 = (bf16[256,256]{1,0:T(8,128)(2,1)S(1)}, bf16[256,256]{1,0:T(8,128)(2,1)S(1)}, u32[]{:S(2)}, u32[]{:S(2)}) collective-permute-start(bf16[256,256]{1,0:T(8,128)(2,1)S(1)} %get-tuple-element.89.refs_0_), channel_id=1, source_target_pairs={{0,4},{1,5},{2,6},{3,7},{4,0},{5,1},{6,2},{7,3},{8,12},{9,13},{10,... | collective-permute-start | bytes 393224 | tf_op jit(solution)/shard_map/ppermute | solution.py:479
  187.5 12.8 %collective-permute-start.52 = (bf16[256,256]{1,0:T(8,128)(2,1)S(1)}, bf16[256,256]{1,0:T(8,128)(2,1)S(1)}, u32[]{:S(2)}, u32[]{:S(2)}) collective-permute-start(bf16[256,256]{1,0:T(8,128)(2,1)S(1)} %get-tuple-element.89.refs_0_), channel_id=1, source_target_pairs={{0,6},{1,7},{2,4},{3,5},{4,2},{5,3},{6,0},{7,1},{8,14},{9,15},{10,... | collective-permute-start | bytes 393224 | tf_op jit(solution)/shard_map/ppermute | solution.py:479
  201.7 11.0 %collective-permute-start.53 = (bf16[16,64,256]{2,1,0:T(8,128)(2,1)}, bf16[16,64,256]{2,1,0:T(8,128)(2,1)}, u32[]{:S(2)}, u32[]{:S(2)}) collective-permute-start(bf16[16,64,256]{2,1,0:T(8,128)(2,1)} %bitcast.30.own_ref), channel_id=1, source_target_pairs={{0,1},{1,0},{2,3},{3,2},{4,5},{5,4},{6,7},{7,6},{8,9},{9,8},{10,11... | collective-permute-start | bytes 1572872 | tf_op jit(solution)/shard_map/ppermute | solution.py:479
  202.9 9.8 %collective-permute-start.49 = (bf16[16,64,128]{2,1,0:T(8,128)(2,1)}, bf16[16,64,128]{2,1,0:T(8,128)(2,1)S(1)}, u32[]{:S(2)}, u32[]{:S(2)}) collective-permute-start(bf16[16,64,128]{2,1,0:T(8,128)(2,1)} %get-tuple-element.88.refs_4_), channel_id=1, source_target_pairs={{0,16},{8,24},{16,0},{24,8},{1,17},{9,25},{17,1},{25,9},{2,18},{10... | collective-permute-start | bytes 786440 | tf_op jit(solution)/shard_map/ppermute | solution.py:476
  207.8 4.6 %collective-permute-start.44 = (f32[24,128]{1,0:T(8,128)S(1)}, f32[24,128]{1,0:T(8,128)S(1)}, u32[]{:S(2)}, u32[]{:S(2)}) collective-permute-start(f32[24,128]{1,0:T(8,128)S(1)} %add.112), channel_id=1, source_target_pairs={{0,4},{1,5},{2,6},{3,7},{4,0},{5,1},{6,2},{7,3},{8,12},{9,13},{10,... | collective-permute-start | bytes 36872 | tf_op jit(solution)/shard_map/ppermute | solution.py:479
  218.3 7.5 %collective-permute-start.54 = (bf16[16,64,128]{2,1,0:T(8,128)(2,1)}, bf16[16,64,128]{2,1,0:T(8,128)(2,1)}, u32[]{:S(2)}, u32[]{:S(2)}) collective-permute-start(bf16[16,64,128]{2,1,0:T(8,128)(2,1)} %get-tuple-element.91), channel_id=1, source_target_pairs={{0,16},{8,24},{16,0},{24,8},{1,17},{9,25},{17,1},{25,9},{2,18},{10... | collective-permute-start | bytes 786440 | tf_op jit(solution)/shard_map/ppermute | solution.py:476
  (49 other events, 471.3 us)

commit v8 on v6

--- a/solution.py
+++ b/solution.py
@@ -507,7 +507,7 @@
     start = right_side.reshape(block, rows, plan.sources)
 
     casts = [cast_call(plan, k, start) for k in chunks]
-    cuts = [cut_call(plan, k, meta, whole, (casts[0],)) for k in chunks]
+    cuts = [cut_call(plan, k, meta, whole) for k in chunks]
     got_b = in_turn(list(casts), to_pair)
     weights = noise_weights
     for level in levels[:2]:

time: 228 us -> 228 us (level)
    unnamed x84 -> x82, local copies, waits for them, and re-layouts: 10.9 us -> 10.6 us
where the time goes in v8:
time: 228 us; the launch traced here: 227 us
  waiting for transfers between devices  76.3 us (33%)
  starting transfers between devices  73 us (32%)
  Pallas kernels  52.7 us (23%)
  local copies, waits for them, and re-layouts  12.6 us (6%)
  between operations  6.55 us (3%)
  other arithmetic  5.97 us (3%)
    ppermute x41, starting transfers between devices, to_src(): return lax.ppermute(array, 'src', [(j, j ^ step) for j in range(n_src)])  64 us
    ppermute x41, waiting for transfers between devices, to_src(): return lax.ppermute(array, 'src', [(j, j ^ step) for j in range(n_src)])  60 us
    pallas_call x4, Pallas kernels, forward_call(): pl.pallas_call(kernel, grid=(1,), in_specs=[pl.BlockSpec(memory_space=plt...  18.8 us
    ppermute x9, waiting for transfers between devices, to_pair(): return lax.ppermute(array, 'sens', [(i, i ^ 2) for i in range(n_sens)])  14.6 us
    pallas_call x4, Pallas kernels, adjoint_call(): pl.pallas_call(kernel, grid=(1,), in_specs=[pl.BlockSpec(memory_space=plt...  12.6 us
    unnamed x82, local copies, waits for them, and re-layouts  10.6 us
    ppermute x9, starting transfers between devices, to_pair(): return lax.ppermute(array, 'sens', [(i, i ^ 2) for i in range(n_sens)])  8.25 us
    pallas_call x2, Pallas kernels, cut_call(): pl.pallas_call(kernel, in_specs=[pl.BlockSpec(memory_space=pltpu.SMEM), A...  6.21 us
  transfers between devices with their start and end apart: 55, of which 26 were waited for; matrix products, arithmetic and copies ran while one was open for 2% of the time, Pallas kernels for 19%

profile of v8, /device:TPU:0, one launch (start us, length us, event | category | flops | bytes accessed | tf_op | source)
XLA Modules:
  0.0 227.2 jit_solution(10131196140663061609)
XLA Ops:
  1.3 3.1 %cut.2 = bf16[2,4096,128]{2,1,0:T(8,128)(2,1)} custom-call(s32[4]{0:T(128)} %pad_add_fusion.m, bf16[2,2,8192,128]{3,2,1,0:T(8,128)(2,1)} %bitcast.60), custom_call_target="tpu_custom_call" | custom-call | bytes 2097 | tf_op jit(solution)/shard_map/cut/pallas_call | solution.py:132
  5.0 3.1 %cut.3.refs_1_ = bf16[2,4096,128]{2,1,0:T(8,128)(2,1)} custom-call(s32[4]{0:T(128)} %pad_add_fusion.m, bf16[2,2,8192,128]{3,2,1,0:T(8,128)(2,1)} %bitcast.61), custom_call_target="tpu_custom_call" | custom-call | bytes 2097 | tf_op jit(solution)/shard_map/cut/pallas_call | solution.py:132
  8.3 2.8 %collective-permute-start = (f32[16,128]{1,0:T(8,128)S(1)}, f32[16,128]{1,0:T(8,128)S(1)}, u32[]{:S(2)}, u32[]{:S(2)}) collective-permute-start(f32[16,128]{1,0:T(8,128)S(1)} %copy-done.40), channel_id=1, source_target_pairs={{0,1},{1,0},{2,3},{3,2},{4,5},{5,4},{6,7},{7,6},{8,9},{9,8},{10,11... | collective-permute-start | bytes 24584 | tf_op jit(solution)/shard_map/ppermute | solution.py:479
  12.8 2.1 collective-permute-start.1
  18.6 4.2 %collective-permute-done.5.two_ref.refs_1_ = bf16[16,64,128]{2,1,0:T(8,128)(2,1)S(1)} collective-permute-done((bf16[16,64,128]{2,1,0:T(8,128)(2,1)}, bf16[16,64,128]{2,1,0:T(8,128)(2,1)S(1)}, u32[]{:S(2)}, u32[]{:S(2)}) %collective-permute-start.5) | collective-permute-done | bytes 262176 | tf_op jit(solution)/shard_map/ppermute | solution.py:476
  23.6 5.5 %forward.4 = (bf16[16,64,256]{2,1,0:T(8,128)(2,1)}, bf16[16,64,256]{2,1,0:T(8,128)(2,1)}, bf16[2,4096,128]{2,1,0:T(8,128)(2,1)}) custom-call(s32[4]{0:T(128)} %pad_add_fusion.m, bf16[2,2,8192,128]{3,2,1,0:T(8,128)(2,1)} %bitcast.62, bf16[2,4096,128]{2,1,0:T(8,128)(2,1)} %collective-permute-done.4.far, f32[32,64,128]{2,1,0:T(8,128)} %bitcast.37, ...), custom_call_target="tpu_custom_call" | custom-call | flops 536870 | bytes 4194 | tf_op jit(solution)/shard_map/forward/pallas_call | solution.py:209
  29.1 1.6 collective-permute-start.6
  33.2 2.6 %collective-permute-start.2 = (f32[64,128]{1,0:T(8,128)S(1)}, f32[64,128]{1,0:T(8,128)S(1)}, u32[]{:S(2)}, u32[]{:S(2)}) collective-permute-start(f32[64,128]{1,0:T(8,128)S(1)} %copy-done.39), channel_id=1, source_target_pairs={{0,4},{1,5},{2,6},{3,7},{4,0},{5,1},{6,2},{7,3},{8,12},{9,13},{10,... | collective-permute-start | bytes 98312 | tf_op jit(solution)/shard_map/ppermute | solution.py:479
  35.8 2.3 %collective-permute-done.8.two_ref = bf16[16,64,128]{2,1,0:T(8,128)(2,1)S(1)} collective-permute-done((bf16[16,64,128]{2,1,0:T(8,128)(2,1)S(1)}, bf16[16,64,128]{2,1,0:T(8,128)(2,1)S(1)}, u32[]{:S(2)}, u32[]{:S(2)}) %collective-permute-start.8) | collective-permute-done | bytes 262176 | tf_op jit(solution)/shard_map/ppermute | solution.py:476
  38.8 5.5 %forward.5 = (bf16[16,64,256]{2,1,0:T(8,128)(2,1)}, bf16[16,64,256]{2,1,0:T(8,128)(2,1)}, bf16[2,4096,128]{2,1,0:T(8,128)(2,1)}) custom-call(s32[4]{0:T(128)} %pad_add_fusion.m, bf16[2,2,8192,128]{3,2,1,0:T(8,128)(2,1)} %bitcast.63, bf16[2,4096,128]{2,1,0:T(8,128)(2,1)} %copy-done.2, f32[32,64,128]{2,1,0:T(8,128)} %bitcast.38, bf16[16,64,128]{2,1,0:T(8,128)(2,1)} %copy-done.38), custom_call_target="tpu_custom_call" | custom-call | flops 536870 | bytes 4194 | tf_op jit(solution)/shard_map/forward/pallas_call | solution.py:209
  45.5 1.8 split.4
  47.4 2.6 %collective-permute-start.10 = (bf16[256,256]{1,0:T(8,128)(2,1)}, bf16[256,256]{1,0:T(8,128)(2,1)}, u32[]{:S(2)}, u32[]{:S(2)}) collective-permute-start(bf16[256,256]{1,0:T(8,128)(2,1)} %get-tuple-element.53), channel_id=1, source_target_pairs={{0,4},{1,5},{2,6},{3,7},{4,0},{5,1},{6,2},{7,3},{8,12},{9,13},{10,... | collective-permute-start | bytes 393224 | tf_op jit(solution)/shard_map/ppermute | solution.py:479
  51.5 8.5 %collective-permute-done.10.refs_4_ = bf16[256,256]{1,0:T(8,128)(2,1)} collective-permute-done((bf16[256,256]{1,0:T(8,128)(2,1)}, bf16[256,256]{1,0:T(8,128)(2,1)}, u32[]{:S(2)}, u32[]{:S(2)}) %collective-permute-start.10) | collective-permute-done | bytes 131104 | tf_op jit(solution)/shard_map/ppermute | solution.py:479
  63.3 1.9 collective-permute-start.19
  67.9 2.6 %collective-permute-done.19.refs_1_ = bf16[256,256]{1,0:T(8,128)(2,1)S(1)} collective-permute-done((bf16[256,256]{1,0:T(8,128)(2,1)S(1)}, bf16[256,256]{1,0:T(8,128)(2,1)S(1)}, u32[]{:S(2)}, u32[]{:S(2)}) %collective-permute-start.19) | collective-permute-done | bytes 131104 | tf_op jit(solution)/shard_map/ppermute | solution.py:479
  70.5 7.6 %collective-permute-done.20.refs_2_ = bf16[256,256]{1,0:T(8,128)(2,1)S(1)} collective-permute-done((bf16[256,256]{1,0:T(8,128)(2,1)S(1)}, bf16[256,256]{1,0:T(8,128)(2,1)S(1)}, u32[]{:S(2)}, u32[]{:S(2)}) %collective-permute-start.20) | collective-permute-done | bytes 131104 | tf_op jit(solution)/shard_map/ppermute | solution.py:479
  78.7 1.7 collective-permute-start.22
  81.6 2.3 %collective-permute-start.13 = (bf16[256,256]{1,0:T(8,128)(2,1)S(1)}, bf16[256,256]{1,0:T(8,128)(2,1)S(1)}, u32[]{:S(2)}, u32[]{:S(2)}) collective-permute-start(bf16[256,256]{1,0:T(8,128)(2,1)S(1)} %get-tuple-element.58), channel_id=1, source_target_pairs={{0,2},{1,3},{2,0},{3,1},{4,6},{5,7},{6,4},{7,5},{8,10},{9,11},{10,... | collective-permute-start | bytes 393224 | tf_op jit(solution)/shard_map/ppermute | solution.py:479
  86.3 3.6 %collective-permute-done.22.got_ref = bf16[16,64,256]{2,1,0:T(8,128)(2,1)S(1)} collective-permute-done((bf16[16,64,256]{2,1,0:T(8,128)(2,1)S(1)}, bf16[16,64,256]{2,1,0:T(8,128)(2,1)S(1)}, u32[]{:S(2)}, u32[]{:S(2)}) %collective-permute-start.22) | collective-permute-done | bytes 524320 | tf_op jit(solution)/shard_map/ppermute | solution.py:479
  89.9 3.0 %adjoint.4.one_ref.mine_ref.refs_4_ = bf16[2,16,64,128]{3,2,1,0:T(8,128)(2,1)S(1)} custom-call(s32[4]{0:T(128)S(1)} %copy-done.32, bf16[2,4096,128]{2,1,0:T(8,128)(2,1)S(1)} %copy-done.7, bf16[2,4096,128]{2,1,0:T(8,128)(2,1)} %collective-permute-done.4.far, bf16[16,64,256]{2,1,0:T(8,128)(2,1)S(1)} %bitcast.48, ...), custom_call_target="tpu_custom_call" | custom-call | flops 536870 | bytes 4194 | tf_op jit(solution)/shard_map/adjoint/pallas_call | solution.py:251
  96.8 3.6 %collective-permute-start.31 = (bf16[256,256]{1,0:T(8,128)(2,1)S(1)}, bf16[256,256]{1,0:T(8,128)(2,1)S(1)}, u32[]{:S(2)}, u32[]{:S(2)}) collective-permute-start(bf16[256,256]{1,0:T(8,128)(2,1)S(1)} %get-tuple-element.75.refs_0_), channel_id=1, source_target_pairs={{0,2},{1,3},{2,0},{3,1},{4,6},{5,7},{6,4},{7,5},{8,10},{9,11},{10,... | collective-permute-start | bytes 393224 | tf_op jit(solution)/shard_map/ppermute | solution.py:479
  101.1 1.8 collective-permute-start.33
  104.4 3.3 %collective-permute-done.17 = f32[24,128]{1,0:T(8,128)S(1)} collective-permute-done((f32[24,128]{1,0:T(8,128)S(1)}, f32[24,128]{1,0:T(8,128)S(1)}, u32[]{:S(2)}, u32[]{:S(2)}) %collective-permute-start.17) | collective-permute-done | bytes 12320 | tf_op jit(solution)/shard_map/ppermute | solution.py:476
  109.2 2.2 collective-permute-done.18
  113.6 4.2 %forward.6 = (bf16[16,64,256]{2,1,0:T(8,128)(2,1)}, bf16[16,64,256]{2,1,0:T(8,128)(2,1)S(1)}) custom-call(s32[4]{0:T(128)S(1)} %copy-done.32, bf16[2,4096,128]{2,1,0:T(8,128)(2,1)S(1)} %copy-done.8, bf16[2,4096,128]{2,1,0:T(8,128)(2,1)} %collective-permute-done.4.far, bf16[2,16,64,128]{3,2,1,0:T(8,128)(2,1)S(1)} %adjoint.4.one_ref.mine_ref.refs_4_, ...), custom_call_target="tpu_custom_call" | custom-call | flops 536870 | bytes 4194 | tf_op jit(solution)/shard_map/forward/pallas_call | solution.py:209
  117.8 1.9 collective-permute-start.24
  119.7 1.9 collective-permute-done.24
  121.6 2.3 %collective-permute-start.25 = (f32[24,128]{1,0:T(8,128)S(1)}, f32[24,128]{1,0:T(8,128)S(1)}, u32[]{:S(2)}, u32[]{:S(2)}) collective-permute-start(f32[24,128]{1,0:T(8,128)S(1)} %add.106), channel_id=1, source_target_pairs={{0,4},{1,5},{2,6},{3,7},{4,0},{5,1},{6,2},{7,3},{8,12},{9,13},{10,... | collective-permute-start | bytes 36872 | tf_op jit(solution)/shard_map/ppermute | solution.py:479
  126.3 3.0 %adjoint.5.mine_ref.one_ref = bf16[2,16,64,128]{3,2,1,0:T(8,128)(2,1)} custom-call(s32[4]{0:T(128)S(1)} %copy-done.32, bf16[2,4096,128]{2,1,0:T(8,128)(2,1)S(1)} %copy-done.4, bf16[2,4096,128]{2,1,0:T(8,128)(2,1)S(1)} %copy-done.3, bf16[16,64,256]{2,1,0:T(8,128)(2,1)S(1)} %bitcast.46, bf16[16,64,256]{2,1,0:T(8,128)(2,1)S(1)} %collective-permute-done.34.got_ref, ...), custom_call_target="tpu_custom_call" | custom-call | flops 536870 | bytes 4194 | tf_op jit(solution)/shard_map/adjoint/pallas_call | solution.py:251
  139.1 2.6 %collective-permute-start.28 = (bf16[256,256]{1,0:T(8,128)(2,1)S(1)}, bf16[256,256]{1,0:T(8,128)(2,1)S(1)}, u32[]{:S(2)}, u32[]{:S(2)}) collective-permute-start(bf16[256,256]{1,0:T(8,128)(2,1)S(1)} %get-tuple-element.69), channel_id=1, source_target_pairs={{0,2},{1,3},{2,0},{3,1},{4,6},{5,7},{6,4},{7,5},{8,10},{9,11},{10,... | collective-permute-start | bytes 393224 | tf_op jit(solution)/shard_map/ppermute | solution.py:479
  142.1 2.1 collective-permute-start.30
  144.2 3.6 %forward.7 = (bf16[16,64,256]{2,1,0:T(8,128)(2,1)S(1)}, bf16[16,64,256]{2,1,0:T(8,128)(2,1)S(1)}) custom-call(s32[4]{0:T(128)S(1)} %copy-done.32, bf16[2,4096,128]{2,1,0:T(8,128)(2,1)S(1)} %copy-done.5, bf16[2,4096,128]{2,1,0:T(8,128)(2,1)S(1)} %copy-done.3, bf16[2,16,64,128]{3,2,1,0:T(8,128)(2,1)} %adjoint.5.mine_ref.one_ref, ...), custom_call_target="tpu_custom_call" | custom-call | flops 536870 | bytes 4194 | tf_op jit(solution)/shard_map/forward/pallas_call | solution.py:209
  149.3 2.1 collective-permute-done.29.refs_7_
  152.1 2.0 collective-permute-start.45
  154.6 2.0 collective-permute-start.47
  157.8 7.2 %collective-permute-done.46.refs_2_ = bf16[256,256]{1,0:T(8,128)(2,1)S(1)} collective-permute-done((bf16[256,256]{1,0:T(8,128)(2,1)S(1)}, bf16[256,256]{1,0:T(8,128)(2,1)S(1)}, u32[]{:S(2)}, u32[]{:S(2)}) %collective-permute-start.46) | collective-permute-done | bytes 131104 | tf_op jit(solution)/shard_map/ppermute | solution.py:479
  168.7 2.6 %collective-permute-start.37 = (bf16[256,256]{1,0:T(8,128)(2,1)S(1)}, bf16[256,256]{1,0:T(8,128)(2,1)S(1)}, u32[]{:S(2)}, u32[]{:S(2)}) collective-permute-start(bf16[256,256]{1,0:T(8,128)(2,1)S(1)} %get-tuple-element.80), channel_id=1, source_target_pairs={{0,2},{1,3},{2,0},{3,1},{4,6},{5,7},{6,4},{7,5},{8,10},{9,11},{10,... | collective-permute-start | bytes 393224 | tf_op jit(solution)/shard_map/ppermute | solution.py:479
  171.2 2.4 %collective-permute-start.39 = (bf16[256,256]{1,0:T(8,128)(2,1)S(1)}, bf16[256,256]{1,0:T(8,128)(2,1)S(1)}, u32[]{:S(2)}, u32[]{:S(2)}) collective-permute-start(bf16[256,256]{1,0:T(8,128)(2,1)S(1)} %get-tuple-element.82), channel_id=1, source_target_pairs={{0,6},{1,7},{2,4},{3,5},{4,2},{5,3},{6,0},{7,1},{8,14},{9,15},{10,... | collective-permute-start | bytes 393224 | tf_op jit(solution)/shard_map/ppermute | solution.py:479
  175.2 7.3 %collective-permute-done.38.refs_7_ = bf16[256,256]{1,0:T(8,128)(2,1)S(1)} collective-permute-done((bf16[256,256]{1,0:T(8,128)(2,1)S(1)}, bf16[256,256]{1,0:T(8,128)(2,1)S(1)}, u32[]{:S(2)}, u32[]{:S(2)}) %collective-permute-start.38) | collective-permute-done | bytes 131104 | tf_op jit(solution)/shard_map/ppermute | solution.py:479
  183.2 2.6 %collective-permute-start.50 = (bf16[256,256]{1,0:T(8,128)(2,1)S(1)}, bf16[256,256]{1,0:T(8,128)(2,1)S(1)}, u32[]{:S(2)}, u32[]{:S(2)}) collective-permute-start(bf16[256,256]{1,0:T(8,128)(2,1)S(1)} %get-tuple-element.89.refs_0_), channel_id=1, source_target_pairs={{0,2},{1,3},{2,0},{3,1},{4,6},{5,7},{6,4},{7,5},{8,10},{9,11},{10,... | collective-permute-start | bytes 393224 | tf_op jit(solution)/shard_map/ppermute | solution.py:479
  185.8 2.4 %collective-permute-start.52 = (bf16[256,256]{1,0:T(8,128)(2,1)S(1)}, bf16[256,256]{1,0:T(8,128)(2,1)S(1)}, u32[]{:S(2)}, u32[]{:S(2)}) collective-permute-start(bf16[256,256]{1,0:T(8,128)(2,1)S(1)} %get-tuple-element.89.refs_0_), channel_id=1, source_target_pairs={{0,6},{1,7},{2,4},{3,5},{4,2},{5,3},{6,0},{7,1},{8,14},{9,15},{10,... | collective-permute-start | bytes 393224 | tf_op jit(solution)/shard_map/ppermute | solution.py:479
  188.8 3.1 %collective-permute-done.40 = f32[24,128]{1,0:T(8,128)S(1)} collective-permute-done((f32[24,128]{1,0:T(8,128)S(1)}, f32[24,128]{1,0:T(8,128)S(1)}, u32[]{:S(2)}, u32[]{:S(2)}) %collective-permute-start.40) | collective-permute-done | bytes 12320 | tf_op jit(solution)/shard_map/ppermute | solution.py:479
  191.9 3.7 %collective-permute-done.41 = f32[24,128]{1,0:T(8,128)S(1)} collective-permute-done((f32[24,128]{1,0:T(8,128)S(1)}, f32[24,128]{1,0:T(8,128)S(1)}, u32[]{:S(2)}, u32[]{:S(2)}) %collective-permute-start.41) | collective-permute-done | bytes 12320 | tf_op jit(solution)/shard_map/ppermute | solution.py:476
  195.6 3.4 %adjoint.6 = (bf16[16,64,128]{2,1,0:T(8,128)(2,1)}, f32[16,64,128]{2,1,0:T(8,128)S(1)}) custom-call(s32[4]{0:T(128)S(1)} %copy-done.32, bf16[2,4096,128]{2,1,0:T(8,128)(2,1)S(1)} %copy-done.9, bf16[2,4096,128]{2,1,0:T(8,128)(2,1)} %collective-permute-done.4.far, bf16[16,64,256]{2,1,0:T(8,128)(2,1)S(1)} %bitcast.50, ...), custom_call_target="tpu_custom_call" | custom-call | flops 536870 | bytes 4194 | tf_op jit(solution)/shard_map/adjoint/pallas_call | solution.py:251
  203.3 2.6 %collective-permute-done.43 = f32[24,128]{1,0:T(8,128)S(1)} collective-permute-done((f32[24,128]{1,0:T(8,128)S(1)}, f32[24,128]{1,0:T(8,128)S(1)}, u32[]{:S(2)}, u32[]{:S(2)}) %collective-permute-start.43) | collective-permute-done | bytes 12320 | tf_op jit(solution)/shard_map/ppermute | solution.py:479
  207.5 3.1 %collective-permute-done.44 = f32[24,128]{1,0:T(8,128)S(1)} collective-permute-done((f32[24,128]{1,0:T(8,128)S(1)}, f32[24,128]{1,0:T(8,128)S(1)}, u32[]{:S(2)}, u32[]{:S(2)}) %collective-permute-start.44) | collective-permute-done | bytes 12320 | tf_op jit(solution)/shard_map/ppermute | solution.py:479
  212.9 3.2 %adjoint.7 = (bf16[16,64,128]{2,1,0:T(8,128)(2,1)}, f32[16,64,128]{2,1,0:T(8,128)S(1)}) custom-call(s32[4]{0:T(128)S(1)} %copy-done.32, bf16[2,4096,128]{2,1,0:T(8,128)(2,1)S(1)} %copy-done.6, bf16[2,4096,128]{2,1,0:T(8,128)(2,1)S(1)} %copy-done.3, bf16[16,64,256]{2,1,0:T(8,128)(2,1)} %bitcast.30.own_ref, ...), custom_call_target="tpu_custom_call" | custom-call | flops 536870 | bytes 4194 | tf_op jit(solution)/shard_map/adjoint/pallas_call | solution.py:251
  225.3 1.9 fusion.2
  (207 shorter events, 68.0 us)
Async XLA Ops:
  4.5 18.4 %collective-permute-start.4 = (bf16[2,4096,128]{2,1,0:T(8,128)(2,1)}, bf16[2,4096,128]{2,1,0:T(8,128)(2,1)}, u32[]{:S(2)}, u32[]{:S(2)}) collective-permute-start(bf16[2,4096,128]{2,1,0:T(8,128)(2,1)} %cut.2), channel_id=1, source_target_pairs={{0,8},{8,0},{16,24},{24,16},{1,9},{9,1},{17,25},{25,17},{2,10},{10... | collective-permute-start | bytes 6291464 | tf_op jit(solution)/shard_map/ppermute | solution.py:473
  8.1 27.7 %collective-permute-start.7 = (bf16[2,4096,128]{2,1,0:T(8,128)(2,1)}, bf16[2,4096,128]{2,1,0:T(8,128)(2,1)S(1)}, u32[]{:S(2)}, u32[]{:S(2)}) collective-permute-start(bf16[2,4096,128]{2,1,0:T(8,128)(2,1)} %cut.3.refs_1_), channel_id=1, source_target_pairs={{0,8},{8,0},{16,24},{24,16},{1,9},{9,1},{17,25},{25,17},{2,10},{10... | collective-permute-start | bytes 6291464 | tf_op jit(solution)/shard_map/ppermute | solution.py:473
  8.3 4.5 %collective-permute-start = (f32[16,128]{1,0:T(8,128)S(1)}, f32[16,128]{1,0:T(8,128)S(1)}, u32[]{:S(2)}, u32[]{:S(2)}) collective-permute-start(f32[16,128]{1,0:T(8,128)S(1)} %copy-done.40), channel_id=1, source_target_pairs={{0,1},{1,0},{2,3},{3,2},{4,5},{5,4},{6,7},{7,6},{8,9},{9,8},{10,11... | collective-permute-start | bytes 24584 | tf_op jit(solution)/shard_map/ppermute | solution.py:479
  12.8 5.2 %collective-permute-start.1 = (f32[32,128]{1,0:T(8,128)S(1)}, f32[32,128]{1,0:T(8,128)S(1)}, u32[]{:S(2)}, u32[]{:S(2)}) collective-permute-start(f32[32,128]{1,0:T(8,128)S(1)} %pad_maximum_fusion.3), channel_id=1, source_target_pairs={{0,2},{1,3},{2,0},{3,1},{4,6},{5,7},{6,4},{7,5},{8,10},{9,11},{10,... | collective-permute-start | bytes 49160 | tf_op jit(solution)/shard_map/ppermute | solution.py:479
  15.7 7.2 %collective-permute-start.5 = (bf16[16,64,128]{2,1,0:T(8,128)(2,1)}, bf16[16,64,128]{2,1,0:T(8,128)(2,1)S(1)}, u32[]{:S(2)}, u32[]{:S(2)}) collective-permute-start(bf16[16,64,128]{2,1,0:T(8,128)(2,1)} %cast.2), channel_id=1, source_target_pairs={{0,16},{8,24},{16,0},{24,8},{1,17},{9,25},{17,1},{25,9},{2,18},{10... | collective-permute-start | bytes 786440 | tf_op jit(solution)/shard_map/ppermute | solution.py:476
  29.1 15.2 %collective-permute-start.6 = (bf16[16,64,256]{2,1,0:T(8,128)(2,1)}, bf16[16,64,256]{2,1,0:T(8,128)(2,1)}, u32[]{:S(2)}, u32[]{:S(2)}) collective-permute-start(bf16[16,64,256]{2,1,0:T(8,128)(2,1)} %get-tuple-element.49), channel_id=1, source_target_pairs={{0,1},{1,0},{2,3},{3,2},{4,5},{5,4},{6,7},{7,6},{8,9},{9,8},{10,11... | collective-permute-start | bytes 1572872 | tf_op jit(solution)/shard_map/ppermute | solution.py:479
  31.7 6.4 %collective-permute-start.8 = (bf16[16,64,128]{2,1,0:T(8,128)(2,1)S(1)}, bf16[16,64,128]{2,1,0:T(8,128)(2,1)S(1)}, u32[]{:S(2)}, u32[]{:S(2)}) collective-permute-start(bf16[16,64,128]{2,1,0:T(8,128)(2,1)S(1)} %ordered.4), channel_id=1, source_target_pairs={{0,16},{8,24},{16,0},{24,8},{1,17},{9,25},{17,1},{25,9},{2,18},{10... | collective-permute-start | bytes 786440 | tf_op jit(solution)/shard_map/ppermute | solution.py:476
  33.2 11.7 %collective-permute-start.2 = (f32[64,128]{1,0:T(8,128)S(1)}, f32[64,128]{1,0:T(8,128)S(1)}, u32[]{:S(2)}, u32[]{:S(2)}) collective-permute-start(f32[64,128]{1,0:T(8,128)S(1)} %copy-done.39), channel_id=1, source_target_pairs={{0,4},{1,5},{2,6},{3,7},{4,0},{5,1},{6,2},{7,3},{8,12},{9,13},{10,... | collective-permute-start | bytes 98312 | tf_op jit(solution)/shard_map/ppermute | solution.py:479
  44.4 17.1 %collective-permute-start.12 = (bf16[16,64,256]{2,1,0:T(8,128)(2,1)}, bf16[16,64,256]{2,1,0:T(8,128)(2,1)}, u32[]{:S(2)}, u32[]{:S(2)}) collective-permute-start(bf16[16,64,256]{2,1,0:T(8,128)(2,1)} %ordered.5.refs_0_), channel_id=1, source_target_pairs={{0,1},{1,0},{2,3},{3,2},{4,5},{5,4},{6,7},{7,6},{8,9},{9,8},{10,11... | collective-permute-start | bytes 1572872 | tf_op jit(solution)/shard_map/ppermute | solution.py:479
  45.5 6.0 %collective-permute-start.3 = (f32[2,32,128]{2,1,0:T(8,128)}, f32[2,32,128]{2,1,0:T(8,128)S(1)}, u32[]{:S(2)}, u32[]{:S(2)}) collective-permute-start(f32[2,32,128]{2,1,0:T(8,128)} %get-tuple-element.100), channel_id=1, source_target_pairs={{0,8},{8,0},{16,24},{24,16},{1,9},{9,1},{17,25},{25,17},{2,10},{10... | collective-permute-start | bytes 98312 | tf_op jit(solution)/shard_map/ppermute | solution.py:473
  47.4 12.7 %collective-permute-start.10 = (bf16[256,256]{1,0:T(8,128)(2,1)}, bf16[256,256]{1,0:T(8,128)(2,1)}, u32[]{:S(2)}, u32[]{:S(2)}) collective-permute-start(bf16[256,256]{1,0:T(8,128)(2,1)} %get-tuple-element.53), channel_id=1, source_target_pairs={{0,4},{1,5},{2,6},{3,7},{4,0},{5,1},{6,2},{7,3},{8,12},{9,13},{10,... | collective-permute-start | bytes 393224 | tf_op jit(solution)/shard_map/ppermute | solution.py:479
  50.0 10.1 %collective-permute-start.11 = (bf16[256,256]{1,0:T(8,128)(2,1)}, bf16[256,256]{1,0:T(8,128)(2,1)}, u32[]{:S(2)}, u32[]{:S(2)}) collective-permute-start(bf16[256,256]{1,0:T(8,128)(2,1)} %get-tuple-element.54), channel_id=1, source_target_pairs={{0,6},{1,7},{2,4},{3,5},{4,2},{5,3},{6,0},{7,1},{8,14},{9,15},{10,... | collective-permute-start | bytes 393224 | tf_op jit(solution)/shard_map/ppermute | solution.py:479
  50.0 11.4 %collective-permute-start.9 = (bf16[256,256]{1,0:T(8,128)(2,1)}, bf16[256,256]{1,0:T(8,128)(2,1)}, u32[]{:S(2)}, u32[]{:S(2)}) collective-permute-start(bf16[256,256]{1,0:T(8,128)(2,1)} %get-tuple-element.52), channel_id=1, source_target_pairs={{0,2},{1,3},{2,0},{3,1},{4,6},{5,7},{6,4},{7,5},{8,10},{9,11},{10,... | collective-permute-start | bytes 393224 | tf_op jit(solution)/shard_map/ppermute | solution.py:479
  63.3 7.2 %collective-permute-start.19 = (bf16[256,256]{1,0:T(8,128)(2,1)S(1)}, bf16[256,256]{1,0:T(8,128)(2,1)S(1)}, u32[]{:S(2)}, u32[]{:S(2)}) collective-permute-start(bf16[256,256]{1,0:T(8,128)(2,1)S(1)} %get-tuple-element.63.refs_0_), channel_id=1, source_target_pairs={{0,2},{1,3},{2,0},{3,1},{4,6},{5,7},{6,4},{7,5},{8,10},{9,11},{10,... | collective-permute-start | bytes 393224 | tf_op jit(solution)/shard_map/ppermute | solution.py:479
  65.2 12.9 %collective-permute-start.20 = (bf16[256,256]{1,0:T(8,128)(2,1)S(1)}, bf16[256,256]{1,0:T(8,128)(2,1)S(1)}, u32[]{:S(2)}, u32[]{:S(2)}) collective-permute-start(bf16[256,256]{1,0:T(8,128)(2,1)S(1)} %get-tuple-element.63.refs_0_), channel_id=1, source_target_pairs={{0,4},{1,5},{2,6},{3,7},{4,0},{5,1},{6,2},{7,3},{8,12},{9,13},{10,... | collective-permute-start | bytes 393224 | tf_op jit(solution)/shard_map/ppermute | solution.py:479
  66.4 11.7 %collective-permute-start.21 = (bf16[256,256]{1,0:T(8,128)(2,1)S(1)}, bf16[256,256]{1,0:T(8,128)(2,1)S(1)}, u32[]{:S(2)}, u32[]{:S(2)}) collective-permute-start(bf16[256,256]{1,0:T(8,128)(2,1)S(1)} %get-tuple-element.63.refs_0_), channel_id=1, source_target_pairs={{0,6},{1,7},{2,4},{3,5},{4,2},{5,3},{6,0},{7,1},{8,14},{9,15},{10,... | collective-permute-start | bytes 393224 | tf_op jit(solution)/shard_map/ppermute | solution.py:479
  78.7 11.2 %collective-permute-start.22 = (bf16[16,64,256]{2,1,0:T(8,128)(2,1)S(1)}, bf16[16,64,256]{2,1,0:T(8,128)(2,1)S(1)}, u32[]{:S(2)}, u32[]{:S(2)}) collective-permute-start(bf16[16,64,256]{2,1,0:T(8,128)(2,1)S(1)} %bitcast.47), channel_id=1, source_target_pairs={{0,1},{1,0},{2,3},{3,2},{4,5},{5,4},{6,7},{7,6},{8,9},{9,8},{10,11... | collective-permute-start | bytes 1572872 | tf_op jit(solution)/shard_map/ppermute | solution.py:479
  81.6 13.6 %collective-permute-start.13 = (bf16[256,256]{1,0:T(8,128)(2,1)S(1)}, bf16[256,256]{1,0:T(8,128)(2,1)S(1)}, u32[]{:S(2)}, u32[]{:S(2)}) collective-permute-start(bf16[256,256]{1,0:T(8,128)(2,1)S(1)} %get-tuple-element.58), channel_id=1, source_target_pairs={{0,2},{1,3},{2,0},{3,1},{4,6},{5,7},{6,4},{7,5},{8,10},{9,11},{10,... | collective-permute-start | bytes 393224 | tf_op jit(solution)/shard_map/ppermute | solution.py:479
  83.9 11.6 %collective-permute-start.14 = (bf16[256,256]{1,0:T(8,128)(2,1)S(1)}, bf16[256,256]{1,0:T(8,128)(2,1)S(1)}, u32[]{:S(2)}, u32[]{:S(2)}) collective-permute-start(bf16[256,256]{1,0:T(8,128)(2,1)S(1)} %get-tuple-element.59), channel_id=1, source_target_pairs={{0,4},{1,5},{2,6},{3,7},{4,0},{5,1},{6,2},{7,3},{8,12},{9,13},{10,... | collective-permute-start | bytes 393224 | tf_op jit(solution)/shard_map/ppermute | solution.py:479
  84.7 10.8 %collective-permute-start.15 = (bf16[256,256]{1,0:T(8,128)(2,1)S(1)}, bf16[256,256]{1,0:T(8,128)(2,1)S(1)}, u32[]{:S(2)}, u32[]{:S(2)}) collective-permute-start(bf16[256,256]{1,0:T(8,128)(2,1)S(1)} %get-tuple-element.60), channel_id=1, source_target_pairs={{0,6},{1,7},{2,4},{3,5},{4,2},{5,3},{6,0},{7,1},{8,14},{9,15},{10,... | collective-permute-start | bytes 393224 | tf_op jit(solution)/shard_map/ppermute | solution.py:479
  92.9 20.6 %collective-permute-start.23 = (bf16[2,16,64,128]{3,2,1,0:T(8,128)(2,1)S(1)}, bf16[2,16,64,128]{3,2,1,0:T(8,128)(2,1)S(1)}, u32[]{:S(2)}, u32[]{:S(2)}) collective-permute-start(bf16[2,16,64,128]{3,2,1,0:T(8,128)(2,1)S(1)} %adjoint.4.one_ref.mine_ref.refs_4_), channel_id=1, source_target_pairs={{0,16},{8,24},{16,0},{24,8},{1,17},{9,25},{17,1},{25,9},{2,18},{10... | collective-permute-start | bytes 1572872 | tf_op jit(solution)/shard_map/ppermute | solution.py:476
  96.8 14.6 %collective-permute-start.31 = (bf16[256,256]{1,0:T(8,128)(2,1)S(1)}, bf16[256,256]{1,0:T(8,128)(2,1)S(1)}, u32[]{:S(2)}, u32[]{:S(2)}) collective-permute-start(bf16[256,256]{1,0:T(8,128)(2,1)S(1)} %get-tuple-element.75.refs_0_), channel_id=1, source_target_pairs={{0,2},{1,3},{2,0},{3,1},{4,6},{5,7},{6,4},{7,5},{8,10},{9,11},{10,... | collective-permute-start | bytes 393224 | tf_op jit(solution)/shard_map/ppermute | solution.py:479
  100.5 11.0 %collective-permute-start.32 = (bf16[256,256]{1,0:T(8,128)(2,1)S(1)}, bf16[256,256]{1,0:T(8,128)(2,1)S(1)}, u32[]{:S(2)}, u32[]{:S(2)}) collective-permute-start(bf16[256,256]{1,0:T(8,128)(2,1)S(1)} %get-tuple-element.75.refs_0_), channel_id=1, source_target_pairs={{0,4},{1,5},{2,6},{3,7},{4,0},{5,1},{6,2},{7,3},{8,12},{9,13},{10,... | collective-permute-start | bytes 393224 | tf_op jit(solution)/shard_map/ppermute | solution.py:479
  101.1 10.4 %collective-permute-start.33 = (bf16[256,256]{1,0:T(8,128)(2,1)S(1)}, bf16[256,256]{1,0:T(8,128)(2,1)S(1)}, u32[]{:S(2)}, u32[]{:S(2)}) collective-permute-start(bf16[256,256]{1,0:T(8,128)(2,1)S(1)} %get-tuple-element.75.refs_0_), channel_id=1, source_target_pairs={{0,6},{1,7},{2,4},{3,5},{4,2},{5,3},{6,0},{7,1},{8,14},{9,15},{10,... | collective-permute-start | bytes 393224 | tf_op jit(solution)/shard_map/ppermute | solution.py:479
  112.0 14.2 %collective-permute-start.34 = (bf16[16,64,256]{2,1,0:T(8,128)(2,1)S(1)}, bf16[16,64,256]{2,1,0:T(8,128)(2,1)S(1)}, u32[]{:S(2)}, u32[]{:S(2)}) collective-permute-start(bf16[16,64,256]{2,1,0:T(8,128)(2,1)S(1)} %bitcast.45), channel_id=1, source_target_pairs={{0,1},{1,0},{2,3},{3,2},{4,5},{5,4},{6,7},{7,6},{8,9},{9,8},{10,11... | collective-permute-start | bytes 1572872 | tf_op jit(solution)/shard_map/ppermute | solution.py:479
  117.8 3.8 %collective-permute-start.24 = (f32[24,128]{1,0:T(8,128)S(1)}, f32[24,128]{1,0:T(8,128)S(1)}, u32[]{:S(2)}, u32[]{:S(2)}) collective-permute-start(f32[24,128]{1,0:T(8,128)S(1)} %ordered.6), channel_id=1, source_target_pairs={{0,2},{1,3},{2,0},{3,1},{4,6},{5,7},{6,4},{7,5},{8,10},{9,11},{10,... | collective-permute-start | bytes 36872 | tf_op jit(solution)/shard_map/ppermute | solution.py:479
  121.6 4.6 %collective-permute-start.25 = (f32[24,128]{1,0:T(8,128)S(1)}, f32[24,128]{1,0:T(8,128)S(1)}, u32[]{:S(2)}, u32[]{:S(2)}) collective-permute-start(f32[24,128]{1,0:T(8,128)S(1)} %add.106), channel_id=1, source_target_pairs={{0,4},{1,5},{2,6},{3,7},{4,0},{5,1},{6,2},{7,3},{8,12},{9,13},{10,... | collective-permute-start | bytes 36872 | tf_op jit(solution)/shard_map/ppermute | solution.py:479
  123.8 12.7 %collective-permute-start.27 = (bf16[16,64,256]{2,1,0:T(8,128)(2,1)}, bf16[16,64,256]{2,1,0:T(8,128)(2,1)}, u32[]{:S(2)}, u32[]{:S(2)}) collective-permute-start(bf16[16,64,256]{2,1,0:T(8,128)(2,1)} %get-tuple-element.64.refs_1_.refs_0_), channel_id=1, source_target_pairs={{0,1},{1,0},{2,3},{3,2},{4,5},{5,4},{6,7},{7,6},{8,9},{9,8},{10,11... | collective-permute-start | bytes 1572872 | tf_op jit(solution)/shard_map/ppermute | solution.py:479
  129.3 14.9 %collective-permute-start.35 = (bf16[2,16,64,128]{3,2,1,0:T(8,128)(2,1)}, bf16[2,16,64,128]{3,2,1,0:T(8,128)(2,1)}, u32[]{:S(2)}, u32[]{:S(2)}) collective-permute-start(bf16[2,16,64,128]{3,2,1,0:T(8,128)(2,1)} %adjoint.5.mine_ref.one_ref), channel_id=1, source_target_pairs={{0,16},{8,24},{16,0},{24,8},{1,17},{9,25},{17,1},{25,9},{2,18},{10... | collective-permute-start | bytes 1572872 | tf_op jit(solution)/shard_map/ppermute | solution.py:476
  130.3 19.0 %collective-permute-start.26 = (f32[32]{0:T(128)S(1)}, f32[32]{0:T(128)S(1)}, u32[]{:S(2)}, u32[]{:S(2)}) collective-permute-start(f32[32]{0:T(128)S(1)} %copy-done.37), channel_id=1, source_target_pairs={{0,16},{8,24},{16,0},{24,8},{1,17},{9,25},{17,1},{25,9},{2,18},{10... | collective-permute-start | bytes 392 | tf_op jit(solution)/shard_map/ppermute | solution.py:476
  139.1 10.2 %collective-permute-start.28 = (bf16[256,256]{1,0:T(8,128)(2,1)S(1)}, bf16[256,256]{1,0:T(8,128)(2,1)S(1)}, u32[]{:S(2)}, u32[]{:S(2)}) collective-permute-start(bf16[256,256]{1,0:T(8,128)(2,1)S(1)} %get-tuple-element.69), channel_id=1, source_target_pairs={{0,2},{1,3},{2,0},{3,1},{4,6},{5,7},{6,4},{7,5},{8,10},{9,11},{10,... | collective-permute-start | bytes 393224 | tf_op jit(solution)/shard_map/ppermute | solution.py:479
  141.7 9.7 %collective-permute-start.29 = (bf16[256,256]{1,0:T(8,128)(2,1)S(1)}, bf16[256,256]{1,0:T(8,128)(2,1)S(1)}, u32[]{:S(2)}, u32[]{:S(2)}) collective-permute-start(bf16[256,256]{1,0:T(8,128)(2,1)S(1)} %get-tuple-element.70), channel_id=1, source_target_pairs={{0,4},{1,5},{2,6},{3,7},{4,0},{5,1},{6,2},{7,3},{8,12},{9,13},{10,... | collective-permute-start | bytes 393224 | tf_op jit(solution)/shard_map/ppermute | solution.py:479
  142.1 9.3 %collective-permute-start.30 = (bf16[256,256]{1,0:T(8,128)(2,1)S(1)}, bf16[256,256]{1,0:T(8,128)(2,1)S(1)}, u32[]{:S(2)}, u32[]{:S(2)}) collective-permute-start(bf16[256,256]{1,0:T(8,128)(2,1)S(1)} %get-tuple-element.71), channel_id=1, source_target_pairs={{0,6},{1,7},{2,4},{3,5},{4,2},{5,3},{6,0},{7,1},{8,14},{9,15},{10,... | collective-permute-start | bytes 393224 | tf_op jit(solution)/shard_map/ppermute | solution.py:479
  147.8 20.2 %collective-permute-start.36 = (bf16[16,64,256]{2,1,0:T(8,128)(2,1)S(1)}, bf16[16,64,256]{2,1,0:T(8,128)(2,1)S(1)}, u32[]{:S(2)}, u32[]{:S(2)}) collective-permute-start(bf16[16,64,256]{2,1,0:T(8,128)(2,1)S(1)} %ordered.7), channel_id=1, source_target_pairs={{0,1},{1,0},{2,3},{3,2},{4,5},{5,4},{6,7},{7,6},{8,9},{9,8},{10,11... | collective-permute-start | bytes 1572872 | tf_op jit(solution)/shard_map/ppermute | solution.py:479
  152.1 5.8 %collective-permute-start.45 = (bf16[256,256]{1,0:T(8,128)(2,1)S(1)}, bf16[256,256]{1,0:T(8,128)(2,1)S(1)}, u32[]{:S(2)}, u32[]{:S(2)}) collective-permute-start(bf16[256,256]{1,0:T(8,128)(2,1)S(1)} %get-tuple-element.86.refs_0_), channel_id=1, source_target_pairs={{0,2},{1,3},{2,0},{3,1},{4,6},{5,7},{6,4},{7,5},{8,10},{9,11},{10,... | collective-permute-start | bytes 393224 | tf_op jit(solution)/shard_map/ppermute | solution.py:479
  154.1 10.9 %collective-permute-start.46 = (bf16[256,256]{1,0:T(8,128)(2,1)S(1)}, bf16[256,256]{1,0:T(8,128)(2,1)S(1)}, u32[]{:S(2)}, u32[]{:S(2)}) collective-permute-start(bf16[256,256]{1,0:T(8,128)(2,1)S(1)} %get-tuple-element.86.refs_0_), channel_id=1, source_target_pairs={{0,4},{1,5},{2,6},{3,7},{4,0},{5,1},{6,2},{7,3},{8,12},{9,13},{10,... | collective-permute-start | bytes 393224 | tf_op jit(solution)/shard_map/ppermute | solution.py:479
  154.6 10.4 %collective-permute-start.47 = (bf16[256,256]{1,0:T(8,128)(2,1)S(1)}, bf16[256,256]{1,0:T(8,128)(2,1)S(1)}, u32[]{:S(2)}, u32[]{:S(2)}) collective-permute-start(bf16[256,256]{1,0:T(8,128)(2,1)S(1)} %get-tuple-element.86.refs_0_), channel_id=1, source_target_pairs={{0,6},{1,7},{2,4},{3,5},{4,2},{5,3},{6,0},{7,1},{8,14},{9,15},{10,... | collective-permute-start | bytes 393224 | tf_op jit(solution)/shard_map/ppermute | solution.py:479
  165.6 30.0 %collective-permute-start.48 = (bf16[16,64,256]{2,1,0:T(8,128)(2,1)S(1)}, bf16[16,64,256]{2,1,0:T(8,128)(2,1)S(1)}, u32[]{:S(2)}, u32[]{:S(2)}) collective-permute-start(bf16[16,64,256]{2,1,0:T(8,128)(2,1)S(1)} %bitcast.49), channel_id=1, source_target_pairs={{0,1},{1,0},{2,3},{3,2},{4,5},{5,4},{6,7},{7,6},{8,9},{9,8},{10,11... | collective-permute-start | bytes 1572872 | tf_op jit(solution)/shard_map/ppermute | solution.py:479
  168.7 6.5 %collective-permute-start.37 = (bf16[256,256]{1,0:T(8,128)(2,1)S(1)}, bf16[256,256]{1,0:T(8,128)(2,1)S(1)}, u32[]{:S(2)}, u32[]{:S(2)}) collective-permute-start(bf16[256,256]{1,0:T(8,128)(2,1)S(1)} %get-tuple-element.80), channel_id=1, source_target_pairs={{0,2},{1,3},{2,0},{3,1},{4,6},{5,7},{6,4},{7,5},{8,10},{9,11},{10,... | collective-permute-start | bytes 393224 | tf_op jit(solution)/shard_map/ppermute | solution.py:479
  171.2 11.2 %collective-permute-start.38 = (bf16[256,256]{1,0:T(8,128)(2,1)S(1)}, bf16[256,256]{1,0:T(8,128)(2,1)S(1)}, u32[]{:S(2)}, u32[]{:S(2)}) collective-permute-start(bf16[256,256]{1,0:T(8,128)(2,1)S(1)} %get-tuple-element.81), channel_id=1, source_target_pairs={{0,4},{1,5},{2,6},{3,7},{4,0},{5,1},{6,2},{7,3},{8,12},{9,13},{10,... | collective-permute-start | bytes 393224 | tf_op jit(solution)/shard_map/ppermute | solution.py:479
  171.2 11.2 %collective-permute-start.39 = (bf16[256,256]{1,0:T(8,128)(2,1)S(1)}, bf16[256,256]{1,0:T(8,128)(2,1)S(1)}, u32[]{:S(2)}, u32[]{:S(2)}) collective-permute-start(bf16[256,256]{1,0:T(8,128)(2,1)S(1)} %get-tuple-element.82), channel_id=1, source_target_pairs={{0,6},{1,7},{2,4},{3,5},{4,2},{5,3},{6,0},{7,1},{8,14},{9,15},{10,... | collective-permute-start | bytes 393224 | tf_op jit(solution)/shard_map/ppermute | solution.py:479
  183.2 15.9 %collective-permute-start.50 = (bf16[256,256]{1,0:T(8,128)(2,1)S(1)}, bf16[256,256]{1,0:T(8,128)(2,1)S(1)}, u32[]{:S(2)}, u32[]{:S(2)}) collective-permute-start(bf16[256,256]{1,0:T(8,128)(2,1)S(1)} %get-tuple-element.89.refs_0_), channel_id=1, source_target_pairs={{0,2},{1,3},{2,0},{3,1},{4,6},{5,7},{6,4},{7,5},{8,10},{9,11},{10,... | collective-permute-start | bytes 393224 | tf_op jit(solution)/shard_map/ppermute | solution.py:479
  185.8 13.3 %collective-permute-start.51 = (bf16[256,256]{1,0:T(8,128)(2,1)S(1)}, bf16[256,256]{1,0:T(8,128)(2,1)S(1)}, u32[]{:S(2)}, u32[]{:S(2)}) collective-permute-start(bf16[256,256]{1,0:T(8,128)(2,1)S(1)} %get-tuple-element.89.refs_0_), channel_id=1, source_target_pairs={{0,4},{1,5},{2,6},{3,7},{4,0},{5,1},{6,2},{7,3},{8,12},{9,13},{10,... | collective-permute-start | bytes 393224 | tf_op jit(solution)/shard_map/ppermute | solution.py:479
  185.8 13.3 %collective-permute-start.52 = (bf16[256,256]{1,0:T(8,128)(2,1)S(1)}, bf16[256,256]{1,0:T(8,128)(2,1)S(1)}, u32[]{:S(2)}, u32[]{:S(2)}) collective-permute-start(bf16[256,256]{1,0:T(8,128)(2,1)S(1)} %get-tuple-element.89.refs_0_), channel_id=1, source_target_pairs={{0,6},{1,7},{2,4},{3,5},{4,2},{5,3},{6,0},{7,1},{8,14},{9,15},{10,... | collective-permute-start | bytes 393224 | tf_op jit(solution)/shard_map/ppermute | solution.py:479
  200.5 10.9 %collective-permute-start.53 = (bf16[16,64,256]{2,1,0:T(8,128)(2,1)}, bf16[16,64,256]{2,1,0:T(8,128)(2,1)}, u32[]{:S(2)}, u32[]{:S(2)}) collective-permute-start(bf16[16,64,256]{2,1,0:T(8,128)(2,1)} %bitcast.30.own_ref), channel_id=1, source_target_pairs={{0,1},{1,0},{2,3},{3,2},{4,5},{5,4},{6,7},{7,6},{8,9},{9,8},{10,11... | collective-permute-start | bytes 1572872 | tf_op jit(solution)/shard_map/ppermute | solution.py:479
  201.1 9.8 %collective-permute-start.49 = (bf16[16,64,128]{2,1,0:T(8,128)(2,1)}, bf16[16,64,128]{2,1,0:T(8,128)(2,1)S(1)}, u32[]{:S(2)}, u32[]{:S(2)}) collective-permute-start(bf16[16,64,128]{2,1,0:T(8,128)(2,1)} %get-tuple-element.88.refs_4_), channel_id=1, source_target_pairs={{0,16},{8,24},{16,0},{24,8},{1,17},{9,25},{17,1},{25,9},{2,18},{10... | collective-permute-start | bytes 786440 | tf_op jit(solution)/shard_map/ppermute | solution.py:476
  206.0 4.6 %collective-permute-start.44 = (f32[24,128]{1,0:T(8,128)S(1)}, f32[24,128]{1,0:T(8,128)S(1)}, u32[]{:S(2)}, u32[]{:S(2)}) collective-permute-start(f32[24,128]{1,0:T(8,128)S(1)} %add.112), channel_id=1, source_target_pairs={{0,4},{1,5},{2,6},{3,7},{4,0},{5,1},{6,2},{7,3},{8,12},{9,13},{10,... | collective-permute-start | bytes 36872 | tf_op jit(solution)/shard_map/ppermute | solution.py:479
  216.9 7.1 %collective-permute-start.54 = (bf16[16,64,128]{2,1,0:T(8,128)(2,1)}, bf16[16,64,128]{2,1,0:T(8,128)(2,1)}, u32[]{:S(2)}, u32[]{:S(2)}) collective-permute-start(bf16[16,64,128]{2,1,0:T(8,128)(2,1)} %get-tuple-element.91), channel_id=1, source_target_pairs={{0,16},{8,24},{16,0},{24,8},{1,17},{9,25},{17,1},{25,9},{2,18},{10... | collective-permute-start | bytes 786440 | tf_op jit(solution)/shard_map/ppermute | solution.py:476
  (48 other events, 457.6 us)
